TPU v7x, 128 devices: a whole 4x4x4 slice. The times are simulated.
128 devices in a mesh: policy: 4 (over x_lo, core), fsdp: 32 (over y, z, x_hi).
Axes of the slice: x: 4 (x_hi: 2, x_lo: 2; x = x_hi * 2 + x_lo), y: 4, z: 4, core: 2. Of those that a mesh axis runs over, the one named last changes fastest.
Arguments:
- policies: float32 [4, 8192, 8192], P('policy', 'fsdp'), may hold values from -6 to 6
- anchor: bfloat16 [8192, 8192], P(None, 'fsdp'), may hold values from -6 to 6
Outputs:
- blended: float32 [8192, 8192], P('fsdp')
- next_anchor: bfloat16 [8192, 8192], P(None, 'fsdp')
All inputs are finite; a program needn't handle non-finite values.
Results may differ from a plain program's by a relative error of at most 0.0065.
Values may be sent and summed in bfloat16 or wider, within the bound.
No kernel may reach another device: no remote copies, remote signals or barrier semaphores. Data moves between devices by JAX's collectives and lax.ppermute only.
A program may use at most 128 MiB of HBM per device.

v0:
```python
import jax
import jax.numpy as jnp
from jax import lax
from jax.sharding import PartitionSpec as P

blend_rate = 0.3


def per_device(policies, anchor):
    local_rows = policies[0]
    groups = lax.axis_size("policy")
    total_sum = lax.psum(local_rows.astype(jnp.bfloat16), "policy").astype(jnp.float32)
    average = total_sum / groups
    fetched = lax.all_to_all(anchor, "fsdp", split_axis=0, concat_axis=1, tiled=True)
    blended = (1.0 - blend_rate) * fetched.astype(jnp.float32) + blend_rate * average
    returned = lax.all_to_all(
        blended.astype(jnp.bfloat16), "fsdp", split_axis=1, concat_axis=0, tiled=True
    )
    return (blended, returned)


def solution(mesh):
    return jax.shard_map(
        per_device,
        mesh=mesh,
        in_specs=(P("policy", "fsdp", None), P(None, "fsdp")),
        out_specs=(P("fsdp", None), P(None, "fsdp")),
        check_vma=False,
    )
```

profile of v0, /device:TPU:1, one launch (start us, length us, event | category | flops | bytes accessed | tf_op | source)
XLA Modules:
  0.0 251.4 jit_solution(108791732416150392)
XLA Ops:
  7.2 11.5 %all-to-all-start = ((bf16[32,256,256]{2,1,0:T(8,128)(2,1)}), bf16[32,256,256]{2,1,0:T(8,128)(2,1)}, u32[]{:S(2)}, u32[]{:S(2)}) async-start(bf16[32,256,256]{2,1,0:T(8,128)(2,1)} %bitcast.14), calls=%async_computation | async-start | bytes 8388608 | tf_op jit(solution)/shard_map/all_to_all | solution.py:14
  18.7 0.0 all-reduce.2.cloned.1.call-start
  18.7 7.2 %copy.8 = bf16[1,256,8192]{1,2,0:T(8,128)(2,1)} copy(f32[1,256,8192]{2,1,0:T(8,128)} %param.2) | data formatting | bytes 12582912 | tf_op args[0]
  25.9 0.0 all-reduce.2.cloned.1.call-update
  26.0 76.0 %all-to-all-done = bf16[32,256,256]{2,1,0:T(8,128)(2,1)} async-done(((bf16[32,256,256]{2,1,0:T(8,128)(2,1)}), bf16[32,256,256]{2,1,0:T(8,128)(2,1)}, u32[]{:S(2)}, u32[]{:S(2)}) %all-to-all-start) | async-done | bytes 4194336 | tf_op jit(solution)/shard_map/all_to_all | solution.py:14
  101.9 6.4 %copy.7 = bf16[32,256,256]{1,2,0:T(8,128)(2,1)} copy(bf16[32,256,256]{2,1,0:T(8,128)(2,1)} %all-to-all-done) | data formatting | bytes 8388608 | tf_op jit(solution)/shard_map/all_to_all | solution.py:14
  108.4 6.7 %convert_multiply_fusion = f32[32,256,256]{1,2,0:T(8,128)} fusion(bf16[32,256,256]{1,2,0:T(8,128)(2,1)} %copy.7), kind=kLoop, calls=%fused_computation.1 | loop fusion | flops 4194304 | bytes 12582912 | tf_op jit(solution)/shard_map/mul | solution.py:15
  115.1 39.2 %all-reduce.2.cloned.1.call-done = bf16[256,8192]{0,1:T(8,128)(2,1)} async-done(((bf16[256,8192]{0,1:T(8,128)(2,1)}), bf16[256,8192]{0,1:T(8,128)(2,1)}) %all-reduce.2.cloned.1.call-update) | async-done | bytes 4194320 | tf_op jit(solution)/shard_map/psum | solution.py:12
  154.2 10.6 %fusion = (bf16[256,8192]{0,1:T(8,128)(2,1)}, f32[256,8192]{0,1:T(8,128)}) fusion(bf16[256,8192]{0,1:T(8,128)(2,1)} %all-reduce.2.cloned.1.call-done, f32[32,256,256]{1,2,0:T(8,128)} %convert_multiply_fusion), kind=kLoop, calls=%fused_computation.3 | loop fusion | flops 8388608 | bytes 25165824 | tf_op jit(solution)/shard_map/convert_element_type | solution.py:17
  164.8 9.2 %all-to-all-start.1 = ((bf16[256,32,256]{0,2,1:T(8,128)(2,1)}), bf16[256,32,256]{0,2,1:T(8,128)(2,1)}, u32[]{:S(2)}, u32[]{:S(2)}) async-start(bf16[256,32,256]{0,2,1:T(8,128)(2,1)} %bitcast.13), calls=%async_computation.1 | async-start | bytes 8388608 | tf_op jit(solution)/shard_map/all_to_all | solution.py:16
  174.0 8.9 %copy.10 = f32[256,8192]{1,0:T(8,128)} copy(f32[256,8192]{0,1:T(8,128)} %get-tuple-element.5) | data formatting | bytes 16777216
  182.9 55.2 %all-to-all-done.1 = bf16[256,32,256]{0,2,1:T(8,128)(2,1)} async-done(((bf16[256,32,256]{0,2,1:T(8,128)(2,1)}), bf16[256,32,256]{0,2,1:T(8,128)(2,1)}, u32[]{:S(2)}, u32[]{:S(2)}) %all-to-all-start.1) | async-done | bytes 4194336 | tf_op jit(solution)/shard_map/all_to_all | solution.py:16
  238.1 6.4 %copy.9 = bf16[32,256,256]{2,1,0:T(8,128)(2,1)} copy(bf16[32,256,256]{1,2,0:T(8,128)(2,1)} %bitcast.5) | data formatting | bytes 8388608 | tf_op jit(solution)/shard_map/all_to_all | solution.py:16
Async XLA Ops:
  7.2 94.8 %all-to-all-start = ((bf16[32,256,256]{2,1,0:T(8,128)(2,1)}), bf16[32,256,256]{2,1,0:T(8,128)(2,1)}, u32[]{:S(2)}, u32[]{:S(2)}) async-start(bf16[32,256,256]{2,1,0:T(8,128)(2,1)} %bitcast.14), calls=%async_computation | async-start | bytes 8388608 | tf_op jit(solution)/shard_map/all_to_all | solution.py:14
  18.7 135.6 %all-reduce.2.cloned.1.call-start = ((), (), s32[]{:S(2)}) async-start(), calls=%async_computation.2 | async-start | bytes 8388608 | tf_op jit(solution)/shard_map/psum | solution.py:12
  164.8 73.3 %all-to-all-start.1 = ((bf16[256,32,256]{0,2,1:T(8,128)(2,1)}), bf16[256,32,256]{0,2,1:T(8,128)(2,1)}, u32[]{:S(2)}, u32[]{:S(2)}) async-start(bf16[256,32,256]{0,2,1:T(8,128)(2,1)} %bitcast.13), calls=%async_computation.1 | async-start | bytes 8388608 | tf_op jit(solution)/shard_map/all_to_all | solution.py:16
Sparse Core Ops, SparseCore 0:
  26.1 128.1 all-reduce.1
where the time goes:
time: 255 us; the launch traced here: 251 us
  waiting for transfers between devices  170 us (67%)
  local copies, waits for them, and re-layouts  29 us (11%)
  starting transfers between devices  20.8 us (8%)
  other arithmetic  17.2 us (7%)
  between operations  14 us (5%)
    all_to_all x1, waiting for transfers between devices, per_device(): lax.all_to_all(anchor, 'fsdp', split_axis=0, concat_axis=1, tiled=True)  76 us
    all_to_all x1, waiting for transfers between devices, per_device(): lax.all_to_all(blended.astype(jnp.bfloat16), 'fsdp', split_axis=1, concat...  55.2 us
    psum x1, waiting for transfers between devices, per_device(): lax.psum(local_rows.astype(jnp.bfloat16), 'policy').astype(jnp.float32)  39.2 us
    unnamed x2, local copies, waits for them, and re-layouts  16.1 us
    all_to_all x1, starting transfers between devices, per_device(): lax.all_to_all(anchor, 'fsdp', split_axis=0, concat_axis=1, tiled=True)  11.5 us
    convert_element_type x1, other arithmetic, per_device(): blended.astype(jnp.bfloat16)  10.6 us
    all_to_all x1, starting transfers between devices, per_device(): lax.all_to_all(blended.astype(jnp.bfloat16), 'fsdp', split_axis=1, concat...  9.23 us
    mul x1, other arithmetic, per_device(): (1.0 - blend_rate) * fetched.astype(jnp.float32) + blend_rate * average  6.68 us
  transfers between devices with their start and end apart: 3, of which 3 were waited for; matrix products, arithmetic and copies ran while one was open for 12% of the time, Pallas kernels for 0%

commit v1 on v0

v1 whole, which is shorter than its diff:
```python
import jax
import jax.numpy as jnp
import numpy as np
from jax import lax
from jax.experimental import pallas as pl
from jax.experimental.pallas import tpu as pltpu
from jax.sharding import Mesh, PartitionSpec as P

blend_rate = 0.3

AXES = ("xl", "c", "y", "z", "xh")
SIZES = (2, 2, 4, 4, 2)
SHARDS = 32
ROWS = 256
WIDTH = 256
D = 8192
HALF = 128
QUARTER = 64
R = 32
BF = jnp.bfloat16
F32 = jnp.float32
VMEM_LIMIT = 10 << 20
PARTS = 8
PER = SHARDS // PARTS
SUM_COST = 30 << 20
WRITE_COST = 11 << 20
LAST_COST = 37 << 20
HBM = pl.BlockSpec(memory_space=pltpu.HBM)
VMEM = pl.BlockSpec(memory_space=pltpu.VMEM)
TOKEN = pltpu.VMEM((8, 128), jnp.int32)


def exchange_groups():
    ids = np.arange(128).reshape(SIZES)
    return [
        [int(ids[flip ^ xh, c, y, z, xh]) for y in range(4) for z in range(4) for xh in range(2)]
        for flip in range(2)
        for c in range(2)
    ]


def in_vmem(x):
    return pltpu.with_memory_space_constraint(x, pltpu.VMEM)


class Order:
    def __init__(self, place):
        self.place = place
        self.token = None

    def run(self, body, name, args, specs, outs, out_specs, scratch, aliases=None, size=1024):
        held = [] if self.token is None else [self.token]

        def ordered(at, *refs):
            ins, rest = refs[: len(args)], refs[len(args) + len(held) :]
            results, token, others = rest[: len(outs)], rest[len(outs)], rest[len(outs) + 1 :]
            body(at, *ins, *results, *others)
            token[...] = jnp.zeros_like(token)

        *results, self.token = pl.pallas_call(
            ordered,
            out_shape=[*outs, TOKEN],
            grid_spec=pltpu.PrefetchScalarGridSpec(
                num_scalar_prefetch=1,
                grid=(),
                in_specs=[*specs, *[VMEM] * len(held)],
                out_specs=[*out_specs, VMEM],
                scratch_shapes=scratch,
            ),
            input_output_aliases=aliases or {},
            compiler_params=pltpu.CompilerParams(vmem_limit_bytes=VMEM_LIMIT),
            cost_estimate=pl.CostEstimate(flops=0, bytes_accessed=size, transcendentals=0),
            name=name,
        )(self.place, *args, *held)
        return results


def columns(g):
    return pl.ds(pl.multiple_of(g * WIDTH, WIDTH), WIDTH)


def each(count, work):
    pl.loop(0, count)(work)


def first_row(at, core, chip, start, xl=None):
    xl = at[0] if xl is None else xl
    half = at[1] if core else 1 - at[1]
    quarter = xl if chip else 1 - xl
    return pl.multiple_of(half * HALF + quarter * QUARTER + start, 16)


def member_row(at, where, xh):
    differs = at[2] if xh == 0 else 1 - at[2]
    return first_row(at, *where, at[0] + differs - 2 * at[0] * differs)


def tiles_out(rows):
    return pltpu.VMEM((SHARDS, rows, WIDTH), BF)


def span_of(p):
    return pl.ds(pl.multiple_of(p * PER * WIDTH, WIDTH), PER * WIDTH)


def cast_rows(order, policy):
    def body(at, x_ref, o_ref, wide, sems):
        held = pl.ds(first_row(at, False, False, 0), QUARTER)

        def copy(p):
            return pltpu.make_async_copy(x_ref.at[held, span_of(p)], wide.at[:, span_of(p)], sems.at[p])

        def work(p):
            copy(p).wait()
            for k in range(PER):
                g = p * PER + k
                o_ref[g] = wide[:, columns(g)].astype(BF)

        each(PARTS, lambda p: copy(p).start())
        each(PARTS, work)

    (out,) = order.run(
        body,
        "cast_rows",
        (policy,),
        [HBM],
        [tiles_out(QUARTER)],
        [VMEM],
        [pltpu.VMEM((QUARTER, D), F32), pltpu.SemaphoreType.DMA((PARTS,))],
    )
    return out


def add_theirs(order, policy, tiles):
    def body(at, x_ref, t_ref, o_ref, wide, held, in_sems, out_sems):
        rows = pl.ds(first_row(at, True, False, 0), QUARTER)

        def fetch(p):
            return pltpu.make_async_copy(x_ref.at[rows, span_of(p)], wide.at[:, span_of(p)], in_sems.at[p])

        def store(p):
            some = pl.ds(p * PER, PER)
            return pltpu.make_async_copy(held.at[some], o_ref.at[some], out_sems.at[p])

        def work(p):
            fetch(p).wait()
            for k in range(PER):
                g = p * PER + k
                held[g] = (wide[:, columns(g)] + t_ref[g].astype(F32)).astype(BF)
            store(p).start()

        each(PARTS, lambda p: fetch(p).start())
        each(PARTS, work)
        each(PARTS, lambda p: store(p).wait())

    (out,) = order.run(
        body,
        "add_theirs",
        (policy, in_vmem(tiles)),
        [HBM, VMEM],
        [pltpu.HBM((SHARDS, QUARTER, WIDTH), BF)],
        [HBM],
        [
            pltpu.VMEM((QUARTER, D), F32),
            pltpu.VMEM((SHARDS, QUARTER, WIDTH), BF),
            pltpu.SemaphoreType.DMA((PARTS,)),
            pltpu.SemaphoreType.DMA((PARTS,)),
        ],
    )
    return out


def add_rows(order, policy, tiles):
    def body(at, x_ref, t_ref, o_ref, wide, sems):
        held = pl.ds(first_row(at, True, True, 0), QUARTER)

        def copy(p):
            return pltpu.make_async_copy(x_ref.at[held, span_of(p)], wide.at[:, span_of(p)], sems.at[p])

        def work(p):
            copy(p).wait()
            for k in range(PER):
                g = p * PER + k
                o_ref[g] = (wide[:, columns(g)] + t_ref[g].astype(F32)).astype(BF)

        each(PARTS, lambda p: copy(p).start())
        each(PARTS, work)

    (out,) = order.run(
        body,
        "add_rows",
        (policy, in_vmem(tiles)),
        [HBM, VMEM],
        [tiles_out(QUARTER)],
        [VMEM],
        [pltpu.VMEM((QUARTER, D), F32), pltpu.SemaphoreType.DMA((PARTS,))],
    )
    return out


def pick_and_cast(order, anchor, policy):
    def body(at, a_ref, x_ref, p_ref, o_ref, held, wide, in_sems, out_sems, x_sems):
        rows = [member_row(at, (True, True, 0), xh) for xh in range(2)]
        mine = pl.ds(first_row(at, False, True, 0), QUARTER)

        def fetch(p, xh):
            some = pl.ds(4 * p, 4)
            return pltpu.make_async_copy(
                a_ref.at[some, xh, pl.ds(rows[xh], QUARTER), :], held.at[some, xh], in_sems.at[xh, p]
            )

        def store(p, xh):
            some = pl.ds(4 * p, 4)
            return pltpu.make_async_copy(held.at[some, xh], p_ref.at[some, xh], out_sems.at[xh, p])

        def copy(p):
            return pltpu.make_async_copy(x_ref.at[mine, span_of(p)], wide.at[:, span_of(p)], x_sems.at[p])

        def forward(p, xh):
            fetch(p, xh).wait()
            store(p, xh).start()

        def work(p):
            copy(p).wait()
            for k in range(PER):
                g = p * PER + k
                o_ref[g] = wide[:, columns(g)].astype(BF)

        for xh in range(2):
            each(4, lambda p, xh=xh: fetch(p, xh).start())
        each(PARTS, lambda p: copy(p).start())
        for xh in range(2):
            each(4, lambda p, xh=xh: forward(p, xh))
        each(PARTS, work)
        for xh in range(2):
            each(4, lambda p, xh=xh: store(p, xh).wait())

    picked, cast = order.run(
        body,
        "pick_and_cast",
        (anchor, policy),
        [HBM, HBM],
        [pltpu.HBM((16, 2, QUARTER, WIDTH), BF), tiles_out(QUARTER)],
        [HBM, VMEM],
        [
            pltpu.VMEM((16, 2, QUARTER, WIDTH), BF),
            pltpu.VMEM((QUARTER, D), F32),
            pltpu.SemaphoreType.DMA((2, 4)),
            pltpu.SemaphoreType.DMA((2, 4)),
            pltpu.SemaphoreType.DMA((PARTS,)),
        ],
    )
    return picked.reshape(SHARDS, QUARTER, WIDTH), cast


def add_tiles(order, a, b, size):
    def body(at, a_ref, b_ref, o_ref):
        def work(g):
            o_ref[g] = (a_ref[g].astype(F32) + b_ref[g].astype(F32)).astype(BF)

        each(SHARDS, work)

    args = [in_vmem(a), in_vmem(b)]
    (out,) = order.run(body, "add_tiles", args, [VMEM] * 2, [tiles_out(a.shape[1])], [VMEM], [], size=size)
    return out


def blend_rows(order, total, anchor):
    def body(at, t_ref, a_ref, o_ref, held, sems):
        def store(p):
            some = pl.ds(p * PER, PER)
            return pltpu.make_async_copy(held.at[some], o_ref.at[some], sems.at[p])

        def work(p):
            for k in range(PER):
                g = p * PER + k
                average = t_ref[g].astype(F32) / 4
                held[g] = ((1.0 - blend_rate) * a_ref[g].astype(F32) + blend_rate * average).astype(BF)
            store(p).start()

        each(PARTS, work)
        each(PARTS, lambda p: store(p).wait())

    args = [in_vmem(total), in_vmem(anchor)]
    (out,) = order.run(
        body,
        "blend_rows",
        args,
        [VMEM] * 2,
        [pltpu.HBM((SHARDS, QUARTER, WIDTH), BF)],
        [HBM],
        [pltpu.VMEM((SHARDS, QUARTER, WIDTH), BF), pltpu.SemaphoreType.DMA((PARTS,))],
    )
    return out


def split_rows(order, finished, back):
    def body(at, f_ref, b_ref, first_ref, second_ref, low_ref, high_ref, held, sems):
        def store(p):
            some = pl.ds(p * PER, PER)
            return pltpu.make_async_copy(held.at[some], first_ref.at[some], sems.at[p])

        def work(p):
            for k in range(PER):
                held[p * PER + k] = f_ref[p * PER + k, :R]
            store(p).start()

        def others(g):
            low_ref[g] = b_ref[g, :R]
            high_ref[g] = b_ref[g, R:]
            second_ref[g] = f_ref[g, R:]

        each(PARTS, work)
        each(SHARDS, others)
        each(PARTS, lambda p: store(p).wait())

    return order.run(
        body,
        "split_rows",
        [in_vmem(finished), in_vmem(back)],
        [VMEM] * 2,
        [pltpu.HBM((SHARDS, R, WIDTH), BF), tiles_out(R), tiles_out(R), tiles_out(R)],
        [HBM, VMEM, VMEM, VMEM],
        [pltpu.VMEM((SHARDS, R, WIDTH), BF), pltpu.SemaphoreType.DMA((PARTS,))],
    )


def copy_tiles(order, tiles):
    def body(at, x_ref, o_ref):
        def work(g):
            o_ref[g] = x_ref[g]

        each(SHARDS, work)

    (out,) = order.run(body, "copy_tiles", [in_vmem(tiles)], [VMEM], [tiles_out(R)], [VMEM], [])
    return out


def widen_rows(order, pieces, blended, size=1024):
    n = len(pieces)
    rows = [tiles.shape[1] for tiles, _ in pieces]

    def body(at, *refs):
        tiles, out_ref, wide, sems = refs[:n], refs[-3], refs[-2], refs[-1]

        def copy(i, p):
            span = pl.ds(pl.multiple_of(p * PER * WIDTH, WIDTH), PER * WIDTH)
            held = pl.ds(first_row(at, *pieces[i][1]), rows[i])
            return pltpu.make_async_copy(
                wide.at[i, pl.ds(0, rows[i]), span], out_ref.at[held, span], sems.at[i, p]
            )

        def work(i, p):
            for k in range(PER):
                g = p * PER + k
                wide[i, : rows[i], columns(g)] = tiles[i][g].astype(F32)
            copy(i, p).start()

        for i in range(n):
            each(PARTS, lambda p, i=i: work(i, p))
        for i in range(n):
            each(PARTS, lambda p, i=i: copy(i, p).wait())

    earlier = [] if blended is None else [blended]
    (out,) = order.run(
        body,
        "widen_rows",
        [in_vmem(tiles) for tiles, _ in pieces] + earlier,
        [VMEM] * n + [HBM] * len(earlier),
        [pltpu.HBM((ROWS, D), F32)],
        [HBM],
        [pltpu.VMEM((n, max(rows), D), F32), pltpu.SemaphoreType.DMA((n, PARTS))],
        {n + 1: 0} if earlier else {},
        size,
    )
    return out


def place_rows(order, pieces, anchor, size=1024):
    n = len(pieces)
    rows = [tiles.shape[1] for tiles, _ in pieces]

    def body(at, *refs):
        tiles, out_ref, sems = refs[:n], refs[-2], refs[-1]

        def copy(i, xh, p):
            some = pl.ds(8 * p, 8)
            held = pl.ds(member_row(at, pieces[i][1], xh), rows[i])
            return pltpu.make_async_copy(
                tiles[i].at[some, xh], out_ref.at[some, xh, held, :], sems.at[i, xh, p]
            )

        both = [(i, xh) for i in range(n) for xh in range(2)]
        for i, xh in both:
            each(2, lambda p, i=i, xh=xh: copy(i, xh, p).start())
        for i, xh in both:
            each(2, lambda p, i=i, xh=xh: copy(i, xh, p).wait())

    earlier = [] if anchor is None else [anchor]
    (out,) = order.run(
        body,
        "place_rows",
        [in_vmem(t.reshape(16, 2, r, WIDTH)) for (t, _), r in zip(pieces, rows)] + earlier,
        [VMEM] * n + [HBM] * len(earlier),
        [pltpu.HBM((16, 2, ROWS, WIDTH), BF)],
        [HBM],
        [pltpu.SemaphoreType.DMA((n, 2, 2))],
        {n + 1: 0} if earlier else {},
        size,
    )
    return out


def per_device(policies, anchor):
    policy = pltpu.with_memory_space_constraint(policies[0], pltpu.HBM)
    shards = pltpu.with_memory_space_constraint(anchor.reshape(16, 2, ROWS, WIDTH), pltpu.HBM)
    order = Order(jnp.stack([lax.axis_index(name) for name in ("xl", "c", "xh")]).astype(jnp.int32))
    swap = [(0, 1), (1, 0)]
    groups = exchange_groups()

    def exchange(tiles):
        return lax.all_to_all(
            tiles, AXES, split_axis=0, concat_axis=0, axis_index_groups=groups, tiled=True
        )

    def core(tiles):
        return lax.ppermute(tiles, "c", swap)

    def chip(tiles):
        return lax.ppermute(tiles, "xl", swap)

    theirs = core(cast_rows(order, policy))
    picked, own = pick_and_cast(order, shards, policy)
    own = core(own)
    other = chip(add_theirs(order, policy, theirs))
    fetched = exchange(picked)
    own = add_rows(order, policy, own)

    own = add_tiles(order, own, other, SUM_COST)
    own = blend_rows(order, own, fetched)
    finished = chip(own)
    back = exchange(own)
    pieces = [(own, (True, True, 0)), (core(own), (False, True, 0))]
    blended = widen_rows(order, pieces, None, WRITE_COST)

    first, second, *back = split_rows(order, finished, back)
    back_first = exchange(first)
    back_second = chip(back[1])
    pieces = []
    for j, tiles in enumerate(back):
        pieces += [(tiles, (True, True, j * R)), (core(tiles), (False, True, j * R))]
    new_anchor = place_rows(order, pieces, None)
    pieces = []
    for j, tiles in enumerate((first, second)):
        pieces += [(tiles, (True, False, j * R)), (core(tiles), (False, False, j * R))]
    blended = widen_rows(order, pieces, blended)
    new_anchor = place_rows(order, [(back_second, (True, False, R))], new_anchor)
    back_first = copy_tiles(order, back_first)
    pieces = [(back_first, (True, False, 0)), (core(back_second), (False, False, R))]
    new_anchor = place_rows(order, pieces, new_anchor, LAST_COST)
    new_anchor = place_rows(order, [(core(back_first), (False, False, 0))], new_anchor)
    return blended, new_anchor.reshape(SHARDS * ROWS, WIDTH)


def solution(mesh):
    fine = Mesh(mesh.devices.reshape(SIZES), AXES)
    shards = ("y", "z", "xh")
    return jax.shard_map(
        per_device,
        mesh=fine,
        in_specs=(P(("xl", "c"), shards, None), P(None, shards)),
        out_specs=(P(shards, None), P(None, shards)),
        check_vma=False,
    )
```

time: 255 us -> 99.5 us (0.39); the launches traced: 251 us -> 98.8 us
  waiting for transfers between devices: 170 us -> 32.5 us
  Pallas kernels: 0 us -> 31.5 us
  local copies, waits for them, and re-layouts: 29 us -> 2.3 us
  other arithmetic: 17.2 us -> 0.08 us
  between operations: 14 us -> 0.83 us
  starting transfers between devices: 20.8 us -> 31.6 us
    all_to_all x2 -> x3, waiting for transfers between devices: 131 us -> 17.5 us  [exchange(): lax.all_to_all(tiles, AXES, split_axis=0, concat_axis=0, axis_index_group...]
    psum x1 -> x0, waiting for transfers between devices: 39.2 us -> none  [per_device(): lax.psum(local_rows.astype(jnp.bfloat16), 'policy').astype(jnp.float32)]
    pallas_call x0 -> x14, Pallas kernels: none -> 31.5 us  [run(): pl.pallas_call(ordered, out_shape=[*outs, TOKEN], grid_spec=pltpu.Prefetc...]
    ppermute x0 -> x12, waiting for transfers between devices: none -> 15 us  [the longest x3 14.9 us: chip(): return lax.ppermute(tiles, 'xl', swap)]
    unnamed x2 -> x4, local copies, waits for them, and re-layouts: 16.1 us -> 2.3 us
    all_to_all x2 -> x0, local copies, waits for them, and re-layouts: 12.8 us -> none  [the longest x1 6.44 us: per_device(): lax.all_to_all(anchor, 'fsdp', split_axis=0, concat_axis=1, tiled=True)]
    convert_element_type x1 -> x0, other arithmetic: 10.6 us -> none  [per_device(): blended.astype(jnp.bfloat16)]
    ppermute x0 -> x12, starting transfers between devices: none -> 9.33 us  [the longest x9 7.95 us: core(): return lax.ppermute(tiles, 'c', swap)]
  transfers between devices with their start and end apart: 3 -> 15, of which waited for: 3 -> 5; matrix products, arithmetic and copies ran while one was open for 12% -> 0% of each run, Pallas kernels for 0% -> 24%
where the time goes in v1:
time: 99.5 us; the launch traced here: 98.8 us
  waiting for transfers between devices  32.5 us (33%)
  starting transfers between devices  31.6 us (32%)
  Pallas kernels  31.5 us (32%)
  local copies, waits for them, and re-layouts  2.3 us (2%)
    pallas_call x14, Pallas kernels, run(): pl.pallas_call(ordered, out_shape=[*outs, TOKEN], grid_spec=pltpu.Prefetc...  31.5 us
    all_to_all x3, starting transfers between devices, exchange(): lax.all_to_all(tiles, AXES, split_axis=0, concat_axis=0, axis_index_group...  22.3 us
    all_to_all x3, waiting for transfers between devices, exchange(): lax.all_to_all(tiles, AXES, split_axis=0, concat_axis=0, axis_index_group...  17.5 us
    ppermute x3, waiting for transfers between devices, chip(): return lax.ppermute(tiles, 'xl', swap)  14.9 us
    ppermute x9, starting transfers between devices, core(): return lax.ppermute(tiles, 'c', swap)  7.95 us
    unnamed x4, local copies, waits for them, and re-layouts  2.3 us
  transfers between devices with their start and end apart: 15, of which 5 were waited for; matrix products, arithmetic and copies ran while one was open for 0% of the time, Pallas kernels for 24%

profile of v1, /device:TPU:1, one launch (start us, length us, event | category | flops | bytes accessed | tf_op | source)
XLA Modules:
  0.0 98.8 jit_solution(7761501446955237133)
XLA Ops:
  0.6 0.1 pad_add_fusion.at
  0.7 2.2 %cast_rows.1 = (bf16[32,64,256]{2,1,0:T(8,128)(2,1)S(1)}, s32[8,128]{1,0:T(8,128)S(1)}) custom-call(s32[3]{0:T(128)S(1)} %pad_add_fusion.at, f32[256,8192]{1,0:T(8,128)} %bitcast.20), custom_call_target="tpu_custom_call" | custom-call | bytes 1024 | tf_op jit(solution)/shard_map/cast_rows/pallas_call | solution.py:60
  2.9 1.5 %collective-permute-start.1 = (bf16[32,64,256]{2,1,0:T(8,128)(2,1)S(1)}, bf16[32,64,256]{2,1,0:T(8,128)(2,1)S(1)}, u32[]{:S(2)}, u32[]{:S(2)}) collective-permute-start(bf16[32,64,256]{2,1,0:T(8,128)(2,1)S(1)} %get-tuple-element.35), channel_id=1, source_target_pairs={{0,32},{32,0},{1,33},{33,1},{2,34},{34,2},{3,35},{35,3},{4,36},{36... | collective-permute-start | bytes 3145736 | tf_op jit(solution)/shard_map/ppermute | solution.py:427
  4.4 4.0 %pick_and_cast.1 = (bf16[16,2,64,256]{3,2,1,0:T(8,128)(2,1)}, bf16[32,64,256]{2,1,0:T(8,128)(2,1)}, s32[8,128]{1,0:T(8,128)S(1)}) custom-call(s32[3]{0:T(128)S(1)} %pad_add_fusion.at, bf16[16,2,256,256]{3,2,1,0:T(8,128)(2,1)} %bitcast.25, f32[256,8192]{1,0:T(8,128)} %bitcast.21, s32[8,128]{1,0:T(8,128)S(1)} %get-tuple-element.33.refs_2_), custom_call_target="tpu_custom_call" | custom-call | bytes 1024 | tf_op jit(solution)/shard_map/pick_and_cast/pallas_call | solution.py:60
  8.4 0.1 collective-permute-start
  8.5 0.0 collective-permute-done.1.refs_1_
  8.5 2.9 %add_theirs.1 = (bf16[32,64,256]{2,1,0:T(8,128)(2,1)}, s32[8,128]{1,0:T(8,128)S(1)}) custom-call(s32[3]{0:T(128)S(1)} %pad_add_fusion.at, f32[256,8192]{1,0:T(8,128)} %bitcast.22, bf16[32,64,256]{2,1,0:T(8,128)(2,1)S(1)} %collective-permute-done.1.refs_1_, s32[8,128]{1,0:T(8,128)S(1)} %get-tuple-element.36.refs_2_), custom_call_target="tpu_custom_call" | custom-call | bytes 1024 | tf_op jit(solution)/shard_map/add_theirs/pallas_call | solution.py:60
  11.4 1.4 %collective-permute-start.2 = (bf16[32,64,256]{2,1,0:T(8,128)(2,1)}, bf16[32,64,256]{2,1,0:T(8,128)(2,1)S(1)}, u32[]{:S(2)}, u32[]{:S(2)}) collective-permute-start(bf16[32,64,256]{2,1,0:T(8,128)(2,1)} %get-tuple-element.39), channel_id=1, source_target_pairs={{0,64},{64,0},{1,65},{65,1},{2,66},{66,2},{3,67},{67,3},{4,68},{68... | collective-permute-start | bytes 3145736 | tf_op jit(solution)/shard_map/ppermute | solution.py:430
  12.8 9.6 %all-to-all-start = ((bf16[32,64,256]{2,1,0:T(8,128)(2,1)}), bf16[32,64,256]{2,1,0:T(8,128)(2,1)S(1)}, u32[]{:S(2)}, u32[]{:S(2)}) async-start(bf16[32,64,256]{2,1,0:T(8,128)(2,1)} %bitcast.26), calls=%async_computation | async-start | bytes 2097152 | tf_op jit(solution)/shard_map/all_to_all | solution.py:422
  22.4 0.0 collective-permute-done.refs_1_
  22.4 2.2 %add_rows.1 = (bf16[32,64,256]{2,1,0:T(8,128)(2,1)S(1)}, s32[8,128]{1,0:T(8,128)S(1)}) custom-call(s32[3]{0:T(128)S(1)} %pad_add_fusion.at, f32[256,8192]{1,0:T(8,128)} %bitcast.23, bf16[32,64,256]{2,1,0:T(8,128)(2,1)S(1)} %collective-permute-done.refs_1_, s32[8,128]{1,0:T(8,128)S(1)} %get-tuple-element.37.refs_2_), custom_call_target="tpu_custom_call" | custom-call | bytes 1024 | tf_op jit(solution)/shard_map/add_rows/pallas_call | solution.py:60
  24.6 11.4 %collective-permute-done.2.refs_1_ = bf16[32,64,256]{2,1,0:T(8,128)(2,1)S(1)} collective-permute-done((bf16[32,64,256]{2,1,0:T(8,128)(2,1)}, bf16[32,64,256]{2,1,0:T(8,128)(2,1)S(1)}, u32[]{:S(2)}, u32[]{:S(2)}) %collective-permute-start.2) | collective-permute-done | bytes 1048608 | tf_op jit(solution)/shard_map/ppermute | solution.py:430
  36.0 0.9 add_tiles.1
  36.9 3.3 %all-to-all-done.refs_1_ = bf16[32,64,256]{2,1,0:T(8,128)(2,1)S(1)} async-done(((bf16[32,64,256]{2,1,0:T(8,128)(2,1)}), bf16[32,64,256]{2,1,0:T(8,128)(2,1)S(1)}, u32[]{:S(2)}, u32[]{:S(2)}) %all-to-all-start) | async-done | bytes 1048608 | tf_op jit(solution)/shard_map/all_to_all | solution.py:422
  40.1 1.7 %blend_rows.1 = (bf16[32,64,256]{2,1,0:T(8,128)(2,1)}, s32[8,128]{1,0:T(8,128)S(1)}) custom-call(s32[3]{0:T(128)S(1)} %pad_add_fusion.at, bf16[32,64,256]{2,1,0:T(8,128)(2,1)S(1)} %get-tuple-element.41.refs_0_, bf16[32,64,256]{2,1,0:T(8,128)(2,1)S(1)} %all-to-all-done.refs_1_, s32[8,128]{1,0:T(8,128)S(1)} %get-tuple-element.43.refs_2_), custom_call_target="tpu_custom_call" | custom-call | bytes 1024 | tf_op jit(solution)/shard_map/blend_rows/pallas_call | solution.py:60
  41.9 2.3 %collective-permute-start.4 = (bf16[32,64,256]{2,1,0:T(8,128)(2,1)}, bf16[32,64,256]{2,1,0:T(8,128)(2,1)S(1)}, u32[]{:S(2)}, u32[]{:S(2)}) collective-permute-start(bf16[32,64,256]{2,1,0:T(8,128)(2,1)} %get-tuple-element.44.refs_0_), channel_id=1, source_target_pairs={{0,32},{32,0},{1,33},{33,1},{2,34},{34,2},{3,35},{35,3},{4,36},{36... | collective-permute-start | bytes 3145736 | tf_op jit(solution)/shard_map/ppermute | solution.py:427
  44.2 0.0 collective-permute-start.3
  44.2 6.7 %all-to-all-start.1 = ((bf16[32,64,256]{2,1,0:T(8,128)(2,1)}), bf16[32,64,256]{2,1,0:T(8,128)(2,1)S(1)}, u32[]{:S(2)}, u32[]{:S(2)}) async-start(bf16[32,64,256]{2,1,0:T(8,128)(2,1)} %get-tuple-element.44.refs_0_), calls=%async_computation.1 | async-start | bytes 2097152 | tf_op jit(solution)/shard_map/all_to_all | solution.py:422
  51.0 0.0 collective-permute-done.4.refs_1_
  51.0 0.0 copy-start
  51.0 1.3 %copy-done = bf16[32,64,256]{2,1,0:T(8,128)(2,1)S(1)} copy-done((bf16[32,64,256]{2,1,0:T(8,128)(2,1)S(1)}, bf16[32,64,256]{2,1,0:T(8,128)(2,1)}, u32[]{:S(2)}) %copy-start) | copy-done | bytes 1048600
  52.2 2.7 %widen_rows.2 = (f32[256,8192]{1,0:T(8,128)}, s32[8,128]{1,0:T(8,128)S(1)}) custom-call(s32[3]{0:T(128)S(1)} %pad_add_fusion.at, bf16[32,64,256]{2,1,0:T(8,128)(2,1)S(1)} %copy-done, bf16[32,64,256]{2,1,0:T(8,128)(2,1)S(1)} %collective-permute-done.4.refs_1_, s32[8,128]{1,0:T(8,128)S(1)} %get-tuple-element.45.refs_2_), custom_call_target="tpu_custom_call" | custom-call | bytes 11534336 | tf_op jit(solution)/shard_map/widen_rows/pallas_call | solution.py:60
  54.9 14.2 %all-to-all-done.1.refs_1_ = bf16[32,64,256]{2,1,0:T(8,128)(2,1)S(1)} async-done(((bf16[32,64,256]{2,1,0:T(8,128)(2,1)}), bf16[32,64,256]{2,1,0:T(8,128)(2,1)S(1)}, u32[]{:S(2)}, u32[]{:S(2)}) %all-to-all-start.1) | async-done | bytes 1048608 | tf_op jit(solution)/shard_map/all_to_all | solution.py:422
  69.2 0.0 collective-permute-done.3.refs_0_
  69.2 2.2 %split_rows.1 = (bf16[32,32,256]{2,1,0:T(8,128)(2,1)}, bf16[32,32,256]{2,1,0:T(8,128)(2,1)S(1)}, bf16[32,32,256]{2,1,0:T(8,128)(2,1)}, bf16[32,32,256]{2,1,0:T(8,128)(2,1)S(1)}, s32[8,128]{1,0:T(8,128)S(1)}) custom-call(s32[3]{0:T(128)S(1)} %pad_add_fusion.at, bf16[32,64,256]{2,1,0:T(8,128)(2,1)S(1)} %collective-permute-done.3.refs_0_, ...), custom_call_target="tpu_custom_call" | custom-call | bytes 1024 | tf_op jit(solution)/shard_map/split_rows/pallas_call | solution.py:60
  71.4 1.9 %collective-permute-start.7 = (bf16[32,32,256]{2,1,0:T(8,128)(2,1)}, bf16[32,32,256]{2,1,0:T(8,128)(2,1)S(1)}, u32[]{:S(2)}, u32[]{:S(2)}) collective-permute-start(bf16[32,32,256]{2,1,0:T(8,128)(2,1)} %get-tuple-element.50), channel_id=1, source_target_pairs={{0,32},{32,0},{1,33},{33,1},{2,34},{34,2},{3,35},{35,3},{4,36},{36... | collective-permute-start | bytes 1572872 | tf_op jit(solution)/shard_map/ppermute | solution.py:427
  73.3 0.1 collective-permute-start.8
  73.4 0.0 collective-permute-start.9
  73.4 0.4 collective-permute-start.5
  73.8 0.1 collective-permute-start.6
  73.9 6.0 %all-to-all-start.2 = ((bf16[32,32,256]{2,1,0:T(8,128)(2,1)}), bf16[32,32,256]{2,1,0:T(8,128)(2,1)S(1)}, u32[]{:S(2)}, u32[]{:S(2)}) async-start(bf16[32,32,256]{2,1,0:T(8,128)(2,1)} %get-tuple-element.47.refs_0_), calls=%async_computation.2 | async-start | bytes 1048576 | tf_op jit(solution)/shard_map/all_to_all | solution.py:422
  79.8 0.0 collective-permute-done.7
  79.8 0.0 collective-permute-done.8
  79.9 3.2 %place_rows.4 = (bf16[16,2,256,256]{3,2,1,0:T(8,128)(2,1)}, s32[8,128]{1,0:T(8,128)S(1)}) custom-call(s32[3]{0:T(128)S(1)} %pad_add_fusion.at, bf16[16,2,32,256]{3,2,1,0:T(8,128)(2,1)} %bitcast.6.refs_0_, bf16[16,2,32,256]{3,2,1,0:T(8,128)(2,1)S(1)} %bitcast.17, bf16[16,2,32,256]{3,2,1,0:T(8,128)(2,1)S(1)} %bitcast.15, ...), custom_call_target="tpu_custom_call" | custom-call | bytes 1024 | tf_op jit(solution)/shard_map/place_rows/pallas_call | solution.py:60
  83.0 3.5 %collective-permute-done.9 = bf16[32,32,256]{2,1,0:T(8,128)(2,1)} collective-permute-done((bf16[32,32,256]{2,1,0:T(8,128)(2,1)S(1)}, bf16[32,32,256]{2,1,0:T(8,128)(2,1)}, u32[]{:S(2)}, u32[]{:S(2)}) %collective-permute-start.9) | collective-permute-done | bytes 524320 | tf_op jit(solution)/shard_map/ppermute | solution.py:430
  86.5 1.3 %collective-permute-start.11 = (bf16[32,32,256]{2,1,0:T(8,128)(2,1)}, bf16[32,32,256]{2,1,0:T(8,128)(2,1)S(1)}, u32[]{:S(2)}, u32[]{:S(2)}) collective-permute-start(bf16[32,32,256]{2,1,0:T(8,128)(2,1)} %collective-permute-done.9), channel_id=1, source_target_pairs={{0,32},{32,0},{1,33},{33,1},{2,34},{34,2},{3,35},{35,3},{4,36},{36... | collective-permute-start | bytes 1572872 | tf_op jit(solution)/shard_map/ppermute | solution.py:427
  87.8 0.0 collective-permute-done.5.refs_1_
  87.8 0.0 collective-permute-done.6.refs_3_
  87.8 1.0 %copy-done.1 = bf16[32,32,256]{2,1,0:T(8,128)(2,1)S(1)} copy-done((bf16[32,32,256]{2,1,0:T(8,128)(2,1)S(1)}, bf16[32,32,256]{2,1,0:T(8,128)(2,1)}, u32[]{:S(2)}) %copy-start.1) | copy-done | bytes 524312
  88.8 2.8 %widen_rows.3 = (f32[256,8192]{1,0:T(8,128)}, s32[8,128]{1,0:T(8,128)S(1)}) custom-call(s32[3]{0:T(128)S(1)} %pad_add_fusion.at, bf16[32,32,256]{2,1,0:T(8,128)(2,1)S(1)} %copy-done.1, bf16[32,32,256]{2,1,0:T(8,128)(2,1)S(1)} %collective-permute-done.5.refs_1_, bf16[32,32,256]{2,1,0:T(8,128)(2,1)S(1)} %get-tuple-element.48.refs_2_, ...), custom_call_target="tpu_custom_call", output_to_operand_aliasing={{0}: (5, {})} | custom-call | bytes 1024 | tf_op jit(solution)/shard_map/widen_rows/pallas_call | solution.py:60
  91.7 2.4 %place_rows.5 = (bf16[16,2,256,256]{3,2,1,0:T(8,128)(2,1)}, s32[8,128]{1,0:T(8,128)S(1)}) custom-call(s32[3]{0:T(128)S(1)} %pad_add_fusion.at, bf16[16,2,32,256]{3,2,1,0:T(8,128)(2,1)} %bitcast.10.refs_0_, bf16[16,2,256,256]{3,2,1,0:T(8,128)(2,1)} %get-tuple-element.55.refs_1_, s32[8,128]{1,0:T(8,128)S(1)} %get-tuple-element.56.refs_2_), custom_call_target="tpu_custom_call", output_to_operand_aliasing={{0}: (2, {})} | custom-call | bytes 1024 | tf_op jit(solution)/shard_map/place_rows/pallas_call | solution.py:60
  94.1 0.0 all-to-all-done.2.refs_0_
  94.1 0.7 copy_tiles.1
  94.8 0.3 collective-permute-start.10
  95.1 0.0 collective-permute-done.11
  95.1 1.6 %place_rows.6 = (bf16[16,2,256,256]{3,2,1,0:T(8,128)(2,1)}, s32[8,128]{1,0:T(8,128)S(1)}) custom-call(s32[3]{0:T(128)S(1)} %pad_add_fusion.at, bf16[16,2,32,256]{3,2,1,0:T(8,128)(2,1)S(1)} %bitcast.18, bf16[16,2,32,256]{3,2,1,0:T(8,128)(2,1)S(1)} %bitcast.16, bf16[16,2,256,256]{3,2,1,0:T(8,128)(2,1)} %get-tuple-element.59.refs_2_, ...), custom_call_target="tpu_custom_call", output_to_operand_aliasing={{0}: (3, {})} | custom-call | bytes 38797312 | tf_op jit(solution)/shard_map/place_rows/pallas_call | solution.py:60
  96.7 0.1 collective-permute-done.10
  96.8 2.0 %place_rows.7 = (bf16[16,2,256,256]{3,2,1,0:T(8,128)(2,1)}, s32[8,128]{1,0:T(8,128)}) custom-call(s32[3]{0:T(128)S(1)} %pad_add_fusion.at, bf16[16,2,32,256]{3,2,1,0:T(8,128)(2,1)S(1)} %bitcast.19, bf16[16,2,256,256]{3,2,1,0:T(8,128)(2,1)} %get-tuple-element.61.refs_1_, s32[8,128]{1,0:T(8,128)S(1)} %get-tuple-element.62.refs_2_), custom_call_target="tpu_custom_call", output_to_operand_aliasing={{0}: (2, {})} | custom-call | bytes 1024 | tf_op jit(solution)/shard_map/place_rows/pallas_call | solution.py:60
  (1 shorter events, 0.0 us)
Async XLA Ops:
  2.9 5.6 %collective-permute-start.1 = (bf16[32,64,256]{2,1,0:T(8,128)(2,1)S(1)}, bf16[32,64,256]{2,1,0:T(8,128)(2,1)S(1)}, u32[]{:S(2)}, u32[]{:S(2)}) collective-permute-start(bf16[32,64,256]{2,1,0:T(8,128)(2,1)S(1)} %get-tuple-element.35), channel_id=1, source_target_pairs={{0,32},{32,0},{1,33},{33,1},{2,34},{34,2},{3,35},{35,3},{4,36},{36... | collective-permute-start | bytes 3145736 | tf_op jit(solution)/shard_map/ppermute | solution.py:427
  8.4 14.0 %collective-permute-start = (bf16[32,64,256]{2,1,0:T(8,128)(2,1)}, bf16[32,64,256]{2,1,0:T(8,128)(2,1)S(1)}, u32[]{:S(2)}, u32[]{:S(2)}) collective-permute-start(bf16[32,64,256]{2,1,0:T(8,128)(2,1)} %get-tuple-element.34), channel_id=1, source_target_pairs={{0,32},{32,0},{1,33},{33,1},{2,34},{34,2},{3,35},{35,3},{4,36},{36... | collective-permute-start | bytes 3145736 | tf_op jit(solution)/shard_map/ppermute | solution.py:427
  11.4 24.5 %collective-permute-start.2 = (bf16[32,64,256]{2,1,0:T(8,128)(2,1)}, bf16[32,64,256]{2,1,0:T(8,128)(2,1)S(1)}, u32[]{:S(2)}, u32[]{:S(2)}) collective-permute-start(bf16[32,64,256]{2,1,0:T(8,128)(2,1)} %get-tuple-element.39), channel_id=1, source_target_pairs={{0,64},{64,0},{1,65},{65,1},{2,66},{66,2},{3,67},{67,3},{4,68},{68... | collective-permute-start | bytes 3145736 | tf_op jit(solution)/shard_map/ppermute | solution.py:430
  12.8 27.3 %all-to-all-start = ((bf16[32,64,256]{2,1,0:T(8,128)(2,1)}), bf16[32,64,256]{2,1,0:T(8,128)(2,1)S(1)}, u32[]{:S(2)}, u32[]{:S(2)}) async-start(bf16[32,64,256]{2,1,0:T(8,128)(2,1)} %bitcast.26), calls=%async_computation | async-start | bytes 2097152 | tf_op jit(solution)/shard_map/all_to_all | solution.py:422
  41.9 9.1 %collective-permute-start.4 = (bf16[32,64,256]{2,1,0:T(8,128)(2,1)}, bf16[32,64,256]{2,1,0:T(8,128)(2,1)S(1)}, u32[]{:S(2)}, u32[]{:S(2)}) collective-permute-start(bf16[32,64,256]{2,1,0:T(8,128)(2,1)} %get-tuple-element.44.refs_0_), channel_id=1, source_target_pairs={{0,32},{32,0},{1,33},{33,1},{2,34},{34,2},{3,35},{35,3},{4,36},{36... | collective-permute-start | bytes 3145736 | tf_op jit(solution)/shard_map/ppermute | solution.py:427
  44.2 24.9 %collective-permute-start.3 = (bf16[32,64,256]{2,1,0:T(8,128)(2,1)}, bf16[32,64,256]{2,1,0:T(8,128)(2,1)S(1)}, u32[]{:S(2)}, u32[]{:S(2)}) collective-permute-start(bf16[32,64,256]{2,1,0:T(8,128)(2,1)} %get-tuple-element.44.refs_0_), channel_id=1, source_target_pairs={{0,64},{64,0},{1,65},{65,1},{2,66},{66,2},{3,67},{67,3},{4,68},{68... | collective-permute-start | bytes 3145736 | tf_op jit(solution)/shard_map/ppermute | solution.py:430
  44.2 24.9 %all-to-all-start.1 = ((bf16[32,64,256]{2,1,0:T(8,128)(2,1)}), bf16[32,64,256]{2,1,0:T(8,128)(2,1)S(1)}, u32[]{:S(2)}, u32[]{:S(2)}) async-start(bf16[32,64,256]{2,1,0:T(8,128)(2,1)} %get-tuple-element.44.refs_0_), calls=%async_computation.1 | async-start | bytes 2097152 | tf_op jit(solution)/shard_map/all_to_all | solution.py:422
  51.0 1.3 %copy-start = (bf16[32,64,256]{2,1,0:T(8,128)(2,1)S(1)}, bf16[32,64,256]{2,1,0:T(8,128)(2,1)}, u32[]{:S(2)}) copy-start(bf16[32,64,256]{2,1,0:T(8,128)(2,1)} %get-tuple-element.44.refs_0_) | copy-start | bytes 3145732
  71.4 8.5 %collective-permute-start.7 = (bf16[32,32,256]{2,1,0:T(8,128)(2,1)}, bf16[32,32,256]{2,1,0:T(8,128)(2,1)S(1)}, u32[]{:S(2)}, u32[]{:S(2)}) collective-permute-start(bf16[32,32,256]{2,1,0:T(8,128)(2,1)} %get-tuple-element.50), channel_id=1, source_target_pairs={{0,32},{32,0},{1,33},{33,1},{2,34},{34,2},{3,35},{35,3},{4,36},{36... | collective-permute-start | bytes 1572872 | tf_op jit(solution)/shard_map/ppermute | solution.py:427
  73.3 6.6 %collective-permute-start.8 = (bf16[32,32,256]{2,1,0:T(8,128)(2,1)S(1)}, bf16[32,32,256]{2,1,0:T(8,128)(2,1)}, u32[]{:S(2)}, u32[]{:S(2)}) collective-permute-start(bf16[32,32,256]{2,1,0:T(8,128)(2,1)S(1)} %get-tuple-element.51), channel_id=1, source_target_pairs={{0,32},{32,0},{1,33},{33,1},{2,34},{34,2},{3,35},{35,3},{4,36},{36... | collective-permute-start | bytes 1572872 | tf_op jit(solution)/shard_map/ppermute | solution.py:427
  73.4 13.2 %collective-permute-start.9 = (bf16[32,32,256]{2,1,0:T(8,128)(2,1)S(1)}, bf16[32,32,256]{2,1,0:T(8,128)(2,1)}, u32[]{:S(2)}, u32[]{:S(2)}) collective-permute-start(bf16[32,32,256]{2,1,0:T(8,128)(2,1)S(1)} %get-tuple-element.51), channel_id=1, source_target_pairs={{0,64},{64,0},{1,65},{65,1},{2,66},{66,2},{3,67},{67,3},{4,68},{68... | collective-permute-start | bytes 1572872 | tf_op jit(solution)/shard_map/ppermute | solution.py:430
  73.4 14.4 %collective-permute-start.5 = (bf16[32,32,256]{2,1,0:T(8,128)(2,1)}, bf16[32,32,256]{2,1,0:T(8,128)(2,1)S(1)}, u32[]{:S(2)}, u32[]{:S(2)}) collective-permute-start(bf16[32,32,256]{2,1,0:T(8,128)(2,1)} %get-tuple-element.47.refs_0_), channel_id=1, source_target_pairs={{0,32},{32,0},{1,33},{33,1},{2,34},{34,2},{3,35},{35,3},{4,36},{36... | collective-permute-start | bytes 1572872 | tf_op jit(solution)/shard_map/ppermute | solution.py:427
  73.8 14.0 %collective-permute-start.6 = (bf16[32,32,256]{2,1,0:T(8,128)(2,1)S(1)}, bf16[32,32,256]{2,1,0:T(8,128)(2,1)S(1)}, u32[]{:S(2)}, u32[]{:S(2)}) collective-permute-start(bf16[32,32,256]{2,1,0:T(8,128)(2,1)S(1)} %get-tuple-element.48.refs_2_), channel_id=1, source_target_pairs={{0,32},{32,0},{1,33},{33,1},{2,34},{34,2},{3,35},{35,3},{4,36},{36... | collective-permute-start | bytes 1572872 | tf_op jit(solution)/shard_map/ppermute | solution.py:427
  73.9 20.2 %all-to-all-start.2 = ((bf16[32,32,256]{2,1,0:T(8,128)(2,1)}), bf16[32,32,256]{2,1,0:T(8,128)(2,1)S(1)}, u32[]{:S(2)}, u32[]{:S(2)}) async-start(bf16[32,32,256]{2,1,0:T(8,128)(2,1)} %get-tuple-element.47.refs_0_), calls=%async_computation.2 | async-start | bytes 1048576 | tf_op jit(solution)/shard_map/all_to_all | solution.py:422
  86.5 8.6 %collective-permute-start.11 = (bf16[32,32,256]{2,1,0:T(8,128)(2,1)}, bf16[32,32,256]{2,1,0:T(8,128)(2,1)S(1)}, u32[]{:S(2)}, u32[]{:S(2)}) collective-permute-start(bf16[32,32,256]{2,1,0:T(8,128)(2,1)} %collective-permute-done.9), channel_id=1, source_target_pairs={{0,32},{32,0},{1,33},{33,1},{2,34},{34,2},{3,35},{35,3},{4,36},{36... | collective-permute-start | bytes 1572872 | tf_op jit(solution)/shard_map/ppermute | solution.py:427
  87.8 1.0 %copy-start.1 = (bf16[32,32,256]{2,1,0:T(8,128)(2,1)S(1)}, bf16[32,32,256]{2,1,0:T(8,128)(2,1)}, u32[]{:S(2)}) copy-start(bf16[32,32,256]{2,1,0:T(8,128)(2,1)} %get-tuple-element.47.refs_0_) | copy-start | bytes 1572868
  94.8 2.0 %collective-permute-start.10 = (bf16[32,32,256]{2,1,0:T(8,128)(2,1)S(1)}, bf16[32,32,256]{2,1,0:T(8,128)(2,1)S(1)}, u32[]{:S(2)}, u32[]{:S(2)}) collective-permute-start(bf16[32,32,256]{2,1,0:T(8,128)(2,1)S(1)} %get-tuple-element.58), channel_id=1, source_target_pairs={{0,32},{32,0},{1,33},{33,1},{2,34},{34,2},{3,35},{35,3},{4,36},{36... | collective-permute-start | bytes 1572872 | tf_op jit(solution)/shard_map/ppermute | solution.py:427

commit v2 on v1

v2 whole, which is shorter than its diff:
```python
import jax
import jax.numpy as jnp
import numpy as np
from jax import lax
from jax.experimental import pallas as pl
from jax.experimental.pallas import tpu as pltpu
from jax.sharding import Mesh, PartitionSpec as P

blend_rate = 0.3

AXES = ("xl", "c", "y", "z", "xh")
SIZES = (2, 2, 4, 4, 2)
SHARDS = 32
ROWS = 256
WIDTH = 256
D = 8192
HALF = 128
QUARTER = 64
R = 32
BF = jnp.bfloat16
F32 = jnp.float32
VMEM_LIMIT = 10 << 20
PARTS = 8
PER = SHARDS // PARTS
WRITE_COST = 11 << 20
LAST_COST = 37 << 20
ANY = pl.BlockSpec(memory_space=pl.ANY)
HBM = pl.BlockSpec(memory_space=pltpu.HBM)
VMEM = pl.BlockSpec(memory_space=pltpu.VMEM)
TOKEN = jax.ShapeDtypeStruct((8, 128), jnp.int32)


def exchange_groups():
    ids = np.arange(128).reshape(SIZES)
    return [
        [int(ids[flip ^ xh, c, y, z, xh]) for y in range(4) for z in range(4) for xh in range(2)]
        for flip in range(2)
        for c in range(2)
    ]


def in_vmem(x):
    return pltpu.with_memory_space_constraint(x, pltpu.VMEM)


class Order:
    def __init__(self, place):
        self.place = place
        self.token = None

    def run(self, body, name, args, specs, outs, out_specs, scratch, aliases=None, size=1024):
        held = [] if self.token is None else [self.token]

        def ordered(at, *refs):
            ins, rest = refs[: len(args)], refs[len(args) + len(held) :]
            results, others = rest[: len(outs)], rest[len(outs) + 1 :]
            body(at, *ins, *results, *others)

        *results, self.token = pl.pallas_call(
            ordered,
            out_shape=[*outs, TOKEN],
            grid_spec=pltpu.PrefetchScalarGridSpec(
                num_scalar_prefetch=1,
                grid=(),
                in_specs=[*specs, *[ANY] * len(held)],
                out_specs=[*out_specs, ANY],
                scratch_shapes=scratch,
            ),
            input_output_aliases=aliases or {},
            compiler_params=pltpu.CompilerParams(vmem_limit_bytes=VMEM_LIMIT),
            cost_estimate=pl.CostEstimate(flops=0, bytes_accessed=size, transcendentals=0),
            name=name,
        )(self.place, *args, *held)
        return results


def columns(g):
    return pl.ds(pl.multiple_of(g * WIDTH, WIDTH), WIDTH)


def each(count, work):
    pl.loop(0, count)(work)


def first_row(at, core, chip, start, xl=None):
    xl = at[0] if xl is None else xl
    half = at[1] if core else 1 - at[1]
    quarter = xl if chip else 1 - xl
    return pl.multiple_of(half * HALF + quarter * QUARTER + start, 16)


def member_row(at, where, xh):
    differs = at[2] if xh == 0 else 1 - at[2]
    return first_row(at, *where, at[0] + differs - 2 * at[0] * differs)


def tiles_out(rows):
    return pltpu.VMEM((SHARDS, rows, WIDTH), BF)


def span_of(p):
    return pl.ds(pl.multiple_of(p * PER * WIDTH, WIDTH), PER * WIDTH)


def cast_rows(order, policy):
    def body(at, x_ref, o_ref, wide, sems):
        held = pl.ds(first_row(at, False, False, 0), QUARTER)

        def copy(p):
            return pltpu.make_async_copy(x_ref.at[held, span_of(p)], wide.at[:, span_of(p)], sems.at[p])

        def work(p):
            copy(p).wait()
            for k in range(PER):
                g = p * PER + k
                o_ref[g] = wide[:, columns(g)].astype(BF)

        each(PARTS, lambda p: copy(p).start())
        each(PARTS, work)

    (out,) = order.run(
        body,
        "cast_rows",
        (policy,),
        [HBM],
        [tiles_out(QUARTER)],
        [VMEM],
        [pltpu.VMEM((QUARTER, D), F32), pltpu.SemaphoreType.DMA((PARTS,))],
    )
    return out


def add_theirs(order, policy, tiles):
    def body(at, x_ref, t_ref, o_ref, wide, held, in_sems, out_sems):
        rows = pl.ds(first_row(at, True, False, 0), QUARTER)

        def fetch(p):
            return pltpu.make_async_copy(x_ref.at[rows, span_of(p)], wide.at[:, span_of(p)], in_sems.at[p])

        def store(p):
            some = pl.ds(p * PER, PER)
            return pltpu.make_async_copy(held.at[some], o_ref.at[some], out_sems.at[p])

        def work(p):
            fetch(p).wait()
            for k in range(PER):
                g = p * PER + k
                held[g] = (wide[:, columns(g)] + t_ref[g].astype(F32)).astype(BF)
            store(p).start()

        each(PARTS, lambda p: fetch(p).start())
        each(PARTS, work)
        each(PARTS, lambda p: store(p).wait())

    (out,) = order.run(
        body,
        "add_theirs",
        (policy, in_vmem(tiles)),
        [HBM, VMEM],
        [pltpu.HBM((SHARDS, QUARTER, WIDTH), BF)],
        [HBM],
        [
            pltpu.VMEM((QUARTER, D), F32),
            pltpu.VMEM((SHARDS, QUARTER, WIDTH), BF),
            pltpu.SemaphoreType.DMA((PARTS,)),
            pltpu.SemaphoreType.DMA((PARTS,)),
        ],
    )
    return out


def cast_own(order, policy):
    def body(at, x_ref, low_ref, high_ref, wide, sems):
        held = pl.ds(first_row(at, False, True, 0), QUARTER)

        def copy(p):
            return pltpu.make_async_copy(x_ref.at[held, span_of(p)], wide.at[:, span_of(p)], sems.at[p])

        def work(p):
            copy(p).wait()
            for k in range(PER):
                g = p * PER + k
                low_ref[g] = wide[:R, columns(g)].astype(BF)
                high_ref[g] = wide[R:, columns(g)].astype(BF)

        each(PARTS, lambda p: copy(p).start())
        each(PARTS, work)

    return order.run(
        body,
        "cast_own",
        (policy,),
        [HBM],
        [tiles_out(R)] * 2,
        [VMEM] * 2,
        [pltpu.VMEM((QUARTER, D), F32), pltpu.SemaphoreType.DMA((PARTS,))],
    )


def add_own(order, policy, chunks):
    def body(at, x_ref, low_ref, high_ref, o_ref, wide, sems):
        held = pl.ds(first_row(at, True, True, 0), QUARTER)

        def copy(p):
            return pltpu.make_async_copy(x_ref.at[held, span_of(p)], wide.at[:, span_of(p)], sems.at[p])

        def work(p):
            copy(p).wait()
            for k in range(PER):
                g = p * PER + k
                o_ref[g, :R] = (wide[:R, columns(g)] + low_ref[g].astype(F32)).astype(BF)
                o_ref[g, R:] = (wide[R:, columns(g)] + high_ref[g].astype(F32)).astype(BF)

        each(PARTS, lambda p: copy(p).start())
        each(PARTS, work)

    (out,) = order.run(
        body,
        "add_own",
        (policy, *[in_vmem(tiles) for tiles in chunks]),
        [HBM, VMEM, VMEM],
        [tiles_out(QUARTER)],
        [VMEM],
        [pltpu.VMEM((QUARTER, D), F32), pltpu.SemaphoreType.DMA((PARTS,))],
    )
    return out


def pick_rows(order, anchor):
    def body(at, a_ref, p_ref, held, in_sems, out_sems):
        rows = [member_row(at, (True, True, 0), xh) for xh in range(2)]

        def fetch(p, xh):
            some = pl.ds(4 * p, 4)
            return pltpu.make_async_copy(
                a_ref.at[some, xh, pl.ds(rows[xh], QUARTER), :], held.at[some, xh], in_sems.at[xh, p]
            )

        def store(p, xh):
            some = pl.ds(4 * p, 4)
            return pltpu.make_async_copy(held.at[some, xh], p_ref.at[some, xh], out_sems.at[xh, p])

        def forward(p, xh):
            fetch(p, xh).wait()
            store(p, xh).start()

        for xh in range(2):
            each(4, lambda p, xh=xh: fetch(p, xh).start())
        for xh in range(2):
            each(4, lambda p, xh=xh: forward(p, xh))
        for xh in range(2):
            each(4, lambda p, xh=xh: store(p, xh).wait())

    (picked,) = order.run(
        body,
        "pick_rows",
        (anchor,),
        [HBM],
        [pltpu.HBM((16, 2, QUARTER, WIDTH), BF)],
        [HBM],
        [
            pltpu.VMEM((16, 2, QUARTER, WIDTH), BF),
            pltpu.SemaphoreType.DMA((2, 4)),
            pltpu.SemaphoreType.DMA((2, 4)),
        ],
    )
    return picked.reshape(SHARDS, QUARTER, WIDTH)


def blend_rows(order, own, other, anchor):
    def body(at, x_ref, t_ref, a_ref, o_ref, held, sems):
        def store(p):
            some = pl.ds(p * PER, PER)
            return pltpu.make_async_copy(held.at[some], o_ref.at[some], sems.at[p])

        def work(p):
            for k in range(PER):
                g = p * PER + k
                average = (x_ref[g].astype(F32) + t_ref[g].astype(F32)) / 4
                held[g] = ((1.0 - blend_rate) * a_ref[g].astype(F32) + blend_rate * average).astype(BF)
            store(p).start()

        each(PARTS, work)
        each(PARTS, lambda p: store(p).wait())

    (out,) = order.run(
        body,
        "blend_rows",
        [in_vmem(x) for x in (own, other, anchor)],
        [VMEM] * 3,
        [pltpu.HBM((SHARDS, QUARTER, WIDTH), BF)],
        [HBM],
        [pltpu.VMEM((SHARDS, QUARTER, WIDTH), BF), pltpu.SemaphoreType.DMA((PARTS,))],
    )
    return out


def split_back(order, back):
    def body(at, b_ref, low_ref, high_ref):
        def work(g):
            high_ref[g] = b_ref[g, R:]
            low_ref[g] = b_ref[g, :R]

        each(SHARDS, work)

    return order.run(
        body, "split_back", [in_vmem(back)], [VMEM], [tiles_out(R)] * 2, [VMEM] * 2, []
    )


def split_finished(order, finished):
    def body(at, f_ref, first_ref, second_ref, sems):
        def store(p):
            some = pl.ds(p * PER, PER)
            return pltpu.make_async_copy(f_ref.at[some, pl.ds(0, R)], first_ref.at[some], sems.at[p])

        def work(g):
            second_ref[g] = f_ref[g, R:]

        each(PARTS, lambda p: store(p).start())
        each(SHARDS, work)
        each(PARTS, lambda p: store(p).wait())

    return order.run(
        body,
        "split_finished",
        [in_vmem(finished)],
        [VMEM],
        [pltpu.HBM((SHARDS, R, WIDTH), BF), tiles_out(R)],
        [HBM, VMEM],
        [pltpu.SemaphoreType.DMA((PARTS,))],
    )


def copy_tiles(order, tiles):
    def body(at, x_ref, o_ref):
        def work(g):
            o_ref[g] = x_ref[g]

        each(SHARDS, work)

    (out,) = order.run(body, "copy_tiles", [in_vmem(tiles)], [VMEM], [tiles_out(R)], [VMEM], [])
    return out


def write_rows(order, wide_pieces, placed_pieces, blended, anchor, size=1024):
    n, m = len(wide_pieces), len(placed_pieces)
    rows = [tiles.shape[1] for tiles, _ in wide_pieces]
    placed_rows = [tiles.shape[1] for tiles, _ in placed_pieces]
    outs = [pltpu.HBM((ROWS, D), F32)] * (n > 0) + [pltpu.HBM((16, 2, ROWS, WIDTH), BF)] * (m > 0)
    earlier = [x for x, k in ((blended, n), (anchor, m)) if k and x is not None]
    tops = max(rows, default=16)

    def body(at, *refs):
        tiles, refs = refs[:n], refs[n:]
        placed, refs = refs[:m], refs[m + len(earlier) :]
        out_refs, (wide, held, sems, placed_sems, held_sem) = refs[: len(outs)], refs[len(outs) :]

        def place(i, xh, p):
            some = pl.ds(8 * p, 8)
            there = pl.ds(member_row(at, placed_pieces[i][1], xh), placed_rows[i])
            return pltpu.make_async_copy(
                placed[i].at[some, xh], out_refs[-1].at[some, xh, there, :], placed_sems.at[i, xh, p]
            )

        def copy(i, p):
            some = pl.ds(0, rows[i])
            there = pl.ds(first_row(at, *wide_pieces[i][1]), rows[i])
            return pltpu.make_async_copy(
                wide.at[i, some, span_of(p)], out_refs[0].at[there, span_of(p)], sems.at[i, p]
            )

        def work(i, ref, p):
            for k in range(PER):
                g = p * PER + k
                wide[i, : rows[i], columns(g)] = ref[g].astype(F32)
            copy(i, p).start()

        both = [(i, xh) for i in range(m) for xh in range(2)]
        if n:
            last = pltpu.make_async_copy(tiles[-1], held, held_sem)
            last.start()
        for i, xh in both:
            each(2, lambda p, i=i, xh=xh: place(i, xh, p).start())
        for i in range(n):
            if i == n - 1:
                last.wait()
            each(PARTS, lambda p, i=i: work(i, held if i == n - 1 else tiles[i], p))
        for i in range(n):
            each(PARTS, lambda p, i=i: copy(i, p).wait())
        for i, xh in both:
            each(2, lambda p, i=i, xh=xh: place(i, xh, p).wait())

    args = [in_vmem(t) for t, _ in wide_pieces[:-1]]
    args += [pltpu.with_memory_space_constraint(t, pltpu.HBM) for t, _ in wide_pieces[-1:]]
    args += [in_vmem(t.reshape(16, 2, r, WIDTH)) for (t, _), r in zip(placed_pieces, placed_rows)]
    specs = [VMEM] * (n - 1) + [HBM] * (n > 0) + [VMEM] * m
    return order.run(
        body,
        "write_rows",
        args + earlier,
        specs + [HBM] * len(earlier),
        outs,
        [HBM] * len(outs),
        [
            pltpu.VMEM((max(n, 1), tops, D if n else 128), F32),
            pltpu.VMEM((SHARDS, rows[-1] if n else 16, WIDTH), BF),
            pltpu.SemaphoreType.DMA((max(n, 1), PARTS)),
            pltpu.SemaphoreType.DMA((max(m, 1), 2, 2)),
            pltpu.SemaphoreType.DMA,
        ],
        {n + m + 1 + k: k for k in range(len(earlier))},
        size,
    )


def per_device(policies, anchor):
    policy = pltpu.with_memory_space_constraint(policies[0], pltpu.HBM)
    shards = pltpu.with_memory_space_constraint(anchor.reshape(16, 2, ROWS, WIDTH), pltpu.HBM)
    order = Order(jnp.stack([lax.axis_index(name) for name in ("xl", "c", "xh")]).astype(jnp.int32))
    swap = [(0, 1), (1, 0)]
    groups = exchange_groups()

    def exchange(tiles):
        return lax.all_to_all(
            tiles, AXES, split_axis=0, concat_axis=0, axis_index_groups=groups, tiled=True
        )

    def core(tiles):
        return lax.ppermute(tiles, "c", swap)

    def chip(tiles):
        return lax.ppermute(tiles, "xl", swap)

    theirs = core(cast_rows(order, policy))
    picked = pick_rows(order, shards)
    other = chip(add_theirs(order, policy, theirs))
    fetched = exchange(picked)
    own = add_own(order, policy, [core(tiles) for tiles in cast_own(order, policy)])

    own = blend_rows(order, own, other, fetched)
    finished = chip(own)
    back = exchange(own)
    pieces = [(core(own), (False, True, 0)), (own, (True, True, 0))]
    (blended,) = write_rows(order, pieces, [], None, None, WRITE_COST)

    back = split_back(order, back)
    first, second = split_finished(order, finished)
    back_first = exchange(first)
    back_second = chip(back[1])
    pieces = []
    for j, tiles in enumerate(back):
        pieces += [(tiles, (True, True, j * R)), (core(tiles), (False, True, j * R))]
    (new_anchor,) = write_rows(order, [], pieces, None, None)
    pieces = []
    for j, tiles in ((1, second), (0, first)):
        pieces += [(core(tiles), (False, False, j * R)), (tiles, (True, False, j * R))]
    blended, new_anchor = write_rows(
        order, pieces, [(back_second, (True, False, R))], blended, new_anchor
    )
    back_first = copy_tiles(order, back_first)
    pieces = [(back_first, (True, False, 0)), (core(back_second), (False, False, R))]
    (new_anchor,) = write_rows(order, [], pieces, None, new_anchor, LAST_COST)
    pieces = [(core(back_first), (False, False, 0))]
    (new_anchor,) = write_rows(order, [], pieces, None, new_anchor)
    return blended, new_anchor.reshape(SHARDS * ROWS, WIDTH)


def solution(mesh):
    fine = Mesh(mesh.devices.reshape(SIZES), AXES)
    shards = ("y", "z", "xh")
    return jax.shard_map(
        per_device,
        mesh=fine,
        in_specs=(P(("xl", "c"), shards, None), P(None, shards)),
        out_specs=(P(shards, None), P(None, shards)),
        check_vma=False,
    )
```

time: 99.5 us -> 95.4 us (0.959)
  local copies, waits for them, and re-layouts: 2.3 us -> 0 us
  starting transfers between devices: 31.6 us -> 30.2 us
    ppermute x3, waiting for transfers between devices: 14.9 us -> 3.52 us  [chip(): return lax.ppermute(tiles, 'xl', swap)]
    all_to_all x3, waiting for transfers between devices: 17.5 us -> 26.5 us  [exchange(): lax.all_to_all(tiles, AXES, split_axis=0, concat_axis=0, axis_index_group...]
    all_to_all x3, starting transfers between devices: 22.3 us -> 19.3 us  [exchange(): lax.all_to_all(tiles, AXES, split_axis=0, concat_axis=0, axis_index_group...]
    unnamed x4 -> x0, local copies, waits for them, and re-layouts: 2.3 us -> none
    ppermute x9 -> x10, waiting for transfers between devices: 0.16 us -> 2.21 us  [core(): return lax.ppermute(tiles, 'c', swap)]
    ppermute x9 -> x10, starting transfers between devices: 7.95 us -> 9.59 us  [core(): return lax.ppermute(tiles, 'c', swap)]
  transfers between devices with their start and end apart: 15 -> 16, of which waited for: 5 -> 6; matrix products, arithmetic and copies ran while one was open for 0% -> 0% of each run, Pallas kernels for 24% -> 24%
where the time goes in v2:
time: 95.4 us; the launch traced here: 94.7 us
  waiting for transfers between devices  32.2 us (34%)
  Pallas kernels  31.3 us (33%)
  starting transfers between devices  30.2 us (32%)
    pallas_call x14, Pallas kernels, run(): pl.pallas_call(ordered, out_shape=[*outs, TOKEN], grid_spec=pltpu.Prefetc...  31.3 us
    all_to_all x3, waiting for transfers between devices, exchange(): lax.all_to_all(tiles, AXES, split_axis=0, concat_axis=0, axis_index_group...  26.5 us
    all_to_all x3, starting transfers between devices, exchange(): lax.all_to_all(tiles, AXES, split_axis=0, concat_axis=0, axis_index_group...  19.3 us
    ppermute x10, starting transfers between devices, core(): return lax.ppermute(tiles, 'c', swap)  9.59 us
    ppermute x3, waiting for transfers between devices, chip(): return lax.ppermute(tiles, 'xl', swap)  3.52 us
    ppermute x10, waiting for transfers between devices, core(): return lax.ppermute(tiles, 'c', swap)  2.21 us
  transfers between devices with their start and end apart: 16, of which 6 were waited for; matrix products, arithmetic and copies ran while one was open for 0% of the time, Pallas kernels for 24%

profile of v2, /device:TPU:1, one launch (start us, length us, event | category | flops | bytes accessed | tf_op | source)
XLA Modules:
  0.0 94.7 jit_solution(9359598199062450628)
XLA Ops:
  0.6 0.1 pad_add_fusion.at
  0.7 2.2 %cast_rows.1 = (bf16[32,64,256]{2,1,0:T(8,128)(2,1)S(1)}, s32[8,128]{1,0:T(8,128)S(1)}) custom-call(s32[3]{0:T(128)S(1)} %pad_add_fusion.at, f32[256,8192]{1,0:T(8,128)} %bitcast.20), custom_call_target="tpu_custom_call" | custom-call | bytes 1024 | tf_op jit(solution)/shard_map/cast_rows/pallas_call | solution.py:59
  2.9 1.5 %collective-permute-start = (bf16[32,64,256]{2,1,0:T(8,128)(2,1)S(1)}, bf16[32,64,256]{2,1,0:T(8,128)(2,1)S(1)}, u32[]{:S(2)}, u32[]{:S(2)}) collective-permute-start(bf16[32,64,256]{2,1,0:T(8,128)(2,1)S(1)} %get-tuple-element.33), channel_id=1, source_target_pairs={{0,32},{32,0},{1,33},{33,1},{2,34},{34,2},{3,35},{35,3},{4,36},{36... | collective-permute-start | bytes 3145736 | tf_op jit(solution)/shard_map/ppermute | solution.py:430
  4.4 2.6 %pick_rows.1 = (bf16[16,2,64,256]{3,2,1,0:T(8,128)(2,1)}, s32[8,128]{1,0:T(8,128)S(1)}) custom-call(s32[3]{0:T(128)S(1)} %pad_add_fusion.at, bf16[16,2,256,256]{3,2,1,0:T(8,128)(2,1)} %bitcast.25, s32[8,128]{1,0:T(8,128)S(1)} %get-tuple-element.34.refs_1_), custom_call_target="tpu_custom_call" | custom-call | bytes 1024 | tf_op jit(solution)/shard_map/pick_rows/pallas_call | solution.py:59
  7.0 0.0 collective-permute-done.refs_1_
  7.0 2.9 %add_theirs.1 = (bf16[32,64,256]{2,1,0:T(8,128)(2,1)}, s32[8,128]{1,0:T(8,128)S(1)}) custom-call(s32[3]{0:T(128)S(1)} %pad_add_fusion.at, f32[256,8192]{1,0:T(8,128)} %bitcast.21, bf16[32,64,256]{2,1,0:T(8,128)(2,1)S(1)} %collective-permute-done.refs_1_, s32[8,128]{1,0:T(8,128)S(1)} %get-tuple-element.35.refs_2_), custom_call_target="tpu_custom_call" | custom-call | bytes 1024 | tf_op jit(solution)/shard_map/add_theirs/pallas_call | solution.py:59
  9.9 1.4 %collective-permute-start.3 = (bf16[32,64,256]{2,1,0:T(8,128)(2,1)}, bf16[32,64,256]{2,1,0:T(8,128)(2,1)S(1)}, u32[]{:S(2)}, u32[]{:S(2)}) collective-permute-start(bf16[32,64,256]{2,1,0:T(8,128)(2,1)} %get-tuple-element.41), channel_id=1, source_target_pairs={{0,64},{64,0},{1,65},{65,1},{2,66},{66,2},{3,67},{67,3},{4,68},{68... | collective-permute-start | bytes 3145736 | tf_op jit(solution)/shard_map/ppermute | solution.py:433
  11.3 9.6 %all-to-all-start = ((bf16[32,64,256]{2,1,0:T(8,128)(2,1)}), bf16[32,64,256]{2,1,0:T(8,128)(2,1)S(1)}, u32[]{:S(2)}, u32[]{:S(2)}) async-start(bf16[32,64,256]{2,1,0:T(8,128)(2,1)} %bitcast.26), calls=%async_computation | async-start | bytes 2097152 | tf_op jit(solution)/shard_map/all_to_all | solution.py:425
  20.9 2.2 %cast_own.1 = (bf16[32,32,256]{2,1,0:T(8,128)(2,1)S(1)}, bf16[32,32,256]{2,1,0:T(8,128)(2,1)S(1)}, s32[8,128]{1,0:T(8,128)S(1)}) custom-call(s32[3]{0:T(128)S(1)} %pad_add_fusion.at, f32[256,8192]{1,0:T(8,128)} %bitcast.22, s32[8,128]{1,0:T(8,128)S(1)} %get-tuple-element.36.refs_1_), custom_call_target="tpu_custom_call" | custom-call | bytes 1024 | tf_op jit(solution)/shard_map/cast_own/pallas_call | solution.py:59
  23.1 0.7 collective-permute-start.1
  23.7 0.1 collective-permute-start.2
  23.8 1.4 %collective-permute-done.1.refs_1_ = bf16[32,32,256]{2,1,0:T(8,128)(2,1)S(1)} collective-permute-done((bf16[32,32,256]{2,1,0:T(8,128)(2,1)S(1)}, bf16[32,32,256]{2,1,0:T(8,128)(2,1)S(1)}, u32[]{:S(2)}, u32[]{:S(2)}) %collective-permute-start.1) | collective-permute-done | bytes 524320 | tf_op jit(solution)/shard_map/ppermute | solution.py:430
  25.3 0.7 collective-permute-done.2.refs_2_
  26.0 2.2 %add_own.1 = (bf16[32,64,256]{2,1,0:T(8,128)(2,1)S(1)}, s32[8,128]{1,0:T(8,128)S(1)}) custom-call(s32[3]{0:T(128)S(1)} %pad_add_fusion.at, f32[256,8192]{1,0:T(8,128)} %bitcast.23, bf16[32,32,256]{2,1,0:T(8,128)(2,1)S(1)} %collective-permute-done.1.refs_1_, bf16[32,32,256]{2,1,0:T(8,128)(2,1)S(1)} %collective-permute-done.2.refs_2_, ...), custom_call_target="tpu_custom_call" | custom-call | bytes 1024 | tf_op jit(solution)/shard_map/add_own/pallas_call | solution.py:59
  28.2 11.0 %all-to-all-done.refs_2_ = bf16[32,64,256]{2,1,0:T(8,128)(2,1)S(1)} async-done(((bf16[32,64,256]{2,1,0:T(8,128)(2,1)}), bf16[32,64,256]{2,1,0:T(8,128)(2,1)S(1)}, u32[]{:S(2)}, u32[]{:S(2)}) %all-to-all-start) | async-done | bytes 1048608 | tf_op jit(solution)/shard_map/all_to_all | solution.py:425
  39.2 0.0 collective-permute-done.3.refs_1_
  39.2 1.9 %blend_rows.1 = (bf16[32,64,256]{2,1,0:T(8,128)(2,1)}, s32[8,128]{1,0:T(8,128)S(1)}) custom-call(s32[3]{0:T(128)S(1)} %pad_add_fusion.at, bf16[32,64,256]{2,1,0:T(8,128)(2,1)S(1)} %get-tuple-element.40.refs_0_, bf16[32,64,256]{2,1,0:T(8,128)(2,1)S(1)} %collective-permute-done.3.refs_1_, bf16[32,64,256]{2,1,0:T(8,128)(2,1)S(1)} %all-to-all-done.refs_2_, ...), custom_call_target="tpu_custom_call" | custom-call | bytes 1024 | tf_op jit(solution)/shard_map/blend_rows/pallas_call | solution.py:59
  41.1 1.8 %collective-permute-start.5 = (bf16[32,64,256]{2,1,0:T(8,128)(2,1)}, bf16[32,64,256]{2,1,0:T(8,128)(2,1)S(1)}, u32[]{:S(2)}, u32[]{:S(2)}) collective-permute-start(bf16[32,64,256]{2,1,0:T(8,128)(2,1)} %get-tuple-element.44.refs_1_), channel_id=1, source_target_pairs={{0,32},{32,0},{1,33},{33,1},{2,34},{34,2},{3,35},{35,3},{4,36},{36... | collective-permute-start | bytes 3145736 | tf_op jit(solution)/shard_map/ppermute | solution.py:430
  42.9 0.0 collective-permute-start.4
  42.9 5.8 %all-to-all-start.1 = ((bf16[32,64,256]{2,1,0:T(8,128)(2,1)}), bf16[32,64,256]{2,1,0:T(8,128)(2,1)S(1)}, u32[]{:S(2)}, u32[]{:S(2)}) async-start(bf16[32,64,256]{2,1,0:T(8,128)(2,1)} %get-tuple-element.44.refs_1_), calls=%async_computation.1 | async-start | bytes 2097152 | tf_op jit(solution)/shard_map/all_to_all | solution.py:425
  48.7 0.0 collective-permute-done.5.refs_0_
  48.7 4.0 %write_rows.5 = (f32[256,8192]{1,0:T(8,128)}, s32[8,128]{1,0:T(8,128)S(1)}) custom-call(s32[3]{0:T(128)S(1)} %pad_add_fusion.at, bf16[32,64,256]{2,1,0:T(8,128)(2,1)S(1)} %collective-permute-done.5.refs_0_, bf16[32,64,256]{2,1,0:T(8,128)(2,1)} %get-tuple-element.44.refs_1_, s32[8,128]{1,0:T(8,128)S(1)} %get-tuple-element.45.refs_2_), custom_call_target="tpu_custom_call" | custom-call | bytes 11534336 | tf_op jit(solution)/shard_map/write_rows/pallas_call | solution.py:59
  52.7 14.2 %all-to-all-done.1.refs_0_ = bf16[32,64,256]{2,1,0:T(8,128)(2,1)S(1)} async-done(((bf16[32,64,256]{2,1,0:T(8,128)(2,1)}), bf16[32,64,256]{2,1,0:T(8,128)(2,1)S(1)}, u32[]{:S(2)}, u32[]{:S(2)}) %all-to-all-start.1) | async-done | bytes 1048608 | tf_op jit(solution)/shard_map/all_to_all | solution.py:425
  66.9 1.6 %split_back.1 = (bf16[32,32,256]{2,1,0:T(8,128)(2,1)}, bf16[32,32,256]{2,1,0:T(8,128)(2,1)S(1)}, s32[8,128]{1,0:T(8,128)S(1)}) custom-call(s32[3]{0:T(128)S(1)} %pad_add_fusion.at, bf16[32,64,256]{2,1,0:T(8,128)(2,1)S(1)} %all-to-all-done.1.refs_0_, s32[8,128]{1,0:T(8,128)S(1)} %get-tuple-element.46.refs_1_), custom_call_target="tpu_custom_call" | custom-call | bytes 1024 | tf_op jit(solution)/shard_map/split_back/pallas_call | solution.py:59
  68.4 1.8 %collective-permute-start.10 = (bf16[32,32,256]{2,1,0:T(8,128)(2,1)S(1)}, bf16[32,32,256]{2,1,0:T(8,128)(2,1)}, u32[]{:S(2)}, u32[]{:S(2)}) collective-permute-start(bf16[32,32,256]{2,1,0:T(8,128)(2,1)S(1)} %get-tuple-element.50), channel_id=1, source_target_pairs={{0,32},{32,0},{1,33},{33,1},{2,34},{34,2},{3,35},{35,3},{4,36},{36... | collective-permute-start | bytes 1572872 | tf_op jit(solution)/shard_map/ppermute | solution.py:430
  70.3 0.0 collective-permute-start.9
  70.3 0.0 collective-permute-start.8
  70.3 0.0 collective-permute-done.4.refs_0_
  70.3 1.4 %split_finished.1 = (bf16[32,32,256]{2,1,0:T(8,128)(2,1)}, bf16[32,32,256]{2,1,0:T(8,128)(2,1)S(1)}, s32[8,128]{1,0:T(8,128)S(1)}) custom-call(s32[3]{0:T(128)S(1)} %pad_add_fusion.at, bf16[32,64,256]{2,1,0:T(8,128)(2,1)S(1)} %collective-permute-done.4.refs_0_, s32[8,128]{1,0:T(8,128)S(1)} %get-tuple-element.47.refs_1_), custom_call_target="tpu_custom_call" | custom-call | bytes 1024 | tf_op jit(solution)/shard_map/split_finished/pallas_call | solution.py:59
  71.7 0.6 collective-permute-start.6
  72.3 0.1 collective-permute-start.7
  72.4 3.9 %all-to-all-start.2 = ((bf16[32,32,256]{2,1,0:T(8,128)(2,1)}), bf16[32,32,256]{2,1,0:T(8,128)(2,1)S(1)}, u32[]{:S(2)}, u32[]{:S(2)}) async-start(bf16[32,32,256]{2,1,0:T(8,128)(2,1)} %get-tuple-element.49.refs_3_), calls=%async_computation.2 | async-start | bytes 1048576 | tf_op jit(solution)/shard_map/all_to_all | solution.py:425
  76.3 0.0 collective-permute-done.10
  76.3 0.0 collective-permute-done.9
  76.3 3.4 %write_rows.6 = (bf16[16,2,256,256]{3,2,1,0:T(8,128)(2,1)}, s32[8,128]{1,0:T(8,128)S(1)}) custom-call(s32[3]{0:T(128)S(1)} %pad_add_fusion.at, bf16[16,2,32,256]{3,2,1,0:T(8,128)(2,1)} %bitcast.7.refs_0_, bf16[16,2,32,256]{3,2,1,0:T(8,128)(2,1)} %bitcast.8.refs_1_, bf16[16,2,32,256]{3,2,1,0:T(8,128)(2,1)S(1)} %bitcast.16, ...), custom_call_target="tpu_custom_call" | custom-call | bytes 1024 | tf_op jit(solution)/shard_map/write_rows/pallas_call | solution.py:59
  79.7 3.5 %collective-permute-done.8 = bf16[32,32,256]{2,1,0:T(8,128)(2,1)S(1)} collective-permute-done((bf16[32,32,256]{2,1,0:T(8,128)(2,1)S(1)}, bf16[32,32,256]{2,1,0:T(8,128)(2,1)S(1)}, u32[]{:S(2)}, u32[]{:S(2)}) %collective-permute-start.8) | collective-permute-done | bytes 524320 | tf_op jit(solution)/shard_map/ppermute | solution.py:433
  83.2 1.4 %collective-permute-start.12 = (bf16[32,32,256]{2,1,0:T(8,128)(2,1)S(1)}, bf16[32,32,256]{2,1,0:T(8,128)(2,1)S(1)}, u32[]{:S(2)}, u32[]{:S(2)}) collective-permute-start(bf16[32,32,256]{2,1,0:T(8,128)(2,1)S(1)} %collective-permute-done.8), channel_id=1, source_target_pairs={{0,32},{32,0},{1,33},{33,1},{2,34},{34,2},{3,35},{35,3},{4,36},{36... | collective-permute-start | bytes 1572872 | tf_op jit(solution)/shard_map/ppermute | solution.py:430
  84.6 0.0 collective-permute-done.6.refs_0_
  84.6 0.0 collective-permute-done.7.refs_2_
  84.6 3.2 %write_rows.7 = (f32[256,8192]{1,0:T(8,128)}, bf16[16,2,256,256]{3,2,1,0:T(8,128)(2,1)}, s32[8,128]{1,0:T(8,128)S(1)}) custom-call(s32[3]{0:T(128)S(1)} %pad_add_fusion.at, bf16[32,32,256]{2,1,0:T(8,128)(2,1)S(1)} %collective-permute-done.6.refs_0_, ...), custom_call_target="tpu_custom_call", output_to_operand_aliasing={{0}: (6, {}), {1}: (7, {})} | custom-call | bytes 1024 | tf_op jit(solution)/shard_map/write_rows/pallas_call | solution.py:59
  87.8 1.3 %all-to-all-done.2.refs_0_ = bf16[32,32,256]{2,1,0:T(8,128)(2,1)S(1)} async-done(((bf16[32,32,256]{2,1,0:T(8,128)(2,1)}), bf16[32,32,256]{2,1,0:T(8,128)(2,1)S(1)}, u32[]{:S(2)}, u32[]{:S(2)}) %all-to-all-start.2) | async-done | bytes 524320 | tf_op jit(solution)/shard_map/all_to_all | solution.py:425
  89.1 0.7 copy_tiles.1
  89.8 1.7 %collective-permute-start.11 = (bf16[32,32,256]{2,1,0:T(8,128)(2,1)S(1)}, bf16[32,32,256]{2,1,0:T(8,128)(2,1)S(1)}, u32[]{:S(2)}, u32[]{:S(2)}) collective-permute-start(bf16[32,32,256]{2,1,0:T(8,128)(2,1)S(1)} %get-tuple-element.58), channel_id=1, source_target_pairs={{0,32},{32,0},{1,33},{33,1},{2,34},{34,2},{3,35},{35,3},{4,36},{36... | collective-permute-start | bytes 1572872 | tf_op jit(solution)/shard_map/ppermute | solution.py:430
  91.5 0.0 collective-permute-done.12
  91.5 1.7 %write_rows.8 = (bf16[16,2,256,256]{3,2,1,0:T(8,128)(2,1)}, s32[8,128]{1,0:T(8,128)S(1)}) custom-call(s32[3]{0:T(128)S(1)} %pad_add_fusion.at, bf16[16,2,32,256]{3,2,1,0:T(8,128)(2,1)S(1)} %bitcast.18, bf16[16,2,32,256]{3,2,1,0:T(8,128)(2,1)S(1)} %bitcast.17, bf16[16,2,256,256]{3,2,1,0:T(8,128)(2,1)} %get-tuple-element.59.refs_2_, ...), custom_call_target="tpu_custom_call", output_to_operand_aliasing={{0}: (3, {})} | custom-call | bytes 38797312 | tf_op jit(solution)/shard_map/write_rows/pallas_call | solution.py:59
  93.2 0.0 collective-permute-done.11
  93.2 1.5 %write_rows.9 = (bf16[16,2,256,256]{3,2,1,0:T(8,128)(2,1)}, s32[8,128]{1,0:T(8,128)}) custom-call(s32[3]{0:T(128)S(1)} %pad_add_fusion.at, bf16[16,2,32,256]{3,2,1,0:T(8,128)(2,1)S(1)} %bitcast.19, bf16[16,2,256,256]{3,2,1,0:T(8,128)(2,1)} %get-tuple-element.61.refs_1_, s32[8,128]{1,0:T(8,128)S(1)} %get-tuple-element.62.refs_2_), custom_call_target="tpu_custom_call", output_to_operand_aliasing={{0}: (2, {})} | custom-call | bytes 1024 | tf_op jit(solution)/shard_map/write_rows/pallas_call | solution.py:59
Async XLA Ops:
  2.9 4.2 %collective-permute-start = (bf16[32,64,256]{2,1,0:T(8,128)(2,1)S(1)}, bf16[32,64,256]{2,1,0:T(8,128)(2,1)S(1)}, u32[]{:S(2)}, u32[]{:S(2)}) collective-permute-start(bf16[32,64,256]{2,1,0:T(8,128)(2,1)S(1)} %get-tuple-element.33), channel_id=1, source_target_pairs={{0,32},{32,0},{1,33},{33,1},{2,34},{34,2},{3,35},{35,3},{4,36},{36... | collective-permute-start | bytes 3145736 | tf_op jit(solution)/shard_map/ppermute | solution.py:430
  9.9 29.2 %collective-permute-start.3 = (bf16[32,64,256]{2,1,0:T(8,128)(2,1)}, bf16[32,64,256]{2,1,0:T(8,128)(2,1)S(1)}, u32[]{:S(2)}, u32[]{:S(2)}) collective-permute-start(bf16[32,64,256]{2,1,0:T(8,128)(2,1)} %get-tuple-element.41), channel_id=1, source_target_pairs={{0,64},{64,0},{1,65},{65,1},{2,66},{66,2},{3,67},{67,3},{4,68},{68... | collective-permute-start | bytes 3145736 | tf_op jit(solution)/shard_map/ppermute | solution.py:433
  11.3 27.9 %all-to-all-start = ((bf16[32,64,256]{2,1,0:T(8,128)(2,1)}), bf16[32,64,256]{2,1,0:T(8,128)(2,1)S(1)}, u32[]{:S(2)}, u32[]{:S(2)}) async-start(bf16[32,64,256]{2,1,0:T(8,128)(2,1)} %bitcast.26), calls=%async_computation | async-start | bytes 2097152 | tf_op jit(solution)/shard_map/all_to_all | solution.py:425
  23.1 2.2 %collective-permute-start.1 = (bf16[32,32,256]{2,1,0:T(8,128)(2,1)S(1)}, bf16[32,32,256]{2,1,0:T(8,128)(2,1)S(1)}, u32[]{:S(2)}, u32[]{:S(2)}) collective-permute-start(bf16[32,32,256]{2,1,0:T(8,128)(2,1)S(1)} %get-tuple-element.37), channel_id=1, source_target_pairs={{0,32},{32,0},{1,33},{33,1},{2,34},{34,2},{3,35},{35,3},{4,36},{36... | collective-permute-start | bytes 1572872 | tf_op jit(solution)/shard_map/ppermute | solution.py:430
  23.7 2.3 %collective-permute-start.2 = (bf16[32,32,256]{2,1,0:T(8,128)(2,1)S(1)}, bf16[32,32,256]{2,1,0:T(8,128)(2,1)S(1)}, u32[]{:S(2)}, u32[]{:S(2)}) collective-permute-start(bf16[32,32,256]{2,1,0:T(8,128)(2,1)S(1)} %get-tuple-element.38), channel_id=1, source_target_pairs={{0,32},{32,0},{1,33},{33,1},{2,34},{34,2},{3,35},{35,3},{4,36},{36... | collective-permute-start | bytes 1572872 | tf_op jit(solution)/shard_map/ppermute | solution.py:430
  41.1 7.6 %collective-permute-start.5 = (bf16[32,64,256]{2,1,0:T(8,128)(2,1)}, bf16[32,64,256]{2,1,0:T(8,128)(2,1)S(1)}, u32[]{:S(2)}, u32[]{:S(2)}) collective-permute-start(bf16[32,64,256]{2,1,0:T(8,128)(2,1)} %get-tuple-element.44.refs_1_), channel_id=1, source_target_pairs={{0,32},{32,0},{1,33},{33,1},{2,34},{34,2},{3,35},{35,3},{4,36},{36... | collective-permute-start | bytes 3145736 | tf_op jit(solution)/shard_map/ppermute | solution.py:430
  42.9 27.4 %collective-permute-start.4 = (bf16[32,64,256]{2,1,0:T(8,128)(2,1)}, bf16[32,64,256]{2,1,0:T(8,128)(2,1)S(1)}, u32[]{:S(2)}, u32[]{:S(2)}) collective-permute-start(bf16[32,64,256]{2,1,0:T(8,128)(2,1)} %get-tuple-element.44.refs_1_), channel_id=1, source_target_pairs={{0,64},{64,0},{1,65},{65,1},{2,66},{66,2},{3,67},{67,3},{4,68},{68... | collective-permute-start | bytes 3145736 | tf_op jit(solution)/shard_map/ppermute | solution.py:433
  42.9 24.0 %all-to-all-start.1 = ((bf16[32,64,256]{2,1,0:T(8,128)(2,1)}), bf16[32,64,256]{2,1,0:T(8,128)(2,1)S(1)}, u32[]{:S(2)}, u32[]{:S(2)}) async-start(bf16[32,64,256]{2,1,0:T(8,128)(2,1)} %get-tuple-element.44.refs_1_), calls=%async_computation.1 | async-start | bytes 2097152 | tf_op jit(solution)/shard_map/all_to_all | solution.py:425
  68.4 7.8 %collective-permute-start.10 = (bf16[32,32,256]{2,1,0:T(8,128)(2,1)S(1)}, bf16[32,32,256]{2,1,0:T(8,128)(2,1)}, u32[]{:S(2)}, u32[]{:S(2)}) collective-permute-start(bf16[32,32,256]{2,1,0:T(8,128)(2,1)S(1)} %get-tuple-element.50), channel_id=1, source_target_pairs={{0,32},{32,0},{1,33},{33,1},{2,34},{34,2},{3,35},{35,3},{4,36},{36... | collective-permute-start | bytes 1572872 | tf_op jit(solution)/shard_map/ppermute | solution.py:430
  70.3 6.0 %collective-permute-start.9 = (bf16[32,32,256]{2,1,0:T(8,128)(2,1)}, bf16[32,32,256]{2,1,0:T(8,128)(2,1)}, u32[]{:S(2)}, u32[]{:S(2)}) collective-permute-start(bf16[32,32,256]{2,1,0:T(8,128)(2,1)} %get-tuple-element.52), channel_id=1, source_target_pairs={{0,32},{32,0},{1,33},{33,1},{2,34},{34,2},{3,35},{35,3},{4,36},{36... | collective-permute-start | bytes 1572872 | tf_op jit(solution)/shard_map/ppermute | solution.py:430
  70.3 13.0 %collective-permute-start.8 = (bf16[32,32,256]{2,1,0:T(8,128)(2,1)S(1)}, bf16[32,32,256]{2,1,0:T(8,128)(2,1)S(1)}, u32[]{:S(2)}, u32[]{:S(2)}) collective-permute-start(bf16[32,32,256]{2,1,0:T(8,128)(2,1)S(1)} %get-tuple-element.50), channel_id=1, source_target_pairs={{0,64},{64,0},{1,65},{65,1},{2,66},{66,2},{3,67},{67,3},{4,68},{68... | collective-permute-start | bytes 1572872 | tf_op jit(solution)/shard_map/ppermute | solution.py:433
  71.7 12.9 %collective-permute-start.6 = (bf16[32,32,256]{2,1,0:T(8,128)(2,1)S(1)}, bf16[32,32,256]{2,1,0:T(8,128)(2,1)S(1)}, u32[]{:S(2)}, u32[]{:S(2)}) collective-permute-start(bf16[32,32,256]{2,1,0:T(8,128)(2,1)S(1)} %get-tuple-element.48.refs_1_), channel_id=1, source_target_pairs={{0,32},{32,0},{1,33},{33,1},{2,34},{34,2},{3,35},{35,3},{4,36},{36... | collective-permute-start | bytes 1572872 | tf_op jit(solution)/shard_map/ppermute | solution.py:430
  72.3 12.3 %collective-permute-start.7 = (bf16[32,32,256]{2,1,0:T(8,128)(2,1)}, bf16[32,32,256]{2,1,0:T(8,128)(2,1)S(1)}, u32[]{:S(2)}, u32[]{:S(2)}) collective-permute-start(bf16[32,32,256]{2,1,0:T(8,128)(2,1)} %get-tuple-element.49.refs_3_), channel_id=1, source_target_pairs={{0,32},{32,0},{1,33},{33,1},{2,34},{34,2},{3,35},{35,3},{4,36},{36... | collective-permute-start | bytes 1572872 | tf_op jit(solution)/shard_map/ppermute | solution.py:430
  72.4 16.7 %all-to-all-start.2 = ((bf16[32,32,256]{2,1,0:T(8,128)(2,1)}), bf16[32,32,256]{2,1,0:T(8,128)(2,1)S(1)}, u32[]{:S(2)}, u32[]{:S(2)}) async-start(bf16[32,32,256]{2,1,0:T(8,128)(2,1)} %get-tuple-element.49.refs_3_), calls=%async_computation.2 | async-start | bytes 1048576 | tf_op jit(solution)/shard_map/all_to_all | solution.py:425
  83.2 8.3 %collective-permute-start.12 = (bf16[32,32,256]{2,1,0:T(8,128)(2,1)S(1)}, bf16[32,32,256]{2,1,0:T(8,128)(2,1)S(1)}, u32[]{:S(2)}, u32[]{:S(2)}) collective-permute-start(bf16[32,32,256]{2,1,0:T(8,128)(2,1)S(1)} %collective-permute-done.8), channel_id=1, source_target_pairs={{0,32},{32,0},{1,33},{33,1},{2,34},{34,2},{3,35},{35,3},{4,36},{36... | collective-permute-start | bytes 1572872 | tf_op jit(solution)/shard_map/ppermute | solution.py:430
  89.8 3.4 %collective-permute-start.11 = (bf16[32,32,256]{2,1,0:T(8,128)(2,1)S(1)}, bf16[32,32,256]{2,1,0:T(8,128)(2,1)S(1)}, u32[]{:S(2)}, u32[]{:S(2)}) collective-permute-start(bf16[32,32,256]{2,1,0:T(8,128)(2,1)S(1)} %get-tuple-element.58), channel_id=1, source_target_pairs={{0,32},{32,0},{1,33},{33,1},{2,34},{34,2},{3,35},{35,3},{4,36},{36... | collective-permute-start | bytes 1572872 | tf_op jit(solution)/shard_map/ppermute | solution.py:430

commit v3 on v2

--- a/solution.py
+++ b/solution.py
@@ -295,40 +295,45 @@
     return out
 
 
-def split_back(order, back):
-    def body(at, b_ref, low_ref, high_ref):
-        def work(g):
-            high_ref[g] = b_ref[g, R:]
-            low_ref[g] = b_ref[g, :R]
-
-        each(SHARDS, work)
-
+def plane(at, same):
+    return at[2] if same else 1 - at[2]
+
+
+def split_planes(order, finished, back):
+    def body(at, f_ref, b_ref, first_ref, low_ref, second_ref, high_ref, sems):
+        def stores(p):
+            some = pl.ds(4 * p, 4)
+            ends = ((f_ref, first_ref), (b_ref, low_ref))
+            return [
+                pltpu.make_async_copy(x.at[some, plane(at, True)], o.at[some], sems.at[i, p])
+                for i, (x, o) in enumerate(ends)
+            ]
+
+        def start(p):
+            for store in stores(p):
+                store.start()
+
+        def work(k):
+            high_ref[k] = b_ref[k, plane(at, False)]
+            second_ref[k] = f_ref[k, plane(at, False)]
+
+        def finish(p):
+            for store in stores(p):
+                store.wait()
+
+        each(4, start)
+        each(16, work)
+        each(4, finish)
+
+    half = (16, QUARTER, WIDTH)
     return order.run(
-        body, "split_back", [in_vmem(back)], [VMEM], [tiles_out(R)] * 2, [VMEM] * 2, []
-    )
-
-
-def split_finished(order, finished):
-    def body(at, f_ref, first_ref, second_ref, sems):
-        def store(p):
-            some = pl.ds(p * PER, PER)
-            return pltpu.make_async_copy(f_ref.at[some, pl.ds(0, R)], first_ref.at[some], sems.at[p])
-
-        def work(g):
-            second_ref[g] = f_ref[g, R:]
-
-        each(PARTS, lambda p: store(p).start())
-        each(SHARDS, work)
-        each(PARTS, lambda p: store(p).wait())
-
-    return order.run(
-        body,
-        "split_finished",
-        [in_vmem(finished)],
-        [VMEM],
-        [pltpu.HBM((SHARDS, R, WIDTH), BF), tiles_out(R)],
-        [HBM, VMEM],
-        [pltpu.SemaphoreType.DMA((PARTS,))],
+        body,
+        "split_planes",
+        [in_vmem(x.reshape(16, 2, QUARTER, WIDTH)) for x in (finished, back)],
+        [VMEM, VMEM],
+        [pltpu.HBM(half, BF), jax.ShapeDtypeStruct(half, BF), pltpu.VMEM(half, BF), pltpu.VMEM(half, BF)],
+        [HBM, ANY, VMEM, VMEM],
+        [pltpu.SemaphoreType.DMA((2, 4))],
     )
 
 
@@ -337,79 +342,85 @@
         def work(g):
             o_ref[g] = x_ref[g]
 
-        each(SHARDS, work)
-
-    (out,) = order.run(body, "copy_tiles", [in_vmem(tiles)], [VMEM], [tiles_out(R)], [VMEM], [])
-    return out
+        each(tiles.shape[0], work)
+
+    out = pltpu.VMEM(tiles.shape, BF)
+    return order.run(body, "copy_tiles", [in_vmem(tiles)], [VMEM], [out], [VMEM], [])[0]
 
 
 def write_rows(order, wide_pieces, placed_pieces, blended, anchor, size=1024):
     n, m = len(wide_pieces), len(placed_pieces)
-    rows = [tiles.shape[1] for tiles, _ in wide_pieces]
-    placed_rows = [tiles.shape[1] for tiles, _ in placed_pieces]
+    counts = [len(arrays) for arrays, _, _ in wide_pieces]
+    flat = [x for arrays, _, _ in wide_pieces for x in arrays]
+    late = sum(counts[:-1])
     outs = [pltpu.HBM((ROWS, D), F32)] * (n > 0) + [pltpu.HBM((16, 2, ROWS, WIDTH), BF)] * (m > 0)
     earlier = [x for x, k in ((blended, n), (anchor, m)) if k and x is not None]
-    tops = max(rows, default=16)
 
     def body(at, *refs):
-        tiles, refs = refs[:n], refs[n:]
+        flat_refs, refs = list(refs[: len(flat)]), refs[len(flat) :]
         placed, refs = refs[:m], refs[m + len(earlier) :]
         out_refs, (wide, held, sems, placed_sems, held_sem) = refs[: len(outs)], refs[len(outs) :]
 
-        def place(i, xh, p):
-            some = pl.ds(8 * p, 8)
-            there = pl.ds(member_row(at, placed_pieces[i][1], xh), placed_rows[i])
+        def place(i, p):
+            some = pl.ds(4 * p, 4)
+            core, chip, same = placed_pieces[i][1:]
+            there = pl.ds(first_row(at, core, chip, 0), QUARTER)
             return pltpu.make_async_copy(
-                placed[i].at[some, xh], out_refs[-1].at[some, xh, there, :], placed_sems.at[i, xh, p]
+                placed[i].at[some], out_refs[-1].at[some, plane(at, same), there, :], placed_sems.at[i, p]
             )
 
         def copy(i, p):
-            some = pl.ds(0, rows[i])
-            there = pl.ds(first_row(at, *wide_pieces[i][1]), rows[i])
+            there = pl.ds(first_row(at, *wide_pieces[i][1:], 0), QUARTER)
             return pltpu.make_async_copy(
-                wide.at[i, some, span_of(p)], out_refs[0].at[there, span_of(p)], sems.at[i, p]
+                wide.at[i, :, span_of(p)], out_refs[0].at[there, span_of(p)], sems.at[i, p]
             )
 
-        def work(i, ref, p):
-            for k in range(PER):
-                g = p * PER + k
-                wide[i, : rows[i], columns(g)] = ref[g].astype(F32)
+        def work(i, tiles, p):
+            if len(tiles) == 1:
+                for k in range(PER):
+                    g = p * PER + k
+                    wide[i, :, columns(g)] = tiles[0][g].astype(F32)
+            else:
+                for k in range(PER // 2):
+                    yz = p * (PER // 2) + k
+                    for ref, same in zip(tiles, (True, False)):
+                        wide[i, :, columns(2 * yz + plane(at, same))] = ref[yz].astype(F32)
             copy(i, p).start()
 
-        both = [(i, xh) for i in range(m) for xh in range(2)]
         if n:
-            last = pltpu.make_async_copy(tiles[-1], held, held_sem)
+            last = pltpu.make_async_copy(flat_refs[late], held, held_sem)
             last.start()
-        for i, xh in both:
-            each(2, lambda p, i=i, xh=xh: place(i, xh, p).start())
+            flat_refs[late] = held
+        for i in range(m):
+            each(4, lambda p, i=i: place(i, p).start())
         for i in range(n):
             if i == n - 1:
                 last.wait()
-            each(PARTS, lambda p, i=i: work(i, held if i == n - 1 else tiles[i], p))
+            tiles = flat_refs[sum(counts[:i]) : sum(counts[: i + 1])]
+            each(PARTS, lambda p, i=i, tiles=tiles: work(i, tiles, p))
         for i in range(n):
             each(PARTS, lambda p, i=i: copy(i, p).wait())
-        for i, xh in both:
-            each(2, lambda p, i=i, xh=xh: place(i, xh, p).wait())
-
-    args = [in_vmem(t) for t, _ in wide_pieces[:-1]]
-    args += [pltpu.with_memory_space_constraint(t, pltpu.HBM) for t, _ in wide_pieces[-1:]]
-    args += [in_vmem(t.reshape(16, 2, r, WIDTH)) for (t, _), r in zip(placed_pieces, placed_rows)]
-    specs = [VMEM] * (n - 1) + [HBM] * (n > 0) + [VMEM] * m
+        for i in range(m):
+            each(4, lambda p, i=i: place(i, p).wait())
+
+    in_hbm = lambda x: pltpu.with_memory_space_constraint(x, pltpu.HBM)
+    args = [in_hbm(x) if i == late else in_vmem(x) for i, x in enumerate(flat)]
+    specs = [HBM if i == late else VMEM for i in range(len(flat))]
     return order.run(
         body,
         "write_rows",
-        args + earlier,
-        specs + [HBM] * len(earlier),
+        args + [in_vmem(x) for x, *_ in placed_pieces] + earlier,
+        specs + [VMEM] * m + [HBM] * len(earlier),
         outs,
         [HBM] * len(outs),
         [
-            pltpu.VMEM((max(n, 1), tops, D if n else 128), F32),
-            pltpu.VMEM((SHARDS, rows[-1] if n else 16, WIDTH), BF),
+            pltpu.VMEM((max(n, 1), QUARTER, D if n else 128), F32),
+            pltpu.VMEM(flat[late].shape if n else (1, 16, 128), BF),
             pltpu.SemaphoreType.DMA((max(n, 1), PARTS)),
-            pltpu.SemaphoreType.DMA((max(m, 1), 2, 2)),
+            pltpu.SemaphoreType.DMA((max(m, 1), 4)),
             pltpu.SemaphoreType.DMA,
         ],
-        {n + m + 1 + k: k for k in range(len(earlier))},
+        {len(flat) + m + 1 + k: k for k in range(len(earlier))},
         size,
     )
 
@@ -441,28 +452,27 @@
     own = blend_rows(order, own, other, fetched)
     finished = chip(own)
     back = exchange(own)
-    pieces = [(core(own), (False, True, 0)), (own, (True, True, 0))]
+    pieces = [([core(own)], False, True), ([own], True, True)]
     (blended,) = write_rows(order, pieces, [], None, None, WRITE_COST)
 
-    back = split_back(order, back)
-    first, second = split_finished(order, finished)
-    back_first = exchange(first)
-    back_second = chip(back[1])
-    pieces = []
-    for j, tiles in enumerate(back):
-        pieces += [(tiles, (True, True, j * R)), (core(tiles), (False, True, j * R))]
+    first, low, second, high = split_planes(order, finished, back)
+    back_first = lax.all_to_all(first, ("y", "z"), split_axis=0, concat_axis=0, tiled=True)
+    back_second = chip(high)
+    pieces = [
+        (low, True, True, True),
+        (core(low), False, True, True),
+        (high, True, False, False),
+        (core(high), False, False, False),
+    ]
     (new_anchor,) = write_rows(order, [], pieces, None, None)
-    pieces = []
-    for j, tiles in ((1, second), (0, first)):
-        pieces += [(core(tiles), (False, False, j * R)), (tiles, (True, False, j * R))]
-    blended, new_anchor = write_rows(
-        order, pieces, [(back_second, (True, False, R))], blended, new_anchor
-    )
+    back_second = copy_tiles(order, back_second)
+    wide_pieces = [([core(first), core(second)], False, False), ([first, second], True, False)]
+    pieces = [(back_second, True, True, False)]
+    blended, new_anchor = write_rows(order, wide_pieces, pieces, blended, new_anchor)
     back_first = copy_tiles(order, back_first)
-    pieces = [(back_first, (True, False, 0)), (core(back_second), (False, False, R))]
+    pieces = [(back_first, True, False, True), (core(back_second), False, True, False)]
     (new_anchor,) = write_rows(order, [], pieces, None, new_anchor, LAST_COST)
-    pieces = [(core(back_first), (False, False, 0))]
-    (new_anchor,) = write_rows(order, [], pieces, None, new_anchor)
+    (new_anchor,) = write_rows(order, [], [(core(back_first), False, False, True)], None, new_anchor)
     return blended, new_anchor.reshape(SHARDS * ROWS, WIDTH)
 
 

time: 95.4 us -> 95 us (level)
  starting transfers between devices: 30.2 us -> 27.9 us
  waiting for transfers between devices: 32.2 us -> 33.8 us
    all_to_all x0 -> x1, starting transfers between devices: none -> 3.96 us  [per_device(): lax.all_to_all(first, ('y', 'z'), split_axis=0, concat_axis=0, tiled=True)]
    all_to_all x3 -> x2, starting transfers between devices: 19.3 us -> 15.4 us  [exchange(): lax.all_to_all(tiles, AXES, split_axis=0, concat_axis=0, axis_index_group...]
    ppermute x3, waiting for transfers between devices: 3.52 us -> 6.18 us  [chip(): return lax.ppermute(tiles, 'xl', swap)]
    ppermute x10, starting transfers between devices: 9.59 us -> 7.23 us  [core(): return lax.ppermute(tiles, 'c', swap)]
    all_to_all x3 -> x2, waiting for transfers between devices: 26.5 us -> 25.2 us  [exchange(): lax.all_to_all(tiles, AXES, split_axis=0, concat_axis=0, axis_index_group...]
  transfers between devices with their start and end apart: 16 -> 16, of which waited for: 6 -> 7; matrix products, arithmetic and copies ran while one was open for 0% -> 0% of each run, Pallas kernels for 24% -> 23%
where the time goes in v3:
time: 95 us; the launch traced here: 94.2 us
  waiting for transfers between devices  33.8 us (36%)
  Pallas kernels  31.6 us (33%)
  starting transfers between devices  27.9 us (29%)
    pallas_call x14, Pallas kernels, run(): pl.pallas_call(ordered, out_shape=[*outs, TOKEN], grid_spec=pltpu.Prefetc...  31.6 us
    all_to_all x2, waiting for transfers between devices, exchange(): lax.all_to_all(tiles, AXES, split_axis=0, concat_axis=0, axis_index_group...  25.2 us
    all_to_all x2, starting transfers between devices, exchange(): lax.all_to_all(tiles, AXES, split_axis=0, concat_axis=0, axis_index_group...  15.4 us
    ppermute x10, starting transfers between devices, core(): return lax.ppermute(tiles, 'c', swap)  7.23 us
    ppermute x3, waiting for transfers between devices, chip(): return lax.ppermute(tiles, 'xl', swap)  6.18 us
    all_to_all x1, starting transfers between devices, per_device(): lax.all_to_all(first, ('y', 'z'), split_axis=0, concat_axis=0, tiled=True)  3.96 us
    ppermute x10, waiting for transfers between devices, core(): return lax.ppermute(tiles, 'c', swap)  2.43 us
  transfers between devices with their start and end apart: 16, of which 7 were waited for; matrix products, arithmetic and copies ran while one was open for 0% of the time, Pallas kernels for 23%

profile of v3, /device:TPU:1, one launch (start us, length us, event | category | flops | bytes accessed | tf_op | source)
XLA Modules:
  0.0 94.2 jit_solution(7161805640829874540)
XLA Ops:
  0.6 0.1 pad_add_fusion.at
  0.7 2.2 %cast_rows.1 = (bf16[32,64,256]{2,1,0:T(8,128)(2,1)S(1)}, s32[8,128]{1,0:T(8,128)S(1)}) custom-call(s32[3]{0:T(128)S(1)} %pad_add_fusion.at, f32[256,8192]{1,0:T(8,128)} %bitcast.11), custom_call_target="tpu_custom_call" | custom-call | bytes 1024 | tf_op jit(solution)/shard_map/cast_rows/pallas_call | solution.py:59
  2.9 1.5 %collective-permute-start = (bf16[32,64,256]{2,1,0:T(8,128)(2,1)S(1)}, bf16[32,64,256]{2,1,0:T(8,128)(2,1)S(1)}, u32[]{:S(2)}, u32[]{:S(2)}) collective-permute-start(bf16[32,64,256]{2,1,0:T(8,128)(2,1)S(1)} %get-tuple-element.34), channel_id=1, source_target_pairs={{0,32},{32,0},{1,33},{33,1},{2,34},{34,2},{3,35},{35,3},{4,36},{36... | collective-permute-start | bytes 3145736 | tf_op jit(solution)/shard_map/ppermute | solution.py:441
  4.4 2.6 %pick_rows.1 = (bf16[16,2,64,256]{3,2,1,0:T(8,128)(2,1)}, s32[8,128]{1,0:T(8,128)S(1)}) custom-call(s32[3]{0:T(128)S(1)} %pad_add_fusion.at, bf16[16,2,256,256]{3,2,1,0:T(8,128)(2,1)} %bitcast.16, s32[8,128]{1,0:T(8,128)S(1)} %get-tuple-element.35.refs_1_), custom_call_target="tpu_custom_call" | custom-call | bytes 1024 | tf_op jit(solution)/shard_map/pick_rows/pallas_call | solution.py:59
  7.0 0.0 collective-permute-done.refs_1_
  7.0 2.9 %add_theirs.1 = (bf16[32,64,256]{2,1,0:T(8,128)(2,1)}, s32[8,128]{1,0:T(8,128)S(1)}) custom-call(s32[3]{0:T(128)S(1)} %pad_add_fusion.at, f32[256,8192]{1,0:T(8,128)} %bitcast.12, bf16[32,64,256]{2,1,0:T(8,128)(2,1)S(1)} %collective-permute-done.refs_1_, s32[8,128]{1,0:T(8,128)S(1)} %get-tuple-element.36.refs_2_), custom_call_target="tpu_custom_call" | custom-call | bytes 1024 | tf_op jit(solution)/shard_map/add_theirs/pallas_call | solution.py:59
  9.9 1.4 %collective-permute-start.3 = (bf16[32,64,256]{2,1,0:T(8,128)(2,1)}, bf16[32,64,256]{2,1,0:T(8,128)(2,1)S(1)}, u32[]{:S(2)}, u32[]{:S(2)}) collective-permute-start(bf16[32,64,256]{2,1,0:T(8,128)(2,1)} %get-tuple-element.42), channel_id=1, source_target_pairs={{0,64},{64,0},{1,65},{65,1},{2,66},{66,2},{3,67},{67,3},{4,68},{68... | collective-permute-start | bytes 3145736 | tf_op jit(solution)/shard_map/ppermute | solution.py:444
  11.3 9.6 %all-to-all-start = ((bf16[32,64,256]{2,1,0:T(8,128)(2,1)}), bf16[32,64,256]{2,1,0:T(8,128)(2,1)S(1)}, u32[]{:S(2)}, u32[]{:S(2)}) async-start(bf16[32,64,256]{2,1,0:T(8,128)(2,1)} %bitcast.17), calls=%async_computation | async-start | bytes 2097152 | tf_op jit(solution)/shard_map/all_to_all | solution.py:436
  20.9 2.2 %cast_own.1 = (bf16[32,32,256]{2,1,0:T(8,128)(2,1)S(1)}, bf16[32,32,256]{2,1,0:T(8,128)(2,1)S(1)}, s32[8,128]{1,0:T(8,128)S(1)}) custom-call(s32[3]{0:T(128)S(1)} %pad_add_fusion.at, f32[256,8192]{1,0:T(8,128)} %bitcast.13, s32[8,128]{1,0:T(8,128)S(1)} %get-tuple-element.37.refs_1_), custom_call_target="tpu_custom_call" | custom-call | bytes 1024 | tf_op jit(solution)/shard_map/cast_own/pallas_call | solution.py:59
  23.1 0.7 collective-permute-start.1
  23.7 0.1 collective-permute-start.2
  23.8 1.4 %collective-permute-done.1.refs_1_ = bf16[32,32,256]{2,1,0:T(8,128)(2,1)S(1)} collective-permute-done((bf16[32,32,256]{2,1,0:T(8,128)(2,1)S(1)}, bf16[32,32,256]{2,1,0:T(8,128)(2,1)S(1)}, u32[]{:S(2)}, u32[]{:S(2)}) %collective-permute-start.1) | collective-permute-done | bytes 524320 | tf_op jit(solution)/shard_map/ppermute | solution.py:441
  25.3 0.7 collective-permute-done.2.refs_2_
  26.0 2.2 %add_own.1 = (bf16[32,64,256]{2,1,0:T(8,128)(2,1)S(1)}, s32[8,128]{1,0:T(8,128)S(1)}) custom-call(s32[3]{0:T(128)S(1)} %pad_add_fusion.at, f32[256,8192]{1,0:T(8,128)} %bitcast.14, bf16[32,32,256]{2,1,0:T(8,128)(2,1)S(1)} %collective-permute-done.1.refs_1_, bf16[32,32,256]{2,1,0:T(8,128)(2,1)S(1)} %collective-permute-done.2.refs_2_, ...), custom_call_target="tpu_custom_call" | custom-call | bytes 1024 | tf_op jit(solution)/shard_map/add_own/pallas_call | solution.py:59
  28.2 11.0 %all-to-all-done.refs_2_ = bf16[32,64,256]{2,1,0:T(8,128)(2,1)S(1)} async-done(((bf16[32,64,256]{2,1,0:T(8,128)(2,1)}), bf16[32,64,256]{2,1,0:T(8,128)(2,1)S(1)}, u32[]{:S(2)}, u32[]{:S(2)}) %all-to-all-start) | async-done | bytes 1048608 | tf_op jit(solution)/shard_map/all_to_all | solution.py:436
  39.2 0.0 collective-permute-done.3.refs_1_
  39.2 1.9 %blend_rows.1 = (bf16[32,64,256]{2,1,0:T(8,128)(2,1)}, s32[8,128]{1,0:T(8,128)S(1)}) custom-call(s32[3]{0:T(128)S(1)} %pad_add_fusion.at, bf16[32,64,256]{2,1,0:T(8,128)(2,1)S(1)} %get-tuple-element.41.refs_0_, bf16[32,64,256]{2,1,0:T(8,128)(2,1)S(1)} %collective-permute-done.3.refs_1_, bf16[32,64,256]{2,1,0:T(8,128)(2,1)S(1)} %all-to-all-done.refs_2_, ...), custom_call_target="tpu_custom_call" | custom-call | bytes 1024 | tf_op jit(solution)/shard_map/blend_rows/pallas_call | solution.py:59
  41.1 1.8 %collective-permute-start.5 = (bf16[32,64,256]{2,1,0:T(8,128)(2,1)}, bf16[32,64,256]{2,1,0:T(8,128)(2,1)S(1)}, u32[]{:S(2)}, u32[]{:S(2)}) collective-permute-start(bf16[32,64,256]{2,1,0:T(8,128)(2,1)} %get-tuple-element.45.refs_1_), channel_id=1, source_target_pairs={{0,32},{32,0},{1,33},{33,1},{2,34},{34,2},{3,35},{35,3},{4,36},{36... | collective-permute-start | bytes 3145736 | tf_op jit(solution)/shard_map/ppermute | solution.py:441
  42.9 0.0 collective-permute-start.4
  42.9 5.8 %all-to-all-start.1 = ((bf16[32,64,256]{2,1,0:T(8,128)(2,1)}), bf16[32,64,256]{2,1,0:T(8,128)(2,1)S(1)}, u32[]{:S(2)}, u32[]{:S(2)}) async-start(bf16[32,64,256]{2,1,0:T(8,128)(2,1)} %get-tuple-element.45.refs_1_), calls=%async_computation.1 | async-start | bytes 2097152 | tf_op jit(solution)/shard_map/all_to_all | solution.py:436
  48.7 0.0 collective-permute-done.5.refs_0_
  48.7 4.0 %write_rows.5 = (f32[256,8192]{1,0:T(8,128)}, s32[8,128]{1,0:T(8,128)S(1)}) custom-call(s32[3]{0:T(128)S(1)} %pad_add_fusion.at, bf16[32,64,256]{2,1,0:T(8,128)(2,1)S(1)} %collective-permute-done.5.refs_0_, bf16[32,64,256]{2,1,0:T(8,128)(2,1)} %get-tuple-element.45.refs_1_, s32[8,128]{1,0:T(8,128)S(1)} %get-tuple-element.46.refs_2_), custom_call_target="tpu_custom_call" | custom-call | bytes 11534336 | tf_op jit(solution)/shard_map/write_rows/pallas_call | solution.py:59
  52.7 14.2 %all-to-all-done.1 = bf16[32,64,256]{2,1,0:T(8,128)(2,1)S(1)} async-done(((bf16[32,64,256]{2,1,0:T(8,128)(2,1)}), bf16[32,64,256]{2,1,0:T(8,128)(2,1)S(1)}, u32[]{:S(2)}, u32[]{:S(2)}) %all-to-all-start.1) | async-done | bytes 1048608 | tf_op jit(solution)/shard_map/all_to_all | solution.py:436
  66.9 0.9 collective-permute-done.4
  67.8 1.6 %split_planes.1 = (bf16[16,64,256]{2,1,0:T(8,128)(2,1)}, bf16[16,64,256]{2,1,0:T(8,128)(2,1)}, bf16[16,64,256]{2,1,0:T(8,128)(2,1)S(1)}, bf16[16,64,256]{2,1,0:T(8,128)(2,1)S(1)}, s32[8,128]{1,0:T(8,128)S(1)}) custom-call(s32[3]{0:T(128)S(1)} %pad_add_fusion.at, bf16[16,2,64,256]{3,2,1,0:T(8,128)(2,1)S(1)} %bitcast.10, bf16[16,2,64,256]{3,2,1,0:T(8,128)(2,1)S(1)} %bitcast.9, ...), custom_call_target="tpu_custom_call" | custom-call | bytes 1024 | tf_op jit(solution)/shard_map/split_planes/pallas_call | solution.py:59
  69.4 1.0 %collective-permute-start.10 = (bf16[16,64,256]{2,1,0:T(8,128)(2,1)S(1)}, bf16[16,64,256]{2,1,0:T(8,128)(2,1)S(1)}, u32[]{:S(2)}, u32[]{:S(2)}) collective-permute-start(bf16[16,64,256]{2,1,0:T(8,128)(2,1)S(1)} %get-tuple-element.50.refs_2_), channel_id=1, source_target_pairs={{0,32},{32,0},{1,33},{33,1},{2,34},{34,2},{3,35},{35,3},{4,36},{36... | collective-permute-start | bytes 1572872 | tf_op jit(solution)/shard_map/ppermute | solution.py:441
  70.4 0.1 collective-permute-start.9
  70.5 0.0 collective-permute-start.8
  70.5 0.7 collective-permute-start.6
  71.2 0.0 collective-permute-start.7
  71.2 4.0 %all-to-all-start.2 = ((bf16[16,64,256]{2,1,0:T(8,128)(2,1)}), bf16[16,64,256]{2,1,0:T(8,128)(2,1)S(1)}, u32[]{:S(2)}, u32[]{:S(2)}) async-start(bf16[16,64,256]{2,1,0:T(8,128)(2,1)} %get-tuple-element.48.refs_2_), calls=%async_computation.2 | async-start | bytes 1048576 | tf_op jit(solution)/shard_map/all_to_all | solution.py:459
  75.1 0.0 collective-permute-done.10.refs_3_
  75.2 0.0 collective-permute-done.9.refs_1_
  75.2 3.3 %write_rows.6 = (bf16[16,2,256,256]{3,2,1,0:T(8,128)(2,1)}, s32[8,128]{1,0:T(8,128)S(1)}) custom-call(s32[3]{0:T(128)S(1)} %pad_add_fusion.at, bf16[16,64,256]{2,1,0:T(8,128)(2,1)} %get-tuple-element.51.refs_0_, bf16[16,64,256]{2,1,0:T(8,128)(2,1)} %collective-permute-done.9.refs_1_, bf16[16,64,256]{2,1,0:T(8,128)(2,1)S(1)} %get-tuple-element.50.refs_2_, ...), custom_call_target="tpu_custom_call" | custom-call | bytes 1024 | tf_op jit(solution)/shard_map/write_rows/pallas_call | solution.py:59
  78.4 5.2 %collective-permute-done.8.refs_0_ = bf16[16,64,256]{2,1,0:T(8,128)(2,1)} collective-permute-done((bf16[16,64,256]{2,1,0:T(8,128)(2,1)S(1)}, bf16[16,64,256]{2,1,0:T(8,128)(2,1)}, u32[]{:S(2)}, u32[]{:S(2)}) %collective-permute-start.8) | collective-permute-done | bytes 524320 | tf_op jit(solution)/shard_map/ppermute | solution.py:444
  83.7 1.7 %copy_tiles.2 = (bf16[16,64,256]{2,1,0:T(8,128)(2,1)S(1)}, s32[8,128]{1,0:T(8,128)S(1)}) custom-call(s32[3]{0:T(128)S(1)} %pad_add_fusion.at, bf16[16,64,256]{2,1,0:T(8,128)(2,1)} %collective-permute-done.8.refs_0_, s32[8,128]{1,0:T(8,128)S(1)} %get-tuple-element.53.refs_1_), custom_call_target="tpu_custom_call" | custom-call | bytes 1024 | tf_op jit(solution)/shard_map/copy_tiles/pallas_call | solution.py:59
  85.3 1.3 %collective-permute-start.12 = (bf16[16,64,256]{2,1,0:T(8,128)(2,1)S(1)}, bf16[16,64,256]{2,1,0:T(8,128)(2,1)S(1)}, u32[]{:S(2)}, u32[]{:S(2)}) collective-permute-start(bf16[16,64,256]{2,1,0:T(8,128)(2,1)S(1)} %get-tuple-element.54.refs_4_), channel_id=1, source_target_pairs={{0,32},{32,0},{1,33},{33,1},{2,34},{34,2},{3,35},{35,3},{4,36},{36... | collective-permute-start | bytes 1572872 | tf_op jit(solution)/shard_map/ppermute | solution.py:441
  86.7 0.0 collective-permute-done.6.refs_0_
  86.7 0.0 collective-permute-done.7.refs_1_
  86.7 3.4 %write_rows.7 = (f32[256,8192]{1,0:T(8,128)}, bf16[16,2,256,256]{3,2,1,0:T(8,128)(2,1)}, s32[8,128]{1,0:T(8,128)S(1)}) custom-call(s32[3]{0:T(128)S(1)} %pad_add_fusion.at, bf16[16,64,256]{2,1,0:T(8,128)(2,1)S(1)} %collective-permute-done.6.refs_0_, ...), custom_call_target="tpu_custom_call", output_to_operand_aliasing={{0}: (6, {}), {1}: (7, {})} | custom-call | bytes 1024 | tf_op jit(solution)/shard_map/write_rows/pallas_call | solution.py:59
  90.1 0.0 all-to-all-done.2.refs_0_
  90.1 0.6 copy_tiles.3
  90.8 0.1 collective-permute-start.11
  90.9 0.0 collective-permute-done.12.refs_1_
  90.9 1.7 %write_rows.8 = (bf16[16,2,256,256]{3,2,1,0:T(8,128)(2,1)}, s32[8,128]{1,0:T(8,128)S(1)}) custom-call(s32[3]{0:T(128)S(1)} %pad_add_fusion.at, bf16[16,64,256]{2,1,0:T(8,128)(2,1)S(1)} %get-tuple-element.60.refs_0_, bf16[16,64,256]{2,1,0:T(8,128)(2,1)S(1)} %collective-permute-done.12.refs_1_, ...), custom_call_target="tpu_custom_call", output_to_operand_aliasing={{0}: (3, {})} | custom-call | bytes 38797312 | tf_op jit(solution)/shard_map/write_rows/pallas_call | solution.py:59
  92.5 0.2 collective-permute-done.11.refs_0_
  92.8 1.4 %write_rows.9 = (bf16[16,2,256,256]{3,2,1,0:T(8,128)(2,1)}, s32[8,128]{1,0:T(8,128)}) custom-call(s32[3]{0:T(128)S(1)} %pad_add_fusion.at, bf16[16,64,256]{2,1,0:T(8,128)(2,1)S(1)} %collective-permute-done.11.refs_0_, bf16[16,2,256,256]{3,2,1,0:T(8,128)(2,1)} %get-tuple-element.63.refs_1_, ...), custom_call_target="tpu_custom_call", output_to_operand_aliasing={{0}: (2, {})} | custom-call | bytes 1024 | tf_op jit(solution)/shard_map/write_rows/pallas_call | solution.py:59
Async XLA Ops:
  2.9 4.2 %collective-permute-start = (bf16[32,64,256]{2,1,0:T(8,128)(2,1)S(1)}, bf16[32,64,256]{2,1,0:T(8,128)(2,1)S(1)}, u32[]{:S(2)}, u32[]{:S(2)}) collective-permute-start(bf16[32,64,256]{2,1,0:T(8,128)(2,1)S(1)} %get-tuple-element.34), channel_id=1, source_target_pairs={{0,32},{32,0},{1,33},{33,1},{2,34},{34,2},{3,35},{35,3},{4,36},{36... | collective-permute-start | bytes 3145736 | tf_op jit(solution)/shard_map/ppermute | solution.py:441
  9.9 29.2 %collective-permute-start.3 = (bf16[32,64,256]{2,1,0:T(8,128)(2,1)}, bf16[32,64,256]{2,1,0:T(8,128)(2,1)S(1)}, u32[]{:S(2)}, u32[]{:S(2)}) collective-permute-start(bf16[32,64,256]{2,1,0:T(8,128)(2,1)} %get-tuple-element.42), channel_id=1, source_target_pairs={{0,64},{64,0},{1,65},{65,1},{2,66},{66,2},{3,67},{67,3},{4,68},{68... | collective-permute-start | bytes 3145736 | tf_op jit(solution)/shard_map/ppermute | solution.py:444
  11.3 27.9 %all-to-all-start = ((bf16[32,64,256]{2,1,0:T(8,128)(2,1)}), bf16[32,64,256]{2,1,0:T(8,128)(2,1)S(1)}, u32[]{:S(2)}, u32[]{:S(2)}) async-start(bf16[32,64,256]{2,1,0:T(8,128)(2,1)} %bitcast.17), calls=%async_computation | async-start | bytes 2097152 | tf_op jit(solution)/shard_map/all_to_all | solution.py:436
  23.1 2.2 %collective-permute-start.1 = (bf16[32,32,256]{2,1,0:T(8,128)(2,1)S(1)}, bf16[32,32,256]{2,1,0:T(8,128)(2,1)S(1)}, u32[]{:S(2)}, u32[]{:S(2)}) collective-permute-start(bf16[32,32,256]{2,1,0:T(8,128)(2,1)S(1)} %get-tuple-element.38), channel_id=1, source_target_pairs={{0,32},{32,0},{1,33},{33,1},{2,34},{34,2},{3,35},{35,3},{4,36},{36... | collective-permute-start | bytes 1572872 | tf_op jit(solution)/shard_map/ppermute | solution.py:441
  23.7 2.3 %collective-permute-start.2 = (bf16[32,32,256]{2,1,0:T(8,128)(2,1)S(1)}, bf16[32,32,256]{2,1,0:T(8,128)(2,1)S(1)}, u32[]{:S(2)}, u32[]{:S(2)}) collective-permute-start(bf16[32,32,256]{2,1,0:T(8,128)(2,1)S(1)} %get-tuple-element.39), channel_id=1, source_target_pairs={{0,32},{32,0},{1,33},{33,1},{2,34},{34,2},{3,35},{35,3},{4,36},{36... | collective-permute-start | bytes 1572872 | tf_op jit(solution)/shard_map/ppermute | solution.py:441
  41.1 7.6 %collective-permute-start.5 = (bf16[32,64,256]{2,1,0:T(8,128)(2,1)}, bf16[32,64,256]{2,1,0:T(8,128)(2,1)S(1)}, u32[]{:S(2)}, u32[]{:S(2)}) collective-permute-start(bf16[32,64,256]{2,1,0:T(8,128)(2,1)} %get-tuple-element.45.refs_1_), channel_id=1, source_target_pairs={{0,32},{32,0},{1,33},{33,1},{2,34},{34,2},{3,35},{35,3},{4,36},{36... | collective-permute-start | bytes 3145736 | tf_op jit(solution)/shard_map/ppermute | solution.py:441
  42.9 24.9 %collective-permute-start.4 = (bf16[32,64,256]{2,1,0:T(8,128)(2,1)}, bf16[32,64,256]{2,1,0:T(8,128)(2,1)S(1)}, u32[]{:S(2)}, u32[]{:S(2)}) collective-permute-start(bf16[32,64,256]{2,1,0:T(8,128)(2,1)} %get-tuple-element.45.refs_1_), channel_id=1, source_target_pairs={{0,64},{64,0},{1,65},{65,1},{2,66},{66,2},{3,67},{67,3},{4,68},{68... | collective-permute-start | bytes 3145736 | tf_op jit(solution)/shard_map/ppermute | solution.py:444
  42.9 24.0 %all-to-all-start.1 = ((bf16[32,64,256]{2,1,0:T(8,128)(2,1)}), bf16[32,64,256]{2,1,0:T(8,128)(2,1)S(1)}, u32[]{:S(2)}, u32[]{:S(2)}) async-start(bf16[32,64,256]{2,1,0:T(8,128)(2,1)} %get-tuple-element.45.refs_1_), calls=%async_computation.1 | async-start | bytes 2097152 | tf_op jit(solution)/shard_map/all_to_all | solution.py:436
  69.4 5.7 %collective-permute-start.10 = (bf16[16,64,256]{2,1,0:T(8,128)(2,1)S(1)}, bf16[16,64,256]{2,1,0:T(8,128)(2,1)S(1)}, u32[]{:S(2)}, u32[]{:S(2)}) collective-permute-start(bf16[16,64,256]{2,1,0:T(8,128)(2,1)S(1)} %get-tuple-element.50.refs_2_), channel_id=1, source_target_pairs={{0,32},{32,0},{1,33},{33,1},{2,34},{34,2},{3,35},{35,3},{4,36},{36... | collective-permute-start | bytes 1572872 | tf_op jit(solution)/shard_map/ppermute | solution.py:441
  70.4 4.8 %collective-permute-start.9 = (bf16[16,64,256]{2,1,0:T(8,128)(2,1)}, bf16[16,64,256]{2,1,0:T(8,128)(2,1)}, u32[]{:S(2)}, u32[]{:S(2)}) collective-permute-start(bf16[16,64,256]{2,1,0:T(8,128)(2,1)} %get-tuple-element.51.refs_0_), channel_id=1, source_target_pairs={{0,32},{32,0},{1,33},{33,1},{2,34},{34,2},{3,35},{35,3},{4,36},{36... | collective-permute-start | bytes 1572872 | tf_op jit(solution)/shard_map/ppermute | solution.py:441
  70.5 13.2 %collective-permute-start.8 = (bf16[16,64,256]{2,1,0:T(8,128)(2,1)S(1)}, bf16[16,64,256]{2,1,0:T(8,128)(2,1)}, u32[]{:S(2)}, u32[]{:S(2)}) collective-permute-start(bf16[16,64,256]{2,1,0:T(8,128)(2,1)S(1)} %get-tuple-element.50.refs_2_), channel_id=1, source_target_pairs={{0,64},{64,0},{1,65},{65,1},{2,66},{66,2},{3,67},{67,3},{4,68},{68... | collective-permute-start | bytes 1572872 | tf_op jit(solution)/shard_map/ppermute | solution.py:444
  70.5 16.2 %collective-permute-start.6 = (bf16[16,64,256]{2,1,0:T(8,128)(2,1)}, bf16[16,64,256]{2,1,0:T(8,128)(2,1)S(1)}, u32[]{:S(2)}, u32[]{:S(2)}) collective-permute-start(bf16[16,64,256]{2,1,0:T(8,128)(2,1)} %get-tuple-element.48.refs_2_), channel_id=1, source_target_pairs={{0,32},{32,0},{1,33},{33,1},{2,34},{34,2},{3,35},{35,3},{4,36},{36... | collective-permute-start | bytes 1572872 | tf_op jit(solution)/shard_map/ppermute | solution.py:441
  71.2 15.5 %collective-permute-start.7 = (bf16[16,64,256]{2,1,0:T(8,128)(2,1)S(1)}, bf16[16,64,256]{2,1,0:T(8,128)(2,1)S(1)}, u32[]{:S(2)}, u32[]{:S(2)}) collective-permute-start(bf16[16,64,256]{2,1,0:T(8,128)(2,1)S(1)} %get-tuple-element.49.refs_3_), channel_id=1, source_target_pairs={{0,32},{32,0},{1,33},{33,1},{2,34},{34,2},{3,35},{35,3},{4,36},{36... | collective-permute-start | bytes 1572872 | tf_op jit(solution)/shard_map/ppermute | solution.py:441
  71.2 18.9 %all-to-all-start.2 = ((bf16[16,64,256]{2,1,0:T(8,128)(2,1)}), bf16[16,64,256]{2,1,0:T(8,128)(2,1)S(1)}, u32[]{:S(2)}, u32[]{:S(2)}) async-start(bf16[16,64,256]{2,1,0:T(8,128)(2,1)} %get-tuple-element.48.refs_2_), calls=%async_computation.2 | async-start | bytes 1048576 | tf_op jit(solution)/shard_map/all_to_all | solution.py:459
  85.3 5.5 %collective-permute-start.12 = (bf16[16,64,256]{2,1,0:T(8,128)(2,1)S(1)}, bf16[16,64,256]{2,1,0:T(8,128)(2,1)S(1)}, u32[]{:S(2)}, u32[]{:S(2)}) collective-permute-start(bf16[16,64,256]{2,1,0:T(8,128)(2,1)S(1)} %get-tuple-element.54.refs_4_), channel_id=1, source_target_pairs={{0,32},{32,0},{1,33},{33,1},{2,34},{34,2},{3,35},{35,3},{4,36},{36... | collective-permute-start | bytes 1572872 | tf_op jit(solution)/shard_map/ppermute | solution.py:441
  90.8 2.0 %collective-permute-start.11 = (bf16[16,64,256]{2,1,0:T(8,128)(2,1)S(1)}, bf16[16,64,256]{2,1,0:T(8,128)(2,1)S(1)}, u32[]{:S(2)}, u32[]{:S(2)}) collective-permute-start(bf16[16,64,256]{2,1,0:T(8,128)(2,1)S(1)} %get-tuple-element.60.refs_0_), channel_id=1, source_target_pairs={{0,32},{32,0},{1,33},{33,1},{2,34},{34,2},{3,35},{35,3},{4,36},{36... | collective-permute-start | bytes 1572872 | tf_op jit(solution)/shard_map/ppermute | solution.py:441

commit v4 on v3

--- a/solution.py
+++ b/solution.py
@@ -337,15 +337,30 @@
     )
 
 
-def copy_tiles(order, tiles):
-    def body(at, x_ref, o_ref):
-        def work(g):
-            o_ref[g] = x_ref[g]
-
-        each(tiles.shape[0], work)
-
-    out = pltpu.VMEM(tiles.shape, BF)
-    return order.run(body, "copy_tiles", [in_vmem(tiles)], [VMEM], [out], [VMEM], [])[0]
+def copy_tiles(order, arrays):
+    n = len(arrays)
+
+    def body(at, *refs):
+        ins, outs, sems = refs[:n], refs[n : 2 * n], refs[2 * n]
+
+        def copy(i, p):
+            some = pl.ds(4 * p, 4)
+            return pltpu.make_async_copy(ins[i].at[some], outs[i].at[some], sems.at[i, p])
+
+        for i in range(n):
+            each(4, lambda p, i=i: copy(i, p).start())
+        for i in range(n):
+            each(4, lambda p, i=i: copy(i, p).wait())
+
+    return order.run(
+        body,
+        "copy_tiles",
+        arrays,
+        [ANY] * n,
+        [pltpu.VMEM(x.shape, BF) for x in arrays],
+        [VMEM] * n,
+        [pltpu.SemaphoreType.DMA((n, 4))],
+    )
 
 
 def write_rows(order, wide_pieces, placed_pieces, blended, anchor, size=1024):
@@ -465,14 +480,13 @@
         (core(high), False, False, False),
     ]
     (new_anchor,) = write_rows(order, [], pieces, None, None)
-    back_second = copy_tiles(order, back_second)
-    wide_pieces = [([core(first), core(second)], False, False), ([first, second], True, False)]
-    pieces = [(back_second, True, True, False)]
-    blended, new_anchor = write_rows(order, wide_pieces, pieces, blended, new_anchor)
-    back_first = copy_tiles(order, back_first)
-    pieces = [(back_first, True, False, True), (core(back_second), False, True, False)]
+    pieces = [([core(first), core(second)], False, False), ([first, second], True, False)]
+    (blended,) = write_rows(order, pieces, [], blended, None)
+    back_first, back_second = copy_tiles(order, [back_first, back_second])
+    pieces = [(back_first, True, False, True), (back_second, True, True, False)]
     (new_anchor,) = write_rows(order, [], pieces, None, new_anchor, LAST_COST)
-    (new_anchor,) = write_rows(order, [], [(core(back_first), False, False, True)], None, new_anchor)
+    pieces = [(core(back_first), False, False, True), (core(back_second), False, True, False)]
+    (new_anchor,) = write_rows(order, [], pieces, None, new_anchor)
     return blended, new_anchor.reshape(SHARDS * ROWS, WIDTH)
 
 

time: 95 us -> 94.6 us (level)
  waiting for transfers between devices: 33.8 us -> 32.5 us
    ppermute x3, waiting for transfers between devices: 6.18 us -> 0.94 us  [chip(): return lax.ppermute(tiles, 'xl', swap)]
    all_to_all x1, waiting for transfers between devices: 0.01 us -> 3.6 us  [per_device(): lax.all_to_all(first, ('y', 'z'), split_axis=0, concat_axis=0, tiled=True)]
    pallas_call x14 -> x13, Pallas kernels: 31.6 us -> 31.8 us  [run(): pl.pallas_call(ordered, out_shape=[*outs, TOKEN], grid_spec=pltpu.Prefetc...]
  transfers between devices with their start and end apart: 16 -> 16, of which waited for: 7 -> 7; matrix products, arithmetic and copies ran while one was open for 0% -> 0% of each run, Pallas kernels for 23% -> 20%
where the time goes in v4:
time: 94.6 us; the launch traced here: 93.8 us
  waiting for transfers between devices  32.5 us (34%)
  Pallas kernels  31.8 us (34%)
  starting transfers between devices  28.6 us (30%)
    pallas_call x13, Pallas kernels, run(): pl.pallas_call(ordered, out_shape=[*outs, TOKEN], grid_spec=pltpu.Prefetc...  31.8 us
    all_to_all x2, waiting for transfers between devices, exchange(): lax.all_to_all(tiles, AXES, split_axis=0, concat_axis=0, axis_index_group...  25.2 us
    all_to_all x2, starting transfers between devices, exchange(): lax.all_to_all(tiles, AXES, split_axis=0, concat_axis=0, axis_index_group...  15.4 us
    ppermute x10, starting transfers between devices, core(): return lax.ppermute(tiles, 'c', swap)  7.93 us
    all_to_all x1, starting transfers between devices, per_device(): lax.all_to_all(first, ('y', 'z'), split_axis=0, concat_axis=0, tiled=True)  3.95 us
    all_to_all x1, waiting for transfers between devices, per_device(): lax.all_to_all(first, ('y', 'z'), split_axis=0, concat_axis=0, tiled=True)  3.6 us
    ppermute x10, waiting for transfers between devices, core(): return lax.ppermute(tiles, 'c', swap)  2.74 us
  transfers between devices with their start and end apart: 16, of which 7 were waited for; matrix products, arithmetic and copies ran while one was open for 0% of the time, Pallas kernels for 20%

profile of v4, /device:TPU:1, one launch (start us, length us, event | category | flops | bytes accessed | tf_op | source)
XLA Modules:
  0.0 93.8 jit_solution(9557583367313185118)
XLA Ops:
  0.6 0.1 pad_add_fusion.at
  0.7 2.2 %cast_rows.1 = (bf16[32,64,256]{2,1,0:T(8,128)(2,1)S(1)}, s32[8,128]{1,0:T(8,128)S(1)}) custom-call(s32[3]{0:T(128)S(1)} %pad_add_fusion.at, f32[256,8192]{1,0:T(8,128)} %bitcast.11), custom_call_target="tpu_custom_call" | custom-call | bytes 1024 | tf_op jit(solution)/shard_map/cast_rows/pallas_call | solution.py:59
  2.9 1.5 %collective-permute-start = (bf16[32,64,256]{2,1,0:T(8,128)(2,1)S(1)}, bf16[32,64,256]{2,1,0:T(8,128)(2,1)S(1)}, u32[]{:S(2)}, u32[]{:S(2)}) collective-permute-start(bf16[32,64,256]{2,1,0:T(8,128)(2,1)S(1)} %get-tuple-element.32), channel_id=1, source_target_pairs={{0,32},{32,0},{1,33},{33,1},{2,34},{34,2},{3,35},{35,3},{4,36},{36... | collective-permute-start | bytes 3145736 | tf_op jit(solution)/shard_map/ppermute | solution.py:456
  4.4 2.6 %pick_rows.1 = (bf16[16,2,64,256]{3,2,1,0:T(8,128)(2,1)}, s32[8,128]{1,0:T(8,128)S(1)}) custom-call(s32[3]{0:T(128)S(1)} %pad_add_fusion.at, bf16[16,2,256,256]{3,2,1,0:T(8,128)(2,1)} %bitcast.16, s32[8,128]{1,0:T(8,128)S(1)} %get-tuple-element.33.refs_1_), custom_call_target="tpu_custom_call" | custom-call | bytes 1024 | tf_op jit(solution)/shard_map/pick_rows/pallas_call | solution.py:59
  7.0 0.0 collective-permute-done.refs_1_
  7.0 2.9 %add_theirs.1 = (bf16[32,64,256]{2,1,0:T(8,128)(2,1)}, s32[8,128]{1,0:T(8,128)S(1)}) custom-call(s32[3]{0:T(128)S(1)} %pad_add_fusion.at, f32[256,8192]{1,0:T(8,128)} %bitcast.12, bf16[32,64,256]{2,1,0:T(8,128)(2,1)S(1)} %collective-permute-done.refs_1_, s32[8,128]{1,0:T(8,128)S(1)} %get-tuple-element.34.refs_2_), custom_call_target="tpu_custom_call" | custom-call | bytes 1024 | tf_op jit(solution)/shard_map/add_theirs/pallas_call | solution.py:59
  9.9 1.4 %collective-permute-start.3 = (bf16[32,64,256]{2,1,0:T(8,128)(2,1)}, bf16[32,64,256]{2,1,0:T(8,128)(2,1)S(1)}, u32[]{:S(2)}, u32[]{:S(2)}) collective-permute-start(bf16[32,64,256]{2,1,0:T(8,128)(2,1)} %get-tuple-element.40), channel_id=1, source_target_pairs={{0,64},{64,0},{1,65},{65,1},{2,66},{66,2},{3,67},{67,3},{4,68},{68... | collective-permute-start | bytes 3145736 | tf_op jit(solution)/shard_map/ppermute | solution.py:459
  11.3 9.6 %all-to-all-start = ((bf16[32,64,256]{2,1,0:T(8,128)(2,1)}), bf16[32,64,256]{2,1,0:T(8,128)(2,1)S(1)}, u32[]{:S(2)}, u32[]{:S(2)}) async-start(bf16[32,64,256]{2,1,0:T(8,128)(2,1)} %bitcast.5), calls=%async_computation | async-start | bytes 2097152 | tf_op jit(solution)/shard_map/all_to_all | solution.py:451
  20.9 2.2 %cast_own.1 = (bf16[32,32,256]{2,1,0:T(8,128)(2,1)S(1)}, bf16[32,32,256]{2,1,0:T(8,128)(2,1)S(1)}, s32[8,128]{1,0:T(8,128)S(1)}) custom-call(s32[3]{0:T(128)S(1)} %pad_add_fusion.at, f32[256,8192]{1,0:T(8,128)} %bitcast.13, s32[8,128]{1,0:T(8,128)S(1)} %get-tuple-element.35.refs_1_), custom_call_target="tpu_custom_call" | custom-call | bytes 1024 | tf_op jit(solution)/shard_map/cast_own/pallas_call | solution.py:59
  23.1 0.7 collective-permute-start.1
  23.7 0.1 collective-permute-start.2
  23.8 1.4 %collective-permute-done.1.refs_1_ = bf16[32,32,256]{2,1,0:T(8,128)(2,1)S(1)} collective-permute-done((bf16[32,32,256]{2,1,0:T(8,128)(2,1)S(1)}, bf16[32,32,256]{2,1,0:T(8,128)(2,1)S(1)}, u32[]{:S(2)}, u32[]{:S(2)}) %collective-permute-start.1) | collective-permute-done | bytes 524320 | tf_op jit(solution)/shard_map/ppermute | solution.py:456
  25.3 0.7 collective-permute-done.2.refs_2_
  26.0 2.2 %add_own.1 = (bf16[32,64,256]{2,1,0:T(8,128)(2,1)S(1)}, s32[8,128]{1,0:T(8,128)S(1)}) custom-call(s32[3]{0:T(128)S(1)} %pad_add_fusion.at, f32[256,8192]{1,0:T(8,128)} %bitcast.14, bf16[32,32,256]{2,1,0:T(8,128)(2,1)S(1)} %collective-permute-done.1.refs_1_, bf16[32,32,256]{2,1,0:T(8,128)(2,1)S(1)} %collective-permute-done.2.refs_2_, ...), custom_call_target="tpu_custom_call" | custom-call | bytes 1024 | tf_op jit(solution)/shard_map/add_own/pallas_call | solution.py:59
  28.2 11.0 %all-to-all-done.refs_2_ = bf16[32,64,256]{2,1,0:T(8,128)(2,1)S(1)} async-done(((bf16[32,64,256]{2,1,0:T(8,128)(2,1)}), bf16[32,64,256]{2,1,0:T(8,128)(2,1)S(1)}, u32[]{:S(2)}, u32[]{:S(2)}) %all-to-all-start) | async-done | bytes 1048608 | tf_op jit(solution)/shard_map/all_to_all | solution.py:451
  39.2 0.0 collective-permute-done.3.refs_1_
  39.2 1.9 %blend_rows.1 = (bf16[32,64,256]{2,1,0:T(8,128)(2,1)}, s32[8,128]{1,0:T(8,128)S(1)}) custom-call(s32[3]{0:T(128)S(1)} %pad_add_fusion.at, bf16[32,64,256]{2,1,0:T(8,128)(2,1)S(1)} %get-tuple-element.39.refs_0_, bf16[32,64,256]{2,1,0:T(8,128)(2,1)S(1)} %collective-permute-done.3.refs_1_, bf16[32,64,256]{2,1,0:T(8,128)(2,1)S(1)} %all-to-all-done.refs_2_, ...), custom_call_target="tpu_custom_call" | custom-call | bytes 1024 | tf_op jit(solution)/shard_map/blend_rows/pallas_call | solution.py:59
  41.1 1.8 %collective-permute-start.5 = (bf16[32,64,256]{2,1,0:T(8,128)(2,1)}, bf16[32,64,256]{2,1,0:T(8,128)(2,1)S(1)}, u32[]{:S(2)}, u32[]{:S(2)}) collective-permute-start(bf16[32,64,256]{2,1,0:T(8,128)(2,1)} %get-tuple-element.43.refs_1_), channel_id=1, source_target_pairs={{0,32},{32,0},{1,33},{33,1},{2,34},{34,2},{3,35},{35,3},{4,36},{36... | collective-permute-start | bytes 3145736 | tf_op jit(solution)/shard_map/ppermute | solution.py:456
  42.9 0.0 collective-permute-start.4
  42.9 5.8 %all-to-all-start.1 = ((bf16[32,64,256]{2,1,0:T(8,128)(2,1)}), bf16[32,64,256]{2,1,0:T(8,128)(2,1)S(1)}, u32[]{:S(2)}, u32[]{:S(2)}) async-start(bf16[32,64,256]{2,1,0:T(8,128)(2,1)} %get-tuple-element.43.refs_1_), calls=%async_computation.1 | async-start | bytes 2097152 | tf_op jit(solution)/shard_map/all_to_all | solution.py:451
  48.7 0.0 collective-permute-done.5.refs_0_
  48.7 4.0 %write_rows.5 = (f32[256,8192]{1,0:T(8,128)}, s32[8,128]{1,0:T(8,128)S(1)}) custom-call(s32[3]{0:T(128)S(1)} %pad_add_fusion.at, bf16[32,64,256]{2,1,0:T(8,128)(2,1)S(1)} %collective-permute-done.5.refs_0_, bf16[32,64,256]{2,1,0:T(8,128)(2,1)} %get-tuple-element.43.refs_1_, s32[8,128]{1,0:T(8,128)S(1)} %get-tuple-element.44.refs_2_), custom_call_target="tpu_custom_call" | custom-call | bytes 11534336 | tf_op jit(solution)/shard_map/write_rows/pallas_call | solution.py:59
  52.7 14.2 %all-to-all-done.1 = bf16[32,64,256]{2,1,0:T(8,128)(2,1)S(1)} async-done(((bf16[32,64,256]{2,1,0:T(8,128)(2,1)}), bf16[32,64,256]{2,1,0:T(8,128)(2,1)S(1)}, u32[]{:S(2)}, u32[]{:S(2)}) %all-to-all-start.1) | async-done | bytes 1048608 | tf_op jit(solution)/shard_map/all_to_all | solution.py:451
  66.9 0.9 collective-permute-done.4
  67.8 1.6 %split_planes.1 = (bf16[16,64,256]{2,1,0:T(8,128)(2,1)}, bf16[16,64,256]{2,1,0:T(8,128)(2,1)}, bf16[16,64,256]{2,1,0:T(8,128)(2,1)S(1)}, bf16[16,64,256]{2,1,0:T(8,128)(2,1)S(1)}, s32[8,128]{1,0:T(8,128)S(1)}) custom-call(s32[3]{0:T(128)S(1)} %pad_add_fusion.at, bf16[16,2,64,256]{3,2,1,0:T(8,128)(2,1)S(1)} %bitcast.10, bf16[16,2,64,256]{3,2,1,0:T(8,128)(2,1)S(1)} %bitcast.9, ...), custom_call_target="tpu_custom_call" | custom-call | bytes 1024 | tf_op jit(solution)/shard_map/split_planes/pallas_call | solution.py:59
  69.4 1.0 %collective-permute-start.8 = (bf16[16,64,256]{2,1,0:T(8,128)(2,1)}, bf16[16,64,256]{2,1,0:T(8,128)(2,1)S(1)}, u32[]{:S(2)}, u32[]{:S(2)}) collective-permute-start(bf16[16,64,256]{2,1,0:T(8,128)(2,1)} %get-tuple-element.49.refs_0_), channel_id=1, source_target_pairs={{0,32},{32,0},{1,33},{33,1},{2,34},{34,2},{3,35},{35,3},{4,36},{36... | collective-permute-start | bytes 1572872 | tf_op jit(solution)/shard_map/ppermute | solution.py:456
  70.4 0.1 collective-permute-start.9
  70.5 0.4 collective-permute-start.6
  70.9 0.1 collective-permute-start.7
  71.0 0.0 collective-permute-start.10
  71.0 4.0 %all-to-all-start.2 = ((bf16[16,64,256]{2,1,0:T(8,128)(2,1)}), bf16[16,64,256]{2,1,0:T(8,128)(2,1)S(1)}, u32[]{:S(2)}, u32[]{:S(2)}) async-start(bf16[16,64,256]{2,1,0:T(8,128)(2,1)} %get-tuple-element.46.refs_2_), calls=%async_computation.2 | async-start | bytes 1048576 | tf_op jit(solution)/shard_map/all_to_all | solution.py:474
  74.9 0.0 collective-permute-done.8.refs_1_
  75.0 0.0 collective-permute-done.9.refs_3_
  75.0 3.3 %write_rows.6 = (bf16[16,2,256,256]{3,2,1,0:T(8,128)(2,1)}, s32[8,128]{1,0:T(8,128)S(1)}) custom-call(s32[3]{0:T(128)S(1)} %pad_add_fusion.at, bf16[16,64,256]{2,1,0:T(8,128)(2,1)} %get-tuple-element.49.refs_0_, bf16[16,64,256]{2,1,0:T(8,128)(2,1)S(1)} %collective-permute-done.8.refs_1_, bf16[16,64,256]{2,1,0:T(8,128)(2,1)S(1)} %get-tuple-element.50.refs_2_, ...), custom_call_target="tpu_custom_call" | custom-call | bytes 1024 | tf_op jit(solution)/shard_map/write_rows/pallas_call | solution.py:59
  78.2 0.0 collective-permute-done.6.refs_0_
  78.2 0.0 collective-permute-done.7.refs_1_
  78.3 3.4 %write_rows.7 = (f32[256,8192]{1,0:T(8,128)}, s32[8,128]{1,0:T(8,128)S(1)}) custom-call(s32[3]{0:T(128)S(1)} %pad_add_fusion.at, bf16[16,64,256]{2,1,0:T(8,128)(2,1)S(1)} %collective-permute-done.6.refs_0_, bf16[16,64,256]{2,1,0:T(8,128)(2,1)S(1)} %collective-permute-done.7.refs_1_, ...), custom_call_target="tpu_custom_call", output_to_operand_aliasing={{0}: (5, {})} | custom-call | bytes 1024 | tf_op jit(solution)/shard_map/write_rows/pallas_call | solution.py:59
  81.6 3.6 %all-to-all-done.2.refs_0_ = bf16[16,64,256]{2,1,0:T(8,128)(2,1)S(1)} async-done(((bf16[16,64,256]{2,1,0:T(8,128)(2,1)}), bf16[16,64,256]{2,1,0:T(8,128)(2,1)S(1)}, u32[]{:S(2)}, u32[]{:S(2)}) %all-to-all-start.2) | async-done | bytes 524320 | tf_op jit(solution)/shard_map/all_to_all | solution.py:474
  85.2 0.0 collective-permute-done.10.refs_1_
  85.2 2.4 %copy_tiles.1 = (bf16[16,64,256]{2,1,0:T(8,128)(2,1)S(1)}, bf16[16,64,256]{2,1,0:T(8,128)(2,1)S(1)}, s32[8,128]{1,0:T(8,128)S(1)}) custom-call(s32[3]{0:T(128)S(1)} %pad_add_fusion.at, bf16[16,64,256]{2,1,0:T(8,128)(2,1)S(1)} %all-to-all-done.2.refs_0_, bf16[16,64,256]{2,1,0:T(8,128)(2,1)} %collective-permute-done.10.refs_1_, ...), custom_call_target="tpu_custom_call" | custom-call | bytes 1024 | tf_op jit(solution)/shard_map/copy_tiles/pallas_call | solution.py:59
  87.7 2.2 %collective-permute-start.11 = (bf16[16,64,256]{2,1,0:T(8,128)(2,1)S(1)}, bf16[16,64,256]{2,1,0:T(8,128)(2,1)S(1)}, u32[]{:S(2)}, u32[]{:S(2)}) collective-permute-start(bf16[16,64,256]{2,1,0:T(8,128)(2,1)S(1)} %get-tuple-element.55.refs_0_), channel_id=1, source_target_pairs={{0,32},{32,0},{1,33},{33,1},{2,34},{34,2},{3,35},{35,3},{4,36},{36... | collective-permute-start | bytes 1572872 | tf_op jit(solution)/shard_map/ppermute | solution.py:456
  89.9 0.1 collective-permute-start.12
  90.0 1.7 %write_rows.8 = (bf16[16,2,256,256]{3,2,1,0:T(8,128)(2,1)}, s32[8,128]{1,0:T(8,128)S(1)}) custom-call(s32[3]{0:T(128)S(1)} %pad_add_fusion.at, bf16[16,64,256]{2,1,0:T(8,128)(2,1)S(1)} %get-tuple-element.55.refs_0_, bf16[16,64,256]{2,1,0:T(8,128)(2,1)S(1)} %get-tuple-element.56.refs_1_, ...), custom_call_target="tpu_custom_call", output_to_operand_aliasing={{0}: (3, {})} | custom-call | bytes 38797312 | tf_op jit(solution)/shard_map/write_rows/pallas_call | solution.py:59
  91.6 0.0 collective-permute-done.11.refs_0_
  91.6 0.5 collective-permute-done.12.refs_1_
  92.2 1.7 %write_rows.9 = (bf16[16,2,256,256]{3,2,1,0:T(8,128)(2,1)}, s32[8,128]{1,0:T(8,128)}) custom-call(s32[3]{0:T(128)S(1)} %pad_add_fusion.at, bf16[16,64,256]{2,1,0:T(8,128)(2,1)S(1)} %collective-permute-done.11.refs_0_, bf16[16,64,256]{2,1,0:T(8,128)(2,1)S(1)} %collective-permute-done.12.refs_1_, ...), custom_call_target="tpu_custom_call", output_to_operand_aliasing={{0}: (3, {})} | custom-call | bytes 1024 | tf_op jit(solution)/shard_map/write_rows/pallas_call | solution.py:59
Async XLA Ops:
  2.9 4.2 %collective-permute-start = (bf16[32,64,256]{2,1,0:T(8,128)(2,1)S(1)}, bf16[32,64,256]{2,1,0:T(8,128)(2,1)S(1)}, u32[]{:S(2)}, u32[]{:S(2)}) collective-permute-start(bf16[32,64,256]{2,1,0:T(8,128)(2,1)S(1)} %get-tuple-element.32), channel_id=1, source_target_pairs={{0,32},{32,0},{1,33},{33,1},{2,34},{34,2},{3,35},{35,3},{4,36},{36... | collective-permute-start | bytes 3145736 | tf_op jit(solution)/shard_map/ppermute | solution.py:456
  9.9 29.2 %collective-permute-start.3 = (bf16[32,64,256]{2,1,0:T(8,128)(2,1)}, bf16[32,64,256]{2,1,0:T(8,128)(2,1)S(1)}, u32[]{:S(2)}, u32[]{:S(2)}) collective-permute-start(bf16[32,64,256]{2,1,0:T(8,128)(2,1)} %get-tuple-element.40), channel_id=1, source_target_pairs={{0,64},{64,0},{1,65},{65,1},{2,66},{66,2},{3,67},{67,3},{4,68},{68... | collective-permute-start | bytes 3145736 | tf_op jit(solution)/shard_map/ppermute | solution.py:459
  11.3 27.9 %all-to-all-start = ((bf16[32,64,256]{2,1,0:T(8,128)(2,1)}), bf16[32,64,256]{2,1,0:T(8,128)(2,1)S(1)}, u32[]{:S(2)}, u32[]{:S(2)}) async-start(bf16[32,64,256]{2,1,0:T(8,128)(2,1)} %bitcast.5), calls=%async_computation | async-start | bytes 2097152 | tf_op jit(solution)/shard_map/all_to_all | solution.py:451
  23.1 2.2 %collective-permute-start.1 = (bf16[32,32,256]{2,1,0:T(8,128)(2,1)S(1)}, bf16[32,32,256]{2,1,0:T(8,128)(2,1)S(1)}, u32[]{:S(2)}, u32[]{:S(2)}) collective-permute-start(bf16[32,32,256]{2,1,0:T(8,128)(2,1)S(1)} %get-tuple-element.36), channel_id=1, source_target_pairs={{0,32},{32,0},{1,33},{33,1},{2,34},{34,2},{3,35},{35,3},{4,36},{36... | collective-permute-start | bytes 1572872 | tf_op jit(solution)/shard_map/ppermute | solution.py:456
  23.7 2.3 %collective-permute-start.2 = (bf16[32,32,256]{2,1,0:T(8,128)(2,1)S(1)}, bf16[32,32,256]{2,1,0:T(8,128)(2,1)S(1)}, u32[]{:S(2)}, u32[]{:S(2)}) collective-permute-start(bf16[32,32,256]{2,1,0:T(8,128)(2,1)S(1)} %get-tuple-element.37), channel_id=1, source_target_pairs={{0,32},{32,0},{1,33},{33,1},{2,34},{34,2},{3,35},{35,3},{4,36},{36... | collective-permute-start | bytes 1572872 | tf_op jit(solution)/shard_map/ppermute | solution.py:456
  41.1 7.6 %collective-permute-start.5 = (bf16[32,64,256]{2,1,0:T(8,128)(2,1)}, bf16[32,64,256]{2,1,0:T(8,128)(2,1)S(1)}, u32[]{:S(2)}, u32[]{:S(2)}) collective-permute-start(bf16[32,64,256]{2,1,0:T(8,128)(2,1)} %get-tuple-element.43.refs_1_), channel_id=1, source_target_pairs={{0,32},{32,0},{1,33},{33,1},{2,34},{34,2},{3,35},{35,3},{4,36},{36... | collective-permute-start | bytes 3145736 | tf_op jit(solution)/shard_map/ppermute | solution.py:456
  42.9 24.9 %collective-permute-start.4 = (bf16[32,64,256]{2,1,0:T(8,128)(2,1)}, bf16[32,64,256]{2,1,0:T(8,128)(2,1)S(1)}, u32[]{:S(2)}, u32[]{:S(2)}) collective-permute-start(bf16[32,64,256]{2,1,0:T(8,128)(2,1)} %get-tuple-element.43.refs_1_), channel_id=1, source_target_pairs={{0,64},{64,0},{1,65},{65,1},{2,66},{66,2},{3,67},{67,3},{4,68},{68... | collective-permute-start | bytes 3145736 | tf_op jit(solution)/shard_map/ppermute | solution.py:459
  42.9 24.0 %all-to-all-start.1 = ((bf16[32,64,256]{2,1,0:T(8,128)(2,1)}), bf16[32,64,256]{2,1,0:T(8,128)(2,1)S(1)}, u32[]{:S(2)}, u32[]{:S(2)}) async-start(bf16[32,64,256]{2,1,0:T(8,128)(2,1)} %get-tuple-element.43.refs_1_), calls=%async_computation.1 | async-start | bytes 2097152 | tf_op jit(solution)/shard_map/all_to_all | solution.py:451
  69.4 5.5 %collective-permute-start.8 = (bf16[16,64,256]{2,1,0:T(8,128)(2,1)}, bf16[16,64,256]{2,1,0:T(8,128)(2,1)S(1)}, u32[]{:S(2)}, u32[]{:S(2)}) collective-permute-start(bf16[16,64,256]{2,1,0:T(8,128)(2,1)} %get-tuple-element.49.refs_0_), channel_id=1, source_target_pairs={{0,32},{32,0},{1,33},{33,1},{2,34},{34,2},{3,35},{35,3},{4,36},{36... | collective-permute-start | bytes 1572872 | tf_op jit(solution)/shard_map/ppermute | solution.py:456
  70.4 4.6 %collective-permute-start.9 = (bf16[16,64,256]{2,1,0:T(8,128)(2,1)S(1)}, bf16[16,64,256]{2,1,0:T(8,128)(2,1)}, u32[]{:S(2)}, u32[]{:S(2)}) collective-permute-start(bf16[16,64,256]{2,1,0:T(8,128)(2,1)S(1)} %get-tuple-element.50.refs_2_), channel_id=1, source_target_pairs={{0,32},{32,0},{1,33},{33,1},{2,34},{34,2},{3,35},{35,3},{4,36},{36... | collective-permute-start | bytes 1572872 | tf_op jit(solution)/shard_map/ppermute | solution.py:456
  70.5 7.8 %collective-permute-start.6 = (bf16[16,64,256]{2,1,0:T(8,128)(2,1)}, bf16[16,64,256]{2,1,0:T(8,128)(2,1)S(1)}, u32[]{:S(2)}, u32[]{:S(2)}) collective-permute-start(bf16[16,64,256]{2,1,0:T(8,128)(2,1)} %get-tuple-element.46.refs_2_), channel_id=1, source_target_pairs={{0,32},{32,0},{1,33},{33,1},{2,34},{34,2},{3,35},{35,3},{4,36},{36... | collective-permute-start | bytes 1572872 | tf_op jit(solution)/shard_map/ppermute | solution.py:456
  70.9 7.4 %collective-permute-start.7 = (bf16[16,64,256]{2,1,0:T(8,128)(2,1)S(1)}, bf16[16,64,256]{2,1,0:T(8,128)(2,1)S(1)}, u32[]{:S(2)}, u32[]{:S(2)}) collective-permute-start(bf16[16,64,256]{2,1,0:T(8,128)(2,1)S(1)} %get-tuple-element.47.refs_3_), channel_id=1, source_target_pairs={{0,32},{32,0},{1,33},{33,1},{2,34},{34,2},{3,35},{35,3},{4,36},{36... | collective-permute-start | bytes 1572872 | tf_op jit(solution)/shard_map/ppermute | solution.py:456
  71.0 14.3 %collective-permute-start.10 = (bf16[16,64,256]{2,1,0:T(8,128)(2,1)S(1)}, bf16[16,64,256]{2,1,0:T(8,128)(2,1)}, u32[]{:S(2)}, u32[]{:S(2)}) collective-permute-start(bf16[16,64,256]{2,1,0:T(8,128)(2,1)S(1)} %get-tuple-element.50.refs_2_), channel_id=1, source_target_pairs={{0,64},{64,0},{1,65},{65,1},{2,66},{66,2},{3,67},{67,3},{4,68},{68... | collective-permute-start | bytes 1572872 | tf_op jit(solution)/shard_map/ppermute | solution.py:459
  71.0 14.3 %all-to-all-start.2 = ((bf16[16,64,256]{2,1,0:T(8,128)(2,1)}), bf16[16,64,256]{2,1,0:T(8,128)(2,1)S(1)}, u32[]{:S(2)}, u32[]{:S(2)}) async-start(bf16[16,64,256]{2,1,0:T(8,128)(2,1)} %get-tuple-element.46.refs_2_), calls=%async_computation.2 | async-start | bytes 1048576 | tf_op jit(solution)/shard_map/all_to_all | solution.py:474
  87.7 4.0 %collective-permute-start.11 = (bf16[16,64,256]{2,1,0:T(8,128)(2,1)S(1)}, bf16[16,64,256]{2,1,0:T(8,128)(2,1)S(1)}, u32[]{:S(2)}, u32[]{:S(2)}) collective-permute-start(bf16[16,64,256]{2,1,0:T(8,128)(2,1)S(1)} %get-tuple-element.55.refs_0_), channel_id=1, source_target_pairs={{0,32},{32,0},{1,33},{33,1},{2,34},{34,2},{3,35},{35,3},{4,36},{36... | collective-permute-start | bytes 1572872 | tf_op jit(solution)/shard_map/ppermute | solution.py:456
  89.9 2.3 %collective-permute-start.12 = (bf16[16,64,256]{2,1,0:T(8,128)(2,1)S(1)}, bf16[16,64,256]{2,1,0:T(8,128)(2,1)S(1)}, u32[]{:S(2)}, u32[]{:S(2)}) collective-permute-start(bf16[16,64,256]{2,1,0:T(8,128)(2,1)S(1)} %get-tuple-element.56.refs_1_), channel_id=1, source_target_pairs={{0,32},{32,0},{1,33},{33,1},{2,34},{34,2},{3,35},{35,3},{4,36},{36... | collective-permute-start | bytes 1572872 | tf_op jit(solution)/shard_map/ppermute | solution.py:456

commit v5 on v3

--- a/solution.py
+++ b/solution.py
@@ -48,6 +48,10 @@
         self.place = place
         self.token = None
 
+    def behind(self, x):
+        x, self.token = lax.optimization_barrier((x, self.token))
+        return x
+
     def run(self, body, name, args, specs, outs, out_specs, scratch, aliases=None, size=1024):
         held = [] if self.token is None else [self.token]
 
@@ -337,17 +341,6 @@
     )
 
 
-def copy_tiles(order, tiles):
-    def body(at, x_ref, o_ref):
-        def work(g):
-            o_ref[g] = x_ref[g]
-
-        each(tiles.shape[0], work)
-
-    out = pltpu.VMEM(tiles.shape, BF)
-    return order.run(body, "copy_tiles", [in_vmem(tiles)], [VMEM], [out], [VMEM], [])[0]
-
-
 def write_rows(order, wide_pieces, placed_pieces, blended, anchor, size=1024):
     n, m = len(wide_pieces), len(placed_pieces)
     counts = [len(arrays) for arrays, _, _ in wide_pieces]
@@ -465,14 +458,14 @@
         (core(high), False, False, False),
     ]
     (new_anchor,) = write_rows(order, [], pieces, None, None)
-    back_second = copy_tiles(order, back_second)
-    wide_pieces = [([core(first), core(second)], False, False), ([first, second], True, False)]
-    pieces = [(back_second, True, True, False)]
-    blended, new_anchor = write_rows(order, wide_pieces, pieces, blended, new_anchor)
-    back_first = copy_tiles(order, back_first)
-    pieces = [(back_first, True, False, True), (core(back_second), False, True, False)]
+    pieces = [([core(first), core(second)], False, False), ([first, second], True, False)]
+    (blended,) = write_rows(order, pieces, [], blended, None)
+    back_second = order.behind(back_second)
+    back_first = order.behind(back_first)
+    pieces = [(back_first, True, False, True), (back_second, True, True, False)]
     (new_anchor,) = write_rows(order, [], pieces, None, new_anchor, LAST_COST)
-    (new_anchor,) = write_rows(order, [], [(core(back_first), False, False, True)], None, new_anchor)
+    pieces = [(core(back_first), False, False, True), (core(back_second), False, True, False)]
+    (new_anchor,) = write_rows(order, [], pieces, None, new_anchor)
     return blended, new_anchor.reshape(SHARDS * ROWS, WIDTH)
 
 

time: 95 us -> 92.1 us (0.969)
  Pallas kernels: 31.6 us -> 29.6 us
  waiting for transfers between devices: 33.8 us -> 32.4 us
    ppermute x3, waiting for transfers between devices: 6.18 us -> 3.21 us  [chip(): return lax.ppermute(tiles, 'xl', swap)]
    pallas_call x14 -> x12, Pallas kernels: 31.6 us -> 29.6 us  [run(): pl.pallas_call(ordered, out_shape=[*outs, TOKEN], grid_spec=pltpu.Prefetc...]
    all_to_all x1, waiting for transfers between devices: 0.01 us -> 1.17 us  [per_device(): lax.all_to_all(first, ('y', 'z'), split_axis=0, concat_axis=0, tiled=True)]
  transfers between devices with their start and end apart: 16 -> 16, of which waited for: 7 -> 8; matrix products, arithmetic and copies ran while one was open for 0% -> 0% of each run, Pallas kernels for 23% -> 21%
where the time goes in v5:
time: 92.1 us; the launch traced here: 91.3 us
  waiting for transfers between devices  32.4 us (35%)
  Pallas kernels  29.6 us (32%)
  starting transfers between devices  28.5 us (31%)
    pallas_call x12, Pallas kernels, run(): pl.pallas_call(ordered, out_shape=[*outs, TOKEN], grid_spec=pltpu.Prefetc...  29.6 us
    all_to_all x2, waiting for transfers between devices, exchange(): lax.all_to_all(tiles, AXES, split_axis=0, concat_axis=0, axis_index_group...  25.2 us
    all_to_all x2, starting transfers between devices, exchange(): lax.all_to_all(tiles, AXES, split_axis=0, concat_axis=0, axis_index_group...  15.4 us
    ppermute x10, starting transfers between devices, core(): return lax.ppermute(tiles, 'c', swap)  7.76 us
    all_to_all x1, starting transfers between devices, per_device(): lax.all_to_all(first, ('y', 'z'), split_axis=0, concat_axis=0, tiled=True)  3.95 us
    ppermute x3, waiting for transfers between devices, chip(): return lax.ppermute(tiles, 'xl', swap)  3.21 us
    ppermute x10, waiting for transfers between devices, core(): return lax.ppermute(tiles, 'c', swap)  2.83 us
  transfers between devices with their start and end apart: 16, of which 8 were waited for; matrix products, arithmetic and copies ran while one was open for 0% of the time, Pallas kernels for 21%

profile of v5, /device:TPU:1, one launch (start us, length us, event | category | flops | bytes accessed | tf_op | source)
XLA Modules:
  0.0 91.3 jit_solution(1167351859319755854)
XLA Ops:
  0.6 0.1 pad_add_fusion.at
  0.7 2.2 %cast_rows.1 = (bf16[32,64,256]{2,1,0:T(8,128)(2,1)S(1)}, s32[8,128]{1,0:T(8,128)S(1)}) custom-call(s32[3]{0:T(128)S(1)} %pad_add_fusion.at, f32[256,8192]{1,0:T(8,128)} %bitcast.11), custom_call_target="tpu_custom_call" | custom-call | bytes 1024 | tf_op jit(solution)/shard_map/cast_rows/pallas_call | solution.py:63
  2.9 1.5 %collective-permute-start = (bf16[32,64,256]{2,1,0:T(8,128)(2,1)S(1)}, bf16[32,64,256]{2,1,0:T(8,128)(2,1)S(1)}, u32[]{:S(2)}, u32[]{:S(2)}) collective-permute-start(bf16[32,64,256]{2,1,0:T(8,128)(2,1)S(1)} %get-tuple-element.33), channel_id=1, source_target_pairs={{0,32},{32,0},{1,33},{33,1},{2,34},{34,2},{3,35},{35,3},{4,36},{36... | collective-permute-start | bytes 3145736 | tf_op jit(solution)/shard_map/ppermute | solution.py:434
  4.4 2.6 %pick_rows.1 = (bf16[16,2,64,256]{3,2,1,0:T(8,128)(2,1)}, s32[8,128]{1,0:T(8,128)S(1)}) custom-call(s32[3]{0:T(128)S(1)} %pad_add_fusion.at, bf16[16,2,256,256]{3,2,1,0:T(8,128)(2,1)} %bitcast.16, s32[8,128]{1,0:T(8,128)S(1)} %get-tuple-element.34.refs_1_), custom_call_target="tpu_custom_call" | custom-call | bytes 1024 | tf_op jit(solution)/shard_map/pick_rows/pallas_call | solution.py:63
  7.0 0.0 collective-permute-done.refs_1_
  7.0 2.9 %add_theirs.1 = (bf16[32,64,256]{2,1,0:T(8,128)(2,1)}, s32[8,128]{1,0:T(8,128)S(1)}) custom-call(s32[3]{0:T(128)S(1)} %pad_add_fusion.at, f32[256,8192]{1,0:T(8,128)} %bitcast.12, bf16[32,64,256]{2,1,0:T(8,128)(2,1)S(1)} %collective-permute-done.refs_1_, s32[8,128]{1,0:T(8,128)S(1)} %get-tuple-element.35.refs_2_), custom_call_target="tpu_custom_call" | custom-call | bytes 1024 | tf_op jit(solution)/shard_map/add_theirs/pallas_call | solution.py:63
  9.9 1.4 %collective-permute-start.3 = (bf16[32,64,256]{2,1,0:T(8,128)(2,1)}, bf16[32,64,256]{2,1,0:T(8,128)(2,1)S(1)}, u32[]{:S(2)}, u32[]{:S(2)}) collective-permute-start(bf16[32,64,256]{2,1,0:T(8,128)(2,1)} %get-tuple-element.41), channel_id=1, source_target_pairs={{0,64},{64,0},{1,65},{65,1},{2,66},{66,2},{3,67},{67,3},{4,68},{68... | collective-permute-start | bytes 3145736 | tf_op jit(solution)/shard_map/ppermute | solution.py:437
  11.3 9.6 %all-to-all-start = ((bf16[32,64,256]{2,1,0:T(8,128)(2,1)}), bf16[32,64,256]{2,1,0:T(8,128)(2,1)S(1)}, u32[]{:S(2)}, u32[]{:S(2)}) async-start(bf16[32,64,256]{2,1,0:T(8,128)(2,1)} %bitcast.17), calls=%async_computation | async-start | bytes 2097152 | tf_op jit(solution)/shard_map/all_to_all | solution.py:429
  20.9 2.2 %cast_own.1 = (bf16[32,32,256]{2,1,0:T(8,128)(2,1)S(1)}, bf16[32,32,256]{2,1,0:T(8,128)(2,1)S(1)}, s32[8,128]{1,0:T(8,128)S(1)}) custom-call(s32[3]{0:T(128)S(1)} %pad_add_fusion.at, f32[256,8192]{1,0:T(8,128)} %bitcast.13, s32[8,128]{1,0:T(8,128)S(1)} %get-tuple-element.36.refs_1_), custom_call_target="tpu_custom_call" | custom-call | bytes 1024 | tf_op jit(solution)/shard_map/cast_own/pallas_call | solution.py:63
  23.1 0.7 collective-permute-start.1
  23.7 0.1 collective-permute-start.2
  23.8 1.4 %collective-permute-done.1.refs_1_ = bf16[32,32,256]{2,1,0:T(8,128)(2,1)S(1)} collective-permute-done((bf16[32,32,256]{2,1,0:T(8,128)(2,1)S(1)}, bf16[32,32,256]{2,1,0:T(8,128)(2,1)S(1)}, u32[]{:S(2)}, u32[]{:S(2)}) %collective-permute-start.1) | collective-permute-done | bytes 524320 | tf_op jit(solution)/shard_map/ppermute | solution.py:434
  25.3 0.7 collective-permute-done.2.refs_2_
  26.0 2.2 %add_own.1 = (bf16[32,64,256]{2,1,0:T(8,128)(2,1)S(1)}, s32[8,128]{1,0:T(8,128)S(1)}) custom-call(s32[3]{0:T(128)S(1)} %pad_add_fusion.at, f32[256,8192]{1,0:T(8,128)} %bitcast.14, bf16[32,32,256]{2,1,0:T(8,128)(2,1)S(1)} %collective-permute-done.1.refs_1_, bf16[32,32,256]{2,1,0:T(8,128)(2,1)S(1)} %collective-permute-done.2.refs_2_, ...), custom_call_target="tpu_custom_call" | custom-call | bytes 1024 | tf_op jit(solution)/shard_map/add_own/pallas_call | solution.py:63
  28.2 11.0 %all-to-all-done.refs_2_ = bf16[32,64,256]{2,1,0:T(8,128)(2,1)S(1)} async-done(((bf16[32,64,256]{2,1,0:T(8,128)(2,1)}), bf16[32,64,256]{2,1,0:T(8,128)(2,1)S(1)}, u32[]{:S(2)}, u32[]{:S(2)}) %all-to-all-start) | async-done | bytes 1048608 | tf_op jit(solution)/shard_map/all_to_all | solution.py:429
  39.2 0.0 collective-permute-done.3.refs_1_
  39.2 1.9 %blend_rows.1 = (bf16[32,64,256]{2,1,0:T(8,128)(2,1)}, s32[8,128]{1,0:T(8,128)S(1)}) custom-call(s32[3]{0:T(128)S(1)} %pad_add_fusion.at, bf16[32,64,256]{2,1,0:T(8,128)(2,1)S(1)} %get-tuple-element.40.refs_0_, bf16[32,64,256]{2,1,0:T(8,128)(2,1)S(1)} %collective-permute-done.3.refs_1_, bf16[32,64,256]{2,1,0:T(8,128)(2,1)S(1)} %all-to-all-done.refs_2_, ...), custom_call_target="tpu_custom_call" | custom-call | bytes 1024 | tf_op jit(solution)/shard_map/blend_rows/pallas_call | solution.py:63
  41.1 1.8 %collective-permute-start.5 = (bf16[32,64,256]{2,1,0:T(8,128)(2,1)}, bf16[32,64,256]{2,1,0:T(8,128)(2,1)S(1)}, u32[]{:S(2)}, u32[]{:S(2)}) collective-permute-start(bf16[32,64,256]{2,1,0:T(8,128)(2,1)} %get-tuple-element.44.refs_1_), channel_id=1, source_target_pairs={{0,32},{32,0},{1,33},{33,1},{2,34},{34,2},{3,35},{35,3},{4,36},{36... | collective-permute-start | bytes 3145736 | tf_op jit(solution)/shard_map/ppermute | solution.py:434
  42.9 0.0 collective-permute-start.4
  42.9 5.8 %all-to-all-start.1 = ((bf16[32,64,256]{2,1,0:T(8,128)(2,1)}), bf16[32,64,256]{2,1,0:T(8,128)(2,1)S(1)}, u32[]{:S(2)}, u32[]{:S(2)}) async-start(bf16[32,64,256]{2,1,0:T(8,128)(2,1)} %get-tuple-element.44.refs_1_), calls=%async_computation.1 | async-start | bytes 2097152 | tf_op jit(solution)/shard_map/all_to_all | solution.py:429
  48.7 0.0 collective-permute-done.5.refs_0_
  48.7 4.0 %write_rows.5 = (f32[256,8192]{1,0:T(8,128)}, s32[8,128]{1,0:T(8,128)S(1)}) custom-call(s32[3]{0:T(128)S(1)} %pad_add_fusion.at, bf16[32,64,256]{2,1,0:T(8,128)(2,1)S(1)} %collective-permute-done.5.refs_0_, bf16[32,64,256]{2,1,0:T(8,128)(2,1)} %get-tuple-element.44.refs_1_, s32[8,128]{1,0:T(8,128)S(1)} %get-tuple-element.45.refs_2_), custom_call_target="tpu_custom_call" | custom-call | bytes 11534336 | tf_op jit(solution)/shard_map/write_rows/pallas_call | solution.py:63
  52.7 14.2 %all-to-all-done.1 = bf16[32,64,256]{2,1,0:T(8,128)(2,1)S(1)} async-done(((bf16[32,64,256]{2,1,0:T(8,128)(2,1)}), bf16[32,64,256]{2,1,0:T(8,128)(2,1)S(1)}, u32[]{:S(2)}, u32[]{:S(2)}) %all-to-all-start.1) | async-done | bytes 1048608 | tf_op jit(solution)/shard_map/all_to_all | solution.py:429
  66.9 0.9 %collective-permute-done.4 = bf16[32,64,256]{2,1,0:T(8,128)(2,1)S(1)} collective-permute-done((bf16[32,64,256]{2,1,0:T(8,128)(2,1)}, bf16[32,64,256]{2,1,0:T(8,128)(2,1)S(1)}, u32[]{:S(2)}, u32[]{:S(2)}) %collective-permute-start.4) | collective-permute-done | bytes 1048608 | tf_op jit(solution)/shard_map/ppermute | solution.py:437
  67.8 1.6 %split_planes.1 = (bf16[16,64,256]{2,1,0:T(8,128)(2,1)}, bf16[16,64,256]{2,1,0:T(8,128)(2,1)}, bf16[16,64,256]{2,1,0:T(8,128)(2,1)S(1)}, bf16[16,64,256]{2,1,0:T(8,128)(2,1)S(1)}, s32[8,128]{1,0:T(8,128)S(1)}) custom-call(s32[3]{0:T(128)S(1)} %pad_add_fusion.at, bf16[16,2,64,256]{3,2,1,0:T(8,128)(2,1)S(1)} %bitcast.10, bf16[16,2,64,256]{3,2,1,0:T(8,128)(2,1)S(1)} %bitcast.9, ...), custom_call_target="tpu_custom_call" | custom-call | bytes 1024 | tf_op jit(solution)/shard_map/split_planes/pallas_call | solution.py:63
  69.4 1.0 %collective-permute-start.8 = (bf16[16,64,256]{2,1,0:T(8,128)(2,1)}, bf16[16,64,256]{2,1,0:T(8,128)(2,1)}, u32[]{:S(2)}, u32[]{:S(2)}) collective-permute-start(bf16[16,64,256]{2,1,0:T(8,128)(2,1)} %get-tuple-element.50.refs_0_), channel_id=1, source_target_pairs={{0,32},{32,0},{1,33},{33,1},{2,34},{34,2},{3,35},{35,3},{4,36},{36... | collective-permute-start | bytes 1572872 | tf_op jit(solution)/shard_map/ppermute | solution.py:434
  70.4 0.1 collective-permute-start.9
  70.5 0.4 collective-permute-start.6
  70.9 0.1 collective-permute-start.7
  71.0 0.0 collective-permute-start.10
  71.0 4.0 %all-to-all-start.2 = ((bf16[16,64,256]{2,1,0:T(8,128)(2,1)}), bf16[16,64,256]{2,1,0:T(8,128)(2,1)S(1)}, u32[]{:S(2)}, u32[]{:S(2)}) async-start(bf16[16,64,256]{2,1,0:T(8,128)(2,1)} %get-tuple-element.47.refs_2_), calls=%async_computation.2 | async-start | bytes 1048576 | tf_op jit(solution)/shard_map/all_to_all | solution.py:452
  75.0 0.0 collective-permute-done.8.refs_1_
  75.0 0.0 collective-permute-done.9.refs_3_
  75.0 3.4 %write_rows.6 = (bf16[16,2,256,256]{3,2,1,0:T(8,128)(2,1)}, s32[8,128]{1,0:T(8,128)S(1)}) custom-call(s32[3]{0:T(128)S(1)} %pad_add_fusion.at, bf16[16,64,256]{2,1,0:T(8,128)(2,1)} %get-tuple-element.50.refs_0_, bf16[16,64,256]{2,1,0:T(8,128)(2,1)} %collective-permute-done.8.refs_1_, bf16[16,64,256]{2,1,0:T(8,128)(2,1)S(1)} %get-tuple-element.51.refs_2_, ...), custom_call_target="tpu_custom_call" | custom-call | bytes 1024 | tf_op jit(solution)/shard_map/write_rows/pallas_call | solution.py:63
  78.4 0.0 collective-permute-done.6.refs_0_
  78.4 0.0 collective-permute-done.7.refs_1_
  78.4 3.4 %write_rows.7 = (f32[256,8192]{1,0:T(8,128)}, s32[8,128]{1,0:T(8,128)S(1)}) custom-call(s32[3]{0:T(128)S(1)} %pad_add_fusion.at, bf16[16,64,256]{2,1,0:T(8,128)(2,1)S(1)} %collective-permute-done.6.refs_0_, bf16[16,64,256]{2,1,0:T(8,128)(2,1)S(1)} %collective-permute-done.7.refs_1_, ...), custom_call_target="tpu_custom_call", output_to_operand_aliasing={{0}: (5, {})} | custom-call | bytes 1024 | tf_op jit(solution)/shard_map/write_rows/pallas_call | solution.py:63
  81.8 2.3 %collective-permute-done.10.refs_1_ = bf16[16,64,256]{2,1,0:T(8,128)(2,1)S(1)} collective-permute-done((bf16[16,64,256]{2,1,0:T(8,128)(2,1)S(1)}, bf16[16,64,256]{2,1,0:T(8,128)(2,1)S(1)}, u32[]{:S(2)}, u32[]{:S(2)}) %collective-permute-start.10) | collective-permute-done | bytes 524320 | tf_op jit(solution)/shard_map/ppermute | solution.py:437
  84.1 1.2 %all-to-all-done.2.refs_0_ = bf16[16,64,256]{2,1,0:T(8,128)(2,1)S(1)} async-done(((bf16[16,64,256]{2,1,0:T(8,128)(2,1)}), bf16[16,64,256]{2,1,0:T(8,128)(2,1)S(1)}, u32[]{:S(2)}, u32[]{:S(2)}) %all-to-all-start.2) | async-done | bytes 524320 | tf_op jit(solution)/shard_map/all_to_all | solution.py:452
  85.3 2.1 %collective-permute-start.11 = (bf16[16,64,256]{2,1,0:T(8,128)(2,1)S(1)}, bf16[16,64,256]{2,1,0:T(8,128)(2,1)S(1)}, u32[]{:S(2)}, u32[]{:S(2)}) collective-permute-start(bf16[16,64,256]{2,1,0:T(8,128)(2,1)S(1)} %all-to-all-done.2.refs_0_), channel_id=1, source_target_pairs={{0,32},{32,0},{1,33},{33,1},{2,34},{34,2},{3,35},{35,3},{4,36},{36... | collective-permute-start | bytes 1572872 | tf_op jit(solution)/shard_map/ppermute | solution.py:434
  87.4 0.0 collective-permute-start.12
  87.4 1.7 %write_rows.8 = (bf16[16,2,256,256]{3,2,1,0:T(8,128)(2,1)}, s32[8,128]{1,0:T(8,128)S(1)}) custom-call(s32[3]{0:T(128)S(1)} %pad_add_fusion.at, bf16[16,64,256]{2,1,0:T(8,128)(2,1)S(1)} %all-to-all-done.2.refs_0_, bf16[16,64,256]{2,1,0:T(8,128)(2,1)S(1)} %collective-permute-done.10.refs_1_, ...), custom_call_target="tpu_custom_call", output_to_operand_aliasing={{0}: (3, {})} | custom-call | bytes 38797312 | tf_op jit(solution)/shard_map/write_rows/pallas_call | solution.py:63
  89.1 0.0 collective-permute-done.11.refs_0_
  89.1 0.6 collective-permute-done.12.refs_1_
  89.7 1.7 %write_rows.9 = (bf16[16,2,256,256]{3,2,1,0:T(8,128)(2,1)}, s32[8,128]{1,0:T(8,128)}) custom-call(s32[3]{0:T(128)S(1)} %pad_add_fusion.at, bf16[16,64,256]{2,1,0:T(8,128)(2,1)S(1)} %collective-permute-done.11.refs_0_, bf16[16,64,256]{2,1,0:T(8,128)(2,1)S(1)} %collective-permute-done.12.refs_1_, ...), custom_call_target="tpu_custom_call", output_to_operand_aliasing={{0}: (3, {})} | custom-call | bytes 1024 | tf_op jit(solution)/shard_map/write_rows/pallas_call | solution.py:63
Async XLA Ops:
  2.9 4.2 %collective-permute-start = (bf16[32,64,256]{2,1,0:T(8,128)(2,1)S(1)}, bf16[32,64,256]{2,1,0:T(8,128)(2,1)S(1)}, u32[]{:S(2)}, u32[]{:S(2)}) collective-permute-start(bf16[32,64,256]{2,1,0:T(8,128)(2,1)S(1)} %get-tuple-element.33), channel_id=1, source_target_pairs={{0,32},{32,0},{1,33},{33,1},{2,34},{34,2},{3,35},{35,3},{4,36},{36... | collective-permute-start | bytes 3145736 | tf_op jit(solution)/shard_map/ppermute | solution.py:434
  9.9 29.2 %collective-permute-start.3 = (bf16[32,64,256]{2,1,0:T(8,128)(2,1)}, bf16[32,64,256]{2,1,0:T(8,128)(2,1)S(1)}, u32[]{:S(2)}, u32[]{:S(2)}) collective-permute-start(bf16[32,64,256]{2,1,0:T(8,128)(2,1)} %get-tuple-element.41), channel_id=1, source_target_pairs={{0,64},{64,0},{1,65},{65,1},{2,66},{66,2},{3,67},{67,3},{4,68},{68... | collective-permute-start | bytes 3145736 | tf_op jit(solution)/shard_map/ppermute | solution.py:437
  11.3 27.9 %all-to-all-start = ((bf16[32,64,256]{2,1,0:T(8,128)(2,1)}), bf16[32,64,256]{2,1,0:T(8,128)(2,1)S(1)}, u32[]{:S(2)}, u32[]{:S(2)}) async-start(bf16[32,64,256]{2,1,0:T(8,128)(2,1)} %bitcast.17), calls=%async_computation | async-start | bytes 2097152 | tf_op jit(solution)/shard_map/all_to_all | solution.py:429
  23.1 2.2 %collective-permute-start.1 = (bf16[32,32,256]{2,1,0:T(8,128)(2,1)S(1)}, bf16[32,32,256]{2,1,0:T(8,128)(2,1)S(1)}, u32[]{:S(2)}, u32[]{:S(2)}) collective-permute-start(bf16[32,32,256]{2,1,0:T(8,128)(2,1)S(1)} %get-tuple-element.37), channel_id=1, source_target_pairs={{0,32},{32,0},{1,33},{33,1},{2,34},{34,2},{3,35},{35,3},{4,36},{36... | collective-permute-start | bytes 1572872 | tf_op jit(solution)/shard_map/ppermute | solution.py:434
  23.7 2.3 %collective-permute-start.2 = (bf16[32,32,256]{2,1,0:T(8,128)(2,1)S(1)}, bf16[32,32,256]{2,1,0:T(8,128)(2,1)S(1)}, u32[]{:S(2)}, u32[]{:S(2)}) collective-permute-start(bf16[32,32,256]{2,1,0:T(8,128)(2,1)S(1)} %get-tuple-element.38), channel_id=1, source_target_pairs={{0,32},{32,0},{1,33},{33,1},{2,34},{34,2},{3,35},{35,3},{4,36},{36... | collective-permute-start | bytes 1572872 | tf_op jit(solution)/shard_map/ppermute | solution.py:434
  41.1 7.6 %collective-permute-start.5 = (bf16[32,64,256]{2,1,0:T(8,128)(2,1)}, bf16[32,64,256]{2,1,0:T(8,128)(2,1)S(1)}, u32[]{:S(2)}, u32[]{:S(2)}) collective-permute-start(bf16[32,64,256]{2,1,0:T(8,128)(2,1)} %get-tuple-element.44.refs_1_), channel_id=1, source_target_pairs={{0,32},{32,0},{1,33},{33,1},{2,34},{34,2},{3,35},{35,3},{4,36},{36... | collective-permute-start | bytes 3145736 | tf_op jit(solution)/shard_map/ppermute | solution.py:434
  42.9 24.9 %collective-permute-start.4 = (bf16[32,64,256]{2,1,0:T(8,128)(2,1)}, bf16[32,64,256]{2,1,0:T(8,128)(2,1)S(1)}, u32[]{:S(2)}, u32[]{:S(2)}) collective-permute-start(bf16[32,64,256]{2,1,0:T(8,128)(2,1)} %get-tuple-element.44.refs_1_), channel_id=1, source_target_pairs={{0,64},{64,0},{1,65},{65,1},{2,66},{66,2},{3,67},{67,3},{4,68},{68... | collective-permute-start | bytes 3145736 | tf_op jit(solution)/shard_map/ppermute | solution.py:437
  42.9 24.0 %all-to-all-start.1 = ((bf16[32,64,256]{2,1,0:T(8,128)(2,1)}), bf16[32,64,256]{2,1,0:T(8,128)(2,1)S(1)}, u32[]{:S(2)}, u32[]{:S(2)}) async-start(bf16[32,64,256]{2,1,0:T(8,128)(2,1)} %get-tuple-element.44.refs_1_), calls=%async_computation.1 | async-start | bytes 2097152 | tf_op jit(solution)/shard_map/all_to_all | solution.py:429
  69.4 5.5 %collective-permute-start.8 = (bf16[16,64,256]{2,1,0:T(8,128)(2,1)}, bf16[16,64,256]{2,1,0:T(8,128)(2,1)}, u32[]{:S(2)}, u32[]{:S(2)}) collective-permute-start(bf16[16,64,256]{2,1,0:T(8,128)(2,1)} %get-tuple-element.50.refs_0_), channel_id=1, source_target_pairs={{0,32},{32,0},{1,33},{33,1},{2,34},{34,2},{3,35},{35,3},{4,36},{36... | collective-permute-start | bytes 1572872 | tf_op jit(solution)/shard_map/ppermute | solution.py:434
  70.4 4.6 %collective-permute-start.9 = (bf16[16,64,256]{2,1,0:T(8,128)(2,1)S(1)}, bf16[16,64,256]{2,1,0:T(8,128)(2,1)}, u32[]{:S(2)}, u32[]{:S(2)}) collective-permute-start(bf16[16,64,256]{2,1,0:T(8,128)(2,1)S(1)} %get-tuple-element.51.refs_2_), channel_id=1, source_target_pairs={{0,32},{32,0},{1,33},{33,1},{2,34},{34,2},{3,35},{35,3},{4,36},{36... | collective-permute-start | bytes 1572872 | tf_op jit(solution)/shard_map/ppermute | solution.py:434
  70.5 7.9 %collective-permute-start.6 = (bf16[16,64,256]{2,1,0:T(8,128)(2,1)}, bf16[16,64,256]{2,1,0:T(8,128)(2,1)S(1)}, u32[]{:S(2)}, u32[]{:S(2)}) collective-permute-start(bf16[16,64,256]{2,1,0:T(8,128)(2,1)} %get-tuple-element.47.refs_2_), channel_id=1, source_target_pairs={{0,32},{32,0},{1,33},{33,1},{2,34},{34,2},{3,35},{35,3},{4,36},{36... | collective-permute-start | bytes 1572872 | tf_op jit(solution)/shard_map/ppermute | solution.py:434
  70.9 7.5 %collective-permute-start.7 = (bf16[16,64,256]{2,1,0:T(8,128)(2,1)S(1)}, bf16[16,64,256]{2,1,0:T(8,128)(2,1)S(1)}, u32[]{:S(2)}, u32[]{:S(2)}) collective-permute-start(bf16[16,64,256]{2,1,0:T(8,128)(2,1)S(1)} %get-tuple-element.48.refs_3_), channel_id=1, source_target_pairs={{0,32},{32,0},{1,33},{33,1},{2,34},{34,2},{3,35},{35,3},{4,36},{36... | collective-permute-start | bytes 1572872 | tf_op jit(solution)/shard_map/ppermute | solution.py:434
  71.0 13.1 %collective-permute-start.10 = (bf16[16,64,256]{2,1,0:T(8,128)(2,1)S(1)}, bf16[16,64,256]{2,1,0:T(8,128)(2,1)S(1)}, u32[]{:S(2)}, u32[]{:S(2)}) collective-permute-start(bf16[16,64,256]{2,1,0:T(8,128)(2,1)S(1)} %get-tuple-element.51.refs_2_), channel_id=1, source_target_pairs={{0,64},{64,0},{1,65},{65,1},{2,66},{66,2},{3,67},{67,3},{4,68},{68... | collective-permute-start | bytes 1572872 | tf_op jit(solution)/shard_map/ppermute | solution.py:437
  71.0 14.3 %all-to-all-start.2 = ((bf16[16,64,256]{2,1,0:T(8,128)(2,1)}), bf16[16,64,256]{2,1,0:T(8,128)(2,1)S(1)}, u32[]{:S(2)}, u32[]{:S(2)}) async-start(bf16[16,64,256]{2,1,0:T(8,128)(2,1)} %get-tuple-element.47.refs_2_), calls=%async_computation.2 | async-start | bytes 1048576 | tf_op jit(solution)/shard_map/all_to_all | solution.py:452
  85.3 3.8 %collective-permute-start.11 = (bf16[16,64,256]{2,1,0:T(8,128)(2,1)S(1)}, bf16[16,64,256]{2,1,0:T(8,128)(2,1)S(1)}, u32[]{:S(2)}, u32[]{:S(2)}) collective-permute-start(bf16[16,64,256]{2,1,0:T(8,128)(2,1)S(1)} %all-to-all-done.2.refs_0_), channel_id=1, source_target_pairs={{0,32},{32,0},{1,33},{33,1},{2,34},{34,2},{3,35},{35,3},{4,36},{36... | collective-permute-start | bytes 1572872 | tf_op jit(solution)/shard_map/ppermute | solution.py:434
  87.4 2.3 %collective-permute-start.12 = (bf16[16,64,256]{2,1,0:T(8,128)(2,1)S(1)}, bf16[16,64,256]{2,1,0:T(8,128)(2,1)S(1)}, u32[]{:S(2)}, u32[]{:S(2)}) collective-permute-start(bf16[16,64,256]{2,1,0:T(8,128)(2,1)S(1)} %collective-permute-done.10.refs_1_), channel_id=1, source_target_pairs={{0,32},{32,0},{1,33},{33,1},{2,34},{34,2},{3,35},{35,3},{4,36},{36... | collective-permute-start | bytes 1572872 | tf_op jit(solution)/shard_map/ppermute | solution.py:434

commit v6 on v5

--- a/solution.py
+++ b/solution.py
@@ -7,6 +7,7 @@
 from jax.sharding import Mesh, PartitionSpec as P
 
 blend_rate = 0.3
+GROUPS = 4
 
 AXES = ("xl", "c", "y", "z", "xh")
 SIZES = (2, 2, 4, 4, 2)
@@ -134,41 +135,29 @@
     return out
 
 
-def add_theirs(order, policy, tiles):
-    def body(at, x_ref, t_ref, o_ref, wide, held, in_sems, out_sems):
-        rows = pl.ds(first_row(at, True, False, 0), QUARTER)
-
-        def fetch(p):
-            return pltpu.make_async_copy(x_ref.at[rows, span_of(p)], wide.at[:, span_of(p)], in_sems.at[p])
-
+def add_theirs(order, rows, tiles):
+    def body(at, x_ref, t_ref, o_ref, held, sems):
         def store(p):
             some = pl.ds(p * PER, PER)
-            return pltpu.make_async_copy(held.at[some], o_ref.at[some], out_sems.at[p])
+            return pltpu.make_async_copy(held.at[some], o_ref.at[some], sems.at[p])
 
         def work(p):
-            fetch(p).wait()
             for k in range(PER):
                 g = p * PER + k
-                held[g] = (wide[:, columns(g)] + t_ref[g].astype(F32)).astype(BF)
+                held[g] = (x_ref[:, columns(g)] + t_ref[g].astype(F32)).astype(BF)
             store(p).start()
 
-        each(PARTS, lambda p: fetch(p).start())
         each(PARTS, work)
         each(PARTS, lambda p: store(p).wait())
 
     (out,) = order.run(
         body,
         "add_theirs",
-        (policy, in_vmem(tiles)),
-        [HBM, VMEM],
+        (in_vmem(rows), in_vmem(tiles)),
+        [VMEM, VMEM],
         [pltpu.HBM((SHARDS, QUARTER, WIDTH), BF)],
         [HBM],
-        [
-            pltpu.VMEM((QUARTER, D), F32),
-            pltpu.VMEM((SHARDS, QUARTER, WIDTH), BF),
-            pltpu.SemaphoreType.DMA((PARTS,)),
-            pltpu.SemaphoreType.DMA((PARTS,)),
-        ],
+        [pltpu.VMEM((SHARDS, QUARTER, WIDTH), BF), pltpu.SemaphoreType.DMA((PARTS,))],
     )
     return out
 
@@ -230,9 +219,10 @@
     return out
 
 
-def pick_rows(order, anchor):
-    def body(at, a_ref, p_ref, held, in_sems, out_sems):
+def pick_rows(order, anchor, policy):
+    def body(at, a_ref, x_ref, p_ref, rows_ref, held, in_sems, out_sems, x_sems):
         rows = [member_row(at, (True, True, 0), xh) for xh in range(2)]
+        theirs = pl.ds(first_row(at, True, False, 0), QUARTER)
 
         def fetch(p, xh):
             some = pl.ds(4 * p, 4)
@@ -244,31 +234,39 @@
             some = pl.ds(4 * p, 4)
             return pltpu.make_async_copy(held.at[some, xh], p_ref.at[some, xh], out_sems.at[xh, p])
 
+        def copy(p):
+            return pltpu.make_async_copy(
+                x_ref.at[theirs, span_of(p)], rows_ref.at[:, span_of(p)], x_sems.at[p]
+            )
+
         def forward(p, xh):
             fetch(p, xh).wait()
             store(p, xh).start()
 
         for xh in range(2):
             each(4, lambda p, xh=xh: fetch(p, xh).start())
+        each(PARTS, lambda p: copy(p).start())
         for xh in range(2):
             each(4, lambda p, xh=xh: forward(p, xh))
+        each(PARTS, lambda p: copy(p).wait())
         for xh in range(2):
             each(4, lambda p, xh=xh: store(p, xh).wait())
 
-    (picked,) = order.run(
+    picked, rows = order.run(
         body,
         "pick_rows",
-        (anchor,),
-        [HBM],
-        [pltpu.HBM((16, 2, QUARTER, WIDTH), BF)],
-        [HBM],
+        (anchor, policy),
+        [HBM, HBM],
+        [pltpu.HBM((16, 2, QUARTER, WIDTH), BF), pltpu.VMEM((QUARTER, D), F32)],
+        [HBM, VMEM],
         [
             pltpu.VMEM((16, 2, QUARTER, WIDTH), BF),
             pltpu.SemaphoreType.DMA((2, 4)),
             pltpu.SemaphoreType.DMA((2, 4)),
+            pltpu.SemaphoreType.DMA((PARTS,)),
         ],
     )
-    return picked.reshape(SHARDS, QUARTER, WIDTH)
+    return picked.reshape(SHARDS, QUARTER, WIDTH), rows
 
 
 def blend_rows(order, own, other, anchor):
@@ -280,8 +278,9 @@
         def work(p):
             for k in range(PER):
                 g = p * PER + k
-                average = (x_ref[g].astype(F32) + t_ref[g].astype(F32)) / 4
-                held[g] = ((1.0 - blend_rate) * a_ref[g].astype(F32) + blend_rate * average).astype(BF)
+                total = x_ref[g].astype(F32) + t_ref[g].astype(F32)
+                new = (1.0 - blend_rate) * a_ref[g].astype(F32) + (blend_rate / GROUPS) * total
+                held[g] = new.astype(BF)
             store(p).start()
 
         each(PARTS, work)
@@ -437,8 +436,8 @@
         return lax.ppermute(tiles, "xl", swap)
 
     theirs = core(cast_rows(order, policy))
-    picked = pick_rows(order, shards)
-    other = chip(add_theirs(order, policy, theirs))
+    picked, rows = pick_rows(order, shards, policy)
+    other = chip(add_theirs(order, rows, theirs))
     fetched = exchange(picked)
     own = add_own(order, policy, [core(tiles) for tiles in cast_own(order, policy)])
 

time: 92.1 us -> 91 us (0.988)
  Pallas kernels: 29.6 us -> 28.6 us
    pallas_call x12, Pallas kernels: 29.6 us -> 28.6 us  [run(): pl.pallas_call(ordered, out_shape=[*outs, TOKEN], grid_spec=pltpu.Prefetc...]
  transfers between devices with their start and end apart: 16 -> 16, of which waited for: 8 -> 8; matrix products, arithmetic and copies ran while one was open for 0% -> 0% of each run, Pallas kernels for 21% -> 22%
where the time goes in v6:
time: 91 us; the launch traced here: 90.3 us
  waiting for transfers between devices  32.4 us (36%)
  Pallas kernels  28.6 us (31%)
  starting transfers between devices  28.5 us (31%)
    pallas_call x12, Pallas kernels, run(): pl.pallas_call(ordered, out_shape=[*outs, TOKEN], grid_spec=pltpu.Prefetc...  28.6 us
    all_to_all x2, waiting for transfers between devices, exchange(): lax.all_to_all(tiles, AXES, split_axis=0, concat_axis=0, axis_index_group...  25.2 us
    all_to_all x2, starting transfers between devices, exchange(): lax.all_to_all(tiles, AXES, split_axis=0, concat_axis=0, axis_index_group...  15.4 us
    ppermute x10, starting transfers between devices, core(): return lax.ppermute(tiles, 'c', swap)  7.77 us
    all_to_all x1, starting transfers between devices, per_device(): lax.all_to_all(first, ('y', 'z'), split_axis=0, concat_axis=0, tiled=True)  3.95 us
    ppermute x3, waiting for transfers between devices, chip(): return lax.ppermute(tiles, 'xl', swap)  3.21 us
    ppermute x10, waiting for transfers between devices, core(): return lax.ppermute(tiles, 'c', swap)  2.83 us
  transfers between devices with their start and end apart: 16, of which 8 were waited for; matrix products, arithmetic and copies ran while one was open for 0% of the time, Pallas kernels for 22%

profile of v6, /device:TPU:1, one launch (start us, length us, event | category | flops | bytes accessed | tf_op | source)
XLA Modules:
  0.0 90.3 jit_solution(15731678279931267892)
XLA Ops:
  0.6 0.1 pad_add_fusion.at
  0.7 2.2 %cast_rows.1 = (bf16[32,64,256]{2,1,0:T(8,128)(2,1)S(1)}, s32[8,128]{1,0:T(8,128)S(1)}) custom-call(s32[3]{0:T(128)S(1)} %pad_add_fusion.at, f32[256,8192]{1,0:T(8,128)} %bitcast.11), custom_call_target="tpu_custom_call" | custom-call | bytes 1024 | tf_op jit(solution)/shard_map/cast_rows/pallas_call | solution.py:64
  2.9 1.5 %collective-permute-start = (bf16[32,64,256]{2,1,0:T(8,128)(2,1)S(1)}, bf16[32,64,256]{2,1,0:T(8,128)(2,1)S(1)}, u32[]{:S(2)}, u32[]{:S(2)}) collective-permute-start(bf16[32,64,256]{2,1,0:T(8,128)(2,1)S(1)} %get-tuple-element.36), channel_id=1, source_target_pairs={{0,32},{32,0},{1,33},{33,1},{2,34},{34,2},{3,35},{35,3},{4,36},{36... | collective-permute-start | bytes 3145736 | tf_op jit(solution)/shard_map/ppermute | solution.py:433
  4.4 3.0 %pick_rows.1 = (bf16[16,2,64,256]{3,2,1,0:T(8,128)(2,1)}, f32[64,8192]{1,0:T(8,128)S(1)}, s32[8,128]{1,0:T(8,128)S(1)}) custom-call(s32[3]{0:T(128)S(1)} %pad_add_fusion.at, bf16[16,2,256,256]{3,2,1,0:T(8,128)(2,1)} %bitcast.16, f32[256,8192]{1,0:T(8,128)} %bitcast.12, s32[8,128]{1,0:T(8,128)S(1)} %get-tuple-element.34.refs_2_), custom_call_target="tpu_custom_call" | custom-call | bytes 1024 | tf_op jit(solution)/shard_map/pick_rows/pallas_call | solution.py:64
  7.4 0.0 collective-permute-done.refs_1_
  7.4 1.6 %add_theirs.1 = (bf16[32,64,256]{2,1,0:T(8,128)(2,1)}, s32[8,128]{1,0:T(8,128)S(1)}) custom-call(s32[3]{0:T(128)S(1)} %pad_add_fusion.at, f32[64,8192]{1,0:T(8,128)S(1)} %get-tuple-element.35.refs_0_, bf16[32,64,256]{2,1,0:T(8,128)(2,1)S(1)} %collective-permute-done.refs_1_, s32[8,128]{1,0:T(8,128)S(1)} %get-tuple-element.37.refs_2_), custom_call_target="tpu_custom_call" | custom-call | bytes 1024 | tf_op jit(solution)/shard_map/add_theirs/pallas_call | solution.py:64
  9.0 1.4 %collective-permute-start.3 = (bf16[32,64,256]{2,1,0:T(8,128)(2,1)}, bf16[32,64,256]{2,1,0:T(8,128)(2,1)S(1)}, u32[]{:S(2)}, u32[]{:S(2)}) collective-permute-start(bf16[32,64,256]{2,1,0:T(8,128)(2,1)} %get-tuple-element.43), channel_id=1, source_target_pairs={{0,64},{64,0},{1,65},{65,1},{2,66},{66,2},{3,67},{67,3},{4,68},{68... | collective-permute-start | bytes 3145736 | tf_op jit(solution)/shard_map/ppermute | solution.py:436
  10.4 9.6 %all-to-all-start = ((bf16[32,64,256]{2,1,0:T(8,128)(2,1)}), bf16[32,64,256]{2,1,0:T(8,128)(2,1)S(1)}, u32[]{:S(2)}, u32[]{:S(2)}) async-start(bf16[32,64,256]{2,1,0:T(8,128)(2,1)} %bitcast.17), calls=%async_computation | async-start | bytes 2097152 | tf_op jit(solution)/shard_map/all_to_all | solution.py:428
  20.0 2.2 %cast_own.1 = (bf16[32,32,256]{2,1,0:T(8,128)(2,1)S(1)}, bf16[32,32,256]{2,1,0:T(8,128)(2,1)S(1)}, s32[8,128]{1,0:T(8,128)S(1)}) custom-call(s32[3]{0:T(128)S(1)} %pad_add_fusion.at, f32[256,8192]{1,0:T(8,128)} %bitcast.13, s32[8,128]{1,0:T(8,128)S(1)} %get-tuple-element.38.refs_1_), custom_call_target="tpu_custom_call" | custom-call | bytes 1024 | tf_op jit(solution)/shard_map/cast_own/pallas_call | solution.py:64
  22.1 0.7 collective-permute-start.1
  22.8 0.1 collective-permute-start.2
  22.9 1.4 %collective-permute-done.1.refs_1_ = bf16[32,32,256]{2,1,0:T(8,128)(2,1)S(1)} collective-permute-done((bf16[32,32,256]{2,1,0:T(8,128)(2,1)S(1)}, bf16[32,32,256]{2,1,0:T(8,128)(2,1)S(1)}, u32[]{:S(2)}, u32[]{:S(2)}) %collective-permute-start.1) | collective-permute-done | bytes 524320 | tf_op jit(solution)/shard_map/ppermute | solution.py:433
  24.3 0.7 collective-permute-done.2.refs_2_
  25.1 2.2 %add_own.1 = (bf16[32,64,256]{2,1,0:T(8,128)(2,1)S(1)}, s32[8,128]{1,0:T(8,128)S(1)}) custom-call(s32[3]{0:T(128)S(1)} %pad_add_fusion.at, f32[256,8192]{1,0:T(8,128)} %bitcast.14, bf16[32,32,256]{2,1,0:T(8,128)(2,1)S(1)} %collective-permute-done.1.refs_1_, bf16[32,32,256]{2,1,0:T(8,128)(2,1)S(1)} %collective-permute-done.2.refs_2_, ...), custom_call_target="tpu_custom_call" | custom-call | bytes 1024 | tf_op jit(solution)/shard_map/add_own/pallas_call | solution.py:64
  27.3 11.0 %all-to-all-done.refs_2_ = bf16[32,64,256]{2,1,0:T(8,128)(2,1)S(1)} async-done(((bf16[32,64,256]{2,1,0:T(8,128)(2,1)}), bf16[32,64,256]{2,1,0:T(8,128)(2,1)S(1)}, u32[]{:S(2)}, u32[]{:S(2)}) %all-to-all-start) | async-done | bytes 1048608 | tf_op jit(solution)/shard_map/all_to_all | solution.py:428
  38.2 0.0 collective-permute-done.3.refs_1_
  38.2 1.8 %blend_rows.1 = (bf16[32,64,256]{2,1,0:T(8,128)(2,1)}, s32[8,128]{1,0:T(8,128)S(1)}) custom-call(s32[3]{0:T(128)S(1)} %pad_add_fusion.at, bf16[32,64,256]{2,1,0:T(8,128)(2,1)S(1)} %get-tuple-element.42.refs_0_, bf16[32,64,256]{2,1,0:T(8,128)(2,1)S(1)} %collective-permute-done.3.refs_1_, bf16[32,64,256]{2,1,0:T(8,128)(2,1)S(1)} %all-to-all-done.refs_2_, ...), custom_call_target="tpu_custom_call" | custom-call | bytes 1024 | tf_op jit(solution)/shard_map/blend_rows/pallas_call | solution.py:64
  40.1 1.8 %collective-permute-start.5 = (bf16[32,64,256]{2,1,0:T(8,128)(2,1)}, bf16[32,64,256]{2,1,0:T(8,128)(2,1)S(1)}, u32[]{:S(2)}, u32[]{:S(2)}) collective-permute-start(bf16[32,64,256]{2,1,0:T(8,128)(2,1)} %get-tuple-element.46.refs_1_), channel_id=1, source_target_pairs={{0,32},{32,0},{1,33},{33,1},{2,34},{34,2},{3,35},{35,3},{4,36},{36... | collective-permute-start | bytes 3145736 | tf_op jit(solution)/shard_map/ppermute | solution.py:433
  41.9 0.0 collective-permute-start.4
  41.9 5.8 %all-to-all-start.1 = ((bf16[32,64,256]{2,1,0:T(8,128)(2,1)}), bf16[32,64,256]{2,1,0:T(8,128)(2,1)S(1)}, u32[]{:S(2)}, u32[]{:S(2)}) async-start(bf16[32,64,256]{2,1,0:T(8,128)(2,1)} %get-tuple-element.46.refs_1_), calls=%async_computation.1 | async-start | bytes 2097152 | tf_op jit(solution)/shard_map/all_to_all | solution.py:428
  47.7 0.0 collective-permute-done.5.refs_0_
  47.7 4.0 %write_rows.5 = (f32[256,8192]{1,0:T(8,128)}, s32[8,128]{1,0:T(8,128)S(1)}) custom-call(s32[3]{0:T(128)S(1)} %pad_add_fusion.at, bf16[32,64,256]{2,1,0:T(8,128)(2,1)S(1)} %collective-permute-done.5.refs_0_, bf16[32,64,256]{2,1,0:T(8,128)(2,1)} %get-tuple-element.46.refs_1_, s32[8,128]{1,0:T(8,128)S(1)} %get-tuple-element.47.refs_2_), custom_call_target="tpu_custom_call" | custom-call | bytes 11534336 | tf_op jit(solution)/shard_map/write_rows/pallas_call | solution.py:64
  51.7 14.2 %all-to-all-done.1 = bf16[32,64,256]{2,1,0:T(8,128)(2,1)S(1)} async-done(((bf16[32,64,256]{2,1,0:T(8,128)(2,1)}), bf16[32,64,256]{2,1,0:T(8,128)(2,1)S(1)}, u32[]{:S(2)}, u32[]{:S(2)}) %all-to-all-start.1) | async-done | bytes 1048608 | tf_op jit(solution)/shard_map/all_to_all | solution.py:428
  65.9 0.9 %collective-permute-done.4 = bf16[32,64,256]{2,1,0:T(8,128)(2,1)S(1)} collective-permute-done((bf16[32,64,256]{2,1,0:T(8,128)(2,1)}, bf16[32,64,256]{2,1,0:T(8,128)(2,1)S(1)}, u32[]{:S(2)}, u32[]{:S(2)}) %collective-permute-start.4) | collective-permute-done | bytes 1048608 | tf_op jit(solution)/shard_map/ppermute | solution.py:436
  66.8 1.6 %split_planes.1 = (bf16[16,64,256]{2,1,0:T(8,128)(2,1)}, bf16[16,64,256]{2,1,0:T(8,128)(2,1)}, bf16[16,64,256]{2,1,0:T(8,128)(2,1)S(1)}, bf16[16,64,256]{2,1,0:T(8,128)(2,1)S(1)}, s32[8,128]{1,0:T(8,128)S(1)}) custom-call(s32[3]{0:T(128)S(1)} %pad_add_fusion.at, bf16[16,2,64,256]{3,2,1,0:T(8,128)(2,1)S(1)} %bitcast.10, bf16[16,2,64,256]{3,2,1,0:T(8,128)(2,1)S(1)} %bitcast.9, ...), custom_call_target="tpu_custom_call" | custom-call | bytes 1024 | tf_op jit(solution)/shard_map/split_planes/pallas_call | solution.py:64
  68.4 1.0 %collective-permute-start.8 = (bf16[16,64,256]{2,1,0:T(8,128)(2,1)}, bf16[16,64,256]{2,1,0:T(8,128)(2,1)}, u32[]{:S(2)}, u32[]{:S(2)}) collective-permute-start(bf16[16,64,256]{2,1,0:T(8,128)(2,1)} %get-tuple-element.52.refs_0_), channel_id=1, source_target_pairs={{0,32},{32,0},{1,33},{33,1},{2,34},{34,2},{3,35},{35,3},{4,36},{36... | collective-permute-start | bytes 1572872 | tf_op jit(solution)/shard_map/ppermute | solution.py:433
  69.4 0.1 collective-permute-start.9
  69.5 0.4 collective-permute-start.6
  69.9 0.1 collective-permute-start.7
  70.0 0.0 collective-permute-start.10
  70.0 4.0 %all-to-all-start.2 = ((bf16[16,64,256]{2,1,0:T(8,128)(2,1)}), bf16[16,64,256]{2,1,0:T(8,128)(2,1)S(1)}, u32[]{:S(2)}, u32[]{:S(2)}) async-start(bf16[16,64,256]{2,1,0:T(8,128)(2,1)} %get-tuple-element.49.refs_2_), calls=%async_computation.2 | async-start | bytes 1048576 | tf_op jit(solution)/shard_map/all_to_all | solution.py:451
  74.0 0.0 collective-permute-done.8.refs_1_
  74.0 0.0 collective-permute-done.9.refs_3_
  74.0 3.4 %write_rows.6 = (bf16[16,2,256,256]{3,2,1,0:T(8,128)(2,1)}, s32[8,128]{1,0:T(8,128)S(1)}) custom-call(s32[3]{0:T(128)S(1)} %pad_add_fusion.at, bf16[16,64,256]{2,1,0:T(8,128)(2,1)} %get-tuple-element.52.refs_0_, bf16[16,64,256]{2,1,0:T(8,128)(2,1)} %collective-permute-done.8.refs_1_, bf16[16,64,256]{2,1,0:T(8,128)(2,1)S(1)} %get-tuple-element.53.refs_2_, ...), custom_call_target="tpu_custom_call" | custom-call | bytes 1024 | tf_op jit(solution)/shard_map/write_rows/pallas_call | solution.py:64
  77.4 0.0 collective-permute-done.6.refs_0_
  77.4 0.0 collective-permute-done.7.refs_1_
  77.4 3.4 %write_rows.7 = (f32[256,8192]{1,0:T(8,128)}, s32[8,128]{1,0:T(8,128)S(1)}) custom-call(s32[3]{0:T(128)S(1)} %pad_add_fusion.at, bf16[16,64,256]{2,1,0:T(8,128)(2,1)S(1)} %collective-permute-done.6.refs_0_, bf16[16,64,256]{2,1,0:T(8,128)(2,1)S(1)} %collective-permute-done.7.refs_1_, ...), custom_call_target="tpu_custom_call", output_to_operand_aliasing={{0}: (5, {})} | custom-call | bytes 1024 | tf_op jit(solution)/shard_map/write_rows/pallas_call | solution.py:64
  80.8 2.3 %collective-permute-done.10.refs_1_ = bf16[16,64,256]{2,1,0:T(8,128)(2,1)S(1)} collective-permute-done((bf16[16,64,256]{2,1,0:T(8,128)(2,1)S(1)}, bf16[16,64,256]{2,1,0:T(8,128)(2,1)S(1)}, u32[]{:S(2)}, u32[]{:S(2)}) %collective-permute-start.10) | collective-permute-done | bytes 524320 | tf_op jit(solution)/shard_map/ppermute | solution.py:436
  83.1 1.2 %all-to-all-done.2.refs_0_ = bf16[16,64,256]{2,1,0:T(8,128)(2,1)S(1)} async-done(((bf16[16,64,256]{2,1,0:T(8,128)(2,1)}), bf16[16,64,256]{2,1,0:T(8,128)(2,1)S(1)}, u32[]{:S(2)}, u32[]{:S(2)}) %all-to-all-start.2) | async-done | bytes 524320 | tf_op jit(solution)/shard_map/all_to_all | solution.py:451
  84.3 2.1 %collective-permute-start.11 = (bf16[16,64,256]{2,1,0:T(8,128)(2,1)S(1)}, bf16[16,64,256]{2,1,0:T(8,128)(2,1)S(1)}, u32[]{:S(2)}, u32[]{:S(2)}) collective-permute-start(bf16[16,64,256]{2,1,0:T(8,128)(2,1)S(1)} %all-to-all-done.2.refs_0_), channel_id=1, source_target_pairs={{0,32},{32,0},{1,33},{33,1},{2,34},{34,2},{3,35},{35,3},{4,36},{36... | collective-permute-start | bytes 1572872 | tf_op jit(solution)/shard_map/ppermute | solution.py:433
  86.4 0.0 collective-permute-start.12
  86.4 1.7 %write_rows.8 = (bf16[16,2,256,256]{3,2,1,0:T(8,128)(2,1)}, s32[8,128]{1,0:T(8,128)S(1)}) custom-call(s32[3]{0:T(128)S(1)} %pad_add_fusion.at, bf16[16,64,256]{2,1,0:T(8,128)(2,1)S(1)} %all-to-all-done.2.refs_0_, bf16[16,64,256]{2,1,0:T(8,128)(2,1)S(1)} %collective-permute-done.10.refs_1_, ...), custom_call_target="tpu_custom_call", output_to_operand_aliasing={{0}: (3, {})} | custom-call | bytes 38797312 | tf_op jit(solution)/shard_map/write_rows/pallas_call | solution.py:64
  88.1 0.0 collective-permute-done.11.refs_0_
  88.1 0.6 collective-permute-done.12.refs_1_
  88.7 1.7 %write_rows.9 = (bf16[16,2,256,256]{3,2,1,0:T(8,128)(2,1)}, s32[8,128]{1,0:T(8,128)}) custom-call(s32[3]{0:T(128)S(1)} %pad_add_fusion.at, bf16[16,64,256]{2,1,0:T(8,128)(2,1)S(1)} %collective-permute-done.11.refs_0_, bf16[16,64,256]{2,1,0:T(8,128)(2,1)S(1)} %collective-permute-done.12.refs_1_, ...), custom_call_target="tpu_custom_call", output_to_operand_aliasing={{0}: (3, {})} | custom-call | bytes 1024 | tf_op jit(solution)/shard_map/write_rows/pallas_call | solution.py:64
Async XLA Ops:
  2.9 4.5 %collective-permute-start = (bf16[32,64,256]{2,1,0:T(8,128)(2,1)S(1)}, bf16[32,64,256]{2,1,0:T(8,128)(2,1)S(1)}, u32[]{:S(2)}, u32[]{:S(2)}) collective-permute-start(bf16[32,64,256]{2,1,0:T(8,128)(2,1)S(1)} %get-tuple-element.36), channel_id=1, source_target_pairs={{0,32},{32,0},{1,33},{33,1},{2,34},{34,2},{3,35},{35,3},{4,36},{36... | collective-permute-start | bytes 3145736 | tf_op jit(solution)/shard_map/ppermute | solution.py:433
  9.0 29.2 %collective-permute-start.3 = (bf16[32,64,256]{2,1,0:T(8,128)(2,1)}, bf16[32,64,256]{2,1,0:T(8,128)(2,1)S(1)}, u32[]{:S(2)}, u32[]{:S(2)}) collective-permute-start(bf16[32,64,256]{2,1,0:T(8,128)(2,1)} %get-tuple-element.43), channel_id=1, source_target_pairs={{0,64},{64,0},{1,65},{65,1},{2,66},{66,2},{3,67},{67,3},{4,68},{68... | collective-permute-start | bytes 3145736 | tf_op jit(solution)/shard_map/ppermute | solution.py:436
  10.4 27.9 %all-to-all-start = ((bf16[32,64,256]{2,1,0:T(8,128)(2,1)}), bf16[32,64,256]{2,1,0:T(8,128)(2,1)S(1)}, u32[]{:S(2)}, u32[]{:S(2)}) async-start(bf16[32,64,256]{2,1,0:T(8,128)(2,1)} %bitcast.17), calls=%async_computation | async-start | bytes 2097152 | tf_op jit(solution)/shard_map/all_to_all | solution.py:428
  22.1 2.2 %collective-permute-start.1 = (bf16[32,32,256]{2,1,0:T(8,128)(2,1)S(1)}, bf16[32,32,256]{2,1,0:T(8,128)(2,1)S(1)}, u32[]{:S(2)}, u32[]{:S(2)}) collective-permute-start(bf16[32,32,256]{2,1,0:T(8,128)(2,1)S(1)} %get-tuple-element.39), channel_id=1, source_target_pairs={{0,32},{32,0},{1,33},{33,1},{2,34},{34,2},{3,35},{35,3},{4,36},{36... | collective-permute-start | bytes 1572872 | tf_op jit(solution)/shard_map/ppermute | solution.py:433
  22.8 2.3 %collective-permute-start.2 = (bf16[32,32,256]{2,1,0:T(8,128)(2,1)S(1)}, bf16[32,32,256]{2,1,0:T(8,128)(2,1)S(1)}, u32[]{:S(2)}, u32[]{:S(2)}) collective-permute-start(bf16[32,32,256]{2,1,0:T(8,128)(2,1)S(1)} %get-tuple-element.40), channel_id=1, source_target_pairs={{0,32},{32,0},{1,33},{33,1},{2,34},{34,2},{3,35},{35,3},{4,36},{36... | collective-permute-start | bytes 1572872 | tf_op jit(solution)/shard_map/ppermute | solution.py:433
  40.1 7.6 %collective-permute-start.5 = (bf16[32,64,256]{2,1,0:T(8,128)(2,1)}, bf16[32,64,256]{2,1,0:T(8,128)(2,1)S(1)}, u32[]{:S(2)}, u32[]{:S(2)}) collective-permute-start(bf16[32,64,256]{2,1,0:T(8,128)(2,1)} %get-tuple-element.46.refs_1_), channel_id=1, source_target_pairs={{0,32},{32,0},{1,33},{33,1},{2,34},{34,2},{3,35},{35,3},{4,36},{36... | collective-permute-start | bytes 3145736 | tf_op jit(solution)/shard_map/ppermute | solution.py:433
  41.9 24.9 %collective-permute-start.4 = (bf16[32,64,256]{2,1,0:T(8,128)(2,1)}, bf16[32,64,256]{2,1,0:T(8,128)(2,1)S(1)}, u32[]{:S(2)}, u32[]{:S(2)}) collective-permute-start(bf16[32,64,256]{2,1,0:T(8,128)(2,1)} %get-tuple-element.46.refs_1_), channel_id=1, source_target_pairs={{0,64},{64,0},{1,65},{65,1},{2,66},{66,2},{3,67},{67,3},{4,68},{68... | collective-permute-start | bytes 3145736 | tf_op jit(solution)/shard_map/ppermute | solution.py:436
  41.9 24.0 %all-to-all-start.1 = ((bf16[32,64,256]{2,1,0:T(8,128)(2,1)}), bf16[32,64,256]{2,1,0:T(8,128)(2,1)S(1)}, u32[]{:S(2)}, u32[]{:S(2)}) async-start(bf16[32,64,256]{2,1,0:T(8,128)(2,1)} %get-tuple-element.46.refs_1_), calls=%async_computation.1 | async-start | bytes 2097152 | tf_op jit(solution)/shard_map/all_to_all | solution.py:428
  68.4 5.5 %collective-permute-start.8 = (bf16[16,64,256]{2,1,0:T(8,128)(2,1)}, bf16[16,64,256]{2,1,0:T(8,128)(2,1)}, u32[]{:S(2)}, u32[]{:S(2)}) collective-permute-start(bf16[16,64,256]{2,1,0:T(8,128)(2,1)} %get-tuple-element.52.refs_0_), channel_id=1, source_target_pairs={{0,32},{32,0},{1,33},{33,1},{2,34},{34,2},{3,35},{35,3},{4,36},{36... | collective-permute-start | bytes 1572872 | tf_op jit(solution)/shard_map/ppermute | solution.py:433
  69.4 4.6 %collective-permute-start.9 = (bf16[16,64,256]{2,1,0:T(8,128)(2,1)S(1)}, bf16[16,64,256]{2,1,0:T(8,128)(2,1)}, u32[]{:S(2)}, u32[]{:S(2)}) collective-permute-start(bf16[16,64,256]{2,1,0:T(8,128)(2,1)S(1)} %get-tuple-element.53.refs_2_), channel_id=1, source_target_pairs={{0,32},{32,0},{1,33},{33,1},{2,34},{34,2},{3,35},{35,3},{4,36},{36... | collective-permute-start | bytes 1572872 | tf_op jit(solution)/shard_map/ppermute | solution.py:433
  69.5 7.9 %collective-permute-start.6 = (bf16[16,64,256]{2,1,0:T(8,128)(2,1)}, bf16[16,64,256]{2,1,0:T(8,128)(2,1)S(1)}, u32[]{:S(2)}, u32[]{:S(2)}) collective-permute-start(bf16[16,64,256]{2,1,0:T(8,128)(2,1)} %get-tuple-element.49.refs_2_), channel_id=1, source_target_pairs={{0,32},{32,0},{1,33},{33,1},{2,34},{34,2},{3,35},{35,3},{4,36},{36... | collective-permute-start | bytes 1572872 | tf_op jit(solution)/shard_map/ppermute | solution.py:433
  69.9 7.5 %collective-permute-start.7 = (bf16[16,64,256]{2,1,0:T(8,128)(2,1)S(1)}, bf16[16,64,256]{2,1,0:T(8,128)(2,1)S(1)}, u32[]{:S(2)}, u32[]{:S(2)}) collective-permute-start(bf16[16,64,256]{2,1,0:T(8,128)(2,1)S(1)} %get-tuple-element.50.refs_3_), channel_id=1, source_target_pairs={{0,32},{32,0},{1,33},{33,1},{2,34},{34,2},{3,35},{35,3},{4,36},{36... | collective-permute-start | bytes 1572872 | tf_op jit(solution)/shard_map/ppermute | solution.py:433
  70.0 13.1 %collective-permute-start.10 = (bf16[16,64,256]{2,1,0:T(8,128)(2,1)S(1)}, bf16[16,64,256]{2,1,0:T(8,128)(2,1)S(1)}, u32[]{:S(2)}, u32[]{:S(2)}) collective-permute-start(bf16[16,64,256]{2,1,0:T(8,128)(2,1)S(1)} %get-tuple-element.53.refs_2_), channel_id=1, source_target_pairs={{0,64},{64,0},{1,65},{65,1},{2,66},{66,2},{3,67},{67,3},{4,68},{68... | collective-permute-start | bytes 1572872 | tf_op jit(solution)/shard_map/ppermute | solution.py:436
  70.0 14.3 %all-to-all-start.2 = ((bf16[16,64,256]{2,1,0:T(8,128)(2,1)}), bf16[16,64,256]{2,1,0:T(8,128)(2,1)S(1)}, u32[]{:S(2)}, u32[]{:S(2)}) async-start(bf16[16,64,256]{2,1,0:T(8,128)(2,1)} %get-tuple-element.49.refs_2_), calls=%async_computation.2 | async-start | bytes 1048576 | tf_op jit(solution)/shard_map/all_to_all | solution.py:451
  84.3 3.8 %collective-permute-start.11 = (bf16[16,64,256]{2,1,0:T(8,128)(2,1)S(1)}, bf16[16,64,256]{2,1,0:T(8,128)(2,1)S(1)}, u32[]{:S(2)}, u32[]{:S(2)}) collective-permute-start(bf16[16,64,256]{2,1,0:T(8,128)(2,1)S(1)} %all-to-all-done.2.refs_0_), channel_id=1, source_target_pairs={{0,32},{32,0},{1,33},{33,1},{2,34},{34,2},{3,35},{35,3},{4,36},{36... | collective-permute-start | bytes 1572872 | tf_op jit(solution)/shard_map/ppermute | solution.py:433
  86.4 2.3 %collective-permute-start.12 = (bf16[16,64,256]{2,1,0:T(8,128)(2,1)S(1)}, bf16[16,64,256]{2,1,0:T(8,128)(2,1)S(1)}, u32[]{:S(2)}, u32[]{:S(2)}) collective-permute-start(bf16[16,64,256]{2,1,0:T(8,128)(2,1)S(1)} %collective-permute-done.10.refs_1_), channel_id=1, source_target_pairs={{0,32},{32,0},{1,33},{33,1},{2,34},{34,2},{3,35},{35,3},{4,36},{36... | collective-permute-start | bytes 1572872 | tf_op jit(solution)/shard_map/ppermute | solution.py:433

commit v7 on v6

--- a/solution.py
+++ b/solution.py
@@ -303,30 +303,17 @@
 
 
 def split_planes(order, finished, back):
-    def body(at, f_ref, b_ref, first_ref, low_ref, second_ref, high_ref, sems):
-        def stores(p):
+    def body(at, f_ref, b_ref, first_ref, high_ref, sems):
+        def store(p):
             some = pl.ds(4 * p, 4)
-            ends = ((f_ref, first_ref), (b_ref, low_ref))
-            return [
-                pltpu.make_async_copy(x.at[some, plane(at, True)], o.at[some], sems.at[i, p])
-                for i, (x, o) in enumerate(ends)
-            ]
-
-        def start(p):
-            for store in stores(p):
-                store.start()
+            return pltpu.make_async_copy(f_ref.at[some, plane(at, True)], first_ref.at[some], sems.at[p])
 
         def work(k):
             high_ref[k] = b_ref[k, plane(at, False)]
-            second_ref[k] = f_ref[k, plane(at, False)]
-
-        def finish(p):
-            for store in stores(p):
-                store.wait()
-
-        each(4, start)
+
+        each(4, lambda p: store(p).start())
         each(16, work)
-        each(4, finish)
+        each(4, lambda p: store(p).wait())
 
     half = (16, QUARTER, WIDTH)
     return order.run(
@@ -334,13 +321,59 @@
         "split_planes",
         [in_vmem(x.reshape(16, 2, QUARTER, WIDTH)) for x in (finished, back)],
         [VMEM, VMEM],
-        [pltpu.HBM(half, BF), jax.ShapeDtypeStruct(half, BF), pltpu.VMEM(half, BF), pltpu.VMEM(half, BF)],
-        [HBM, ANY, VMEM, VMEM],
-        [pltpu.SemaphoreType.DMA((2, 4))],
-    )
-
-
-def write_rows(order, wide_pieces, placed_pieces, blended, anchor, size=1024):
+        [pltpu.HBM(half, BF), pltpu.VMEM(half, BF)],
+        [HBM, VMEM],
+        [pltpu.SemaphoreType.DMA((4,))],
+    )
+
+
+def place_back(order, own, other):
+    def body(at, own_ref, other_ref, out_ref, held, sems, held_sems):
+        def there(core, same, p):
+            row = first_row(at, core, same, 0)
+            return out_ref.at[pl.ds(4 * p, 4), plane(at, same), pl.ds(row, QUARTER), :]
+
+        def place(ref, core, same, p):
+            return pltpu.make_async_copy(
+                ref.at[pl.ds(4 * p, 4), plane(at, same)],
+                there(core, same, p),
+                sems.at[int(core), int(same), p],
+            )
+
+        def fetch(p):
+            some = pl.ds(4 * p, 4)
+            return pltpu.make_async_copy(other_ref.at[some], held.at[some], held_sems.at[p])
+
+        def forward(p):
+            fetch(p).wait()
+            for same in (True, False):
+                place(held, False, same, p).start()
+
+        each(4, lambda p: fetch(p).start())
+        for same in (True, False):
+            each(4, lambda p, same=same: place(own_ref, True, same, p).start())
+        each(4, forward)
+        for ref, core in ((own_ref, True), (held, False)):
+            for same in (True, False):
+                each(4, lambda p, ref=ref, core=core, same=same: place(ref, core, same, p).wait())
+
+    shape = (16, 2, QUARTER, WIDTH)
+    return order.run(
+        body,
+        "place_back",
+        [in_vmem(own.reshape(shape)), other.reshape(shape)],
+        [VMEM, ANY],
+        [pltpu.HBM((16, 2, ROWS, WIDTH), BF)],
+        [HBM],
+        [
+            pltpu.VMEM(shape, BF),
+            pltpu.SemaphoreType.DMA((2, 2, 4)),
+            pltpu.SemaphoreType.DMA((4,)),
+        ],
+    )[0]
+
+
+def write_rows(order, wide_pieces, placed_pieces, blended, anchor, size=1024, late_in_hbm=False):
     n, m = len(wide_pieces), len(placed_pieces)
     counts = [len(arrays) for arrays, _, _ in wide_pieces]
     flat = [x for arrays, _, _ in wide_pieces for x in arrays]
@@ -395,9 +428,11 @@
         for i in range(m):
             each(4, lambda p, i=i: place(i, p).wait())
 
-    in_hbm = lambda x: pltpu.with_memory_space_constraint(x, pltpu.HBM)
-    args = [in_hbm(x) if i == late else in_vmem(x) for i, x in enumerate(flat)]
-    specs = [HBM if i == late else VMEM for i in range(len(flat))]
+    args = [x if i == late else in_vmem(x) for i, x in enumerate(flat)]
+    specs = [ANY if i == late else VMEM for i in range(len(flat))]
+    if late_in_hbm:
+        args[late] = pltpu.with_memory_space_constraint(args[late], pltpu.HBM)
+        specs[late] = HBM
     return order.run(
         body,
         "write_rows",
@@ -445,19 +480,14 @@
     finished = chip(own)
     back = exchange(own)
     pieces = [([core(own)], False, True), ([own], True, True)]
-    (blended,) = write_rows(order, pieces, [], None, None, WRITE_COST)
-
-    first, low, second, high = split_planes(order, finished, back)
+    (blended,) = write_rows(order, pieces, [], None, None, WRITE_COST, late_in_hbm=True)
+
+    first, high = split_planes(order, finished, back)
     back_first = lax.all_to_all(first, ("y", "z"), split_axis=0, concat_axis=0, tiled=True)
     back_second = chip(high)
-    pieces = [
-        (low, True, True, True),
-        (core(low), False, True, True),
-        (high, True, False, False),
-        (core(high), False, False, False),
-    ]
-    (new_anchor,) = write_rows(order, [], pieces, None, None)
-    pieces = [([core(first), core(second)], False, False), ([first, second], True, False)]
+    finished, back = order.behind(finished), order.behind(back)
+    new_anchor = place_back(order, back, core(back))
+    pieces = [([finished], True, False), ([core(finished)], False, False)]
     (blended,) = write_rows(order, pieces, [], blended, None)
     back_second = order.behind(back_second)
     back_first = order.behind(back_first)

time: 91 us -> 91.1 us (level)
    ppermute x10 -> x8, starting transfers between devices: 7.77 us -> 7.26 us  [core(): return lax.ppermute(tiles, 'c', swap)]
    ppermute x10 -> x8, waiting for transfers between devices: 2.83 us -> 2.82 us  [core(): return lax.ppermute(tiles, 'c', swap)]
  transfers between devices with their start and end apart: 16 -> 14, of which waited for: 8 -> 8; matrix products, arithmetic and copies ran while one was open for 0% -> 0% of each run, Pallas kernels for 22% -> 22%
where the time goes in v7:
time: 91.1 us; the launch traced here: 90.4 us
  waiting for transfers between devices  32.3 us (35%)
  Pallas kernels  29.3 us (32%)
  starting transfers between devices  28 us (31%)
    pallas_call x12, Pallas kernels, run(): pl.pallas_call(ordered, out_shape=[*outs, TOKEN], grid_spec=pltpu.Prefetc...  29.3 us
    all_to_all x2, waiting for transfers between devices, exchange(): lax.all_to_all(tiles, AXES, split_axis=0, concat_axis=0, axis_index_group...  25.2 us
    all_to_all x2, starting transfers between devices, exchange(): lax.all_to_all(tiles, AXES, split_axis=0, concat_axis=0, axis_index_group...  15.4 us
    ppermute x8, starting transfers between devices, core(): return lax.ppermute(tiles, 'c', swap)  7.26 us
    all_to_all x1, starting transfers between devices, per_device(): lax.all_to_all(first, ('y', 'z'), split_axis=0, concat_axis=0, tiled=True)  3.95 us
    ppermute x3, waiting for transfers between devices, chip(): return lax.ppermute(tiles, 'xl', swap)  3.29 us
    ppermute x8, waiting for transfers between devices, core(): return lax.ppermute(tiles, 'c', swap)  2.82 us
  transfers between devices with their start and end apart: 14, of which 8 were waited for; matrix products, arithmetic and copies ran while one was open for 0% of the time, Pallas kernels for 22%

profile of v7, /device:TPU:1, one launch (start us, length us, event | category | flops | bytes accessed | tf_op | source)
XLA Modules:
  0.0 90.4 jit_solution(818257071287905676)
XLA Ops:
  0.6 0.1 pad_add_fusion.at
  0.7 2.2 %cast_rows.1 = (bf16[32,64,256]{2,1,0:T(8,128)(2,1)S(1)}, s32[8,128]{1,0:T(8,128)S(1)}) custom-call(s32[3]{0:T(128)S(1)} %pad_add_fusion.at, f32[256,8192]{1,0:T(8,128)} %bitcast.14), custom_call_target="tpu_custom_call" | custom-call | bytes 1024 | tf_op jit(solution)/shard_map/cast_rows/pallas_call | solution.py:64
  2.9 1.5 %collective-permute-start = (bf16[32,64,256]{2,1,0:T(8,128)(2,1)S(1)}, bf16[32,64,256]{2,1,0:T(8,128)(2,1)S(1)}, u32[]{:S(2)}, u32[]{:S(2)}) collective-permute-start(bf16[32,64,256]{2,1,0:T(8,128)(2,1)S(1)} %get-tuple-element.38), channel_id=1, source_target_pairs={{0,32},{32,0},{1,33},{33,1},{2,34},{34,2},{3,35},{35,3},{4,36},{36... | collective-permute-start | bytes 3145736 | tf_op jit(solution)/shard_map/ppermute | solution.py:468
  4.4 3.0 %pick_rows.1 = (bf16[16,2,64,256]{3,2,1,0:T(8,128)(2,1)}, f32[64,8192]{1,0:T(8,128)S(1)}, s32[8,128]{1,0:T(8,128)S(1)}) custom-call(s32[3]{0:T(128)S(1)} %pad_add_fusion.at, bf16[16,2,256,256]{3,2,1,0:T(8,128)(2,1)} %bitcast.19, f32[256,8192]{1,0:T(8,128)} %bitcast.15, s32[8,128]{1,0:T(8,128)S(1)} %get-tuple-element.36.refs_2_), custom_call_target="tpu_custom_call" | custom-call | bytes 1024 | tf_op jit(solution)/shard_map/pick_rows/pallas_call | solution.py:64
  7.4 0.0 collective-permute-done.refs_1_
  7.4 1.6 %add_theirs.1 = (bf16[32,64,256]{2,1,0:T(8,128)(2,1)}, s32[8,128]{1,0:T(8,128)S(1)}) custom-call(s32[3]{0:T(128)S(1)} %pad_add_fusion.at, f32[64,8192]{1,0:T(8,128)S(1)} %get-tuple-element.37.refs_0_, bf16[32,64,256]{2,1,0:T(8,128)(2,1)S(1)} %collective-permute-done.refs_1_, s32[8,128]{1,0:T(8,128)S(1)} %get-tuple-element.39.refs_2_), custom_call_target="tpu_custom_call" | custom-call | bytes 1024 | tf_op jit(solution)/shard_map/add_theirs/pallas_call | solution.py:64
  9.0 1.4 %collective-permute-start.3 = (bf16[32,64,256]{2,1,0:T(8,128)(2,1)}, bf16[32,64,256]{2,1,0:T(8,128)(2,1)S(1)}, u32[]{:S(2)}, u32[]{:S(2)}) collective-permute-start(bf16[32,64,256]{2,1,0:T(8,128)(2,1)} %get-tuple-element.45), channel_id=1, source_target_pairs={{0,64},{64,0},{1,65},{65,1},{2,66},{66,2},{3,67},{67,3},{4,68},{68... | collective-permute-start | bytes 3145736 | tf_op jit(solution)/shard_map/ppermute | solution.py:471
  10.4 9.6 %all-to-all-start = ((bf16[32,64,256]{2,1,0:T(8,128)(2,1)}), bf16[32,64,256]{2,1,0:T(8,128)(2,1)S(1)}, u32[]{:S(2)}, u32[]{:S(2)}) async-start(bf16[32,64,256]{2,1,0:T(8,128)(2,1)} %bitcast.20), calls=%async_computation | async-start | bytes 2097152 | tf_op jit(solution)/shard_map/all_to_all | solution.py:463
  20.0 2.2 %cast_own.1 = (bf16[32,32,256]{2,1,0:T(8,128)(2,1)S(1)}, bf16[32,32,256]{2,1,0:T(8,128)(2,1)S(1)}, s32[8,128]{1,0:T(8,128)S(1)}) custom-call(s32[3]{0:T(128)S(1)} %pad_add_fusion.at, f32[256,8192]{1,0:T(8,128)} %bitcast.16, s32[8,128]{1,0:T(8,128)S(1)} %get-tuple-element.40.refs_1_), custom_call_target="tpu_custom_call" | custom-call | bytes 1024 | tf_op jit(solution)/shard_map/cast_own/pallas_call | solution.py:64
  22.1 0.7 collective-permute-start.1
  22.8 0.1 collective-permute-start.2
  22.9 1.4 %collective-permute-done.1.refs_1_ = bf16[32,32,256]{2,1,0:T(8,128)(2,1)S(1)} collective-permute-done((bf16[32,32,256]{2,1,0:T(8,128)(2,1)S(1)}, bf16[32,32,256]{2,1,0:T(8,128)(2,1)S(1)}, u32[]{:S(2)}, u32[]{:S(2)}) %collective-permute-start.1) | collective-permute-done | bytes 524320 | tf_op jit(solution)/shard_map/ppermute | solution.py:468
  24.3 0.7 collective-permute-done.2.refs_2_
  25.1 2.2 %add_own.1 = (bf16[32,64,256]{2,1,0:T(8,128)(2,1)S(1)}, s32[8,128]{1,0:T(8,128)S(1)}) custom-call(s32[3]{0:T(128)S(1)} %pad_add_fusion.at, f32[256,8192]{1,0:T(8,128)} %bitcast.17, bf16[32,32,256]{2,1,0:T(8,128)(2,1)S(1)} %collective-permute-done.1.refs_1_, bf16[32,32,256]{2,1,0:T(8,128)(2,1)S(1)} %collective-permute-done.2.refs_2_, ...), custom_call_target="tpu_custom_call" | custom-call | bytes 1024 | tf_op jit(solution)/shard_map/add_own/pallas_call | solution.py:64
  27.3 11.0 %all-to-all-done.refs_2_ = bf16[32,64,256]{2,1,0:T(8,128)(2,1)S(1)} async-done(((bf16[32,64,256]{2,1,0:T(8,128)(2,1)}), bf16[32,64,256]{2,1,0:T(8,128)(2,1)S(1)}, u32[]{:S(2)}, u32[]{:S(2)}) %all-to-all-start) | async-done | bytes 1048608 | tf_op jit(solution)/shard_map/all_to_all | solution.py:463
  38.2 0.0 collective-permute-done.3.refs_1_
  38.2 1.8 %blend_rows.1 = (bf16[32,64,256]{2,1,0:T(8,128)(2,1)}, s32[8,128]{1,0:T(8,128)S(1)}) custom-call(s32[3]{0:T(128)S(1)} %pad_add_fusion.at, bf16[32,64,256]{2,1,0:T(8,128)(2,1)S(1)} %get-tuple-element.44.refs_0_, bf16[32,64,256]{2,1,0:T(8,128)(2,1)S(1)} %collective-permute-done.3.refs_1_, bf16[32,64,256]{2,1,0:T(8,128)(2,1)S(1)} %all-to-all-done.refs_2_, ...), custom_call_target="tpu_custom_call" | custom-call | bytes 1024 | tf_op jit(solution)/shard_map/blend_rows/pallas_call | solution.py:64
  40.1 1.8 %collective-permute-start.5 = (bf16[32,64,256]{2,1,0:T(8,128)(2,1)}, bf16[32,64,256]{2,1,0:T(8,128)(2,1)S(1)}, u32[]{:S(2)}, u32[]{:S(2)}) collective-permute-start(bf16[32,64,256]{2,1,0:T(8,128)(2,1)} %get-tuple-element.48.refs_1_), channel_id=1, source_target_pairs={{0,32},{32,0},{1,33},{33,1},{2,34},{34,2},{3,35},{35,3},{4,36},{36... | collective-permute-start | bytes 3145736 | tf_op jit(solution)/shard_map/ppermute | solution.py:468
  41.9 0.0 collective-permute-start.4
  41.9 5.8 %all-to-all-start.1 = ((bf16[32,64,256]{2,1,0:T(8,128)(2,1)}), bf16[32,64,256]{2,1,0:T(8,128)(2,1)S(1)}, u32[]{:S(2)}, u32[]{:S(2)}) async-start(bf16[32,64,256]{2,1,0:T(8,128)(2,1)} %get-tuple-element.48.refs_1_), calls=%async_computation.1 | async-start | bytes 2097152 | tf_op jit(solution)/shard_map/all_to_all | solution.py:463
  47.7 0.0 collective-permute-done.5.refs_0_
  47.7 4.0 %write_rows.4 = (f32[256,8192]{1,0:T(8,128)}, s32[8,128]{1,0:T(8,128)S(1)}) custom-call(s32[3]{0:T(128)S(1)} %pad_add_fusion.at, bf16[32,64,256]{2,1,0:T(8,128)(2,1)S(1)} %collective-permute-done.5.refs_0_, bf16[32,64,256]{2,1,0:T(8,128)(2,1)} %get-tuple-element.48.refs_1_, s32[8,128]{1,0:T(8,128)S(1)} %get-tuple-element.49.refs_2_), custom_call_target="tpu_custom_call" | custom-call | bytes 11534336 | tf_op jit(solution)/shard_map/write_rows/pallas_call | solution.py:64
  51.7 14.2 %all-to-all-done.1 = bf16[32,64,256]{2,1,0:T(8,128)(2,1)S(1)} async-done(((bf16[32,64,256]{2,1,0:T(8,128)(2,1)}), bf16[32,64,256]{2,1,0:T(8,128)(2,1)S(1)}, u32[]{:S(2)}, u32[]{:S(2)}) %all-to-all-start.1) | async-done | bytes 1048608 | tf_op jit(solution)/shard_map/all_to_all | solution.py:463
  65.9 0.9 %collective-permute-done.4.refs_0_ = bf16[32,64,256]{2,1,0:T(8,128)(2,1)S(1)} collective-permute-done((bf16[32,64,256]{2,1,0:T(8,128)(2,1)}, bf16[32,64,256]{2,1,0:T(8,128)(2,1)S(1)}, u32[]{:S(2)}, u32[]{:S(2)}) %collective-permute-start.4) | collective-permute-done | bytes 1048608 | tf_op jit(solution)/shard_map/ppermute | solution.py:471
  66.8 2.2 %split_planes.1 = (bf16[16,64,256]{2,1,0:T(8,128)(2,1)}, bf16[16,64,256]{2,1,0:T(8,128)(2,1)}, s32[8,128]{1,0:T(8,128)S(1)}) custom-call(s32[3]{0:T(128)S(1)} %pad_add_fusion.at, bf16[16,2,64,256]{3,2,1,0:T(8,128)(2,1)S(1)} %bitcast.13, bf16[16,2,64,256]{3,2,1,0:T(8,128)(2,1)S(1)} %bitcast.11, s32[8,128]{1,0:T(8,128)S(1)} %get-tuple-element.50.refs_2_), custom_call_target="tpu_custom_call" | custom-call | bytes 1024 | tf_op jit(solution)/shard_map/split_planes/pallas_call | solution.py:64
  69.0 1.0 %collective-permute-start.7 = (bf16[32,64,256]{2,1,0:T(8,128)(2,1)S(1)}, bf16[32,64,256]{2,1,0:T(8,128)(2,1)}, u32[]{:S(2)}, u32[]{:S(2)}) collective-permute-start(bf16[32,64,256]{2,1,0:T(8,128)(2,1)S(1)} %all-to-all-done.1), channel_id=1, source_target_pairs={{0,32},{32,0},{1,33},{33,1},{2,34},{34,2},{3,35},{35,3},{4,36},{36... | collective-permute-start | bytes 3145736 | tf_op jit(solution)/shard_map/ppermute | solution.py:468
  70.0 0.1 collective-permute-start.6
  70.1 0.0 collective-permute-start.8
  70.1 4.0 %all-to-all-start.2 = ((bf16[16,64,256]{2,1,0:T(8,128)(2,1)}), bf16[16,64,256]{2,1,0:T(8,128)(2,1)S(1)}, u32[]{:S(2)}, u32[]{:S(2)}) async-start(bf16[16,64,256]{2,1,0:T(8,128)(2,1)} %get-tuple-element.59), calls=%async_computation.2 | async-start | bytes 1048576 | tf_op jit(solution)/shard_map/all_to_all | solution.py:486
  74.0 0.0 collective-permute-done.7
  74.0 3.0 %place_back.1 = (bf16[16,2,256,256]{3,2,1,0:T(8,128)(2,1)}, s32[8,128]{1,0:T(8,128)S(1)}) custom-call(s32[3]{0:T(128)S(1)} %pad_add_fusion.at, bf16[16,2,64,256]{3,2,1,0:T(8,128)(2,1)S(1)} %bitcast.12, bf16[16,2,64,256]{3,2,1,0:T(8,128)(2,1)} %bitcast.9.refs_1_, s32[8,128]{1,0:T(8,128)S(1)} %get-tuple-element.56.refs_2_), custom_call_target="tpu_custom_call" | custom-call | bytes 1024 | tf_op jit(solution)/shard_map/place_back/pallas_call | solution.py:64
  77.0 0.0 collective-permute-done.6.refs_1_
  77.0 4.0 %write_rows.5 = (f32[256,8192]{1,0:T(8,128)}, s32[8,128]{1,0:T(8,128)S(1)}) custom-call(s32[3]{0:T(128)S(1)} %pad_add_fusion.at, bf16[32,64,256]{2,1,0:T(8,128)(2,1)S(1)} %collective-permute-done.4.refs_0_, bf16[32,64,256]{2,1,0:T(8,128)(2,1)} %collective-permute-done.6.refs_1_, ...), custom_call_target="tpu_custom_call", output_to_operand_aliasing={{0}: (3, {})} | custom-call | bytes 1024 | tf_op jit(solution)/shard_map/write_rows/pallas_call | solution.py:64
  81.0 2.3 %collective-permute-done.8.refs_1_ = bf16[16,64,256]{2,1,0:T(8,128)(2,1)S(1)} collective-permute-done((bf16[16,64,256]{2,1,0:T(8,128)(2,1)}, bf16[16,64,256]{2,1,0:T(8,128)(2,1)S(1)}, u32[]{:S(2)}, u32[]{:S(2)}) %collective-permute-start.8) | collective-permute-done | bytes 524320 | tf_op jit(solution)/shard_map/ppermute | solution.py:471
  83.4 1.0 %all-to-all-done.2.refs_0_ = bf16[16,64,256]{2,1,0:T(8,128)(2,1)S(1)} async-done(((bf16[16,64,256]{2,1,0:T(8,128)(2,1)}), bf16[16,64,256]{2,1,0:T(8,128)(2,1)S(1)}, u32[]{:S(2)}, u32[]{:S(2)}) %all-to-all-start.2) | async-done | bytes 524320 | tf_op jit(solution)/shard_map/all_to_all | solution.py:486
  84.3 2.1 %collective-permute-start.9 = (bf16[16,64,256]{2,1,0:T(8,128)(2,1)S(1)}, bf16[16,64,256]{2,1,0:T(8,128)(2,1)S(1)}, u32[]{:S(2)}, u32[]{:S(2)}) collective-permute-start(bf16[16,64,256]{2,1,0:T(8,128)(2,1)S(1)} %all-to-all-done.2.refs_0_), channel_id=1, source_target_pairs={{0,32},{32,0},{1,33},{33,1},{2,34},{34,2},{3,35},{35,3},{4,36},{36... | collective-permute-start | bytes 1572872 | tf_op jit(solution)/shard_map/ppermute | solution.py:468
  86.5 0.0 collective-permute-start.10
  86.5 1.7 %write_rows.6 = (bf16[16,2,256,256]{3,2,1,0:T(8,128)(2,1)}, s32[8,128]{1,0:T(8,128)S(1)}) custom-call(s32[3]{0:T(128)S(1)} %pad_add_fusion.at, bf16[16,64,256]{2,1,0:T(8,128)(2,1)S(1)} %all-to-all-done.2.refs_0_, bf16[16,64,256]{2,1,0:T(8,128)(2,1)S(1)} %collective-permute-done.8.refs_1_, ...), custom_call_target="tpu_custom_call", output_to_operand_aliasing={{0}: (3, {})} | custom-call | bytes 38797312 | tf_op jit(solution)/shard_map/write_rows/pallas_call | solution.py:64
  88.1 0.0 collective-permute-done.9.refs_0_
  88.1 0.6 collective-permute-done.10.refs_1_
  88.8 1.7 %write_rows.7 = (bf16[16,2,256,256]{3,2,1,0:T(8,128)(2,1)}, s32[8,128]{1,0:T(8,128)}) custom-call(s32[3]{0:T(128)S(1)} %pad_add_fusion.at, bf16[16,64,256]{2,1,0:T(8,128)(2,1)S(1)} %collective-permute-done.9.refs_0_, bf16[16,64,256]{2,1,0:T(8,128)(2,1)S(1)} %collective-permute-done.10.refs_1_, ...), custom_call_target="tpu_custom_call", output_to_operand_aliasing={{0}: (3, {})} | custom-call | bytes 1024 | tf_op jit(solution)/shard_map/write_rows/pallas_call | solution.py:64
Async XLA Ops:
  2.9 4.5 %collective-permute-start = (bf16[32,64,256]{2,1,0:T(8,128)(2,1)S(1)}, bf16[32,64,256]{2,1,0:T(8,128)(2,1)S(1)}, u32[]{:S(2)}, u32[]{:S(2)}) collective-permute-start(bf16[32,64,256]{2,1,0:T(8,128)(2,1)S(1)} %get-tuple-element.38), channel_id=1, source_target_pairs={{0,32},{32,0},{1,33},{33,1},{2,34},{34,2},{3,35},{35,3},{4,36},{36... | collective-permute-start | bytes 3145736 | tf_op jit(solution)/shard_map/ppermute | solution.py:468
  9.0 29.2 %collective-permute-start.3 = (bf16[32,64,256]{2,1,0:T(8,128)(2,1)}, bf16[32,64,256]{2,1,0:T(8,128)(2,1)S(1)}, u32[]{:S(2)}, u32[]{:S(2)}) collective-permute-start(bf16[32,64,256]{2,1,0:T(8,128)(2,1)} %get-tuple-element.45), channel_id=1, source_target_pairs={{0,64},{64,0},{1,65},{65,1},{2,66},{66,2},{3,67},{67,3},{4,68},{68... | collective-permute-start | bytes 3145736 | tf_op jit(solution)/shard_map/ppermute | solution.py:471
  10.4 27.9 %all-to-all-start = ((bf16[32,64,256]{2,1,0:T(8,128)(2,1)}), bf16[32,64,256]{2,1,0:T(8,128)(2,1)S(1)}, u32[]{:S(2)}, u32[]{:S(2)}) async-start(bf16[32,64,256]{2,1,0:T(8,128)(2,1)} %bitcast.20), calls=%async_computation | async-start | bytes 2097152 | tf_op jit(solution)/shard_map/all_to_all | solution.py:463
  22.1 2.2 %collective-permute-start.1 = (bf16[32,32,256]{2,1,0:T(8,128)(2,1)S(1)}, bf16[32,32,256]{2,1,0:T(8,128)(2,1)S(1)}, u32[]{:S(2)}, u32[]{:S(2)}) collective-permute-start(bf16[32,32,256]{2,1,0:T(8,128)(2,1)S(1)} %get-tuple-element.41), channel_id=1, source_target_pairs={{0,32},{32,0},{1,33},{33,1},{2,34},{34,2},{3,35},{35,3},{4,36},{36... | collective-permute-start | bytes 1572872 | tf_op jit(solution)/shard_map/ppermute | solution.py:468
  22.8 2.3 %collective-permute-start.2 = (bf16[32,32,256]{2,1,0:T(8,128)(2,1)S(1)}, bf16[32,32,256]{2,1,0:T(8,128)(2,1)S(1)}, u32[]{:S(2)}, u32[]{:S(2)}) collective-permute-start(bf16[32,32,256]{2,1,0:T(8,128)(2,1)S(1)} %get-tuple-element.42), channel_id=1, source_target_pairs={{0,32},{32,0},{1,33},{33,1},{2,34},{34,2},{3,35},{35,3},{4,36},{36... | collective-permute-start | bytes 1572872 | tf_op jit(solution)/shard_map/ppermute | solution.py:468
  40.1 7.6 %collective-permute-start.5 = (bf16[32,64,256]{2,1,0:T(8,128)(2,1)}, bf16[32,64,256]{2,1,0:T(8,128)(2,1)S(1)}, u32[]{:S(2)}, u32[]{:S(2)}) collective-permute-start(bf16[32,64,256]{2,1,0:T(8,128)(2,1)} %get-tuple-element.48.refs_1_), channel_id=1, source_target_pairs={{0,32},{32,0},{1,33},{33,1},{2,34},{34,2},{3,35},{35,3},{4,36},{36... | collective-permute-start | bytes 3145736 | tf_op jit(solution)/shard_map/ppermute | solution.py:468
  41.9 24.9 %collective-permute-start.4 = (bf16[32,64,256]{2,1,0:T(8,128)(2,1)}, bf16[32,64,256]{2,1,0:T(8,128)(2,1)S(1)}, u32[]{:S(2)}, u32[]{:S(2)}) collective-permute-start(bf16[32,64,256]{2,1,0:T(8,128)(2,1)} %get-tuple-element.48.refs_1_), channel_id=1, source_target_pairs={{0,64},{64,0},{1,65},{65,1},{2,66},{66,2},{3,67},{67,3},{4,68},{68... | collective-permute-start | bytes 3145736 | tf_op jit(solution)/shard_map/ppermute | solution.py:471
  41.9 24.0 %all-to-all-start.1 = ((bf16[32,64,256]{2,1,0:T(8,128)(2,1)}), bf16[32,64,256]{2,1,0:T(8,128)(2,1)S(1)}, u32[]{:S(2)}, u32[]{:S(2)}) async-start(bf16[32,64,256]{2,1,0:T(8,128)(2,1)} %get-tuple-element.48.refs_1_), calls=%async_computation.1 | async-start | bytes 2097152 | tf_op jit(solution)/shard_map/all_to_all | solution.py:463
  69.0 5.0 %collective-permute-start.7 = (bf16[32,64,256]{2,1,0:T(8,128)(2,1)S(1)}, bf16[32,64,256]{2,1,0:T(8,128)(2,1)}, u32[]{:S(2)}, u32[]{:S(2)}) collective-permute-start(bf16[32,64,256]{2,1,0:T(8,128)(2,1)S(1)} %all-to-all-done.1), channel_id=1, source_target_pairs={{0,32},{32,0},{1,33},{33,1},{2,34},{34,2},{3,35},{35,3},{4,36},{36... | collective-permute-start | bytes 3145736 | tf_op jit(solution)/shard_map/ppermute | solution.py:468
  70.0 7.1 %collective-permute-start.6 = (bf16[32,64,256]{2,1,0:T(8,128)(2,1)S(1)}, bf16[32,64,256]{2,1,0:T(8,128)(2,1)}, u32[]{:S(2)}, u32[]{:S(2)}) collective-permute-start(bf16[32,64,256]{2,1,0:T(8,128)(2,1)S(1)} %collective-permute-done.4.refs_0_), channel_id=1, source_target_pairs={{0,32},{32,0},{1,33},{33,1},{2,34},{34,2},{3,35},{35,3},{4,36},{36... | collective-permute-start | bytes 3145736 | tf_op jit(solution)/shard_map/ppermute | solution.py:468
  70.1 13.3 %collective-permute-start.8 = (bf16[16,64,256]{2,1,0:T(8,128)(2,1)}, bf16[16,64,256]{2,1,0:T(8,128)(2,1)S(1)}, u32[]{:S(2)}, u32[]{:S(2)}) collective-permute-start(bf16[16,64,256]{2,1,0:T(8,128)(2,1)} %get-tuple-element.60), channel_id=1, source_target_pairs={{0,64},{64,0},{1,65},{65,1},{2,66},{66,2},{3,67},{67,3},{4,68},{68... | collective-permute-start | bytes 1572872 | tf_op jit(solution)/shard_map/ppermute | solution.py:471
  70.1 14.3 %all-to-all-start.2 = ((bf16[16,64,256]{2,1,0:T(8,128)(2,1)}), bf16[16,64,256]{2,1,0:T(8,128)(2,1)S(1)}, u32[]{:S(2)}, u32[]{:S(2)}) async-start(bf16[16,64,256]{2,1,0:T(8,128)(2,1)} %get-tuple-element.59), calls=%async_computation.2 | async-start | bytes 1048576 | tf_op jit(solution)/shard_map/all_to_all | solution.py:486
  84.3 3.8 %collective-permute-start.9 = (bf16[16,64,256]{2,1,0:T(8,128)(2,1)S(1)}, bf16[16,64,256]{2,1,0:T(8,128)(2,1)S(1)}, u32[]{:S(2)}, u32[]{:S(2)}) collective-permute-start(bf16[16,64,256]{2,1,0:T(8,128)(2,1)S(1)} %all-to-all-done.2.refs_0_), channel_id=1, source_target_pairs={{0,32},{32,0},{1,33},{33,1},{2,34},{34,2},{3,35},{35,3},{4,36},{36... | collective-permute-start | bytes 1572872 | tf_op jit(solution)/shard_map/ppermute | solution.py:468
  86.5 2.3 %collective-permute-start.10 = (bf16[16,64,256]{2,1,0:T(8,128)(2,1)S(1)}, bf16[16,64,256]{2,1,0:T(8,128)(2,1)S(1)}, u32[]{:S(2)}, u32[]{:S(2)}) collective-permute-start(bf16[16,64,256]{2,1,0:T(8,128)(2,1)S(1)} %collective-permute-done.8.refs_1_), channel_id=1, source_target_pairs={{0,32},{32,0},{1,33},{33,1},{2,34},{34,2},{3,35},{35,3},{4,36},{36... | collective-permute-start | bytes 1572872 | tf_op jit(solution)/shard_map/ppermute | solution.py:468

commit v8 on v7

--- a/solution.py
+++ b/solution.py
@@ -135,11 +135,15 @@
     return out
 
 
-def add_theirs(order, rows, tiles):
-    def body(at, x_ref, t_ref, o_ref, held, sems):
+def add_theirs(order, rows, tiles, picked):
+    def body(at, x_ref, t_ref, p_ref, o_ref, q_ref, held, sems, picked_sems):
         def store(p):
             some = pl.ds(p * PER, PER)
             return pltpu.make_async_copy(held.at[some], o_ref.at[some], sems.at[p])
+
+        def copy(p):
+            some = pl.ds(p * PER, PER)
+            return pltpu.make_async_copy(p_ref.at[some], q_ref.at[some], picked_sems.at[p])
 
         def work(p):
             for k in range(PER):
@@ -147,19 +151,24 @@
                 held[g] = (x_ref[:, columns(g)] + t_ref[g].astype(F32)).astype(BF)
             store(p).start()
 
+        each(PARTS, lambda p: copy(p).start())
         each(PARTS, work)
+        each(PARTS, lambda p: copy(p).wait())
         each(PARTS, lambda p: store(p).wait())
 
-    (out,) = order.run(
+    return order.run(
         body,
         "add_theirs",
-        (in_vmem(rows), in_vmem(tiles)),
-        [VMEM, VMEM],
-        [pltpu.HBM((SHARDS, QUARTER, WIDTH), BF)],
-        [HBM],
-        [pltpu.VMEM((SHARDS, QUARTER, WIDTH), BF), pltpu.SemaphoreType.DMA((PARTS,))],
-    )
-    return out
+        [in_vmem(x) for x in (rows, tiles, picked)],
+        [VMEM] * 3,
+        [pltpu.HBM((SHARDS, QUARTER, WIDTH), BF)] * 2,
+        [HBM] * 2,
+        [
+            pltpu.VMEM((SHARDS, QUARTER, WIDTH), BF),
+            pltpu.SemaphoreType.DMA((PARTS,)),
+            pltpu.SemaphoreType.DMA((PARTS,)),
+        ],
+    )
 
 
 def cast_own(order, policy):
@@ -220,51 +229,36 @@
 
 
 def pick_rows(order, anchor, policy):
-    def body(at, a_ref, x_ref, p_ref, rows_ref, held, in_sems, out_sems, x_sems):
+    def body(at, a_ref, x_ref, p_ref, rows_ref, a_sems, x_sems):
         rows = [member_row(at, (True, True, 0), xh) for xh in range(2)]
         theirs = pl.ds(first_row(at, True, False, 0), QUARTER)
 
         def fetch(p, xh):
             some = pl.ds(4 * p, 4)
             return pltpu.make_async_copy(
-                a_ref.at[some, xh, pl.ds(rows[xh], QUARTER), :], held.at[some, xh], in_sems.at[xh, p]
+                a_ref.at[some, xh, pl.ds(rows[xh], QUARTER), :], p_ref.at[some, xh], a_sems.at[xh, p]
             )
-
-        def store(p, xh):
-            some = pl.ds(4 * p, 4)
-            return pltpu.make_async_copy(held.at[some, xh], p_ref.at[some, xh], out_sems.at[xh, p])
 
         def copy(p):
             return pltpu.make_async_copy(
                 x_ref.at[theirs, span_of(p)], rows_ref.at[:, span_of(p)], x_sems.at[p]
             )
 
-        def forward(p, xh):
-            fetch(p, xh).wait()
-            store(p, xh).start()
-
+        each(PARTS, lambda p: copy(p).start())
         for xh in range(2):
             each(4, lambda p, xh=xh: fetch(p, xh).start())
-        each(PARTS, lambda p: copy(p).start())
-        for xh in range(2):
-            each(4, lambda p, xh=xh: forward(p, xh))
         each(PARTS, lambda p: copy(p).wait())
         for xh in range(2):
-            each(4, lambda p, xh=xh: store(p, xh).wait())
+            each(4, lambda p, xh=xh: fetch(p, xh).wait())
 
     picked, rows = order.run(
         body,
         "pick_rows",
         (anchor, policy),
         [HBM, HBM],
-        [pltpu.HBM((16, 2, QUARTER, WIDTH), BF), pltpu.VMEM((QUARTER, D), F32)],
-        [HBM, VMEM],
-        [
-            pltpu.VMEM((16, 2, QUARTER, WIDTH), BF),
-            pltpu.SemaphoreType.DMA((2, 4)),
-            pltpu.SemaphoreType.DMA((2, 4)),
-            pltpu.SemaphoreType.DMA((PARTS,)),
-        ],
+        [pltpu.VMEM((16, 2, QUARTER, WIDTH), BF), pltpu.VMEM((QUARTER, D), F32)],
+        [VMEM, VMEM],
+        [pltpu.SemaphoreType.DMA((2, 4)), pltpu.SemaphoreType.DMA((PARTS,))],
     )
     return picked.reshape(SHARDS, QUARTER, WIDTH), rows
 
@@ -304,16 +298,24 @@
 
 def split_planes(order, finished, back):
     def body(at, f_ref, b_ref, first_ref, high_ref, sems):
-        def store(p):
+        def stores(p):
             some = pl.ds(4 * p, 4)
-            return pltpu.make_async_copy(f_ref.at[some, plane(at, True)], first_ref.at[some], sems.at[p])
-
-        def work(k):
-            high_ref[k] = b_ref[k, plane(at, False)]
-
-        each(4, lambda p: store(p).start())
-        each(16, work)
-        each(4, lambda p: store(p).wait())
+            ends = ((f_ref, True, first_ref), (b_ref, False, high_ref))
+            return [
+                pltpu.make_async_copy(x.at[some, plane(at, same)], o.at[some], sems.at[i, p])
+                for i, (x, same, o) in enumerate(ends)
+            ]
+
+        def start(p):
+            for store in stores(p):
+                store.start()
+
+        def finish(p):
+            for store in stores(p):
+                store.wait()
+
+        each(4, start)
+        each(4, finish)
 
     half = (16, QUARTER, WIDTH)
     return order.run(
@@ -321,9 +323,9 @@
         "split_planes",
         [in_vmem(x.reshape(16, 2, QUARTER, WIDTH)) for x in (finished, back)],
         [VMEM, VMEM],
-        [pltpu.HBM(half, BF), pltpu.VMEM(half, BF)],
-        [HBM, VMEM],
-        [pltpu.SemaphoreType.DMA((4,))],
+        [pltpu.HBM(half, BF)] * 2,
+        [HBM] * 2,
+        [pltpu.SemaphoreType.DMA((2, 4))],
     )
 
 
@@ -472,7 +474,8 @@
 
     theirs = core(cast_rows(order, policy))
     picked, rows = pick_rows(order, shards, policy)
-    other = chip(add_theirs(order, rows, theirs))
+    theirs, picked = add_theirs(order, rows, theirs, picked)
+    other = chip(theirs)
     fetched = exchange(picked)
     own = add_own(order, policy, [core(tiles) for tiles in cast_own(order, policy)])
 

time: 91.1 us -> 90.4 us (level)
  no operation moved by 1% of the time
where the time goes in v8:
time: 90.4 us; the launch traced here: 89.8 us
  waiting for transfers between devices  32.1 us (36%)
  Pallas kernels  28.6 us (32%)
  starting transfers between devices  28.1 us (31%)
    pallas_call x12, Pallas kernels, run(): pl.pallas_call(ordered, out_shape=[*outs, TOKEN], grid_spec=pltpu.Prefetc...  28.6 us
    all_to_all x2, waiting for transfers between devices, exchange(): lax.all_to_all(tiles, AXES, split_axis=0, concat_axis=0, axis_index_group...  25.1 us
    all_to_all x2, starting transfers between devices, exchange(): lax.all_to_all(tiles, AXES, split_axis=0, concat_axis=0, axis_index_group...  15.4 us
    ppermute x8, starting transfers between devices, core(): return lax.ppermute(tiles, 'c', swap)  7.39 us
    all_to_all x1, starting transfers between devices, per_device(): lax.all_to_all(first, ('y', 'z'), split_axis=0, concat_axis=0, tiled=True)  3.95 us
    ppermute x3, waiting for transfers between devices, chip(): return lax.ppermute(tiles, 'xl', swap)  3.29 us
    ppermute x8, waiting for transfers between devices, core(): return lax.ppermute(tiles, 'c', swap)  2.82 us
  transfers between devices with their start and end apart: 14, of which 8 were waited for; matrix products, arithmetic and copies ran while one was open for 0% of the time, Pallas kernels for 22%

profile of v8, /device:TPU:1, one launch (start us, length us, event | category | flops | bytes accessed | tf_op | source)
XLA Modules:
  0.0 89.8 jit_solution(14824934207162572682)
XLA Ops:
  0.6 0.1 pad_add_fusion.at
  0.7 2.2 %cast_rows.1 = (bf16[32,64,256]{2,1,0:T(8,128)(2,1)S(1)}, s32[8,128]{1,0:T(8,128)S(1)}) custom-call(s32[3]{0:T(128)S(1)} %pad_add_fusion.at, f32[256,8192]{1,0:T(8,128)} %bitcast.15), custom_call_target="tpu_custom_call" | custom-call | bytes 1024 | tf_op jit(solution)/shard_map/cast_rows/pallas_call | solution.py:64
  2.9 1.5 %collective-permute-start = (bf16[32,64,256]{2,1,0:T(8,128)(2,1)S(1)}, bf16[32,64,256]{2,1,0:T(8,128)(2,1)S(1)}, u32[]{:S(2)}, u32[]{:S(2)}) collective-permute-start(bf16[32,64,256]{2,1,0:T(8,128)(2,1)S(1)} %get-tuple-element.39), channel_id=1, source_target_pairs={{0,32},{32,0},{1,33},{33,1},{2,34},{34,2},{3,35},{35,3},{4,36},{36... | collective-permute-start | bytes 3145736 | tf_op jit(solution)/shard_map/ppermute | solution.py:470
  4.4 2.5 %pick_rows.1 = (bf16[16,2,64,256]{3,2,1,0:T(8,128)(2,1)S(1)}, f32[64,8192]{1,0:T(8,128)S(1)}, s32[8,128]{1,0:T(8,128)S(1)}) custom-call(s32[3]{0:T(128)S(1)} %pad_add_fusion.at, bf16[16,2,256,256]{3,2,1,0:T(8,128)(2,1)} %bitcast.20, f32[256,8192]{1,0:T(8,128)} %bitcast.16, s32[8,128]{1,0:T(8,128)S(1)} %get-tuple-element.37.refs_2_), custom_call_target="tpu_custom_call" | custom-call | bytes 1024 | tf_op jit(solution)/shard_map/pick_rows/pallas_call | solution.py:64
  6.9 0.0 collective-permute-done.refs_1_
  6.9 2.0 %add_theirs.1 = (bf16[32,64,256]{2,1,0:T(8,128)(2,1)}, bf16[32,64,256]{2,1,0:T(8,128)(2,1)}, s32[8,128]{1,0:T(8,128)S(1)}) custom-call(s32[3]{0:T(128)S(1)} %pad_add_fusion.at, f32[64,8192]{1,0:T(8,128)S(1)} %get-tuple-element.38.refs_0_, bf16[32,64,256]{2,1,0:T(8,128)(2,1)S(1)} %collective-permute-done.refs_1_, bf16[32,64,256]{2,1,0:T(8,128)(2,1)S(1)} %bitcast.14, ...), custom_call_target="tpu_custom_call" | custom-call | bytes 1024 | tf_op jit(solution)/shard_map/add_theirs/pallas_call | solution.py:64
  8.9 1.4 %collective-permute-start.3 = (bf16[32,64,256]{2,1,0:T(8,128)(2,1)}, bf16[32,64,256]{2,1,0:T(8,128)(2,1)S(1)}, u32[]{:S(2)}, u32[]{:S(2)}) collective-permute-start(bf16[32,64,256]{2,1,0:T(8,128)(2,1)} %get-tuple-element.47), channel_id=1, source_target_pairs={{0,64},{64,0},{1,65},{65,1},{2,66},{66,2},{3,67},{67,3},{4,68},{68... | collective-permute-start | bytes 3145736 | tf_op jit(solution)/shard_map/ppermute | solution.py:473
  10.3 9.6 %all-to-all-start = ((bf16[32,64,256]{2,1,0:T(8,128)(2,1)}), bf16[32,64,256]{2,1,0:T(8,128)(2,1)S(1)}, u32[]{:S(2)}, u32[]{:S(2)}) async-start(bf16[32,64,256]{2,1,0:T(8,128)(2,1)} %get-tuple-element.48), calls=%async_computation | async-start | bytes 2097152 | tf_op jit(solution)/shard_map/all_to_all | solution.py:465
  19.9 2.2 %cast_own.1 = (bf16[32,32,256]{2,1,0:T(8,128)(2,1)S(1)}, bf16[32,32,256]{2,1,0:T(8,128)(2,1)S(1)}, s32[8,128]{1,0:T(8,128)S(1)}) custom-call(s32[3]{0:T(128)S(1)} %pad_add_fusion.at, f32[256,8192]{1,0:T(8,128)} %bitcast.17, s32[8,128]{1,0:T(8,128)S(1)} %get-tuple-element.42.refs_1_), custom_call_target="tpu_custom_call" | custom-call | bytes 1024 | tf_op jit(solution)/shard_map/cast_own/pallas_call | solution.py:64
  22.1 0.7 collective-permute-start.1
  22.8 0.1 collective-permute-start.2
  22.9 1.4 %collective-permute-done.1.refs_1_ = bf16[32,32,256]{2,1,0:T(8,128)(2,1)S(1)} collective-permute-done((bf16[32,32,256]{2,1,0:T(8,128)(2,1)S(1)}, bf16[32,32,256]{2,1,0:T(8,128)(2,1)S(1)}, u32[]{:S(2)}, u32[]{:S(2)}) %collective-permute-start.1) | collective-permute-done | bytes 524320 | tf_op jit(solution)/shard_map/ppermute | solution.py:470
  24.3 0.7 collective-permute-done.2.refs_2_
  25.1 2.2 %add_own.1 = (bf16[32,64,256]{2,1,0:T(8,128)(2,1)S(1)}, s32[8,128]{1,0:T(8,128)S(1)}) custom-call(s32[3]{0:T(128)S(1)} %pad_add_fusion.at, f32[256,8192]{1,0:T(8,128)} %bitcast.18, bf16[32,32,256]{2,1,0:T(8,128)(2,1)S(1)} %collective-permute-done.1.refs_1_, bf16[32,32,256]{2,1,0:T(8,128)(2,1)S(1)} %collective-permute-done.2.refs_2_, ...), custom_call_target="tpu_custom_call" | custom-call | bytes 1024 | tf_op jit(solution)/shard_map/add_own/pallas_call | solution.py:64
  27.3 10.9 %all-to-all-done.refs_2_ = bf16[32,64,256]{2,1,0:T(8,128)(2,1)S(1)} async-done(((bf16[32,64,256]{2,1,0:T(8,128)(2,1)}), bf16[32,64,256]{2,1,0:T(8,128)(2,1)S(1)}, u32[]{:S(2)}, u32[]{:S(2)}) %all-to-all-start) | async-done | bytes 1048608 | tf_op jit(solution)/shard_map/all_to_all | solution.py:465
  38.1 0.0 collective-permute-done.3.refs_1_
  38.1 1.8 %blend_rows.1 = (bf16[32,64,256]{2,1,0:T(8,128)(2,1)}, s32[8,128]{1,0:T(8,128)S(1)}) custom-call(s32[3]{0:T(128)S(1)} %pad_add_fusion.at, bf16[32,64,256]{2,1,0:T(8,128)(2,1)S(1)} %get-tuple-element.46.refs_0_, bf16[32,64,256]{2,1,0:T(8,128)(2,1)S(1)} %collective-permute-done.3.refs_1_, bf16[32,64,256]{2,1,0:T(8,128)(2,1)S(1)} %all-to-all-done.refs_2_, ...), custom_call_target="tpu_custom_call" | custom-call | bytes 1024 | tf_op jit(solution)/shard_map/blend_rows/pallas_call | solution.py:64
  39.9 1.9 %collective-permute-start.5 = (bf16[32,64,256]{2,1,0:T(8,128)(2,1)}, bf16[32,64,256]{2,1,0:T(8,128)(2,1)S(1)}, u32[]{:S(2)}, u32[]{:S(2)}) collective-permute-start(bf16[32,64,256]{2,1,0:T(8,128)(2,1)} %get-tuple-element.50.refs_1_), channel_id=1, source_target_pairs={{0,32},{32,0},{1,33},{33,1},{2,34},{34,2},{3,35},{35,3},{4,36},{36... | collective-permute-start | bytes 3145736 | tf_op jit(solution)/shard_map/ppermute | solution.py:470
  41.8 0.0 collective-permute-start.4
  41.8 5.8 %all-to-all-start.1 = ((bf16[32,64,256]{2,1,0:T(8,128)(2,1)}), bf16[32,64,256]{2,1,0:T(8,128)(2,1)S(1)}, u32[]{:S(2)}, u32[]{:S(2)}) async-start(bf16[32,64,256]{2,1,0:T(8,128)(2,1)} %get-tuple-element.50.refs_1_), calls=%async_computation.1 | async-start | bytes 2097152 | tf_op jit(solution)/shard_map/all_to_all | solution.py:465
  47.6 0.0 collective-permute-done.5.refs_0_
  47.6 4.0 %write_rows.4 = (f32[256,8192]{1,0:T(8,128)}, s32[8,128]{1,0:T(8,128)S(1)}) custom-call(s32[3]{0:T(128)S(1)} %pad_add_fusion.at, bf16[32,64,256]{2,1,0:T(8,128)(2,1)S(1)} %collective-permute-done.5.refs_0_, bf16[32,64,256]{2,1,0:T(8,128)(2,1)} %get-tuple-element.50.refs_1_, s32[8,128]{1,0:T(8,128)S(1)} %get-tuple-element.51.refs_2_), custom_call_target="tpu_custom_call" | custom-call | bytes 11534336 | tf_op jit(solution)/shard_map/write_rows/pallas_call | solution.py:64
  51.6 14.2 %all-to-all-done.1 = bf16[32,64,256]{2,1,0:T(8,128)(2,1)S(1)} async-done(((bf16[32,64,256]{2,1,0:T(8,128)(2,1)}), bf16[32,64,256]{2,1,0:T(8,128)(2,1)S(1)}, u32[]{:S(2)}, u32[]{:S(2)}) %all-to-all-start.1) | async-done | bytes 1048608 | tf_op jit(solution)/shard_map/all_to_all | solution.py:465
  65.8 0.9 %collective-permute-done.4.refs_0_ = bf16[32,64,256]{2,1,0:T(8,128)(2,1)S(1)} collective-permute-done((bf16[32,64,256]{2,1,0:T(8,128)(2,1)}, bf16[32,64,256]{2,1,0:T(8,128)(2,1)S(1)}, u32[]{:S(2)}, u32[]{:S(2)}) %collective-permute-start.4) | collective-permute-done | bytes 1048608 | tf_op jit(solution)/shard_map/ppermute | solution.py:473
  66.7 1.6 %split_planes.1 = (bf16[16,64,256]{2,1,0:T(8,128)(2,1)}, bf16[16,64,256]{2,1,0:T(8,128)(2,1)}, s32[8,128]{1,0:T(8,128)S(1)}) custom-call(s32[3]{0:T(128)S(1)} %pad_add_fusion.at, bf16[16,2,64,256]{3,2,1,0:T(8,128)(2,1)S(1)} %bitcast.13, bf16[16,2,64,256]{3,2,1,0:T(8,128)(2,1)S(1)} %bitcast.11, s32[8,128]{1,0:T(8,128)S(1)} %get-tuple-element.52.refs_2_), custom_call_target="tpu_custom_call" | custom-call | bytes 1024 | tf_op jit(solution)/shard_map/split_planes/pallas_call | solution.py:64
  68.4 1.0 %collective-permute-start.7 = (bf16[32,64,256]{2,1,0:T(8,128)(2,1)S(1)}, bf16[32,64,256]{2,1,0:T(8,128)(2,1)}, u32[]{:S(2)}, u32[]{:S(2)}) collective-permute-start(bf16[32,64,256]{2,1,0:T(8,128)(2,1)S(1)} %all-to-all-done.1), channel_id=1, source_target_pairs={{0,32},{32,0},{1,33},{33,1},{2,34},{34,2},{3,35},{35,3},{4,36},{36... | collective-permute-start | bytes 3145736 | tf_op jit(solution)/shard_map/ppermute | solution.py:470
  69.3 0.1 collective-permute-start.6
  69.4 0.0 collective-permute-start.8
  69.4 4.0 %all-to-all-start.2 = ((bf16[16,64,256]{2,1,0:T(8,128)(2,1)}), bf16[16,64,256]{2,1,0:T(8,128)(2,1)S(1)}, u32[]{:S(2)}, u32[]{:S(2)}) async-start(bf16[16,64,256]{2,1,0:T(8,128)(2,1)} %get-tuple-element.61), calls=%async_computation.2 | async-start | bytes 1048576 | tf_op jit(solution)/shard_map/all_to_all | solution.py:489
  73.4 0.0 collective-permute-done.7
  73.4 3.0 %place_back.1 = (bf16[16,2,256,256]{3,2,1,0:T(8,128)(2,1)}, s32[8,128]{1,0:T(8,128)S(1)}) custom-call(s32[3]{0:T(128)S(1)} %pad_add_fusion.at, bf16[16,2,64,256]{3,2,1,0:T(8,128)(2,1)S(1)} %bitcast.12, bf16[16,2,64,256]{3,2,1,0:T(8,128)(2,1)} %bitcast.9.refs_1_, s32[8,128]{1,0:T(8,128)S(1)} %get-tuple-element.58.refs_2_), custom_call_target="tpu_custom_call" | custom-call | bytes 1024 | tf_op jit(solution)/shard_map/place_back/pallas_call | solution.py:64
  76.4 0.0 collective-permute-done.6.refs_1_
  76.4 4.0 %write_rows.5 = (f32[256,8192]{1,0:T(8,128)}, s32[8,128]{1,0:T(8,128)S(1)}) custom-call(s32[3]{0:T(128)S(1)} %pad_add_fusion.at, bf16[32,64,256]{2,1,0:T(8,128)(2,1)S(1)} %collective-permute-done.4.refs_0_, bf16[32,64,256]{2,1,0:T(8,128)(2,1)} %collective-permute-done.6.refs_1_, ...), custom_call_target="tpu_custom_call", output_to_operand_aliasing={{0}: (3, {})} | custom-call | bytes 1024 | tf_op jit(solution)/shard_map/write_rows/pallas_call | solution.py:64
  80.4 2.3 %collective-permute-done.8.refs_1_ = bf16[16,64,256]{2,1,0:T(8,128)(2,1)S(1)} collective-permute-done((bf16[16,64,256]{2,1,0:T(8,128)(2,1)}, bf16[16,64,256]{2,1,0:T(8,128)(2,1)S(1)}, u32[]{:S(2)}, u32[]{:S(2)}) %collective-permute-start.8) | collective-permute-done | bytes 524320 | tf_op jit(solution)/shard_map/ppermute | solution.py:473
  82.7 1.0 %all-to-all-done.2.refs_0_ = bf16[16,64,256]{2,1,0:T(8,128)(2,1)S(1)} async-done(((bf16[16,64,256]{2,1,0:T(8,128)(2,1)}), bf16[16,64,256]{2,1,0:T(8,128)(2,1)S(1)}, u32[]{:S(2)}, u32[]{:S(2)}) %all-to-all-start.2) | async-done | bytes 524320 | tf_op jit(solution)/shard_map/all_to_all | solution.py:489
  83.7 2.1 %collective-permute-start.9 = (bf16[16,64,256]{2,1,0:T(8,128)(2,1)S(1)}, bf16[16,64,256]{2,1,0:T(8,128)(2,1)S(1)}, u32[]{:S(2)}, u32[]{:S(2)}) collective-permute-start(bf16[16,64,256]{2,1,0:T(8,128)(2,1)S(1)} %all-to-all-done.2.refs_0_), channel_id=1, source_target_pairs={{0,32},{32,0},{1,33},{33,1},{2,34},{34,2},{3,35},{35,3},{4,36},{36... | collective-permute-start | bytes 1572872 | tf_op jit(solution)/shard_map/ppermute | solution.py:470
  85.8 0.0 collective-permute-start.10
  85.8 1.7 %write_rows.6 = (bf16[16,2,256,256]{3,2,1,0:T(8,128)(2,1)}, s32[8,128]{1,0:T(8,128)S(1)}) custom-call(s32[3]{0:T(128)S(1)} %pad_add_fusion.at, bf16[16,64,256]{2,1,0:T(8,128)(2,1)S(1)} %all-to-all-done.2.refs_0_, bf16[16,64,256]{2,1,0:T(8,128)(2,1)S(1)} %collective-permute-done.8.refs_1_, ...), custom_call_target="tpu_custom_call", output_to_operand_aliasing={{0}: (3, {})} | custom-call | bytes 38797312 | tf_op jit(solution)/shard_map/write_rows/pallas_call | solution.py:64
  87.5 0.0 collective-permute-done.9.refs_0_
  87.5 0.6 collective-permute-done.10.refs_1_
  88.1 1.7 %write_rows.7 = (bf16[16,2,256,256]{3,2,1,0:T(8,128)(2,1)}, s32[8,128]{1,0:T(8,128)}) custom-call(s32[3]{0:T(128)S(1)} %pad_add_fusion.at, bf16[16,64,256]{2,1,0:T(8,128)(2,1)S(1)} %collective-permute-done.9.refs_0_, bf16[16,64,256]{2,1,0:T(8,128)(2,1)S(1)} %collective-permute-done.10.refs_1_, ...), custom_call_target="tpu_custom_call", output_to_operand_aliasing={{0}: (3, {})} | custom-call | bytes 1024 | tf_op jit(solution)/shard_map/write_rows/pallas_call | solution.py:64
Async XLA Ops:
  2.9 4.0 %collective-permute-start = (bf16[32,64,256]{2,1,0:T(8,128)(2,1)S(1)}, bf16[32,64,256]{2,1,0:T(8,128)(2,1)S(1)}, u32[]{:S(2)}, u32[]{:S(2)}) collective-permute-start(bf16[32,64,256]{2,1,0:T(8,128)(2,1)S(1)} %get-tuple-element.39), channel_id=1, source_target_pairs={{0,32},{32,0},{1,33},{33,1},{2,34},{34,2},{3,35},{35,3},{4,36},{36... | collective-permute-start | bytes 3145736 | tf_op jit(solution)/shard_map/ppermute | solution.py:470
  8.9 29.2 %collective-permute-start.3 = (bf16[32,64,256]{2,1,0:T(8,128)(2,1)}, bf16[32,64,256]{2,1,0:T(8,128)(2,1)S(1)}, u32[]{:S(2)}, u32[]{:S(2)}) collective-permute-start(bf16[32,64,256]{2,1,0:T(8,128)(2,1)} %get-tuple-element.47), channel_id=1, source_target_pairs={{0,64},{64,0},{1,65},{65,1},{2,66},{66,2},{3,67},{67,3},{4,68},{68... | collective-permute-start | bytes 3145736 | tf_op jit(solution)/shard_map/ppermute | solution.py:473
  10.3 27.8 %all-to-all-start = ((bf16[32,64,256]{2,1,0:T(8,128)(2,1)}), bf16[32,64,256]{2,1,0:T(8,128)(2,1)S(1)}, u32[]{:S(2)}, u32[]{:S(2)}) async-start(bf16[32,64,256]{2,1,0:T(8,128)(2,1)} %get-tuple-element.48), calls=%async_computation | async-start | bytes 2097152 | tf_op jit(solution)/shard_map/all_to_all | solution.py:465
  22.1 2.3 %collective-permute-start.1 = (bf16[32,32,256]{2,1,0:T(8,128)(2,1)S(1)}, bf16[32,32,256]{2,1,0:T(8,128)(2,1)S(1)}, u32[]{:S(2)}, u32[]{:S(2)}) collective-permute-start(bf16[32,32,256]{2,1,0:T(8,128)(2,1)S(1)} %get-tuple-element.43), channel_id=1, source_target_pairs={{0,32},{32,0},{1,33},{33,1},{2,34},{34,2},{3,35},{35,3},{4,36},{36... | collective-permute-start | bytes 1572872 | tf_op jit(solution)/shard_map/ppermute | solution.py:470
  22.8 2.3 %collective-permute-start.2 = (bf16[32,32,256]{2,1,0:T(8,128)(2,1)S(1)}, bf16[32,32,256]{2,1,0:T(8,128)(2,1)S(1)}, u32[]{:S(2)}, u32[]{:S(2)}) collective-permute-start(bf16[32,32,256]{2,1,0:T(8,128)(2,1)S(1)} %get-tuple-element.44), channel_id=1, source_target_pairs={{0,32},{32,0},{1,33},{33,1},{2,34},{34,2},{3,35},{35,3},{4,36},{36... | collective-permute-start | bytes 1572872 | tf_op jit(solution)/shard_map/ppermute | solution.py:470
  39.9 7.7 %collective-permute-start.5 = (bf16[32,64,256]{2,1,0:T(8,128)(2,1)}, bf16[32,64,256]{2,1,0:T(8,128)(2,1)S(1)}, u32[]{:S(2)}, u32[]{:S(2)}) collective-permute-start(bf16[32,64,256]{2,1,0:T(8,128)(2,1)} %get-tuple-element.50.refs_1_), channel_id=1, source_target_pairs={{0,32},{32,0},{1,33},{33,1},{2,34},{34,2},{3,35},{35,3},{4,36},{36... | collective-permute-start | bytes 3145736 | tf_op jit(solution)/shard_map/ppermute | solution.py:470
  41.8 24.9 %collective-permute-start.4 = (bf16[32,64,256]{2,1,0:T(8,128)(2,1)}, bf16[32,64,256]{2,1,0:T(8,128)(2,1)S(1)}, u32[]{:S(2)}, u32[]{:S(2)}) collective-permute-start(bf16[32,64,256]{2,1,0:T(8,128)(2,1)} %get-tuple-element.50.refs_1_), channel_id=1, source_target_pairs={{0,64},{64,0},{1,65},{65,1},{2,66},{66,2},{3,67},{67,3},{4,68},{68... | collective-permute-start | bytes 3145736 | tf_op jit(solution)/shard_map/ppermute | solution.py:473
  41.8 24.0 %all-to-all-start.1 = ((bf16[32,64,256]{2,1,0:T(8,128)(2,1)}), bf16[32,64,256]{2,1,0:T(8,128)(2,1)S(1)}, u32[]{:S(2)}, u32[]{:S(2)}) async-start(bf16[32,64,256]{2,1,0:T(8,128)(2,1)} %get-tuple-element.50.refs_1_), calls=%async_computation.1 | async-start | bytes 2097152 | tf_op jit(solution)/shard_map/all_to_all | solution.py:465
  68.4 5.0 %collective-permute-start.7 = (bf16[32,64,256]{2,1,0:T(8,128)(2,1)S(1)}, bf16[32,64,256]{2,1,0:T(8,128)(2,1)}, u32[]{:S(2)}, u32[]{:S(2)}) collective-permute-start(bf16[32,64,256]{2,1,0:T(8,128)(2,1)S(1)} %all-to-all-done.1), channel_id=1, source_target_pairs={{0,32},{32,0},{1,33},{33,1},{2,34},{34,2},{3,35},{35,3},{4,36},{36... | collective-permute-start | bytes 3145736 | tf_op jit(solution)/shard_map/ppermute | solution.py:470
  69.3 7.1 %collective-permute-start.6 = (bf16[32,64,256]{2,1,0:T(8,128)(2,1)S(1)}, bf16[32,64,256]{2,1,0:T(8,128)(2,1)}, u32[]{:S(2)}, u32[]{:S(2)}) collective-permute-start(bf16[32,64,256]{2,1,0:T(8,128)(2,1)S(1)} %collective-permute-done.4.refs_0_), channel_id=1, source_target_pairs={{0,32},{32,0},{1,33},{33,1},{2,34},{34,2},{3,35},{35,3},{4,36},{36... | collective-permute-start | bytes 3145736 | tf_op jit(solution)/shard_map/ppermute | solution.py:470
  69.4 13.3 %collective-permute-start.8 = (bf16[16,64,256]{2,1,0:T(8,128)(2,1)}, bf16[16,64,256]{2,1,0:T(8,128)(2,1)S(1)}, u32[]{:S(2)}, u32[]{:S(2)}) collective-permute-start(bf16[16,64,256]{2,1,0:T(8,128)(2,1)} %get-tuple-element.62), channel_id=1, source_target_pairs={{0,64},{64,0},{1,65},{65,1},{2,66},{66,2},{3,67},{67,3},{4,68},{68... | collective-permute-start | bytes 1572872 | tf_op jit(solution)/shard_map/ppermute | solution.py:473
  69.4 14.3 %all-to-all-start.2 = ((bf16[16,64,256]{2,1,0:T(8,128)(2,1)}), bf16[16,64,256]{2,1,0:T(8,128)(2,1)S(1)}, u32[]{:S(2)}, u32[]{:S(2)}) async-start(bf16[16,64,256]{2,1,0:T(8,128)(2,1)} %get-tuple-element.61), calls=%async_computation.2 | async-start | bytes 1048576 | tf_op jit(solution)/shard_map/all_to_all | solution.py:489
  83.7 3.8 %collective-permute-start.9 = (bf16[16,64,256]{2,1,0:T(8,128)(2,1)S(1)}, bf16[16,64,256]{2,1,0:T(8,128)(2,1)S(1)}, u32[]{:S(2)}, u32[]{:S(2)}) collective-permute-start(bf16[16,64,256]{2,1,0:T(8,128)(2,1)S(1)} %all-to-all-done.2.refs_0_), channel_id=1, source_target_pairs={{0,32},{32,0},{1,33},{33,1},{2,34},{34,2},{3,35},{35,3},{4,36},{36... | collective-permute-start | bytes 1572872 | tf_op jit(solution)/shard_map/ppermute | solution.py:470
  85.8 2.3 %collective-permute-start.10 = (bf16[16,64,256]{2,1,0:T(8,128)(2,1)S(1)}, bf16[16,64,256]{2,1,0:T(8,128)(2,1)S(1)}, u32[]{:S(2)}, u32[]{:S(2)}) collective-permute-start(bf16[16,64,256]{2,1,0:T(8,128)(2,1)S(1)} %collective-permute-done.8.refs_1_), channel_id=1, source_target_pairs={{0,32},{32,0},{1,33},{33,1},{2,34},{34,2},{3,35},{35,3},{4,36},{36... | collective-permute-start | bytes 1572872 | tf_op jit(solution)/shard_map/ppermute | solution.py:470

commit v9 on v8

--- a/solution.py
+++ b/solution.py
@@ -34,7 +34,7 @@
 def exchange_groups():
     ids = np.arange(128).reshape(SIZES)
     return [
-        [int(ids[flip ^ xh, c, y, z, xh]) for y in range(4) for z in range(4) for xh in range(2)]
+        [int(ids[flip ^ xh, c, y, z, xh]) for xh in range(2) for y in range(4) for z in range(4)]
         for flip in range(2)
         for c in range(2)
     ]
@@ -83,6 +83,10 @@
     return pl.ds(pl.multiple_of(g * WIDTH, WIDTH), WIDTH)
 
 
+def slot(p, k):
+    return (k % 2) * 16 + p * (PER // 2) + k // 2
+
+
 def each(count, work):
     pl.loop(0, count)(work)
 
@@ -118,7 +122,7 @@
             copy(p).wait()
             for k in range(PER):
                 g = p * PER + k
-                o_ref[g] = wide[:, columns(g)].astype(BF)
+                o_ref[slot(p, k)] = wide[:, columns(g)].astype(BF)
 
         each(PARTS, lambda p: copy(p).start())
         each(PARTS, work)
@@ -147,8 +151,9 @@
 
         def work(p):
             for k in range(PER):
-                g = p * PER + k
-                held[g] = (x_ref[:, columns(g)] + t_ref[g].astype(F32)).astype(BF)
+                at_slot = p * PER + k
+                g = 2 * ((p & 3) * PER + k) + (p >> 2)
+                held[at_slot] = (x_ref[:, columns(g)] + t_ref[at_slot].astype(F32)).astype(BF)
             store(p).start()
 
         each(PARTS, lambda p: copy(p).start())
@@ -182,8 +187,8 @@
             copy(p).wait()
             for k in range(PER):
                 g = p * PER + k
-                low_ref[g] = wide[:R, columns(g)].astype(BF)
-                high_ref[g] = wide[R:, columns(g)].astype(BF)
+                low_ref[slot(p, k)] = wide[:R, columns(g)].astype(BF)
+                high_ref[slot(p, k)] = wide[R:, columns(g)].astype(BF)
 
         each(PARTS, lambda p: copy(p).start())
         each(PARTS, work)
@@ -210,8 +215,8 @@
             copy(p).wait()
             for k in range(PER):
                 g = p * PER + k
-                o_ref[g, :R] = (wide[:R, columns(g)] + low_ref[g].astype(F32)).astype(BF)
-                o_ref[g, R:] = (wide[R:, columns(g)] + high_ref[g].astype(F32)).astype(BF)
+                o_ref[slot(p, k), :R] = (wide[:R, columns(g)] + low_ref[slot(p, k)].astype(F32)).astype(BF)
+                o_ref[slot(p, k), R:] = (wide[R:, columns(g)] + high_ref[slot(p, k)].astype(F32)).astype(BF)
 
         each(PARTS, lambda p: copy(p).start())
         each(PARTS, work)
@@ -236,7 +241,7 @@
         def fetch(p, xh):
             some = pl.ds(4 * p, 4)
             return pltpu.make_async_copy(
-                a_ref.at[some, xh, pl.ds(rows[xh], QUARTER), :], p_ref.at[some, xh], a_sems.at[xh, p]
+                a_ref.at[some, xh, pl.ds(rows[xh], QUARTER), :], p_ref.at[xh, some], a_sems.at[xh, p]
             )
 
         def copy(p):
@@ -256,7 +261,7 @@
         "pick_rows",
         (anchor, policy),
         [HBM, HBM],
-        [pltpu.VMEM((16, 2, QUARTER, WIDTH), BF), pltpu.VMEM((QUARTER, D), F32)],
+        [pltpu.VMEM((2, 16, QUARTER, WIDTH), BF), pltpu.VMEM((QUARTER, D), F32)],
         [VMEM, VMEM],
         [pltpu.SemaphoreType.DMA((2, 4)), pltpu.SemaphoreType.DMA((PARTS,))],
     )
@@ -302,7 +307,7 @@
             some = pl.ds(4 * p, 4)
             ends = ((f_ref, True, first_ref), (b_ref, False, high_ref))
             return [
-                pltpu.make_async_copy(x.at[some, plane(at, same)], o.at[some], sems.at[i, p])
+                pltpu.make_async_copy(x.at[plane(at, same), some], o.at[some], sems.at[i, p])
                 for i, (x, same, o) in enumerate(ends)
             ]
 
@@ -321,7 +326,7 @@
     return order.run(
         body,
         "split_planes",
-        [in_vmem(x.reshape(16, 2, QUARTER, WIDTH)) for x in (finished, back)],
+        [in_vmem(x.reshape(2, 16, QUARTER, WIDTH)) for x in (finished, back)],
         [VMEM, VMEM],
         [pltpu.HBM(half, BF)] * 2,
         [HBM] * 2,
@@ -337,21 +342,23 @@
 
         def place(ref, core, same, p):
             return pltpu.make_async_copy(
-                ref.at[pl.ds(4 * p, 4), plane(at, same)],
+                ref.at[plane(at, same), pl.ds(4 * p, 4)],
                 there(core, same, p),
                 sems.at[int(core), int(same), p],
             )
 
-        def fetch(p):
+        def fetch(xh, p):
             some = pl.ds(4 * p, 4)
-            return pltpu.make_async_copy(other_ref.at[some], held.at[some], held_sems.at[p])
+            return pltpu.make_async_copy(other_ref.at[xh, some], held.at[xh, some], held_sems.at[xh, p])
 
         def forward(p):
-            fetch(p).wait()
+            for xh in range(2):
+                fetch(xh, p).wait()
             for same in (True, False):
                 place(held, False, same, p).start()
 
-        each(4, lambda p: fetch(p).start())
+        for xh in range(2):
+            each(4, lambda p, xh=xh: fetch(xh, p).start())
         for same in (True, False):
             each(4, lambda p, same=same: place(own_ref, True, same, p).start())
         each(4, forward)
@@ -359,7 +366,7 @@
             for same in (True, False):
                 each(4, lambda p, ref=ref, core=core, same=same: place(ref, core, same, p).wait())
 
-    shape = (16, 2, QUARTER, WIDTH)
+    shape = (2, 16, QUARTER, WIDTH)
     return order.run(
         body,
         "place_back",
@@ -370,16 +377,15 @@
         [
             pltpu.VMEM(shape, BF),
             pltpu.SemaphoreType.DMA((2, 2, 4)),
-            pltpu.SemaphoreType.DMA((4,)),
+            pltpu.SemaphoreType.DMA((2, 4)),
         ],
     )[0]
 
 
 def write_rows(order, wide_pieces, placed_pieces, blended, anchor, size=1024, late_in_hbm=False):
     n, m = len(wide_pieces), len(placed_pieces)
-    counts = [len(arrays) for arrays, _, _ in wide_pieces]
-    flat = [x for arrays, _, _ in wide_pieces for x in arrays]
-    late = sum(counts[:-1])
+    flat = [tiles for tiles, _, _ in wide_pieces]
+    late = n - 1
     outs = [pltpu.HBM((ROWS, D), F32)] * (n > 0) + [pltpu.HBM((16, 2, ROWS, WIDTH), BF)] * (m > 0)
     earlier = [x for x, k in ((blended, n), (anchor, m)) if k and x is not None]
 
@@ -403,15 +409,8 @@
             )
 
         def work(i, tiles, p):
-            if len(tiles) == 1:
-                for k in range(PER):
-                    g = p * PER + k
-                    wide[i, :, columns(g)] = tiles[0][g].astype(F32)
-            else:
-                for k in range(PER // 2):
-                    yz = p * (PER // 2) + k
-                    for ref, same in zip(tiles, (True, False)):
-                        wide[i, :, columns(2 * yz + plane(at, same))] = ref[yz].astype(F32)
+            for k in range(PER):
+                wide[i, :, columns(p * PER + k)] = tiles[slot(p, k)].astype(F32)
             copy(i, p).start()
 
         if n:
@@ -423,8 +422,7 @@
         for i in range(n):
             if i == n - 1:
                 last.wait()
-            tiles = flat_refs[sum(counts[:i]) : sum(counts[: i + 1])]
-            each(PARTS, lambda p, i=i, tiles=tiles: work(i, tiles, p))
+            each(PARTS, lambda p, i=i, tiles=flat_refs[i]: work(i, tiles, p))
         for i in range(n):
             each(PARTS, lambda p, i=i: copy(i, p).wait())
         for i in range(m):
@@ -482,7 +480,7 @@
     own = blend_rows(order, own, other, fetched)
     finished = chip(own)
     back = exchange(own)
-    pieces = [([core(own)], False, True), ([own], True, True)]
+    pieces = [(core(own), False, True), (own, True, True)]
     (blended,) = write_rows(order, pieces, [], None, None, WRITE_COST, late_in_hbm=True)
 
     first, high = split_planes(order, finished, back)
@@ -490,7 +488,7 @@
     back_second = chip(high)
     finished, back = order.behind(finished), order.behind(back)
     new_anchor = place_back(order, back, core(back))
-    pieces = [([finished], True, False), ([core(finished)], False, False)]
+    pieces = [(finished, True, False), (core(finished), False, False)]
     (blended,) = write_rows(order, pieces, [], blended, None)
     back_second = order.behind(back_second)
     back_first = order.behind(back_first)

time: 90.4 us -> 90.4 us (level)
  waiting for transfers between devices: 32.1 us -> 28.3 us
  starting transfers between devices: 28.1 us -> 31.7 us
    all_to_all x2, waiting for transfers between devices: 25.1 us -> 21 us  [exchange(): lax.all_to_all(tiles, AXES, split_axis=0, concat_axis=0, axis_index_group...]
    all_to_all x2, starting transfers between devices: 15.4 us -> 17 us  [exchange(): lax.all_to_all(tiles, AXES, split_axis=0, concat_axis=0, axis_index_group...]
    all_to_all x1, waiting for transfers between devices: 0.97 us -> 2.55 us  [per_device(): lax.all_to_all(first, ('y', 'z'), split_axis=0, concat_axis=0, tiled=True)]
    all_to_all x1, starting transfers between devices: 3.95 us -> 5.54 us  [per_device(): lax.all_to_all(first, ('y', 'z'), split_axis=0, concat_axis=0, tiled=True)]
    ppermute x3, waiting for transfers between devices: 3.29 us -> 1.86 us  [chip(): return lax.ppermute(tiles, 'xl', swap)]
where the time goes in v9:
time: 90.4 us; the launch traced here: 89.8 us
  starting transfers between devices  31.7 us (35%)
  Pallas kernels  28.9 us (32%)
  waiting for transfers between devices  28.3 us (31%)
    pallas_call x12, Pallas kernels, run(): pl.pallas_call(ordered, out_shape=[*outs, TOKEN], grid_spec=pltpu.Prefetc...  28.9 us
    all_to_all x2, waiting for transfers between devices, exchange(): lax.all_to_all(tiles, AXES, split_axis=0, concat_axis=0, axis_index_group...  21 us
    all_to_all x2, starting transfers between devices, exchange(): lax.all_to_all(tiles, AXES, split_axis=0, concat_axis=0, axis_index_group...  17 us
    ppermute x8, starting transfers between devices, core(): return lax.ppermute(tiles, 'c', swap)  7.81 us
    all_to_all x1, starting transfers between devices, per_device(): lax.all_to_all(first, ('y', 'z'), split_axis=0, concat_axis=0, tiled=True)  5.54 us
    ppermute x8, waiting for transfers between devices, core(): return lax.ppermute(tiles, 'c', swap)  2.82 us
    all_to_all x1, waiting for transfers between devices, per_device(): lax.all_to_all(first, ('y', 'z'), split_axis=0, concat_axis=0, tiled=True)  2.55 us
    ppermute x3, waiting for transfers between devices, chip(): return lax.ppermute(tiles, 'xl', swap)  1.86 us
  transfers between devices with their start and end apart: 14, of which 8 were waited for; matrix products, arithmetic and copies ran while one was open for 0% of the time, Pallas kernels for 22%

profile of v9, /device:TPU:1, one launch (start us, length us, event | category | flops | bytes accessed | tf_op | source)
XLA Modules:
  0.0 89.8 jit_solution(14866814547051542048)
XLA Ops:
  0.6 0.1 pad_add_fusion.at
  0.7 2.2 %cast_rows.1 = (bf16[32,64,256]{2,1,0:T(8,128)(2,1)S(1)}, s32[8,128]{1,0:T(8,128)S(1)}) custom-call(s32[3]{0:T(128)S(1)} %pad_add_fusion.at, f32[256,8192]{1,0:T(8,128)} %bitcast.15), custom_call_target="tpu_custom_call" | custom-call | bytes 1024 | tf_op jit(solution)/shard_map/cast_rows/pallas_call | solution.py:64
  2.9 1.5 %collective-permute-start = (bf16[32,64,256]{2,1,0:T(8,128)(2,1)S(1)}, bf16[32,64,256]{2,1,0:T(8,128)(2,1)S(1)}, u32[]{:S(2)}, u32[]{:S(2)}) collective-permute-start(bf16[32,64,256]{2,1,0:T(8,128)(2,1)S(1)} %get-tuple-element.39), channel_id=1, source_target_pairs={{0,32},{32,0},{1,33},{33,1},{2,34},{34,2},{3,35},{35,3},{4,36},{36... | collective-permute-start | bytes 3145736 | tf_op jit(solution)/shard_map/ppermute | solution.py:468
  4.4 2.5 %pick_rows.1 = (bf16[2,16,64,256]{3,2,1,0:T(8,128)(2,1)S(1)}, f32[64,8192]{1,0:T(8,128)S(1)}, s32[8,128]{1,0:T(8,128)S(1)}) custom-call(s32[3]{0:T(128)S(1)} %pad_add_fusion.at, bf16[16,2,256,256]{3,2,1,0:T(8,128)(2,1)} %bitcast.20, f32[256,8192]{1,0:T(8,128)} %bitcast.16, s32[8,128]{1,0:T(8,128)S(1)} %get-tuple-element.37.refs_2_), custom_call_target="tpu_custom_call" | custom-call | bytes 1024 | tf_op jit(solution)/shard_map/pick_rows/pallas_call | solution.py:64
  6.9 0.0 collective-permute-done.refs_1_
  6.9 2.0 %add_theirs.1 = (bf16[32,64,256]{2,1,0:T(8,128)(2,1)}, bf16[32,64,256]{2,1,0:T(8,128)(2,1)}, s32[8,128]{1,0:T(8,128)S(1)}) custom-call(s32[3]{0:T(128)S(1)} %pad_add_fusion.at, f32[64,8192]{1,0:T(8,128)S(1)} %get-tuple-element.38.refs_0_, bf16[32,64,256]{2,1,0:T(8,128)(2,1)S(1)} %collective-permute-done.refs_1_, bf16[32,64,256]{2,1,0:T(8,128)(2,1)S(1)} %bitcast.14, ...), custom_call_target="tpu_custom_call" | custom-call | bytes 1024 | tf_op jit(solution)/shard_map/add_theirs/pallas_call | solution.py:64
  8.9 1.4 %collective-permute-start.3 = (bf16[32,64,256]{2,1,0:T(8,128)(2,1)}, bf16[32,64,256]{2,1,0:T(8,128)(2,1)S(1)}, u32[]{:S(2)}, u32[]{:S(2)}) collective-permute-start(bf16[32,64,256]{2,1,0:T(8,128)(2,1)} %get-tuple-element.47), channel_id=1, source_target_pairs={{0,64},{64,0},{1,65},{65,1},{2,66},{66,2},{3,67},{67,3},{4,68},{68... | collective-permute-start | bytes 3145736 | tf_op jit(solution)/shard_map/ppermute | solution.py:471
  10.3 9.6 %all-to-all-start = ((bf16[32,64,256]{2,1,0:T(8,128)(2,1)}), bf16[32,64,256]{2,1,0:T(8,128)(2,1)S(1)}, u32[]{:S(2)}, u32[]{:S(2)}) async-start(bf16[32,64,256]{2,1,0:T(8,128)(2,1)} %get-tuple-element.48), calls=%async_computation | async-start | bytes 2097152 | tf_op jit(solution)/shard_map/all_to_all | solution.py:463
  19.9 2.2 %cast_own.1 = (bf16[32,32,256]{2,1,0:T(8,128)(2,1)S(1)}, bf16[32,32,256]{2,1,0:T(8,128)(2,1)S(1)}, s32[8,128]{1,0:T(8,128)S(1)}) custom-call(s32[3]{0:T(128)S(1)} %pad_add_fusion.at, f32[256,8192]{1,0:T(8,128)} %bitcast.17, s32[8,128]{1,0:T(8,128)S(1)} %get-tuple-element.42.refs_1_), custom_call_target="tpu_custom_call" | custom-call | bytes 1024 | tf_op jit(solution)/shard_map/cast_own/pallas_call | solution.py:64
  22.1 0.7 collective-permute-start.1
  22.8 0.1 collective-permute-start.2
  22.9 1.4 %collective-permute-done.1.refs_1_ = bf16[32,32,256]{2,1,0:T(8,128)(2,1)S(1)} collective-permute-done((bf16[32,32,256]{2,1,0:T(8,128)(2,1)S(1)}, bf16[32,32,256]{2,1,0:T(8,128)(2,1)S(1)}, u32[]{:S(2)}, u32[]{:S(2)}) %collective-permute-start.1) | collective-permute-done | bytes 524320 | tf_op jit(solution)/shard_map/ppermute | solution.py:468
  24.3 0.7 collective-permute-done.2.refs_2_
  25.1 2.2 %add_own.1 = (bf16[32,64,256]{2,1,0:T(8,128)(2,1)S(1)}, s32[8,128]{1,0:T(8,128)S(1)}) custom-call(s32[3]{0:T(128)S(1)} %pad_add_fusion.at, f32[256,8192]{1,0:T(8,128)} %bitcast.18, bf16[32,32,256]{2,1,0:T(8,128)(2,1)S(1)} %collective-permute-done.1.refs_1_, bf16[32,32,256]{2,1,0:T(8,128)(2,1)S(1)} %collective-permute-done.2.refs_2_, ...), custom_call_target="tpu_custom_call" | custom-call | bytes 1024 | tf_op jit(solution)/shard_map/add_own/pallas_call | solution.py:64
  27.3 8.8 %all-to-all-done.refs_2_ = bf16[32,64,256]{2,1,0:T(8,128)(2,1)S(1)} async-done(((bf16[32,64,256]{2,1,0:T(8,128)(2,1)}), bf16[32,64,256]{2,1,0:T(8,128)(2,1)S(1)}, u32[]{:S(2)}, u32[]{:S(2)}) %all-to-all-start) | async-done | bytes 1048608 | tf_op jit(solution)/shard_map/all_to_all | solution.py:463
  36.1 0.0 collective-permute-done.3.refs_1_
  36.1 1.8 %blend_rows.1 = (bf16[32,64,256]{2,1,0:T(8,128)(2,1)}, s32[8,128]{1,0:T(8,128)S(1)}) custom-call(s32[3]{0:T(128)S(1)} %pad_add_fusion.at, bf16[32,64,256]{2,1,0:T(8,128)(2,1)S(1)} %get-tuple-element.46.refs_0_, bf16[32,64,256]{2,1,0:T(8,128)(2,1)S(1)} %collective-permute-done.3.refs_1_, bf16[32,64,256]{2,1,0:T(8,128)(2,1)S(1)} %all-to-all-done.refs_2_, ...), custom_call_target="tpu_custom_call" | custom-call | bytes 1024 | tf_op jit(solution)/shard_map/blend_rows/pallas_call | solution.py:64
  37.9 2.3 %collective-permute-start.5 = (bf16[32,64,256]{2,1,0:T(8,128)(2,1)}, bf16[32,64,256]{2,1,0:T(8,128)(2,1)S(1)}, u32[]{:S(2)}, u32[]{:S(2)}) collective-permute-start(bf16[32,64,256]{2,1,0:T(8,128)(2,1)} %get-tuple-element.50.refs_1_), channel_id=1, source_target_pairs={{0,32},{32,0},{1,33},{33,1},{2,34},{34,2},{3,35},{35,3},{4,36},{36... | collective-permute-start | bytes 3145736 | tf_op jit(solution)/shard_map/ppermute | solution.py:468
  40.2 0.0 collective-permute-start.4
  40.2 7.4 %all-to-all-start.1 = ((bf16[32,64,256]{2,1,0:T(8,128)(2,1)}), bf16[32,64,256]{2,1,0:T(8,128)(2,1)S(1)}, u32[]{:S(2)}, u32[]{:S(2)}) async-start(bf16[32,64,256]{2,1,0:T(8,128)(2,1)} %get-tuple-element.50.refs_1_), calls=%async_computation.1 | async-start | bytes 2097152 | tf_op jit(solution)/shard_map/all_to_all | solution.py:463
  47.6 0.0 collective-permute-done.5.refs_0_
  47.6 4.0 %write_rows.4 = (f32[256,8192]{1,0:T(8,128)}, s32[8,128]{1,0:T(8,128)S(1)}) custom-call(s32[3]{0:T(128)S(1)} %pad_add_fusion.at, bf16[32,64,256]{2,1,0:T(8,128)(2,1)S(1)} %collective-permute-done.5.refs_0_, bf16[32,64,256]{2,1,0:T(8,128)(2,1)} %get-tuple-element.50.refs_1_, s32[8,128]{1,0:T(8,128)S(1)} %get-tuple-element.51.refs_2_), custom_call_target="tpu_custom_call" | custom-call | bytes 11534336 | tf_op jit(solution)/shard_map/write_rows/pallas_call | solution.py:64
  51.6 12.2 %all-to-all-done.1 = bf16[32,64,256]{2,1,0:T(8,128)(2,1)S(1)} async-done(((bf16[32,64,256]{2,1,0:T(8,128)(2,1)}), bf16[32,64,256]{2,1,0:T(8,128)(2,1)S(1)}, u32[]{:S(2)}, u32[]{:S(2)}) %all-to-all-start.1) | async-done | bytes 1048608 | tf_op jit(solution)/shard_map/all_to_all | solution.py:463
  63.8 1.4 %collective-permute-done.4.refs_0_ = bf16[32,64,256]{2,1,0:T(8,128)(2,1)S(1)} collective-permute-done((bf16[32,64,256]{2,1,0:T(8,128)(2,1)}, bf16[32,64,256]{2,1,0:T(8,128)(2,1)S(1)}, u32[]{:S(2)}, u32[]{:S(2)}) %collective-permute-start.4) | collective-permute-done | bytes 1048608 | tf_op jit(solution)/shard_map/ppermute | solution.py:471
  65.2 1.6 %split_planes.1 = (bf16[16,64,256]{2,1,0:T(8,128)(2,1)}, bf16[16,64,256]{2,1,0:T(8,128)(2,1)}, s32[8,128]{1,0:T(8,128)S(1)}) custom-call(s32[3]{0:T(128)S(1)} %pad_add_fusion.at, bf16[2,16,64,256]{3,2,1,0:T(8,128)(2,1)S(1)} %bitcast.13, bf16[2,16,64,256]{3,2,1,0:T(8,128)(2,1)S(1)} %bitcast.11, s32[8,128]{1,0:T(8,128)S(1)} %get-tuple-element.52.refs_2_), custom_call_target="tpu_custom_call" | custom-call | bytes 1024 | tf_op jit(solution)/shard_map/split_planes/pallas_call | solution.py:64
  66.8 1.0 %collective-permute-start.7 = (bf16[32,64,256]{2,1,0:T(8,128)(2,1)S(1)}, bf16[32,64,256]{2,1,0:T(8,128)(2,1)}, u32[]{:S(2)}, u32[]{:S(2)}) collective-permute-start(bf16[32,64,256]{2,1,0:T(8,128)(2,1)S(1)} %all-to-all-done.1), channel_id=1, source_target_pairs={{0,32},{32,0},{1,33},{33,1},{2,34},{34,2},{3,35},{35,3},{4,36},{36... | collective-permute-start | bytes 3145736 | tf_op jit(solution)/shard_map/ppermute | solution.py:468
  67.7 0.1 collective-permute-start.6
  67.8 0.0 collective-permute-start.8
  67.8 5.5 %all-to-all-start.2 = ((bf16[16,64,256]{2,1,0:T(8,128)(2,1)}), bf16[16,64,256]{2,1,0:T(8,128)(2,1)S(1)}, u32[]{:S(2)}, u32[]{:S(2)}) async-start(bf16[16,64,256]{2,1,0:T(8,128)(2,1)} %get-tuple-element.61), calls=%async_computation.2 | async-start | bytes 1048576 | tf_op jit(solution)/shard_map/all_to_all | solution.py:487
  73.4 0.0 collective-permute-done.7
  73.4 3.3 %place_back.1 = (bf16[16,2,256,256]{3,2,1,0:T(8,128)(2,1)}, s32[8,128]{1,0:T(8,128)S(1)}) custom-call(s32[3]{0:T(128)S(1)} %pad_add_fusion.at, bf16[2,16,64,256]{3,2,1,0:T(8,128)(2,1)S(1)} %bitcast.12, bf16[2,16,64,256]{3,2,1,0:T(8,128)(2,1)} %bitcast.9.refs_1_, s32[8,128]{1,0:T(8,128)S(1)} %get-tuple-element.58.refs_2_), custom_call_target="tpu_custom_call" | custom-call | bytes 1024 | tf_op jit(solution)/shard_map/place_back/pallas_call | solution.py:64
  76.6 0.0 collective-permute-done.6.refs_1_
  76.7 4.0 %write_rows.5 = (f32[256,8192]{1,0:T(8,128)}, s32[8,128]{1,0:T(8,128)S(1)}) custom-call(s32[3]{0:T(128)S(1)} %pad_add_fusion.at, bf16[32,64,256]{2,1,0:T(8,128)(2,1)S(1)} %collective-permute-done.4.refs_0_, bf16[32,64,256]{2,1,0:T(8,128)(2,1)} %collective-permute-done.6.refs_1_, ...), custom_call_target="tpu_custom_call", output_to_operand_aliasing={{0}: (3, {})} | custom-call | bytes 1024 | tf_op jit(solution)/shard_map/write_rows/pallas_call | solution.py:64
  80.6 0.5 collective-permute-done.8.refs_1_
  81.1 2.6 %all-to-all-done.2.refs_0_ = bf16[16,64,256]{2,1,0:T(8,128)(2,1)S(1)} async-done(((bf16[16,64,256]{2,1,0:T(8,128)(2,1)}), bf16[16,64,256]{2,1,0:T(8,128)(2,1)S(1)}, u32[]{:S(2)}, u32[]{:S(2)}) %all-to-all-start.2) | async-done | bytes 524320 | tf_op jit(solution)/shard_map/all_to_all | solution.py:487
  83.7 2.1 %collective-permute-start.9 = (bf16[16,64,256]{2,1,0:T(8,128)(2,1)S(1)}, bf16[16,64,256]{2,1,0:T(8,128)(2,1)S(1)}, u32[]{:S(2)}, u32[]{:S(2)}) collective-permute-start(bf16[16,64,256]{2,1,0:T(8,128)(2,1)S(1)} %all-to-all-done.2.refs_0_), channel_id=1, source_target_pairs={{0,32},{32,0},{1,33},{33,1},{2,34},{34,2},{3,35},{35,3},{4,36},{36... | collective-permute-start | bytes 1572872 | tf_op jit(solution)/shard_map/ppermute | solution.py:468
  85.8 0.0 collective-permute-start.10
  85.8 1.7 %write_rows.6 = (bf16[16,2,256,256]{3,2,1,0:T(8,128)(2,1)}, s32[8,128]{1,0:T(8,128)S(1)}) custom-call(s32[3]{0:T(128)S(1)} %pad_add_fusion.at, bf16[16,64,256]{2,1,0:T(8,128)(2,1)S(1)} %all-to-all-done.2.refs_0_, bf16[16,64,256]{2,1,0:T(8,128)(2,1)S(1)} %collective-permute-done.8.refs_1_, ...), custom_call_target="tpu_custom_call", output_to_operand_aliasing={{0}: (3, {})} | custom-call | bytes 38797312 | tf_op jit(solution)/shard_map/write_rows/pallas_call | solution.py:64
  87.5 0.0 collective-permute-done.9.refs_0_
  87.5 0.6 collective-permute-done.10.refs_1_
  88.1 1.7 %write_rows.7 = (bf16[16,2,256,256]{3,2,1,0:T(8,128)(2,1)}, s32[8,128]{1,0:T(8,128)}) custom-call(s32[3]{0:T(128)S(1)} %pad_add_fusion.at, bf16[16,64,256]{2,1,0:T(8,128)(2,1)S(1)} %collective-permute-done.9.refs_0_, bf16[16,64,256]{2,1,0:T(8,128)(2,1)S(1)} %collective-permute-done.10.refs_1_, ...), custom_call_target="tpu_custom_call", output_to_operand_aliasing={{0}: (3, {})} | custom-call | bytes 1024 | tf_op jit(solution)/shard_map/write_rows/pallas_call | solution.py:64
Async XLA Ops:
  2.9 4.0 %collective-permute-start = (bf16[32,64,256]{2,1,0:T(8,128)(2,1)S(1)}, bf16[32,64,256]{2,1,0:T(8,128)(2,1)S(1)}, u32[]{:S(2)}, u32[]{:S(2)}) collective-permute-start(bf16[32,64,256]{2,1,0:T(8,128)(2,1)S(1)} %get-tuple-element.39), channel_id=1, source_target_pairs={{0,32},{32,0},{1,33},{33,1},{2,34},{34,2},{3,35},{35,3},{4,36},{36... | collective-permute-start | bytes 3145736 | tf_op jit(solution)/shard_map/ppermute | solution.py:468
  8.9 27.2 %collective-permute-start.3 = (bf16[32,64,256]{2,1,0:T(8,128)(2,1)}, bf16[32,64,256]{2,1,0:T(8,128)(2,1)S(1)}, u32[]{:S(2)}, u32[]{:S(2)}) collective-permute-start(bf16[32,64,256]{2,1,0:T(8,128)(2,1)} %get-tuple-element.47), channel_id=1, source_target_pairs={{0,64},{64,0},{1,65},{65,1},{2,66},{66,2},{3,67},{67,3},{4,68},{68... | collective-permute-start | bytes 3145736 | tf_op jit(solution)/shard_map/ppermute | solution.py:471
  10.3 25.8 %all-to-all-start = ((bf16[32,64,256]{2,1,0:T(8,128)(2,1)}), bf16[32,64,256]{2,1,0:T(8,128)(2,1)S(1)}, u32[]{:S(2)}, u32[]{:S(2)}) async-start(bf16[32,64,256]{2,1,0:T(8,128)(2,1)} %get-tuple-element.48), calls=%async_computation | async-start | bytes 2097152 | tf_op jit(solution)/shard_map/all_to_all | solution.py:463
  22.1 2.3 %collective-permute-start.1 = (bf16[32,32,256]{2,1,0:T(8,128)(2,1)S(1)}, bf16[32,32,256]{2,1,0:T(8,128)(2,1)S(1)}, u32[]{:S(2)}, u32[]{:S(2)}) collective-permute-start(bf16[32,32,256]{2,1,0:T(8,128)(2,1)S(1)} %get-tuple-element.43), channel_id=1, source_target_pairs={{0,32},{32,0},{1,33},{33,1},{2,34},{34,2},{3,35},{35,3},{4,36},{36... | collective-permute-start | bytes 1572872 | tf_op jit(solution)/shard_map/ppermute | solution.py:468
  22.8 2.3 %collective-permute-start.2 = (bf16[32,32,256]{2,1,0:T(8,128)(2,1)S(1)}, bf16[32,32,256]{2,1,0:T(8,128)(2,1)S(1)}, u32[]{:S(2)}, u32[]{:S(2)}) collective-permute-start(bf16[32,32,256]{2,1,0:T(8,128)(2,1)S(1)} %get-tuple-element.44), channel_id=1, source_target_pairs={{0,32},{32,0},{1,33},{33,1},{2,34},{34,2},{3,35},{35,3},{4,36},{36... | collective-permute-start | bytes 1572872 | tf_op jit(solution)/shard_map/ppermute | solution.py:468
  37.9 9.7 %collective-permute-start.5 = (bf16[32,64,256]{2,1,0:T(8,128)(2,1)}, bf16[32,64,256]{2,1,0:T(8,128)(2,1)S(1)}, u32[]{:S(2)}, u32[]{:S(2)}) collective-permute-start(bf16[32,64,256]{2,1,0:T(8,128)(2,1)} %get-tuple-element.50.refs_1_), channel_id=1, source_target_pairs={{0,32},{32,0},{1,33},{33,1},{2,34},{34,2},{3,35},{35,3},{4,36},{36... | collective-permute-start | bytes 3145736 | tf_op jit(solution)/shard_map/ppermute | solution.py:468
  40.2 24.9 %collective-permute-start.4 = (bf16[32,64,256]{2,1,0:T(8,128)(2,1)}, bf16[32,64,256]{2,1,0:T(8,128)(2,1)S(1)}, u32[]{:S(2)}, u32[]{:S(2)}) collective-permute-start(bf16[32,64,256]{2,1,0:T(8,128)(2,1)} %get-tuple-element.50.refs_1_), channel_id=1, source_target_pairs={{0,64},{64,0},{1,65},{65,1},{2,66},{66,2},{3,67},{67,3},{4,68},{68... | collective-permute-start | bytes 3145736 | tf_op jit(solution)/shard_map/ppermute | solution.py:471
  40.2 23.6 %all-to-all-start.1 = ((bf16[32,64,256]{2,1,0:T(8,128)(2,1)}), bf16[32,64,256]{2,1,0:T(8,128)(2,1)S(1)}, u32[]{:S(2)}, u32[]{:S(2)}) async-start(bf16[32,64,256]{2,1,0:T(8,128)(2,1)} %get-tuple-element.50.refs_1_), calls=%async_computation.1 | async-start | bytes 2097152 | tf_op jit(solution)/shard_map/all_to_all | solution.py:463
  66.8 6.6 %collective-permute-start.7 = (bf16[32,64,256]{2,1,0:T(8,128)(2,1)S(1)}, bf16[32,64,256]{2,1,0:T(8,128)(2,1)}, u32[]{:S(2)}, u32[]{:S(2)}) collective-permute-start(bf16[32,64,256]{2,1,0:T(8,128)(2,1)S(1)} %all-to-all-done.1), channel_id=1, source_target_pairs={{0,32},{32,0},{1,33},{33,1},{2,34},{34,2},{3,35},{35,3},{4,36},{36... | collective-permute-start | bytes 3145736 | tf_op jit(solution)/shard_map/ppermute | solution.py:468
  67.7 8.9 %collective-permute-start.6 = (bf16[32,64,256]{2,1,0:T(8,128)(2,1)S(1)}, bf16[32,64,256]{2,1,0:T(8,128)(2,1)}, u32[]{:S(2)}, u32[]{:S(2)}) collective-permute-start(bf16[32,64,256]{2,1,0:T(8,128)(2,1)S(1)} %collective-permute-done.4.refs_0_), channel_id=1, source_target_pairs={{0,32},{32,0},{1,33},{33,1},{2,34},{34,2},{3,35},{35,3},{4,36},{36... | collective-permute-start | bytes 3145736 | tf_op jit(solution)/shard_map/ppermute | solution.py:468
  67.8 13.3 %collective-permute-start.8 = (bf16[16,64,256]{2,1,0:T(8,128)(2,1)}, bf16[16,64,256]{2,1,0:T(8,128)(2,1)S(1)}, u32[]{:S(2)}, u32[]{:S(2)}) collective-permute-start(bf16[16,64,256]{2,1,0:T(8,128)(2,1)} %get-tuple-element.62), channel_id=1, source_target_pairs={{0,64},{64,0},{1,65},{65,1},{2,66},{66,2},{3,67},{67,3},{4,68},{68... | collective-permute-start | bytes 1572872 | tf_op jit(solution)/shard_map/ppermute | solution.py:471
  67.8 15.8 %all-to-all-start.2 = ((bf16[16,64,256]{2,1,0:T(8,128)(2,1)}), bf16[16,64,256]{2,1,0:T(8,128)(2,1)S(1)}, u32[]{:S(2)}, u32[]{:S(2)}) async-start(bf16[16,64,256]{2,1,0:T(8,128)(2,1)} %get-tuple-element.61), calls=%async_computation.2 | async-start | bytes 1048576 | tf_op jit(solution)/shard_map/all_to_all | solution.py:487
  83.7 3.8 %collective-permute-start.9 = (bf16[16,64,256]{2,1,0:T(8,128)(2,1)S(1)}, bf16[16,64,256]{2,1,0:T(8,128)(2,1)S(1)}, u32[]{:S(2)}, u32[]{:S(2)}) collective-permute-start(bf16[16,64,256]{2,1,0:T(8,128)(2,1)S(1)} %all-to-all-done.2.refs_0_), channel_id=1, source_target_pairs={{0,32},{32,0},{1,33},{33,1},{2,34},{34,2},{3,35},{35,3},{4,36},{36... | collective-permute-start | bytes 1572872 | tf_op jit(solution)/shard_map/ppermute | solution.py:468
  85.8 2.3 %collective-permute-start.10 = (bf16[16,64,256]{2,1,0:T(8,128)(2,1)S(1)}, bf16[16,64,256]{2,1,0:T(8,128)(2,1)S(1)}, u32[]{:S(2)}, u32[]{:S(2)}) collective-permute-start(bf16[16,64,256]{2,1,0:T(8,128)(2,1)S(1)} %collective-permute-done.8.refs_1_), channel_id=1, source_target_pairs={{0,32},{32,0},{1,33},{33,1},{2,34},{34,2},{3,35},{35,3},{4,36},{36... | collective-permute-start | bytes 1572872 | tf_op jit(solution)/shard_map/ppermute | solution.py:468

commit v10 on v9

--- a/solution.py
+++ b/solution.py
@@ -139,15 +139,11 @@
     return out
 
 
-def add_theirs(order, rows, tiles, picked):
-    def body(at, x_ref, t_ref, p_ref, o_ref, q_ref, held, sems, picked_sems):
+def add_theirs(order, rows, tiles):
+    def body(at, x_ref, t_ref, o_ref, held, sems):
         def store(p):
             some = pl.ds(p * PER, PER)
             return pltpu.make_async_copy(held.at[some], o_ref.at[some], sems.at[p])
-
-        def copy(p):
-            some = pl.ds(p * PER, PER)
-            return pltpu.make_async_copy(p_ref.at[some], q_ref.at[some], picked_sems.at[p])
 
         def work(p):
             for k in range(PER):
@@ -156,24 +152,38 @@
                 held[at_slot] = (x_ref[:, columns(g)] + t_ref[at_slot].astype(F32)).astype(BF)
             store(p).start()
 
+        each(PARTS, work)
+        each(PARTS, lambda p: store(p).wait())
+
+    return order.run(
+        body,
+        "add_theirs",
+        [in_vmem(x) for x in (rows, tiles)],
+        [VMEM] * 2,
+        [pltpu.HBM((SHARDS, QUARTER, WIDTH), BF)],
+        [HBM],
+        [pltpu.VMEM((SHARDS, QUARTER, WIDTH), BF), pltpu.SemaphoreType.DMA((PARTS,))],
+    )[0]
+
+
+def store_tiles(order, tiles):
+    def body(at, x_ref, o_ref, sems):
+        def copy(p):
+            some = pl.ds(p * PER, PER)
+            return pltpu.make_async_copy(x_ref.at[some], o_ref.at[some], sems.at[p])
+
         each(PARTS, lambda p: copy(p).start())
-        each(PARTS, work)
         each(PARTS, lambda p: copy(p).wait())
-        each(PARTS, lambda p: store(p).wait())
-
-    return order.run(
-        body,
-        "add_theirs",
-        [in_vmem(x) for x in (rows, tiles, picked)],
-        [VMEM] * 3,
-        [pltpu.HBM((SHARDS, QUARTER, WIDTH), BF)] * 2,
-        [HBM] * 2,
-        [
-            pltpu.VMEM((SHARDS, QUARTER, WIDTH), BF),
-            pltpu.SemaphoreType.DMA((PARTS,)),
-            pltpu.SemaphoreType.DMA((PARTS,)),
-        ],
-    )
+
+    return order.run(
+        body,
+        "store_tiles",
+        [in_vmem(tiles)],
+        [VMEM],
+        [pltpu.HBM(tiles.shape, BF)],
+        [HBM],
+        [pltpu.SemaphoreType.DMA((PARTS,))],
+    )[0]
 
 
 def cast_own(order, policy):
@@ -269,32 +279,45 @@
 
 
 def blend_rows(order, own, other, anchor):
-    def body(at, x_ref, t_ref, a_ref, o_ref, held, sems):
-        def store(p):
+    def body(at, x_ref, t_ref, a_ref, o_ref, *rest):
+        planes, held, sems = rest[:2], rest[2], rest[3]
+
+        def stores(xh, p):
             some = pl.ds(p * PER, PER)
-            return pltpu.make_async_copy(held.at[some], o_ref.at[some], sems.at[p])
-
-        def work(p):
+            all_some = pl.ds(xh * 16 + p * PER, PER)
+            ends = (o_ref.at[all_some], planes[xh].at[some])
+            return [
+                pltpu.make_async_copy(held.at[all_some], end, sems.at[i, xh, p])
+                for i, end in enumerate(ends)
+            ]
+
+        def work(xh, p):
             for k in range(PER):
-                g = p * PER + k
+                g = xh * 16 + p * PER + k
                 total = x_ref[g].astype(F32) + t_ref[g].astype(F32)
                 new = (1.0 - blend_rate) * a_ref[g].astype(F32) + (blend_rate / GROUPS) * total
                 held[g] = new.astype(BF)
-            store(p).start()
-
-        each(PARTS, work)
-        each(PARTS, lambda p: store(p).wait())
-
-    (out,) = order.run(
+            for store in stores(xh, p):
+                store.start()
+
+        def finish(xh, p):
+            for store in stores(xh, p):
+                store.wait()
+
+        for xh in range(2):
+            each(4, lambda p, xh=xh: work(xh, p))
+        for xh in range(2):
+            each(4, lambda p, xh=xh: finish(xh, p))
+
+    return order.run(
         body,
         "blend_rows",
         [in_vmem(x) for x in (own, other, anchor)],
         [VMEM] * 3,
-        [pltpu.HBM((SHARDS, QUARTER, WIDTH), BF)],
-        [HBM],
-        [pltpu.VMEM((SHARDS, QUARTER, WIDTH), BF), pltpu.SemaphoreType.DMA((PARTS,))],
-    )
-    return out
+        [pltpu.HBM((n, QUARTER, WIDTH), BF) for n in (SHARDS, 16, 16)],
+        [HBM] * 3,
+        [pltpu.VMEM((SHARDS, QUARTER, WIDTH), BF), pltpu.SemaphoreType.DMA((2, 2, 4))],
+    )
 
 
 def plane(at, same):
@@ -384,8 +407,9 @@
 
 def write_rows(order, wide_pieces, placed_pieces, blended, anchor, size=1024, late_in_hbm=False):
     n, m = len(wide_pieces), len(placed_pieces)
-    flat = [tiles for tiles, _, _ in wide_pieces]
-    late = n - 1
+    counts = [len(arrays) for arrays, _, _ in wide_pieces]
+    flat = [x for arrays, _, _ in wide_pieces for x in arrays]
+    late = len(flat) - 1
     outs = [pltpu.HBM((ROWS, D), F32)] * (n > 0) + [pltpu.HBM((16, 2, ROWS, WIDTH), BF)] * (m > 0)
     earlier = [x for x, k in ((blended, n), (anchor, m)) if k and x is not None]
 
@@ -410,7 +434,11 @@
 
         def work(i, tiles, p):
             for k in range(PER):
-                wide[i, :, columns(p * PER + k)] = tiles[slot(p, k)].astype(F32)
+                if len(tiles) == 1:
+                    tile = tiles[0][slot(p, k)]
+                else:
+                    tile = tiles[k % 2][p * (PER // 2) + k // 2]
+                wide[i, :, columns(p * PER + k)] = tile.astype(F32)
             copy(i, p).start()
 
         if n:
@@ -422,7 +450,8 @@
         for i in range(n):
             if i == n - 1:
                 last.wait()
-            each(PARTS, lambda p, i=i, tiles=flat_refs[i]: work(i, tiles, p))
+            tiles = flat_refs[sum(counts[:i]) : sum(counts[: i + 1])]
+            each(PARTS, lambda p, i=i, tiles=tiles: work(i, tiles, p))
         for i in range(n):
             each(PARTS, lambda p, i=i: copy(i, p).wait())
         for i in range(m):
@@ -472,15 +501,14 @@
 
     theirs = core(cast_rows(order, policy))
     picked, rows = pick_rows(order, shards, policy)
-    theirs, picked = add_theirs(order, rows, theirs, picked)
-    other = chip(theirs)
-    fetched = exchange(picked)
+    other = chip(add_theirs(order, rows, theirs))
+    fetched = exchange(store_tiles(order, picked))
     own = add_own(order, policy, [core(tiles) for tiles in cast_own(order, policy)])
 
-    own = blend_rows(order, own, other, fetched)
+    own, *planes = blend_rows(order, own, other, fetched)
     finished = chip(own)
     back = exchange(own)
-    pieces = [(core(own), False, True), (own, True, True)]
+    pieces = [([core(tiles) for tiles in planes], False, True), ([own], True, True)]
     (blended,) = write_rows(order, pieces, [], None, None, WRITE_COST, late_in_hbm=True)
 
     first, high = split_planes(order, finished, back)
@@ -488,7 +516,7 @@
     back_second = chip(high)
     finished, back = order.behind(finished), order.behind(back)
     new_anchor = place_back(order, back, core(back))
-    pieces = [(finished, True, False), (core(finished), False, False)]
+    pieces = [([finished], True, False), ([core(finished)], False, False)]
     (blended,) = write_rows(order, pieces, [], blended, None)
     back_second = order.behind(back_second)
     back_first = order.behind(back_first)

time: 90.4 us -> 89.4 us (0.989)
  waiting for transfers between devices: 28.3 us -> 24.6 us
  Pallas kernels: 28.9 us -> 30.3 us
  starting transfers between devices: 31.7 us -> 32.9 us
    all_to_all x2, waiting for transfers between devices: 21 us -> 16 us  [exchange(): lax.all_to_all(tiles, AXES, split_axis=0, concat_axis=0, axis_index_group...]
    ppermute x8 -> x9, waiting for transfers between devices: 2.82 us -> 5.22 us  [core(): return lax.ppermute(tiles, 'c', swap)]
    ppermute x8 -> x9, starting transfers between devices: 7.81 us -> 9.39 us  [core(): return lax.ppermute(tiles, 'c', swap)]
    pallas_call x12 -> x13, Pallas kernels: 28.9 us -> 30.3 us  [run(): pl.pallas_call(ordered, out_shape=[*outs, TOKEN], grid_spec=pltpu.Prefetc...]
  transfers between devices with their start and end apart: 14 -> 15, of which waited for: 8 -> 10; matrix products, arithmetic and copies ran while one was open for 0% -> 0% of each run, Pallas kernels for 22% -> 24%
where the time goes in v10:
time: 89.4 us; the launch traced here: 88.7 us
  starting transfers between devices  32.9 us (37%)
  Pallas kernels  30.3 us (34%)
  waiting for transfers between devices  24.6 us (28%)
    pallas_call x13, Pallas kernels, run(): pl.pallas_call(ordered, out_shape=[*outs, TOKEN], grid_spec=pltpu.Prefetc...  30.3 us
    all_to_all x2, starting transfers between devices, exchange(): lax.all_to_all(tiles, AXES, split_axis=0, concat_axis=0, axis_index_group...  16.7 us
    all_to_all x2, waiting for transfers between devices, exchange(): lax.all_to_all(tiles, AXES, split_axis=0, concat_axis=0, axis_index_group...  16 us
    ppermute x9, starting transfers between devices, core(): return lax.ppermute(tiles, 'c', swap)  9.39 us
    all_to_all x1, starting transfers between devices, per_device(): lax.all_to_all(first, ('y', 'z'), split_axis=0, concat_axis=0, tiled=True)  5.31 us
    ppermute x9, waiting for transfers between devices, core(): return lax.ppermute(tiles, 'c', swap)  5.22 us
    all_to_all x1, waiting for transfers between devices, per_device(): lax.all_to_all(first, ('y', 'z'), split_axis=0, concat_axis=0, tiled=True)  2.32 us
  transfers between devices with their start and end apart: 15, of which 10 were waited for; matrix products, arithmetic and copies ran while one was open for 0% of the time, Pallas kernels for 24%

profile of v10, /device:TPU:1, one launch (start us, length us, event | category | flops | bytes accessed | tf_op | source)
XLA Modules:
  0.0 88.7 jit_solution(11256849082388547952)
XLA Ops:
  0.6 0.1 pad_add_fusion.at
  0.7 2.2 %cast_rows.1 = (bf16[32,64,256]{2,1,0:T(8,128)(2,1)S(1)}, s32[8,128]{1,0:T(8,128)S(1)}) custom-call(s32[3]{0:T(128)S(1)} %pad_add_fusion.at, f32[256,8192]{1,0:T(8,128)} %bitcast.15), custom_call_target="tpu_custom_call" | custom-call | bytes 1024 | tf_op jit(solution)/shard_map/cast_rows/pallas_call | solution.py:64
  2.9 1.5 %collective-permute-start = (bf16[32,64,256]{2,1,0:T(8,128)(2,1)S(1)}, bf16[32,64,256]{2,1,0:T(8,128)(2,1)S(1)}, u32[]{:S(2)}, u32[]{:S(2)}) collective-permute-start(bf16[32,64,256]{2,1,0:T(8,128)(2,1)S(1)} %get-tuple-element.43), channel_id=1, source_target_pairs={{0,32},{32,0},{1,33},{33,1},{2,34},{34,2},{3,35},{35,3},{4,36},{36... | collective-permute-start | bytes 3145736 | tf_op jit(solution)/shard_map/ppermute | solution.py:497
  4.4 2.5 %pick_rows.1 = (bf16[2,16,64,256]{3,2,1,0:T(8,128)(2,1)S(1)}, f32[64,8192]{1,0:T(8,128)S(1)}, s32[8,128]{1,0:T(8,128)S(1)}) custom-call(s32[3]{0:T(128)S(1)} %pad_add_fusion.at, bf16[16,2,256,256]{3,2,1,0:T(8,128)(2,1)} %bitcast.20, f32[256,8192]{1,0:T(8,128)} %bitcast.16, s32[8,128]{1,0:T(8,128)S(1)} %get-tuple-element.40.refs_2_), custom_call_target="tpu_custom_call" | custom-call | bytes 1024 | tf_op jit(solution)/shard_map/pick_rows/pallas_call | solution.py:64
  6.9 0.0 collective-permute-done.refs_1_
  6.9 1.6 %add_theirs.1 = (bf16[32,64,256]{2,1,0:T(8,128)(2,1)}, s32[8,128]{1,0:T(8,128)S(1)}) custom-call(s32[3]{0:T(128)S(1)} %pad_add_fusion.at, f32[64,8192]{1,0:T(8,128)S(1)} %get-tuple-element.42.refs_0_, bf16[32,64,256]{2,1,0:T(8,128)(2,1)S(1)} %collective-permute-done.refs_1_, s32[8,128]{1,0:T(8,128)S(1)} %get-tuple-element.44.refs_2_), custom_call_target="tpu_custom_call" | custom-call | bytes 1024 | tf_op jit(solution)/shard_map/add_theirs/pallas_call | solution.py:64
  8.5 1.4 %collective-permute-start.3 = (bf16[32,64,256]{2,1,0:T(8,128)(2,1)}, bf16[32,64,256]{2,1,0:T(8,128)(2,1)S(1)}, u32[]{:S(2)}, u32[]{:S(2)}) collective-permute-start(bf16[32,64,256]{2,1,0:T(8,128)(2,1)} %get-tuple-element.51), channel_id=1, source_target_pairs={{0,64},{64,0},{1,65},{65,1},{2,66},{66,2},{3,67},{67,3},{4,68},{68... | collective-permute-start | bytes 3145736 | tf_op jit(solution)/shard_map/ppermute | solution.py:500
  9.9 1.6 %store_tiles.1 = (bf16[32,64,256]{2,1,0:T(8,128)(2,1)}, s32[8,128]{1,0:T(8,128)S(1)}) custom-call(s32[3]{0:T(128)S(1)} %pad_add_fusion.at, bf16[32,64,256]{2,1,0:T(8,128)(2,1)S(1)} %bitcast.14, s32[8,128]{1,0:T(8,128)S(1)} %get-tuple-element.45.refs_1_), custom_call_target="tpu_custom_call" | custom-call | bytes 1024 | tf_op jit(solution)/shard_map/store_tiles/pallas_call | solution.py:64
  11.5 9.6 %all-to-all-start = ((bf16[32,64,256]{2,1,0:T(8,128)(2,1)}), bf16[32,64,256]{2,1,0:T(8,128)(2,1)S(1)}, u32[]{:S(2)}, u32[]{:S(2)}) async-start(bf16[32,64,256]{2,1,0:T(8,128)(2,1)} %get-tuple-element.52), calls=%async_computation | async-start | bytes 2097152 | tf_op jit(solution)/shard_map/all_to_all | solution.py:492
  21.1 2.2 %cast_own.1 = (bf16[32,32,256]{2,1,0:T(8,128)(2,1)S(1)}, bf16[32,32,256]{2,1,0:T(8,128)(2,1)S(1)}, s32[8,128]{1,0:T(8,128)S(1)}) custom-call(s32[3]{0:T(128)S(1)} %pad_add_fusion.at, f32[256,8192]{1,0:T(8,128)} %bitcast.17, s32[8,128]{1,0:T(8,128)S(1)} %get-tuple-element.46.refs_1_), custom_call_target="tpu_custom_call" | custom-call | bytes 1024 | tf_op jit(solution)/shard_map/cast_own/pallas_call | solution.py:64
  23.3 0.7 collective-permute-start.1
  24.0 0.1 collective-permute-start.2
  24.1 1.4 %collective-permute-done.1.refs_1_ = bf16[32,32,256]{2,1,0:T(8,128)(2,1)S(1)} collective-permute-done((bf16[32,32,256]{2,1,0:T(8,128)(2,1)S(1)}, bf16[32,32,256]{2,1,0:T(8,128)(2,1)S(1)}, u32[]{:S(2)}, u32[]{:S(2)}) %collective-permute-start.1) | collective-permute-done | bytes 524320 | tf_op jit(solution)/shard_map/ppermute | solution.py:497
  25.5 0.7 collective-permute-done.2.refs_2_
  26.3 2.2 %add_own.1 = (bf16[32,64,256]{2,1,0:T(8,128)(2,1)S(1)}, s32[8,128]{1,0:T(8,128)S(1)}) custom-call(s32[3]{0:T(128)S(1)} %pad_add_fusion.at, f32[256,8192]{1,0:T(8,128)} %bitcast.18, bf16[32,32,256]{2,1,0:T(8,128)(2,1)S(1)} %collective-permute-done.1.refs_1_, bf16[32,32,256]{2,1,0:T(8,128)(2,1)S(1)} %collective-permute-done.2.refs_2_, ...), custom_call_target="tpu_custom_call" | custom-call | bytes 1024 | tf_op jit(solution)/shard_map/add_own/pallas_call | solution.py:64
  28.5 8.8 %all-to-all-done.refs_2_ = bf16[32,64,256]{2,1,0:T(8,128)(2,1)S(1)} async-done(((bf16[32,64,256]{2,1,0:T(8,128)(2,1)}), bf16[32,64,256]{2,1,0:T(8,128)(2,1)S(1)}, u32[]{:S(2)}, u32[]{:S(2)}) %all-to-all-start) | async-done | bytes 1048608 | tf_op jit(solution)/shard_map/all_to_all | solution.py:492
  37.3 0.0 collective-permute-done.3.refs_1_
  37.3 2.0 %blend_rows.1 = (bf16[32,64,256]{2,1,0:T(8,128)(2,1)}, bf16[16,64,256]{2,1,0:T(8,128)(2,1)}, bf16[16,64,256]{2,1,0:T(8,128)(2,1)}, s32[8,128]{1,0:T(8,128)S(1)}) custom-call(s32[3]{0:T(128)S(1)} %pad_add_fusion.at, bf16[32,64,256]{2,1,0:T(8,128)(2,1)S(1)} %get-tuple-element.50.refs_0_, bf16[32,64,256]{2,1,0:T(8,128)(2,1)S(1)} %collective-permute-done.3.refs_1_, ...), custom_call_target="tpu_custom_call" | custom-call | bytes 1024 | tf_op jit(solution)/shard_map/blend_rows/pallas_call | solution.py:64
  39.4 0.1 collective-permute-start.4
  39.4 7.1 %all-to-all-start.1 = ((bf16[32,64,256]{2,1,0:T(8,128)(2,1)}), bf16[32,64,256]{2,1,0:T(8,128)(2,1)S(1)}, u32[]{:S(2)}, u32[]{:S(2)}) async-start(bf16[32,64,256]{2,1,0:T(8,128)(2,1)} %get-tuple-element.54.refs_2_), calls=%async_computation.1 | async-start | bytes 2097152 | tf_op jit(solution)/shard_map/all_to_all | solution.py:492
  46.6 1.5 %collective-permute-start.5 = (bf16[16,64,256]{2,1,0:T(8,128)(2,1)}, bf16[16,64,256]{2,1,0:T(8,128)(2,1)S(1)}, u32[]{:S(2)}, u32[]{:S(2)}) collective-permute-start(bf16[16,64,256]{2,1,0:T(8,128)(2,1)} %get-tuple-element.55), channel_id=1, source_target_pairs={{0,32},{32,0},{1,33},{33,1},{2,34},{34,2},{3,35},{35,3},{4,36},{36... | collective-permute-start | bytes 1572872 | tf_op jit(solution)/shard_map/ppermute | solution.py:497
  48.1 0.1 collective-permute-start.6
  48.2 1.7 %collective-permute-done.5.refs_0_ = bf16[16,64,256]{2,1,0:T(8,128)(2,1)S(1)} collective-permute-done((bf16[16,64,256]{2,1,0:T(8,128)(2,1)}, bf16[16,64,256]{2,1,0:T(8,128)(2,1)S(1)}, u32[]{:S(2)}, u32[]{:S(2)}) %collective-permute-start.5) | collective-permute-done | bytes 524320 | tf_op jit(solution)/shard_map/ppermute | solution.py:497
  49.8 0.7 collective-permute-done.6.refs_1_
  50.6 4.0 %write_rows.4 = (f32[256,8192]{1,0:T(8,128)}, s32[8,128]{1,0:T(8,128)S(1)}) custom-call(s32[3]{0:T(128)S(1)} %pad_add_fusion.at, bf16[16,64,256]{2,1,0:T(8,128)(2,1)S(1)} %collective-permute-done.5.refs_0_, bf16[16,64,256]{2,1,0:T(8,128)(2,1)S(1)} %collective-permute-done.6.refs_1_, bf16[32,64,256]{2,1,0:T(8,128)(2,1)} %get-tuple-element.54.refs_2_, ...), custom_call_target="tpu_custom_call" | custom-call | bytes 11534336 | tf_op jit(solution)/shard_map/write_rows/pallas_call | solution.py:64
  54.5 7.2 %all-to-all-done.1 = bf16[32,64,256]{2,1,0:T(8,128)(2,1)S(1)} async-done(((bf16[32,64,256]{2,1,0:T(8,128)(2,1)}), bf16[32,64,256]{2,1,0:T(8,128)(2,1)S(1)}, u32[]{:S(2)}, u32[]{:S(2)}) %all-to-all-start.1) | async-done | bytes 1048608 | tf_op jit(solution)/shard_map/all_to_all | solution.py:492
  61.7 0.4 collective-permute-done.4.refs_0_
  62.1 1.6 %split_planes.1 = (bf16[16,64,256]{2,1,0:T(8,128)(2,1)}, bf16[16,64,256]{2,1,0:T(8,128)(2,1)}, s32[8,128]{1,0:T(8,128)S(1)}) custom-call(s32[3]{0:T(128)S(1)} %pad_add_fusion.at, bf16[2,16,64,256]{3,2,1,0:T(8,128)(2,1)S(1)} %bitcast.13, bf16[2,16,64,256]{3,2,1,0:T(8,128)(2,1)S(1)} %bitcast.11, s32[8,128]{1,0:T(8,128)S(1)} %get-tuple-element.58.refs_2_), custom_call_target="tpu_custom_call" | custom-call | bytes 1024 | tf_op jit(solution)/shard_map/split_planes/pallas_call | solution.py:64
  63.7 3.2 %collective-permute-start.8 = (bf16[32,64,256]{2,1,0:T(8,128)(2,1)S(1)}, bf16[32,64,256]{2,1,0:T(8,128)(2,1)}, u32[]{:S(2)}, u32[]{:S(2)}) collective-permute-start(bf16[32,64,256]{2,1,0:T(8,128)(2,1)S(1)} %all-to-all-done.1), channel_id=1, source_target_pairs={{0,32},{32,0},{1,33},{33,1},{2,34},{34,2},{3,35},{35,3},{4,36},{36... | collective-permute-start | bytes 3145736 | tf_op jit(solution)/shard_map/ppermute | solution.py:497
  66.9 0.1 collective-permute-start.7
  67.0 0.0 collective-permute-start.9
  67.0 5.3 %all-to-all-start.2 = ((bf16[16,64,256]{2,1,0:T(8,128)(2,1)}), bf16[16,64,256]{2,1,0:T(8,128)(2,1)S(1)}, u32[]{:S(2)}, u32[]{:S(2)}) async-start(bf16[16,64,256]{2,1,0:T(8,128)(2,1)} %get-tuple-element.67), calls=%async_computation.2 | async-start | bytes 1048576 | tf_op jit(solution)/shard_map/all_to_all | solution.py:515
  72.3 0.0 collective-permute-done.8
  72.3 3.3 %place_back.1 = (bf16[16,2,256,256]{3,2,1,0:T(8,128)(2,1)}, s32[8,128]{1,0:T(8,128)S(1)}) custom-call(s32[3]{0:T(128)S(1)} %pad_add_fusion.at, bf16[2,16,64,256]{3,2,1,0:T(8,128)(2,1)S(1)} %bitcast.12, bf16[2,16,64,256]{3,2,1,0:T(8,128)(2,1)} %bitcast.9.refs_1_, s32[8,128]{1,0:T(8,128)S(1)} %get-tuple-element.64.refs_2_), custom_call_target="tpu_custom_call" | custom-call | bytes 1024 | tf_op jit(solution)/shard_map/place_back/pallas_call | solution.py:64
  75.6 0.0 collective-permute-done.7.refs_1_
  75.6 4.0 %write_rows.5 = (f32[256,8192]{1,0:T(8,128)}, s32[8,128]{1,0:T(8,128)S(1)}) custom-call(s32[3]{0:T(128)S(1)} %pad_add_fusion.at, bf16[32,64,256]{2,1,0:T(8,128)(2,1)S(1)} %collective-permute-done.4.refs_0_, bf16[32,64,256]{2,1,0:T(8,128)(2,1)} %collective-permute-done.7.refs_1_, ...), custom_call_target="tpu_custom_call", output_to_operand_aliasing={{0}: (3, {})} | custom-call | bytes 1024 | tf_op jit(solution)/shard_map/write_rows/pallas_call | solution.py:64
  79.6 0.7 collective-permute-done.9.refs_1_
  80.3 2.3 %all-to-all-done.2.refs_0_ = bf16[16,64,256]{2,1,0:T(8,128)(2,1)S(1)} async-done(((bf16[16,64,256]{2,1,0:T(8,128)(2,1)}), bf16[16,64,256]{2,1,0:T(8,128)(2,1)S(1)}, u32[]{:S(2)}, u32[]{:S(2)}) %all-to-all-start.2) | async-done | bytes 524320 | tf_op jit(solution)/shard_map/all_to_all | solution.py:515
  82.6 2.1 %collective-permute-start.10 = (bf16[16,64,256]{2,1,0:T(8,128)(2,1)S(1)}, bf16[16,64,256]{2,1,0:T(8,128)(2,1)S(1)}, u32[]{:S(2)}, u32[]{:S(2)}) collective-permute-start(bf16[16,64,256]{2,1,0:T(8,128)(2,1)S(1)} %all-to-all-done.2.refs_0_), channel_id=1, source_target_pairs={{0,32},{32,0},{1,33},{33,1},{2,34},{34,2},{3,35},{35,3},{4,36},{36... | collective-permute-start | bytes 1572872 | tf_op jit(solution)/shard_map/ppermute | solution.py:497
  84.8 0.0 collective-permute-start.11
  84.8 1.7 %write_rows.6 = (bf16[16,2,256,256]{3,2,1,0:T(8,128)(2,1)}, s32[8,128]{1,0:T(8,128)S(1)}) custom-call(s32[3]{0:T(128)S(1)} %pad_add_fusion.at, bf16[16,64,256]{2,1,0:T(8,128)(2,1)S(1)} %all-to-all-done.2.refs_0_, bf16[16,64,256]{2,1,0:T(8,128)(2,1)S(1)} %collective-permute-done.9.refs_1_, ...), custom_call_target="tpu_custom_call", output_to_operand_aliasing={{0}: (3, {})} | custom-call | bytes 38797312 | tf_op jit(solution)/shard_map/write_rows/pallas_call | solution.py:64
  86.4 0.0 collective-permute-done.10.refs_0_
  86.4 0.6 collective-permute-done.11.refs_1_
  87.0 1.7 %write_rows.7 = (bf16[16,2,256,256]{3,2,1,0:T(8,128)(2,1)}, s32[8,128]{1,0:T(8,128)}) custom-call(s32[3]{0:T(128)S(1)} %pad_add_fusion.at, bf16[16,64,256]{2,1,0:T(8,128)(2,1)S(1)} %collective-permute-done.10.refs_0_, bf16[16,64,256]{2,1,0:T(8,128)(2,1)S(1)} %collective-permute-done.11.refs_1_, ...), custom_call_target="tpu_custom_call", output_to_operand_aliasing={{0}: (3, {})} | custom-call | bytes 1024 | tf_op jit(solution)/shard_map/write_rows/pallas_call | solution.py:64
Async XLA Ops:
  2.9 4.0 %collective-permute-start = (bf16[32,64,256]{2,1,0:T(8,128)(2,1)S(1)}, bf16[32,64,256]{2,1,0:T(8,128)(2,1)S(1)}, u32[]{:S(2)}, u32[]{:S(2)}) collective-permute-start(bf16[32,64,256]{2,1,0:T(8,128)(2,1)S(1)} %get-tuple-element.43), channel_id=1, source_target_pairs={{0,32},{32,0},{1,33},{33,1},{2,34},{34,2},{3,35},{35,3},{4,36},{36... | collective-permute-start | bytes 3145736 | tf_op jit(solution)/shard_map/ppermute | solution.py:497
  8.5 28.8 %collective-permute-start.3 = (bf16[32,64,256]{2,1,0:T(8,128)(2,1)}, bf16[32,64,256]{2,1,0:T(8,128)(2,1)S(1)}, u32[]{:S(2)}, u32[]{:S(2)}) collective-permute-start(bf16[32,64,256]{2,1,0:T(8,128)(2,1)} %get-tuple-element.51), channel_id=1, source_target_pairs={{0,64},{64,0},{1,65},{65,1},{2,66},{66,2},{3,67},{67,3},{4,68},{68... | collective-permute-start | bytes 3145736 | tf_op jit(solution)/shard_map/ppermute | solution.py:500
  11.5 25.8 %all-to-all-start = ((bf16[32,64,256]{2,1,0:T(8,128)(2,1)}), bf16[32,64,256]{2,1,0:T(8,128)(2,1)S(1)}, u32[]{:S(2)}, u32[]{:S(2)}) async-start(bf16[32,64,256]{2,1,0:T(8,128)(2,1)} %get-tuple-element.52), calls=%async_computation | async-start | bytes 2097152 | tf_op jit(solution)/shard_map/all_to_all | solution.py:492
  23.3 2.3 %collective-permute-start.1 = (bf16[32,32,256]{2,1,0:T(8,128)(2,1)S(1)}, bf16[32,32,256]{2,1,0:T(8,128)(2,1)S(1)}, u32[]{:S(2)}, u32[]{:S(2)}) collective-permute-start(bf16[32,32,256]{2,1,0:T(8,128)(2,1)S(1)} %get-tuple-element.47), channel_id=1, source_target_pairs={{0,32},{32,0},{1,33},{33,1},{2,34},{34,2},{3,35},{35,3},{4,36},{36... | collective-permute-start | bytes 1572872 | tf_op jit(solution)/shard_map/ppermute | solution.py:497
  24.0 2.3 %collective-permute-start.2 = (bf16[32,32,256]{2,1,0:T(8,128)(2,1)S(1)}, bf16[32,32,256]{2,1,0:T(8,128)(2,1)S(1)}, u32[]{:S(2)}, u32[]{:S(2)}) collective-permute-start(bf16[32,32,256]{2,1,0:T(8,128)(2,1)S(1)} %get-tuple-element.48), channel_id=1, source_target_pairs={{0,32},{32,0},{1,33},{33,1},{2,34},{34,2},{3,35},{35,3},{4,36},{36... | collective-permute-start | bytes 1572872 | tf_op jit(solution)/shard_map/ppermute | solution.py:497
  39.4 22.7 %collective-permute-start.4 = (bf16[32,64,256]{2,1,0:T(8,128)(2,1)}, bf16[32,64,256]{2,1,0:T(8,128)(2,1)S(1)}, u32[]{:S(2)}, u32[]{:S(2)}) collective-permute-start(bf16[32,64,256]{2,1,0:T(8,128)(2,1)} %get-tuple-element.54.refs_2_), channel_id=1, source_target_pairs={{0,64},{64,0},{1,65},{65,1},{2,66},{66,2},{3,67},{67,3},{4,68},{68... | collective-permute-start | bytes 3145736 | tf_op jit(solution)/shard_map/ppermute | solution.py:500
  39.4 22.3 %all-to-all-start.1 = ((bf16[32,64,256]{2,1,0:T(8,128)(2,1)}), bf16[32,64,256]{2,1,0:T(8,128)(2,1)S(1)}, u32[]{:S(2)}, u32[]{:S(2)}) async-start(bf16[32,64,256]{2,1,0:T(8,128)(2,1)} %get-tuple-element.54.refs_2_), calls=%async_computation.1 | async-start | bytes 2097152 | tf_op jit(solution)/shard_map/all_to_all | solution.py:492
  46.6 3.3 %collective-permute-start.5 = (bf16[16,64,256]{2,1,0:T(8,128)(2,1)}, bf16[16,64,256]{2,1,0:T(8,128)(2,1)S(1)}, u32[]{:S(2)}, u32[]{:S(2)}) collective-permute-start(bf16[16,64,256]{2,1,0:T(8,128)(2,1)} %get-tuple-element.55), channel_id=1, source_target_pairs={{0,32},{32,0},{1,33},{33,1},{2,34},{34,2},{3,35},{35,3},{4,36},{36... | collective-permute-start | bytes 1572872 | tf_op jit(solution)/shard_map/ppermute | solution.py:497
  48.1 2.5 %collective-permute-start.6 = (bf16[16,64,256]{2,1,0:T(8,128)(2,1)}, bf16[16,64,256]{2,1,0:T(8,128)(2,1)S(1)}, u32[]{:S(2)}, u32[]{:S(2)}) collective-permute-start(bf16[16,64,256]{2,1,0:T(8,128)(2,1)} %get-tuple-element.56), channel_id=1, source_target_pairs={{0,32},{32,0},{1,33},{33,1},{2,34},{34,2},{3,35},{35,3},{4,36},{36... | collective-permute-start | bytes 1572872 | tf_op jit(solution)/shard_map/ppermute | solution.py:497
  63.7 8.6 %collective-permute-start.8 = (bf16[32,64,256]{2,1,0:T(8,128)(2,1)S(1)}, bf16[32,64,256]{2,1,0:T(8,128)(2,1)}, u32[]{:S(2)}, u32[]{:S(2)}) collective-permute-start(bf16[32,64,256]{2,1,0:T(8,128)(2,1)S(1)} %all-to-all-done.1), channel_id=1, source_target_pairs={{0,32},{32,0},{1,33},{33,1},{2,34},{34,2},{3,35},{35,3},{4,36},{36... | collective-permute-start | bytes 3145736 | tf_op jit(solution)/shard_map/ppermute | solution.py:497
  66.9 8.7 %collective-permute-start.7 = (bf16[32,64,256]{2,1,0:T(8,128)(2,1)S(1)}, bf16[32,64,256]{2,1,0:T(8,128)(2,1)}, u32[]{:S(2)}, u32[]{:S(2)}) collective-permute-start(bf16[32,64,256]{2,1,0:T(8,128)(2,1)S(1)} %collective-permute-done.4.refs_0_), channel_id=1, source_target_pairs={{0,32},{32,0},{1,33},{33,1},{2,34},{34,2},{3,35},{35,3},{4,36},{36... | collective-permute-start | bytes 3145736 | tf_op jit(solution)/shard_map/ppermute | solution.py:497
  67.0 13.3 %collective-permute-start.9 = (bf16[16,64,256]{2,1,0:T(8,128)(2,1)}, bf16[16,64,256]{2,1,0:T(8,128)(2,1)S(1)}, u32[]{:S(2)}, u32[]{:S(2)}) collective-permute-start(bf16[16,64,256]{2,1,0:T(8,128)(2,1)} %get-tuple-element.68), channel_id=1, source_target_pairs={{0,64},{64,0},{1,65},{65,1},{2,66},{66,2},{3,67},{67,3},{4,68},{68... | collective-permute-start | bytes 1572872 | tf_op jit(solution)/shard_map/ppermute | solution.py:500
  67.0 15.6 %all-to-all-start.2 = ((bf16[16,64,256]{2,1,0:T(8,128)(2,1)}), bf16[16,64,256]{2,1,0:T(8,128)(2,1)S(1)}, u32[]{:S(2)}, u32[]{:S(2)}) async-start(bf16[16,64,256]{2,1,0:T(8,128)(2,1)} %get-tuple-element.67), calls=%async_computation.2 | async-start | bytes 1048576 | tf_op jit(solution)/shard_map/all_to_all | solution.py:515
  82.6 3.8 %collective-permute-start.10 = (bf16[16,64,256]{2,1,0:T(8,128)(2,1)S(1)}, bf16[16,64,256]{2,1,0:T(8,128)(2,1)S(1)}, u32[]{:S(2)}, u32[]{:S(2)}) collective-permute-start(bf16[16,64,256]{2,1,0:T(8,128)(2,1)S(1)} %all-to-all-done.2.refs_0_), channel_id=1, source_target_pairs={{0,32},{32,0},{1,33},{33,1},{2,34},{34,2},{3,35},{35,3},{4,36},{36... | collective-permute-start | bytes 1572872 | tf_op jit(solution)/shard_map/ppermute | solution.py:497
  84.8 2.3 %collective-permute-start.11 = (bf16[16,64,256]{2,1,0:T(8,128)(2,1)S(1)}, bf16[16,64,256]{2,1,0:T(8,128)(2,1)S(1)}, u32[]{:S(2)}, u32[]{:S(2)}) collective-permute-start(bf16[16,64,256]{2,1,0:T(8,128)(2,1)S(1)} %collective-permute-done.9.refs_1_), channel_id=1, source_target_pairs={{0,32},{32,0},{1,33},{33,1},{2,34},{34,2},{3,35},{35,3},{4,36},{36... | collective-permute-start | bytes 1572872 | tf_op jit(solution)/shard_map/ppermute | solution.py:497

commit v11 on v10

--- a/solution.py
+++ b/solution.py
@@ -139,11 +139,15 @@
     return out
 
 
-def add_theirs(order, rows, tiles):
-    def body(at, x_ref, t_ref, o_ref, held, sems):
+def add_theirs(order, rows, tiles, picked):
+    def body(at, x_ref, t_ref, p_ref, o_ref, q_ref, held, sems, picked_sems):
         def store(p):
             some = pl.ds(p * PER, PER)
             return pltpu.make_async_copy(held.at[some], o_ref.at[some], sems.at[p])
+
+        def copy(p):
+            some = pl.ds(p * PER, PER)
+            return pltpu.make_async_copy(p_ref.at[some], q_ref.at[some], picked_sems.at[p])
 
         def work(p):
             for k in range(PER):
@@ -152,38 +156,24 @@
                 held[at_slot] = (x_ref[:, columns(g)] + t_ref[at_slot].astype(F32)).astype(BF)
             store(p).start()
 
+        each(PARTS, lambda p: copy(p).start())
         each(PARTS, work)
+        each(PARTS, lambda p: copy(p).wait())
         each(PARTS, lambda p: store(p).wait())
 
     return order.run(
         body,
         "add_theirs",
-        [in_vmem(x) for x in (rows, tiles)],
-        [VMEM] * 2,
-        [pltpu.HBM((SHARDS, QUARTER, WIDTH), BF)],
-        [HBM],
-        [pltpu.VMEM((SHARDS, QUARTER, WIDTH), BF), pltpu.SemaphoreType.DMA((PARTS,))],
-    )[0]
-
-
-def store_tiles(order, tiles):
-    def body(at, x_ref, o_ref, sems):
-        def copy(p):
-            some = pl.ds(p * PER, PER)
-            return pltpu.make_async_copy(x_ref.at[some], o_ref.at[some], sems.at[p])
-
-        each(PARTS, lambda p: copy(p).start())
-        each(PARTS, lambda p: copy(p).wait())
-
-    return order.run(
-        body,
-        "store_tiles",
-        [in_vmem(tiles)],
-        [VMEM],
-        [pltpu.HBM(tiles.shape, BF)],
-        [HBM],
-        [pltpu.SemaphoreType.DMA((PARTS,))],
-    )[0]
+        [in_vmem(x) for x in (rows, tiles, picked)],
+        [VMEM] * 3,
+        [pltpu.HBM((SHARDS, QUARTER, WIDTH), BF)] * 2,
+        [HBM] * 2,
+        [
+            pltpu.VMEM((SHARDS, QUARTER, WIDTH), BF),
+            pltpu.SemaphoreType.DMA((PARTS,)),
+            pltpu.SemaphoreType.DMA((PARTS,)),
+        ],
+    )
 
 
 def cast_own(order, policy):
@@ -501,8 +491,9 @@
 
     theirs = core(cast_rows(order, policy))
     picked, rows = pick_rows(order, shards, policy)
-    other = chip(add_theirs(order, rows, theirs))
-    fetched = exchange(store_tiles(order, picked))
+    theirs, picked = add_theirs(order, rows, theirs, picked)
+    other = chip(theirs)
+    fetched = exchange(picked)
     own = add_own(order, policy, [core(tiles) for tiles in cast_own(order, policy)])
 
     own, *planes = blend_rows(order, own, other, fetched)

time: 89.4 us -> 89.8 us (level)
  starting transfers between devices: 32.9 us -> 34.8 us
  Pallas kernels: 30.3 us -> 29.1 us
    all_to_all x2, starting transfers between devices: 16.7 us -> 18.3 us  [exchange(): lax.all_to_all(tiles, AXES, split_axis=0, concat_axis=0, axis_index_group...]
    pallas_call x13 -> x12, Pallas kernels: 30.3 us -> 29.1 us  [run(): pl.pallas_call(ordered, out_shape=[*outs, TOKEN], grid_spec=pltpu.Prefetc...]
  transfers between devices with their start and end apart: 15 -> 15, of which waited for: 10 -> 9; matrix products, arithmetic and copies ran while one was open for 0% -> 0% of each run, Pallas kernels for 24% -> 22%
where the time goes in v11:
time: 89.8 us; the launch traced here: 89.1 us
  starting transfers between devices  34.8 us (39%)
  Pallas kernels  29.1 us (32%)
  waiting for transfers between devices  24.3 us (27%)
    pallas_call x12, Pallas kernels, run(): pl.pallas_call(ordered, out_shape=[*outs, TOKEN], grid_spec=pltpu.Prefetc...  29.1 us
    all_to_all x2, starting transfers between devices, exchange(): lax.all_to_all(tiles, AXES, split_axis=0, concat_axis=0, axis_index_group...  18.3 us
    all_to_all x2, waiting for transfers between devices, exchange(): lax.all_to_all(tiles, AXES, split_axis=0, concat_axis=0, axis_index_group...  16 us
    ppermute x9, starting transfers between devices, core(): return lax.ppermute(tiles, 'c', swap)  9.67 us
    all_to_all x1, starting transfers between devices, per_device(): lax.all_to_all(first, ('y', 'z'), split_axis=0, concat_axis=0, tiled=True)  5.37 us
    ppermute x9, waiting for transfers between devices, core(): return lax.ppermute(tiles, 'c', swap)  5.22 us
    all_to_all x1, waiting for transfers between devices, per_device(): lax.all_to_all(first, ('y', 'z'), split_axis=0, concat_axis=0, tiled=True)  2.38 us
  transfers between devices with their start and end apart: 15, of which 9 were waited for; matrix products, arithmetic and copies ran while one was open for 0% of the time, Pallas kernels for 22%

profile of v11, /device:TPU:1, one launch (start us, length us, event | category | flops | bytes accessed | tf_op | source)
XLA Modules:
  0.0 89.1 jit_solution(5819499924970120195)
XLA Ops:
  0.6 0.1 pad_add_fusion.at
  0.7 2.2 %cast_rows.1 = (bf16[32,64,256]{2,1,0:T(8,128)(2,1)S(1)}, s32[8,128]{1,0:T(8,128)S(1)}) custom-call(s32[3]{0:T(128)S(1)} %pad_add_fusion.at, f32[256,8192]{1,0:T(8,128)} %bitcast.15), custom_call_target="tpu_custom_call" | custom-call | bytes 1024 | tf_op jit(solution)/shard_map/cast_rows/pallas_call | solution.py:64
  2.9 1.5 %collective-permute-start = (bf16[32,64,256]{2,1,0:T(8,128)(2,1)S(1)}, bf16[32,64,256]{2,1,0:T(8,128)(2,1)S(1)}, u32[]{:S(2)}, u32[]{:S(2)}) collective-permute-start(bf16[32,64,256]{2,1,0:T(8,128)(2,1)S(1)} %get-tuple-element.41), channel_id=1, source_target_pairs={{0,32},{32,0},{1,33},{33,1},{2,34},{34,2},{3,35},{35,3},{4,36},{36... | collective-permute-start | bytes 3145736 | tf_op jit(solution)/shard_map/ppermute | solution.py:487
  4.4 2.5 %pick_rows.1 = (bf16[2,16,64,256]{3,2,1,0:T(8,128)(2,1)S(1)}, f32[64,8192]{1,0:T(8,128)S(1)}, s32[8,128]{1,0:T(8,128)S(1)}) custom-call(s32[3]{0:T(128)S(1)} %pad_add_fusion.at, bf16[16,2,256,256]{3,2,1,0:T(8,128)(2,1)} %bitcast.20, f32[256,8192]{1,0:T(8,128)} %bitcast.16, s32[8,128]{1,0:T(8,128)S(1)} %get-tuple-element.39.refs_2_), custom_call_target="tpu_custom_call" | custom-call | bytes 1024 | tf_op jit(solution)/shard_map/pick_rows/pallas_call | solution.py:64
  6.9 0.0 collective-permute-done.refs_1_
  6.9 2.0 %add_theirs.1 = (bf16[32,64,256]{2,1,0:T(8,128)(2,1)}, bf16[32,64,256]{2,1,0:T(8,128)(2,1)}, s32[8,128]{1,0:T(8,128)S(1)}) custom-call(s32[3]{0:T(128)S(1)} %pad_add_fusion.at, f32[64,8192]{1,0:T(8,128)S(1)} %get-tuple-element.40.refs_0_, bf16[32,64,256]{2,1,0:T(8,128)(2,1)S(1)} %collective-permute-done.refs_1_, bf16[32,64,256]{2,1,0:T(8,128)(2,1)S(1)} %bitcast.14, ...), custom_call_target="tpu_custom_call" | custom-call | bytes 1024 | tf_op jit(solution)/shard_map/add_theirs/pallas_call | solution.py:64
  8.9 1.4 %collective-permute-start.3 = (bf16[32,64,256]{2,1,0:T(8,128)(2,1)}, bf16[32,64,256]{2,1,0:T(8,128)(2,1)S(1)}, u32[]{:S(2)}, u32[]{:S(2)}) collective-permute-start(bf16[32,64,256]{2,1,0:T(8,128)(2,1)} %get-tuple-element.49), channel_id=1, source_target_pairs={{0,64},{64,0},{1,65},{65,1},{2,66},{66,2},{3,67},{67,3},{4,68},{68... | collective-permute-start | bytes 3145736 | tf_op jit(solution)/shard_map/ppermute | solution.py:490
  10.3 9.6 %all-to-all-start = ((bf16[32,64,256]{2,1,0:T(8,128)(2,1)}), bf16[32,64,256]{2,1,0:T(8,128)(2,1)S(1)}, u32[]{:S(2)}, u32[]{:S(2)}) async-start(bf16[32,64,256]{2,1,0:T(8,128)(2,1)} %get-tuple-element.50), calls=%async_computation | async-start | bytes 2097152 | tf_op jit(solution)/shard_map/all_to_all | solution.py:482
  19.9 2.2 %cast_own.1 = (bf16[32,32,256]{2,1,0:T(8,128)(2,1)S(1)}, bf16[32,32,256]{2,1,0:T(8,128)(2,1)S(1)}, s32[8,128]{1,0:T(8,128)S(1)}) custom-call(s32[3]{0:T(128)S(1)} %pad_add_fusion.at, f32[256,8192]{1,0:T(8,128)} %bitcast.17, s32[8,128]{1,0:T(8,128)S(1)} %get-tuple-element.44.refs_1_), custom_call_target="tpu_custom_call" | custom-call | bytes 1024 | tf_op jit(solution)/shard_map/cast_own/pallas_call | solution.py:64
  22.1 0.7 collective-permute-start.1
  22.8 0.1 collective-permute-start.2
  22.9 1.4 %collective-permute-done.1.refs_1_ = bf16[32,32,256]{2,1,0:T(8,128)(2,1)S(1)} collective-permute-done((bf16[32,32,256]{2,1,0:T(8,128)(2,1)S(1)}, bf16[32,32,256]{2,1,0:T(8,128)(2,1)S(1)}, u32[]{:S(2)}, u32[]{:S(2)}) %collective-permute-start.1) | collective-permute-done | bytes 524320 | tf_op jit(solution)/shard_map/ppermute | solution.py:487
  24.3 0.7 collective-permute-done.2.refs_2_
  25.1 2.2 %add_own.1 = (bf16[32,64,256]{2,1,0:T(8,128)(2,1)S(1)}, s32[8,128]{1,0:T(8,128)S(1)}) custom-call(s32[3]{0:T(128)S(1)} %pad_add_fusion.at, f32[256,8192]{1,0:T(8,128)} %bitcast.18, bf16[32,32,256]{2,1,0:T(8,128)(2,1)S(1)} %collective-permute-done.1.refs_1_, bf16[32,32,256]{2,1,0:T(8,128)(2,1)S(1)} %collective-permute-done.2.refs_2_, ...), custom_call_target="tpu_custom_call" | custom-call | bytes 1024 | tf_op jit(solution)/shard_map/add_own/pallas_call | solution.py:64
  27.3 8.8 %all-to-all-done.refs_2_ = bf16[32,64,256]{2,1,0:T(8,128)(2,1)S(1)} async-done(((bf16[32,64,256]{2,1,0:T(8,128)(2,1)}), bf16[32,64,256]{2,1,0:T(8,128)(2,1)S(1)}, u32[]{:S(2)}, u32[]{:S(2)}) %all-to-all-start) | async-done | bytes 1048608 | tf_op jit(solution)/shard_map/all_to_all | solution.py:482
  36.1 0.0 collective-permute-done.3.refs_1_
  36.1 2.0 %blend_rows.1 = (bf16[32,64,256]{2,1,0:T(8,128)(2,1)}, bf16[16,64,256]{2,1,0:T(8,128)(2,1)}, bf16[16,64,256]{2,1,0:T(8,128)(2,1)}, s32[8,128]{1,0:T(8,128)S(1)}) custom-call(s32[3]{0:T(128)S(1)} %pad_add_fusion.at, bf16[32,64,256]{2,1,0:T(8,128)(2,1)S(1)} %get-tuple-element.48.refs_0_, bf16[32,64,256]{2,1,0:T(8,128)(2,1)S(1)} %collective-permute-done.3.refs_1_, ...), custom_call_target="tpu_custom_call" | custom-call | bytes 1024 | tf_op jit(solution)/shard_map/blend_rows/pallas_call | solution.py:64
  38.1 0.1 collective-permute-start.4
  38.2 8.7 %all-to-all-start.1 = ((bf16[32,64,256]{2,1,0:T(8,128)(2,1)}), bf16[32,64,256]{2,1,0:T(8,128)(2,1)S(1)}, u32[]{:S(2)}, u32[]{:S(2)}) async-start(bf16[32,64,256]{2,1,0:T(8,128)(2,1)} %get-tuple-element.52.refs_2_), calls=%async_computation.1 | async-start | bytes 2097152 | tf_op jit(solution)/shard_map/all_to_all | solution.py:482
  47.0 1.5 %collective-permute-start.5 = (bf16[16,64,256]{2,1,0:T(8,128)(2,1)}, bf16[16,64,256]{2,1,0:T(8,128)(2,1)S(1)}, u32[]{:S(2)}, u32[]{:S(2)}) collective-permute-start(bf16[16,64,256]{2,1,0:T(8,128)(2,1)} %get-tuple-element.53), channel_id=1, source_target_pairs={{0,32},{32,0},{1,33},{33,1},{2,34},{34,2},{3,35},{35,3},{4,36},{36... | collective-permute-start | bytes 1572872 | tf_op jit(solution)/shard_map/ppermute | solution.py:487
  48.5 0.1 collective-permute-start.6
  48.6 1.7 %collective-permute-done.5.refs_0_ = bf16[16,64,256]{2,1,0:T(8,128)(2,1)S(1)} collective-permute-done((bf16[16,64,256]{2,1,0:T(8,128)(2,1)}, bf16[16,64,256]{2,1,0:T(8,128)(2,1)S(1)}, u32[]{:S(2)}, u32[]{:S(2)}) %collective-permute-start.5) | collective-permute-done | bytes 524320 | tf_op jit(solution)/shard_map/ppermute | solution.py:487
  50.2 0.7 collective-permute-done.6.refs_1_
  51.0 4.0 %write_rows.4 = (f32[256,8192]{1,0:T(8,128)}, s32[8,128]{1,0:T(8,128)S(1)}) custom-call(s32[3]{0:T(128)S(1)} %pad_add_fusion.at, bf16[16,64,256]{2,1,0:T(8,128)(2,1)S(1)} %collective-permute-done.5.refs_0_, bf16[16,64,256]{2,1,0:T(8,128)(2,1)S(1)} %collective-permute-done.6.refs_1_, bf16[32,64,256]{2,1,0:T(8,128)(2,1)} %get-tuple-element.52.refs_2_, ...), custom_call_target="tpu_custom_call" | custom-call | bytes 11534336 | tf_op jit(solution)/shard_map/write_rows/pallas_call | solution.py:64
  54.9 7.2 %all-to-all-done.1 = bf16[32,64,256]{2,1,0:T(8,128)(2,1)S(1)} async-done(((bf16[32,64,256]{2,1,0:T(8,128)(2,1)}), bf16[32,64,256]{2,1,0:T(8,128)(2,1)S(1)}, u32[]{:S(2)}, u32[]{:S(2)}) %all-to-all-start.1) | async-done | bytes 1048608 | tf_op jit(solution)/shard_map/all_to_all | solution.py:482
  62.1 0.0 collective-permute-done.4.refs_0_
  62.1 1.6 %split_planes.1 = (bf16[16,64,256]{2,1,0:T(8,128)(2,1)}, bf16[16,64,256]{2,1,0:T(8,128)(2,1)}, s32[8,128]{1,0:T(8,128)S(1)}) custom-call(s32[3]{0:T(128)S(1)} %pad_add_fusion.at, bf16[2,16,64,256]{3,2,1,0:T(8,128)(2,1)S(1)} %bitcast.13, bf16[2,16,64,256]{3,2,1,0:T(8,128)(2,1)S(1)} %bitcast.11, s32[8,128]{1,0:T(8,128)S(1)} %get-tuple-element.56.refs_2_), custom_call_target="tpu_custom_call" | custom-call | bytes 1024 | tf_op jit(solution)/shard_map/split_planes/pallas_call | solution.py:64
  63.7 3.5 %collective-permute-start.8 = (bf16[32,64,256]{2,1,0:T(8,128)(2,1)S(1)}, bf16[32,64,256]{2,1,0:T(8,128)(2,1)}, u32[]{:S(2)}, u32[]{:S(2)}) collective-permute-start(bf16[32,64,256]{2,1,0:T(8,128)(2,1)S(1)} %all-to-all-done.1), channel_id=1, source_target_pairs={{0,32},{32,0},{1,33},{33,1},{2,34},{34,2},{3,35},{35,3},{4,36},{36... | collective-permute-start | bytes 3145736 | tf_op jit(solution)/shard_map/ppermute | solution.py:487
  67.2 0.1 collective-permute-start.7
  67.3 0.0 collective-permute-start.9
  67.3 5.4 %all-to-all-start.2 = ((bf16[16,64,256]{2,1,0:T(8,128)(2,1)}), bf16[16,64,256]{2,1,0:T(8,128)(2,1)S(1)}, u32[]{:S(2)}, u32[]{:S(2)}) async-start(bf16[16,64,256]{2,1,0:T(8,128)(2,1)} %get-tuple-element.65), calls=%async_computation.2 | async-start | bytes 1048576 | tf_op jit(solution)/shard_map/all_to_all | solution.py:506
  72.7 0.0 collective-permute-done.8
  72.7 3.3 %place_back.1 = (bf16[16,2,256,256]{3,2,1,0:T(8,128)(2,1)}, s32[8,128]{1,0:T(8,128)S(1)}) custom-call(s32[3]{0:T(128)S(1)} %pad_add_fusion.at, bf16[2,16,64,256]{3,2,1,0:T(8,128)(2,1)S(1)} %bitcast.12, bf16[2,16,64,256]{3,2,1,0:T(8,128)(2,1)} %bitcast.9.refs_1_, s32[8,128]{1,0:T(8,128)S(1)} %get-tuple-element.62.refs_2_), custom_call_target="tpu_custom_call" | custom-call | bytes 1024 | tf_op jit(solution)/shard_map/place_back/pallas_call | solution.py:64
  76.0 0.0 collective-permute-done.7.refs_1_
  76.0 4.0 %write_rows.5 = (f32[256,8192]{1,0:T(8,128)}, s32[8,128]{1,0:T(8,128)S(1)}) custom-call(s32[3]{0:T(128)S(1)} %pad_add_fusion.at, bf16[32,64,256]{2,1,0:T(8,128)(2,1)S(1)} %collective-permute-done.4.refs_0_, bf16[32,64,256]{2,1,0:T(8,128)(2,1)} %collective-permute-done.7.refs_1_, ...), custom_call_target="tpu_custom_call", output_to_operand_aliasing={{0}: (3, {})} | custom-call | bytes 1024 | tf_op jit(solution)/shard_map/write_rows/pallas_call | solution.py:64
  80.0 0.7 collective-permute-done.9.refs_1_
  80.6 2.4 %all-to-all-done.2.refs_0_ = bf16[16,64,256]{2,1,0:T(8,128)(2,1)S(1)} async-done(((bf16[16,64,256]{2,1,0:T(8,128)(2,1)}), bf16[16,64,256]{2,1,0:T(8,128)(2,1)S(1)}, u32[]{:S(2)}, u32[]{:S(2)}) %all-to-all-start.2) | async-done | bytes 524320 | tf_op jit(solution)/shard_map/all_to_all | solution.py:506
  83.0 2.1 %collective-permute-start.10 = (bf16[16,64,256]{2,1,0:T(8,128)(2,1)S(1)}, bf16[16,64,256]{2,1,0:T(8,128)(2,1)S(1)}, u32[]{:S(2)}, u32[]{:S(2)}) collective-permute-start(bf16[16,64,256]{2,1,0:T(8,128)(2,1)S(1)} %all-to-all-done.2.refs_0_), channel_id=1, source_target_pairs={{0,32},{32,0},{1,33},{33,1},{2,34},{34,2},{3,35},{35,3},{4,36},{36... | collective-permute-start | bytes 1572872 | tf_op jit(solution)/shard_map/ppermute | solution.py:487
  85.2 0.0 collective-permute-start.11
  85.2 1.7 %write_rows.6 = (bf16[16,2,256,256]{3,2,1,0:T(8,128)(2,1)}, s32[8,128]{1,0:T(8,128)S(1)}) custom-call(s32[3]{0:T(128)S(1)} %pad_add_fusion.at, bf16[16,64,256]{2,1,0:T(8,128)(2,1)S(1)} %all-to-all-done.2.refs_0_, bf16[16,64,256]{2,1,0:T(8,128)(2,1)S(1)} %collective-permute-done.9.refs_1_, ...), custom_call_target="tpu_custom_call", output_to_operand_aliasing={{0}: (3, {})} | custom-call | bytes 38797312 | tf_op jit(solution)/shard_map/write_rows/pallas_call | solution.py:64
  86.8 0.0 collective-permute-done.10.refs_0_
  86.8 0.6 collective-permute-done.11.refs_1_
  87.4 1.7 %write_rows.7 = (bf16[16,2,256,256]{3,2,1,0:T(8,128)(2,1)}, s32[8,128]{1,0:T(8,128)}) custom-call(s32[3]{0:T(128)S(1)} %pad_add_fusion.at, bf16[16,64,256]{2,1,0:T(8,128)(2,1)S(1)} %collective-permute-done.10.refs_0_, bf16[16,64,256]{2,1,0:T(8,128)(2,1)S(1)} %collective-permute-done.11.refs_1_, ...), custom_call_target="tpu_custom_call", output_to_operand_aliasing={{0}: (3, {})} | custom-call | bytes 1024 | tf_op jit(solution)/shard_map/write_rows/pallas_call | solution.py:64
Async XLA Ops:
  2.9 4.0 %collective-permute-start = (bf16[32,64,256]{2,1,0:T(8,128)(2,1)S(1)}, bf16[32,64,256]{2,1,0:T(8,128)(2,1)S(1)}, u32[]{:S(2)}, u32[]{:S(2)}) collective-permute-start(bf16[32,64,256]{2,1,0:T(8,128)(2,1)S(1)} %get-tuple-element.41), channel_id=1, source_target_pairs={{0,32},{32,0},{1,33},{33,1},{2,34},{34,2},{3,35},{35,3},{4,36},{36... | collective-permute-start | bytes 3145736 | tf_op jit(solution)/shard_map/ppermute | solution.py:487
  8.9 27.2 %collective-permute-start.3 = (bf16[32,64,256]{2,1,0:T(8,128)(2,1)}, bf16[32,64,256]{2,1,0:T(8,128)(2,1)S(1)}, u32[]{:S(2)}, u32[]{:S(2)}) collective-permute-start(bf16[32,64,256]{2,1,0:T(8,128)(2,1)} %get-tuple-element.49), channel_id=1, source_target_pairs={{0,64},{64,0},{1,65},{65,1},{2,66},{66,2},{3,67},{67,3},{4,68},{68... | collective-permute-start | bytes 3145736 | tf_op jit(solution)/shard_map/ppermute | solution.py:490
  10.3 25.8 %all-to-all-start = ((bf16[32,64,256]{2,1,0:T(8,128)(2,1)}), bf16[32,64,256]{2,1,0:T(8,128)(2,1)S(1)}, u32[]{:S(2)}, u32[]{:S(2)}) async-start(bf16[32,64,256]{2,1,0:T(8,128)(2,1)} %get-tuple-element.50), calls=%async_computation | async-start | bytes 2097152 | tf_op jit(solution)/shard_map/all_to_all | solution.py:482
  22.1 2.3 %collective-permute-start.1 = (bf16[32,32,256]{2,1,0:T(8,128)(2,1)S(1)}, bf16[32,32,256]{2,1,0:T(8,128)(2,1)S(1)}, u32[]{:S(2)}, u32[]{:S(2)}) collective-permute-start(bf16[32,32,256]{2,1,0:T(8,128)(2,1)S(1)} %get-tuple-element.45), channel_id=1, source_target_pairs={{0,32},{32,0},{1,33},{33,1},{2,34},{34,2},{3,35},{35,3},{4,36},{36... | collective-permute-start | bytes 1572872 | tf_op jit(solution)/shard_map/ppermute | solution.py:487
  22.8 2.3 %collective-permute-start.2 = (bf16[32,32,256]{2,1,0:T(8,128)(2,1)S(1)}, bf16[32,32,256]{2,1,0:T(8,128)(2,1)S(1)}, u32[]{:S(2)}, u32[]{:S(2)}) collective-permute-start(bf16[32,32,256]{2,1,0:T(8,128)(2,1)S(1)} %get-tuple-element.46), channel_id=1, source_target_pairs={{0,32},{32,0},{1,33},{33,1},{2,34},{34,2},{3,35},{35,3},{4,36},{36... | collective-permute-start | bytes 1572872 | tf_op jit(solution)/shard_map/ppermute | solution.py:487
  38.1 24.0 %collective-permute-start.4 = (bf16[32,64,256]{2,1,0:T(8,128)(2,1)}, bf16[32,64,256]{2,1,0:T(8,128)(2,1)S(1)}, u32[]{:S(2)}, u32[]{:S(2)}) collective-permute-start(bf16[32,64,256]{2,1,0:T(8,128)(2,1)} %get-tuple-element.52.refs_2_), channel_id=1, source_target_pairs={{0,64},{64,0},{1,65},{65,1},{2,66},{66,2},{3,67},{67,3},{4,68},{68... | collective-permute-start | bytes 3145736 | tf_op jit(solution)/shard_map/ppermute | solution.py:490
  38.2 23.9 %all-to-all-start.1 = ((bf16[32,64,256]{2,1,0:T(8,128)(2,1)}), bf16[32,64,256]{2,1,0:T(8,128)(2,1)S(1)}, u32[]{:S(2)}, u32[]{:S(2)}) async-start(bf16[32,64,256]{2,1,0:T(8,128)(2,1)} %get-tuple-element.52.refs_2_), calls=%async_computation.1 | async-start | bytes 2097152 | tf_op jit(solution)/shard_map/all_to_all | solution.py:482
  47.0 3.3 %collective-permute-start.5 = (bf16[16,64,256]{2,1,0:T(8,128)(2,1)}, bf16[16,64,256]{2,1,0:T(8,128)(2,1)S(1)}, u32[]{:S(2)}, u32[]{:S(2)}) collective-permute-start(bf16[16,64,256]{2,1,0:T(8,128)(2,1)} %get-tuple-element.53), channel_id=1, source_target_pairs={{0,32},{32,0},{1,33},{33,1},{2,34},{34,2},{3,35},{35,3},{4,36},{36... | collective-permute-start | bytes 1572872 | tf_op jit(solution)/shard_map/ppermute | solution.py:487
  48.5 2.5 %collective-permute-start.6 = (bf16[16,64,256]{2,1,0:T(8,128)(2,1)}, bf16[16,64,256]{2,1,0:T(8,128)(2,1)S(1)}, u32[]{:S(2)}, u32[]{:S(2)}) collective-permute-start(bf16[16,64,256]{2,1,0:T(8,128)(2,1)} %get-tuple-element.54), channel_id=1, source_target_pairs={{0,32},{32,0},{1,33},{33,1},{2,34},{34,2},{3,35},{35,3},{4,36},{36... | collective-permute-start | bytes 1572872 | tf_op jit(solution)/shard_map/ppermute | solution.py:487
  63.7 9.0 %collective-permute-start.8 = (bf16[32,64,256]{2,1,0:T(8,128)(2,1)S(1)}, bf16[32,64,256]{2,1,0:T(8,128)(2,1)}, u32[]{:S(2)}, u32[]{:S(2)}) collective-permute-start(bf16[32,64,256]{2,1,0:T(8,128)(2,1)S(1)} %all-to-all-done.1), channel_id=1, source_target_pairs={{0,32},{32,0},{1,33},{33,1},{2,34},{34,2},{3,35},{35,3},{4,36},{36... | collective-permute-start | bytes 3145736 | tf_op jit(solution)/shard_map/ppermute | solution.py:487
  67.2 8.7 %collective-permute-start.7 = (bf16[32,64,256]{2,1,0:T(8,128)(2,1)S(1)}, bf16[32,64,256]{2,1,0:T(8,128)(2,1)}, u32[]{:S(2)}, u32[]{:S(2)}) collective-permute-start(bf16[32,64,256]{2,1,0:T(8,128)(2,1)S(1)} %collective-permute-done.4.refs_0_), channel_id=1, source_target_pairs={{0,32},{32,0},{1,33},{33,1},{2,34},{34,2},{3,35},{35,3},{4,36},{36... | collective-permute-start | bytes 3145736 | tf_op jit(solution)/shard_map/ppermute | solution.py:487
  67.3 13.3 %collective-permute-start.9 = (bf16[16,64,256]{2,1,0:T(8,128)(2,1)}, bf16[16,64,256]{2,1,0:T(8,128)(2,1)S(1)}, u32[]{:S(2)}, u32[]{:S(2)}) collective-permute-start(bf16[16,64,256]{2,1,0:T(8,128)(2,1)} %get-tuple-element.66), channel_id=1, source_target_pairs={{0,64},{64,0},{1,65},{65,1},{2,66},{66,2},{3,67},{67,3},{4,68},{68... | collective-permute-start | bytes 1572872 | tf_op jit(solution)/shard_map/ppermute | solution.py:490
  67.3 15.7 %all-to-all-start.2 = ((bf16[16,64,256]{2,1,0:T(8,128)(2,1)}), bf16[16,64,256]{2,1,0:T(8,128)(2,1)S(1)}, u32[]{:S(2)}, u32[]{:S(2)}) async-start(bf16[16,64,256]{2,1,0:T(8,128)(2,1)} %get-tuple-element.65), calls=%async_computation.2 | async-start | bytes 1048576 | tf_op jit(solution)/shard_map/all_to_all | solution.py:506
  83.0 3.8 %collective-permute-start.10 = (bf16[16,64,256]{2,1,0:T(8,128)(2,1)S(1)}, bf16[16,64,256]{2,1,0:T(8,128)(2,1)S(1)}, u32[]{:S(2)}, u32[]{:S(2)}) collective-permute-start(bf16[16,64,256]{2,1,0:T(8,128)(2,1)S(1)} %all-to-all-done.2.refs_0_), channel_id=1, source_target_pairs={{0,32},{32,0},{1,33},{33,1},{2,34},{34,2},{3,35},{35,3},{4,36},{36... | collective-permute-start | bytes 1572872 | tf_op jit(solution)/shard_map/ppermute | solution.py:487
  85.2 2.3 %collective-permute-start.11 = (bf16[16,64,256]{2,1,0:T(8,128)(2,1)S(1)}, bf16[16,64,256]{2,1,0:T(8,128)(2,1)S(1)}, u32[]{:S(2)}, u32[]{:S(2)}) collective-permute-start(bf16[16,64,256]{2,1,0:T(8,128)(2,1)S(1)} %collective-permute-done.9.refs_1_), channel_id=1, source_target_pairs={{0,32},{32,0},{1,33},{33,1},{2,34},{34,2},{3,35},{35,3},{4,36},{36... | collective-permute-start | bytes 1572872 | tf_op jit(solution)/shard_map/ppermute | solution.py:487

commit v12 on v11

--- a/solution.py
+++ b/solution.py
@@ -502,10 +502,11 @@
     pieces = [([core(tiles) for tiles in planes], False, True), ([own], True, True)]
     (blended,) = write_rows(order, pieces, [], None, None, WRITE_COST, late_in_hbm=True)
 
+    back = order.behind(back)
+    finished = order.behind(finished)
     first, high = split_planes(order, finished, back)
     back_first = lax.all_to_all(first, ("y", "z"), split_axis=0, concat_axis=0, tiled=True)
     back_second = chip(high)
-    finished, back = order.behind(finished), order.behind(back)
     new_anchor = place_back(order, back, core(back))
     pieces = [([finished], True, False), ([core(finished)], False, False)]
     (blended,) = write_rows(order, pieces, [], blended, None)

time: 89.8 us -> 89.7 us (level)
  transfers between devices with their start and end apart: 15 -> 15, of which waited for: 9 -> 9; matrix products, arithmetic and copies ran while one was open for 0% -> 0% of each run, Pallas kernels for 22% -> 24%
where the time goes in v12:
time: 89.7 us; the launch traced here: 89 us
  starting transfers between devices  34.7 us (39%)
  Pallas kernels  29.1 us (32%)
  waiting for transfers between devices  24.3 us (27%)
    pallas_call x12, Pallas kernels, run(): pl.pallas_call(ordered, out_shape=[*outs, TOKEN], grid_spec=pltpu.Prefetc...  29.1 us
    all_to_all x2, starting transfers between devices, exchange(): lax.all_to_all(tiles, AXES, split_axis=0, concat_axis=0, axis_index_group...  18.3 us
    all_to_all x2, waiting for transfers between devices, exchange(): lax.all_to_all(tiles, AXES, split_axis=0, concat_axis=0, axis_index_group...  16 us
    ppermute x9, starting transfers between devices, core(): return lax.ppermute(tiles, 'c', swap)  9.45 us
    all_to_all x1, starting transfers between devices, per_device(): lax.all_to_all(first, ('y', 'z'), split_axis=0, concat_axis=0, tiled=True)  5.35 us
    ppermute x9, waiting for transfers between devices, core(): return lax.ppermute(tiles, 'c', swap)  5.22 us
    all_to_all x1, waiting for transfers between devices, per_device(): lax.all_to_all(first, ('y', 'z'), split_axis=0, concat_axis=0, tiled=True)  2.54 us
  transfers between devices with their start and end apart: 15, of which 9 were waited for; matrix products, arithmetic and copies ran while one was open for 0% of the time, Pallas kernels for 24%

profile of v12, /device:TPU:1, one launch (start us, length us, event | category | flops | bytes accessed | tf_op | source)
XLA Modules:
  0.0 89.0 jit_solution(16399007484766390428)
XLA Ops:
  0.6 0.1 pad_add_fusion.at
  0.7 2.2 %cast_rows.1 = (bf16[32,64,256]{2,1,0:T(8,128)(2,1)S(1)}, s32[8,128]{1,0:T(8,128)S(1)}) custom-call(s32[3]{0:T(128)S(1)} %pad_add_fusion.at, f32[256,8192]{1,0:T(8,128)} %bitcast.14), custom_call_target="tpu_custom_call" | custom-call | bytes 1024 | tf_op jit(solution)/shard_map/cast_rows/pallas_call | solution.py:64
  2.9 1.5 %collective-permute-start = (bf16[32,64,256]{2,1,0:T(8,128)(2,1)S(1)}, bf16[32,64,256]{2,1,0:T(8,128)(2,1)S(1)}, u32[]{:S(2)}, u32[]{:S(2)}) collective-permute-start(bf16[32,64,256]{2,1,0:T(8,128)(2,1)S(1)} %get-tuple-element.41), channel_id=1, source_target_pairs={{0,32},{32,0},{1,33},{33,1},{2,34},{34,2},{3,35},{35,3},{4,36},{36... | collective-permute-start | bytes 3145736 | tf_op jit(solution)/shard_map/ppermute | solution.py:487
  4.4 2.5 %pick_rows.1 = (bf16[2,16,64,256]{3,2,1,0:T(8,128)(2,1)S(1)}, f32[64,8192]{1,0:T(8,128)S(1)}, s32[8,128]{1,0:T(8,128)S(1)}) custom-call(s32[3]{0:T(128)S(1)} %pad_add_fusion.at, bf16[16,2,256,256]{3,2,1,0:T(8,128)(2,1)} %bitcast.19, f32[256,8192]{1,0:T(8,128)} %bitcast.15, s32[8,128]{1,0:T(8,128)S(1)} %get-tuple-element.39.refs_2_), custom_call_target="tpu_custom_call" | custom-call | bytes 1024 | tf_op jit(solution)/shard_map/pick_rows/pallas_call | solution.py:64
  6.9 0.0 collective-permute-done.refs_1_
  6.9 2.0 %add_theirs.1 = (bf16[32,64,256]{2,1,0:T(8,128)(2,1)}, bf16[32,64,256]{2,1,0:T(8,128)(2,1)}, s32[8,128]{1,0:T(8,128)S(1)}) custom-call(s32[3]{0:T(128)S(1)} %pad_add_fusion.at, f32[64,8192]{1,0:T(8,128)S(1)} %get-tuple-element.40.refs_0_, bf16[32,64,256]{2,1,0:T(8,128)(2,1)S(1)} %collective-permute-done.refs_1_, bf16[32,64,256]{2,1,0:T(8,128)(2,1)S(1)} %bitcast.13, ...), custom_call_target="tpu_custom_call" | custom-call | bytes 1024 | tf_op jit(solution)/shard_map/add_theirs/pallas_call | solution.py:64
  8.9 1.4 %collective-permute-start.3 = (bf16[32,64,256]{2,1,0:T(8,128)(2,1)}, bf16[32,64,256]{2,1,0:T(8,128)(2,1)S(1)}, u32[]{:S(2)}, u32[]{:S(2)}) collective-permute-start(bf16[32,64,256]{2,1,0:T(8,128)(2,1)} %get-tuple-element.49), channel_id=1, source_target_pairs={{0,64},{64,0},{1,65},{65,1},{2,66},{66,2},{3,67},{67,3},{4,68},{68... | collective-permute-start | bytes 3145736 | tf_op jit(solution)/shard_map/ppermute | solution.py:490
  10.3 9.6 %all-to-all-start = ((bf16[32,64,256]{2,1,0:T(8,128)(2,1)}), bf16[32,64,256]{2,1,0:T(8,128)(2,1)S(1)}, u32[]{:S(2)}, u32[]{:S(2)}) async-start(bf16[32,64,256]{2,1,0:T(8,128)(2,1)} %get-tuple-element.50), calls=%async_computation | async-start | bytes 2097152 | tf_op jit(solution)/shard_map/all_to_all | solution.py:482
  19.9 2.2 %cast_own.1 = (bf16[32,32,256]{2,1,0:T(8,128)(2,1)S(1)}, bf16[32,32,256]{2,1,0:T(8,128)(2,1)S(1)}, s32[8,128]{1,0:T(8,128)S(1)}) custom-call(s32[3]{0:T(128)S(1)} %pad_add_fusion.at, f32[256,8192]{1,0:T(8,128)} %bitcast.16, s32[8,128]{1,0:T(8,128)S(1)} %get-tuple-element.44.refs_1_), custom_call_target="tpu_custom_call" | custom-call | bytes 1024 | tf_op jit(solution)/shard_map/cast_own/pallas_call | solution.py:64
  22.1 0.7 collective-permute-start.1
  22.8 0.1 collective-permute-start.2
  22.9 1.4 %collective-permute-done.1.refs_1_ = bf16[32,32,256]{2,1,0:T(8,128)(2,1)S(1)} collective-permute-done((bf16[32,32,256]{2,1,0:T(8,128)(2,1)S(1)}, bf16[32,32,256]{2,1,0:T(8,128)(2,1)S(1)}, u32[]{:S(2)}, u32[]{:S(2)}) %collective-permute-start.1) | collective-permute-done | bytes 524320 | tf_op jit(solution)/shard_map/ppermute | solution.py:487
  24.3 0.7 collective-permute-done.2.refs_2_
  25.1 2.2 %add_own.1 = (bf16[32,64,256]{2,1,0:T(8,128)(2,1)S(1)}, s32[8,128]{1,0:T(8,128)S(1)}) custom-call(s32[3]{0:T(128)S(1)} %pad_add_fusion.at, f32[256,8192]{1,0:T(8,128)} %bitcast.17, bf16[32,32,256]{2,1,0:T(8,128)(2,1)S(1)} %collective-permute-done.1.refs_1_, bf16[32,32,256]{2,1,0:T(8,128)(2,1)S(1)} %collective-permute-done.2.refs_2_, ...), custom_call_target="tpu_custom_call" | custom-call | bytes 1024 | tf_op jit(solution)/shard_map/add_own/pallas_call | solution.py:64
  27.3 8.8 %all-to-all-done.refs_2_ = bf16[32,64,256]{2,1,0:T(8,128)(2,1)S(1)} async-done(((bf16[32,64,256]{2,1,0:T(8,128)(2,1)}), bf16[32,64,256]{2,1,0:T(8,128)(2,1)S(1)}, u32[]{:S(2)}, u32[]{:S(2)}) %all-to-all-start) | async-done | bytes 1048608 | tf_op jit(solution)/shard_map/all_to_all | solution.py:482
  36.1 0.0 collective-permute-done.3.refs_1_
  36.1 2.0 %blend_rows.1 = (bf16[32,64,256]{2,1,0:T(8,128)(2,1)}, bf16[16,64,256]{2,1,0:T(8,128)(2,1)}, bf16[16,64,256]{2,1,0:T(8,128)(2,1)}, s32[8,128]{1,0:T(8,128)S(1)}) custom-call(s32[3]{0:T(128)S(1)} %pad_add_fusion.at, bf16[32,64,256]{2,1,0:T(8,128)(2,1)S(1)} %get-tuple-element.48.refs_0_, bf16[32,64,256]{2,1,0:T(8,128)(2,1)S(1)} %collective-permute-done.3.refs_1_, ...), custom_call_target="tpu_custom_call" | custom-call | bytes 1024 | tf_op jit(solution)/shard_map/blend_rows/pallas_call | solution.py:64
  38.1 0.1 collective-permute-start.4
  38.2 8.7 %all-to-all-start.1 = ((bf16[32,64,256]{2,1,0:T(8,128)(2,1)}), bf16[32,64,256]{2,1,0:T(8,128)(2,1)S(1)}, u32[]{:S(2)}, u32[]{:S(2)}) async-start(bf16[32,64,256]{2,1,0:T(8,128)(2,1)} %get-tuple-element.52.refs_2_), calls=%async_computation.1 | async-start | bytes 2097152 | tf_op jit(solution)/shard_map/all_to_all | solution.py:482
  47.0 1.5 %collective-permute-start.5 = (bf16[16,64,256]{2,1,0:T(8,128)(2,1)}, bf16[16,64,256]{2,1,0:T(8,128)(2,1)S(1)}, u32[]{:S(2)}, u32[]{:S(2)}) collective-permute-start(bf16[16,64,256]{2,1,0:T(8,128)(2,1)} %get-tuple-element.53), channel_id=1, source_target_pairs={{0,32},{32,0},{1,33},{33,1},{2,34},{34,2},{3,35},{35,3},{4,36},{36... | collective-permute-start | bytes 1572872 | tf_op jit(solution)/shard_map/ppermute | solution.py:487
  48.5 0.1 collective-permute-start.6
  48.6 1.7 %collective-permute-done.5.refs_0_ = bf16[16,64,256]{2,1,0:T(8,128)(2,1)S(1)} collective-permute-done((bf16[16,64,256]{2,1,0:T(8,128)(2,1)}, bf16[16,64,256]{2,1,0:T(8,128)(2,1)S(1)}, u32[]{:S(2)}, u32[]{:S(2)}) %collective-permute-start.5) | collective-permute-done | bytes 524320 | tf_op jit(solution)/shard_map/ppermute | solution.py:487
  50.2 0.7 collective-permute-done.6.refs_1_
  51.0 4.0 %write_rows.4 = (f32[256,8192]{1,0:T(8,128)}, s32[8,128]{1,0:T(8,128)S(1)}) custom-call(s32[3]{0:T(128)S(1)} %pad_add_fusion.at, bf16[16,64,256]{2,1,0:T(8,128)(2,1)S(1)} %collective-permute-done.5.refs_0_, bf16[16,64,256]{2,1,0:T(8,128)(2,1)S(1)} %collective-permute-done.6.refs_1_, bf16[32,64,256]{2,1,0:T(8,128)(2,1)} %get-tuple-element.52.refs_2_, ...), custom_call_target="tpu_custom_call" | custom-call | bytes 11534336 | tf_op jit(solution)/shard_map/write_rows/pallas_call | solution.py:64
  54.9 7.2 %all-to-all-done.1 = bf16[32,64,256]{2,1,0:T(8,128)(2,1)S(1)} async-done(((bf16[32,64,256]{2,1,0:T(8,128)(2,1)}), bf16[32,64,256]{2,1,0:T(8,128)(2,1)S(1)}, u32[]{:S(2)}, u32[]{:S(2)}) %all-to-all-start.1) | async-done | bytes 1048608 | tf_op jit(solution)/shard_map/all_to_all | solution.py:482
  62.1 3.4 %collective-permute-start.8 = (bf16[32,64,256]{2,1,0:T(8,128)(2,1)S(1)}, bf16[32,64,256]{2,1,0:T(8,128)(2,1)}, u32[]{:S(2)}, u32[]{:S(2)}) collective-permute-start(bf16[32,64,256]{2,1,0:T(8,128)(2,1)S(1)} %all-to-all-done.1), channel_id=1, source_target_pairs={{0,32},{32,0},{1,33},{33,1},{2,34},{34,2},{3,35},{35,3},{4,36},{36... | collective-permute-start | bytes 3145736 | tf_op jit(solution)/shard_map/ppermute | solution.py:487
  65.5 0.0 collective-permute-done.4.refs_0_
  65.5 0.0 collective-permute-start.7
  65.5 1.6 %split_planes.1 = (bf16[16,64,256]{2,1,0:T(8,128)(2,1)}, bf16[16,64,256]{2,1,0:T(8,128)(2,1)}, s32[8,128]{1,0:T(8,128)S(1)}) custom-call(s32[3]{0:T(128)S(1)} %pad_add_fusion.at, bf16[2,16,64,256]{3,2,1,0:T(8,128)(2,1)S(1)} %bitcast.12, bf16[2,16,64,256]{3,2,1,0:T(8,128)(2,1)S(1)} %bitcast.10, s32[8,128]{1,0:T(8,128)S(1)} %get-tuple-element.61.refs_2_), custom_call_target="tpu_custom_call" | custom-call | bytes 1024 | tf_op jit(solution)/shard_map/split_planes/pallas_call | solution.py:64
  67.2 0.1 collective-permute-start.9
  67.3 5.4 %all-to-all-start.2 = ((bf16[16,64,256]{2,1,0:T(8,128)(2,1)}), bf16[16,64,256]{2,1,0:T(8,128)(2,1)S(1)}, u32[]{:S(2)}, u32[]{:S(2)}) async-start(bf16[16,64,256]{2,1,0:T(8,128)(2,1)} %get-tuple-element.65), calls=%async_computation.2 | async-start | bytes 1048576 | tf_op jit(solution)/shard_map/all_to_all | solution.py:508
  72.6 0.0 collective-permute-done.8
  72.6 3.3 %place_back.1 = (bf16[16,2,256,256]{3,2,1,0:T(8,128)(2,1)}, s32[8,128]{1,0:T(8,128)S(1)}) custom-call(s32[3]{0:T(128)S(1)} %pad_add_fusion.at, bf16[2,16,64,256]{3,2,1,0:T(8,128)(2,1)S(1)} %bitcast.11, bf16[2,16,64,256]{3,2,1,0:T(8,128)(2,1)} %bitcast.7.refs_1_, s32[8,128]{1,0:T(8,128)S(1)} %get-tuple-element.62.refs_2_), custom_call_target="tpu_custom_call" | custom-call | bytes 1024 | tf_op jit(solution)/shard_map/place_back/pallas_call | solution.py:64
  75.9 0.0 collective-permute-done.7.refs_1_
  75.9 4.0 %write_rows.5 = (f32[256,8192]{1,0:T(8,128)}, s32[8,128]{1,0:T(8,128)S(1)}) custom-call(s32[3]{0:T(128)S(1)} %pad_add_fusion.at, bf16[32,64,256]{2,1,0:T(8,128)(2,1)S(1)} %collective-permute-done.4.refs_0_, bf16[32,64,256]{2,1,0:T(8,128)(2,1)} %collective-permute-done.7.refs_1_, ...), custom_call_target="tpu_custom_call", output_to_operand_aliasing={{0}: (3, {})} | custom-call | bytes 1024 | tf_op jit(solution)/shard_map/write_rows/pallas_call | solution.py:64
  79.9 0.6 collective-permute-done.9.refs_1_
  80.4 2.5 %all-to-all-done.2.refs_0_ = bf16[16,64,256]{2,1,0:T(8,128)(2,1)S(1)} async-done(((bf16[16,64,256]{2,1,0:T(8,128)(2,1)}), bf16[16,64,256]{2,1,0:T(8,128)(2,1)S(1)}, u32[]{:S(2)}, u32[]{:S(2)}) %all-to-all-start.2) | async-done | bytes 524320 | tf_op jit(solution)/shard_map/all_to_all | solution.py:508
  83.0 2.1 %collective-permute-start.10 = (bf16[16,64,256]{2,1,0:T(8,128)(2,1)S(1)}, bf16[16,64,256]{2,1,0:T(8,128)(2,1)S(1)}, u32[]{:S(2)}, u32[]{:S(2)}) collective-permute-start(bf16[16,64,256]{2,1,0:T(8,128)(2,1)S(1)} %all-to-all-done.2.refs_0_), channel_id=1, source_target_pairs={{0,32},{32,0},{1,33},{33,1},{2,34},{34,2},{3,35},{35,3},{4,36},{36... | collective-permute-start | bytes 1572872 | tf_op jit(solution)/shard_map/ppermute | solution.py:487
  85.1 0.0 collective-permute-start.11
  85.1 1.7 %write_rows.6 = (bf16[16,2,256,256]{3,2,1,0:T(8,128)(2,1)}, s32[8,128]{1,0:T(8,128)S(1)}) custom-call(s32[3]{0:T(128)S(1)} %pad_add_fusion.at, bf16[16,64,256]{2,1,0:T(8,128)(2,1)S(1)} %all-to-all-done.2.refs_0_, bf16[16,64,256]{2,1,0:T(8,128)(2,1)S(1)} %collective-permute-done.9.refs_1_, ...), custom_call_target="tpu_custom_call", output_to_operand_aliasing={{0}: (3, {})} | custom-call | bytes 38797312 | tf_op jit(solution)/shard_map/write_rows/pallas_call | solution.py:64
  86.7 0.0 collective-permute-done.10.refs_0_
  86.7 0.6 collective-permute-done.11.refs_1_
  87.3 1.7 %write_rows.7 = (bf16[16,2,256,256]{3,2,1,0:T(8,128)(2,1)}, s32[8,128]{1,0:T(8,128)}) custom-call(s32[3]{0:T(128)S(1)} %pad_add_fusion.at, bf16[16,64,256]{2,1,0:T(8,128)(2,1)S(1)} %collective-permute-done.10.refs_0_, bf16[16,64,256]{2,1,0:T(8,128)(2,1)S(1)} %collective-permute-done.11.refs_1_, ...), custom_call_target="tpu_custom_call", output_to_operand_aliasing={{0}: (3, {})} | custom-call | bytes 1024 | tf_op jit(solution)/shard_map/write_rows/pallas_call | solution.py:64
Async XLA Ops:
  2.9 4.0 %collective-permute-start = (bf16[32,64,256]{2,1,0:T(8,128)(2,1)S(1)}, bf16[32,64,256]{2,1,0:T(8,128)(2,1)S(1)}, u32[]{:S(2)}, u32[]{:S(2)}) collective-permute-start(bf16[32,64,256]{2,1,0:T(8,128)(2,1)S(1)} %get-tuple-element.41), channel_id=1, source_target_pairs={{0,32},{32,0},{1,33},{33,1},{2,34},{34,2},{3,35},{35,3},{4,36},{36... | collective-permute-start | bytes 3145736 | tf_op jit(solution)/shard_map/ppermute | solution.py:487
  8.9 27.2 %collective-permute-start.3 = (bf16[32,64,256]{2,1,0:T(8,128)(2,1)}, bf16[32,64,256]{2,1,0:T(8,128)(2,1)S(1)}, u32[]{:S(2)}, u32[]{:S(2)}) collective-permute-start(bf16[32,64,256]{2,1,0:T(8,128)(2,1)} %get-tuple-element.49), channel_id=1, source_target_pairs={{0,64},{64,0},{1,65},{65,1},{2,66},{66,2},{3,67},{67,3},{4,68},{68... | collective-permute-start | bytes 3145736 | tf_op jit(solution)/shard_map/ppermute | solution.py:490
  10.3 25.8 %all-to-all-start = ((bf16[32,64,256]{2,1,0:T(8,128)(2,1)}), bf16[32,64,256]{2,1,0:T(8,128)(2,1)S(1)}, u32[]{:S(2)}, u32[]{:S(2)}) async-start(bf16[32,64,256]{2,1,0:T(8,128)(2,1)} %get-tuple-element.50), calls=%async_computation | async-start | bytes 2097152 | tf_op jit(solution)/shard_map/all_to_all | solution.py:482
  22.1 2.3 %collective-permute-start.1 = (bf16[32,32,256]{2,1,0:T(8,128)(2,1)S(1)}, bf16[32,32,256]{2,1,0:T(8,128)(2,1)S(1)}, u32[]{:S(2)}, u32[]{:S(2)}) collective-permute-start(bf16[32,32,256]{2,1,0:T(8,128)(2,1)S(1)} %get-tuple-element.45), channel_id=1, source_target_pairs={{0,32},{32,0},{1,33},{33,1},{2,34},{34,2},{3,35},{35,3},{4,36},{36... | collective-permute-start | bytes 1572872 | tf_op jit(solution)/shard_map/ppermute | solution.py:487
  22.8 2.3 %collective-permute-start.2 = (bf16[32,32,256]{2,1,0:T(8,128)(2,1)S(1)}, bf16[32,32,256]{2,1,0:T(8,128)(2,1)S(1)}, u32[]{:S(2)}, u32[]{:S(2)}) collective-permute-start(bf16[32,32,256]{2,1,0:T(8,128)(2,1)S(1)} %get-tuple-element.46), channel_id=1, source_target_pairs={{0,32},{32,0},{1,33},{33,1},{2,34},{34,2},{3,35},{35,3},{4,36},{36... | collective-permute-start | bytes 1572872 | tf_op jit(solution)/shard_map/ppermute | solution.py:487
  38.1 27.4 %collective-permute-start.4 = (bf16[32,64,256]{2,1,0:T(8,128)(2,1)}, bf16[32,64,256]{2,1,0:T(8,128)(2,1)S(1)}, u32[]{:S(2)}, u32[]{:S(2)}) collective-permute-start(bf16[32,64,256]{2,1,0:T(8,128)(2,1)} %get-tuple-element.52.refs_2_), channel_id=1, source_target_pairs={{0,64},{64,0},{1,65},{65,1},{2,66},{66,2},{3,67},{67,3},{4,68},{68... | collective-permute-start | bytes 3145736 | tf_op jit(solution)/shard_map/ppermute | solution.py:490
  38.2 23.9 %all-to-all-start.1 = ((bf16[32,64,256]{2,1,0:T(8,128)(2,1)}), bf16[32,64,256]{2,1,0:T(8,128)(2,1)S(1)}, u32[]{:S(2)}, u32[]{:S(2)}) async-start(bf16[32,64,256]{2,1,0:T(8,128)(2,1)} %get-tuple-element.52.refs_2_), calls=%async_computation.1 | async-start | bytes 2097152 | tf_op jit(solution)/shard_map/all_to_all | solution.py:482
  47.0 3.3 %collective-permute-start.5 = (bf16[16,64,256]{2,1,0:T(8,128)(2,1)}, bf16[16,64,256]{2,1,0:T(8,128)(2,1)S(1)}, u32[]{:S(2)}, u32[]{:S(2)}) collective-permute-start(bf16[16,64,256]{2,1,0:T(8,128)(2,1)} %get-tuple-element.53), channel_id=1, source_target_pairs={{0,32},{32,0},{1,33},{33,1},{2,34},{34,2},{3,35},{35,3},{4,36},{36... | collective-permute-start | bytes 1572872 | tf_op jit(solution)/shard_map/ppermute | solution.py:487
  48.5 2.5 %collective-permute-start.6 = (bf16[16,64,256]{2,1,0:T(8,128)(2,1)}, bf16[16,64,256]{2,1,0:T(8,128)(2,1)S(1)}, u32[]{:S(2)}, u32[]{:S(2)}) collective-permute-start(bf16[16,64,256]{2,1,0:T(8,128)(2,1)} %get-tuple-element.54), channel_id=1, source_target_pairs={{0,32},{32,0},{1,33},{33,1},{2,34},{34,2},{3,35},{35,3},{4,36},{36... | collective-permute-start | bytes 1572872 | tf_op jit(solution)/shard_map/ppermute | solution.py:487
  62.1 10.5 %collective-permute-start.8 = (bf16[32,64,256]{2,1,0:T(8,128)(2,1)S(1)}, bf16[32,64,256]{2,1,0:T(8,128)(2,1)}, u32[]{:S(2)}, u32[]{:S(2)}) collective-permute-start(bf16[32,64,256]{2,1,0:T(8,128)(2,1)S(1)} %all-to-all-done.1), channel_id=1, source_target_pairs={{0,32},{32,0},{1,33},{33,1},{2,34},{34,2},{3,35},{35,3},{4,36},{36... | collective-permute-start | bytes 3145736 | tf_op jit(solution)/shard_map/ppermute | solution.py:487
  65.5 10.3 %collective-permute-start.7 = (bf16[32,64,256]{2,1,0:T(8,128)(2,1)S(1)}, bf16[32,64,256]{2,1,0:T(8,128)(2,1)}, u32[]{:S(2)}, u32[]{:S(2)}) collective-permute-start(bf16[32,64,256]{2,1,0:T(8,128)(2,1)S(1)} %collective-permute-done.4.refs_0_), channel_id=1, source_target_pairs={{0,32},{32,0},{1,33},{33,1},{2,34},{34,2},{3,35},{35,3},{4,36},{36... | collective-permute-start | bytes 3145736 | tf_op jit(solution)/shard_map/ppermute | solution.py:487
  67.2 13.3 %collective-permute-start.9 = (bf16[16,64,256]{2,1,0:T(8,128)(2,1)}, bf16[16,64,256]{2,1,0:T(8,128)(2,1)S(1)}, u32[]{:S(2)}, u32[]{:S(2)}) collective-permute-start(bf16[16,64,256]{2,1,0:T(8,128)(2,1)} %get-tuple-element.66), channel_id=1, source_target_pairs={{0,64},{64,0},{1,65},{65,1},{2,66},{66,2},{3,67},{67,3},{4,68},{68... | collective-permute-start | bytes 1572872 | tf_op jit(solution)/shard_map/ppermute | solution.py:490
  67.3 15.7 %all-to-all-start.2 = ((bf16[16,64,256]{2,1,0:T(8,128)(2,1)}), bf16[16,64,256]{2,1,0:T(8,128)(2,1)S(1)}, u32[]{:S(2)}, u32[]{:S(2)}) async-start(bf16[16,64,256]{2,1,0:T(8,128)(2,1)} %get-tuple-element.65), calls=%async_computation.2 | async-start | bytes 1048576 | tf_op jit(solution)/shard_map/all_to_all | solution.py:508
  83.0 3.8 %collective-permute-start.10 = (bf16[16,64,256]{2,1,0:T(8,128)(2,1)S(1)}, bf16[16,64,256]{2,1,0:T(8,128)(2,1)S(1)}, u32[]{:S(2)}, u32[]{:S(2)}) collective-permute-start(bf16[16,64,256]{2,1,0:T(8,128)(2,1)S(1)} %all-to-all-done.2.refs_0_), channel_id=1, source_target_pairs={{0,32},{32,0},{1,33},{33,1},{2,34},{34,2},{3,35},{35,3},{4,36},{36... | collective-permute-start | bytes 1572872 | tf_op jit(solution)/shard_map/ppermute | solution.py:487
  85.1 2.3 %collective-permute-start.11 = (bf16[16,64,256]{2,1,0:T(8,128)(2,1)S(1)}, bf16[16,64,256]{2,1,0:T(8,128)(2,1)S(1)}, u32[]{:S(2)}, u32[]{:S(2)}) collective-permute-start(bf16[16,64,256]{2,1,0:T(8,128)(2,1)S(1)} %collective-permute-done.9.refs_1_), channel_id=1, source_target_pairs={{0,32},{32,0},{1,33},{33,1},{2,34},{34,2},{3,35},{35,3},{4,36},{36... | collective-permute-start | bytes 1572872 | tf_op jit(solution)/shard_map/ppermute | solution.py:487

commit v13 on v12

--- a/solution.py
+++ b/solution.py
@@ -24,7 +24,7 @@
 PARTS = 8
 PER = SHARDS // PARTS
 WRITE_COST = 11 << 20
-LAST_COST = 37 << 20
+LAST_COST = 4 << 20
 ANY = pl.BlockSpec(memory_space=pl.ANY)
 HBM = pl.BlockSpec(memory_space=pltpu.HBM)
 VMEM = pl.BlockSpec(memory_space=pltpu.VMEM)
@@ -511,11 +511,13 @@
     pieces = [([finished], True, False), ([core(finished)], False, False)]
     (blended,) = write_rows(order, pieces, [], blended, None)
     back_second = order.behind(back_second)
+    there_second = core(back_second)
+    (new_anchor,) = write_rows(order, [], [(back_second, True, True, False)], None, new_anchor)
     back_first = order.behind(back_first)
-    pieces = [(back_first, True, False, True), (back_second, True, True, False)]
+    there_first = core(back_first)
+    pieces = [(back_first, True, False, True), (there_second, False, True, False)]
     (new_anchor,) = write_rows(order, [], pieces, None, new_anchor, LAST_COST)
-    pieces = [(core(back_first), False, False, True), (core(back_second), False, True, False)]
-    (new_anchor,) = write_rows(order, [], pieces, None, new_anchor)
+    (new_anchor,) = write_rows(order, [], [(there_first, False, False, True)], None, new_anchor)
     return blended, new_anchor.reshape(SHARDS * ROWS, WIDTH)
 
 

time: 89.7 us -> 88.9 us (level)
  waiting for transfers between devices: 24.3 us -> 21.2 us
  Pallas kernels: 29.1 us -> 30.4 us
  starting transfers between devices: 34.7 us -> 35.7 us
    all_to_all x1, waiting for transfers between devices: 2.54 us -> 0.01 us  [per_device(): lax.all_to_all(first, ('y', 'z'), split_axis=0, concat_axis=0, tiled=True)]
    pallas_call x12 -> x13, Pallas kernels: 29.1 us -> 30.4 us  [run(): pl.pallas_call(ordered, out_shape=[*outs, TOKEN], grid_spec=pltpu.Prefetc...]
    ppermute x9, starting transfers between devices: 9.45 us -> 10.5 us  [core(): return lax.ppermute(tiles, 'c', swap)]
  transfers between devices with their start and end apart: 15 -> 15, of which waited for: 9 -> 7; matrix products, arithmetic and copies ran while one was open for 0% -> 0% of each run, Pallas kernels for 24% -> 26%
where the time goes in v13:
time: 88.9 us; the launch traced here: 88.2 us
  starting transfers between devices  35.7 us (40%)
  Pallas kernels  30.4 us (34%)
  waiting for transfers between devices  21.2 us (24%)
    pallas_call x13, Pallas kernels, run(): pl.pallas_call(ordered, out_shape=[*outs, TOKEN], grid_spec=pltpu.Prefetc...  30.4 us
    all_to_all x2, starting transfers between devices, exchange(): lax.all_to_all(tiles, AXES, split_axis=0, concat_axis=0, axis_index_group...  18.3 us
    all_to_all x2, waiting for transfers between devices, exchange(): lax.all_to_all(tiles, AXES, split_axis=0, concat_axis=0, axis_index_group...  16 us
    ppermute x9, starting transfers between devices, core(): return lax.ppermute(tiles, 'c', swap)  10.5 us
    all_to_all x1, starting transfers between devices, per_device(): lax.all_to_all(first, ('y', 'z'), split_axis=0, concat_axis=0, tiled=True)  5.35 us
    ppermute x9, waiting for transfers between devices, core(): return lax.ppermute(tiles, 'c', swap)  4.61 us
  transfers between devices with their start and end apart: 15, of which 7 were waited for; matrix products, arithmetic and copies ran while one was open for 0% of the time, Pallas kernels for 26%

profile of v13, /device:TPU:1, one launch (start us, length us, event | category | flops | bytes accessed | tf_op | source)
XLA Modules:
  0.0 88.2 jit_solution(12007859031413040183)
XLA Ops:
  0.6 0.1 pad_add_fusion.at
  0.7 2.2 %cast_rows.1 = (bf16[32,64,256]{2,1,0:T(8,128)(2,1)S(1)}, s32[8,128]{1,0:T(8,128)S(1)}) custom-call(s32[3]{0:T(128)S(1)} %pad_add_fusion.at, f32[256,8192]{1,0:T(8,128)} %bitcast.14), custom_call_target="tpu_custom_call" | custom-call | bytes 1024 | tf_op jit(solution)/shard_map/cast_rows/pallas_call | solution.py:64
  2.9 1.5 %collective-permute-start = (bf16[32,64,256]{2,1,0:T(8,128)(2,1)S(1)}, bf16[32,64,256]{2,1,0:T(8,128)(2,1)S(1)}, u32[]{:S(2)}, u32[]{:S(2)}) collective-permute-start(bf16[32,64,256]{2,1,0:T(8,128)(2,1)S(1)} %get-tuple-element.43), channel_id=1, source_target_pairs={{0,32},{32,0},{1,33},{33,1},{2,34},{34,2},{3,35},{35,3},{4,36},{36... | collective-permute-start | bytes 3145736 | tf_op jit(solution)/shard_map/ppermute | solution.py:487
  4.4 2.5 %pick_rows.1 = (bf16[2,16,64,256]{3,2,1,0:T(8,128)(2,1)S(1)}, f32[64,8192]{1,0:T(8,128)S(1)}, s32[8,128]{1,0:T(8,128)S(1)}) custom-call(s32[3]{0:T(128)S(1)} %pad_add_fusion.at, bf16[16,2,256,256]{3,2,1,0:T(8,128)(2,1)} %bitcast.19, f32[256,8192]{1,0:T(8,128)} %bitcast.15, s32[8,128]{1,0:T(8,128)S(1)} %get-tuple-element.41.refs_2_), custom_call_target="tpu_custom_call" | custom-call | bytes 1024 | tf_op jit(solution)/shard_map/pick_rows/pallas_call | solution.py:64
  6.9 0.0 collective-permute-done.refs_1_
  6.9 2.0 %add_theirs.1 = (bf16[32,64,256]{2,1,0:T(8,128)(2,1)}, bf16[32,64,256]{2,1,0:T(8,128)(2,1)}, s32[8,128]{1,0:T(8,128)S(1)}) custom-call(s32[3]{0:T(128)S(1)} %pad_add_fusion.at, f32[64,8192]{1,0:T(8,128)S(1)} %get-tuple-element.42.refs_0_, bf16[32,64,256]{2,1,0:T(8,128)(2,1)S(1)} %collective-permute-done.refs_1_, bf16[32,64,256]{2,1,0:T(8,128)(2,1)S(1)} %bitcast.13, ...), custom_call_target="tpu_custom_call" | custom-call | bytes 1024 | tf_op jit(solution)/shard_map/add_theirs/pallas_call | solution.py:64
  8.9 1.4 %collective-permute-start.3 = (bf16[32,64,256]{2,1,0:T(8,128)(2,1)}, bf16[32,64,256]{2,1,0:T(8,128)(2,1)S(1)}, u32[]{:S(2)}, u32[]{:S(2)}) collective-permute-start(bf16[32,64,256]{2,1,0:T(8,128)(2,1)} %get-tuple-element.51), channel_id=1, source_target_pairs={{0,64},{64,0},{1,65},{65,1},{2,66},{66,2},{3,67},{67,3},{4,68},{68... | collective-permute-start | bytes 3145736 | tf_op jit(solution)/shard_map/ppermute | solution.py:490
  10.3 9.6 %all-to-all-start = ((bf16[32,64,256]{2,1,0:T(8,128)(2,1)}), bf16[32,64,256]{2,1,0:T(8,128)(2,1)S(1)}, u32[]{:S(2)}, u32[]{:S(2)}) async-start(bf16[32,64,256]{2,1,0:T(8,128)(2,1)} %get-tuple-element.52), calls=%async_computation | async-start | bytes 2097152 | tf_op jit(solution)/shard_map/all_to_all | solution.py:482
  19.9 2.2 %cast_own.1 = (bf16[32,32,256]{2,1,0:T(8,128)(2,1)S(1)}, bf16[32,32,256]{2,1,0:T(8,128)(2,1)S(1)}, s32[8,128]{1,0:T(8,128)S(1)}) custom-call(s32[3]{0:T(128)S(1)} %pad_add_fusion.at, f32[256,8192]{1,0:T(8,128)} %bitcast.16, s32[8,128]{1,0:T(8,128)S(1)} %get-tuple-element.46.refs_1_), custom_call_target="tpu_custom_call" | custom-call | bytes 1024 | tf_op jit(solution)/shard_map/cast_own/pallas_call | solution.py:64
  22.1 0.7 collective-permute-start.1
  22.8 0.1 collective-permute-start.2
  22.9 1.4 %collective-permute-done.1.refs_1_ = bf16[32,32,256]{2,1,0:T(8,128)(2,1)S(1)} collective-permute-done((bf16[32,32,256]{2,1,0:T(8,128)(2,1)S(1)}, bf16[32,32,256]{2,1,0:T(8,128)(2,1)S(1)}, u32[]{:S(2)}, u32[]{:S(2)}) %collective-permute-start.1) | collective-permute-done | bytes 524320 | tf_op jit(solution)/shard_map/ppermute | solution.py:487
  24.3 0.7 collective-permute-done.2.refs_2_
  25.1 2.2 %add_own.1 = (bf16[32,64,256]{2,1,0:T(8,128)(2,1)S(1)}, s32[8,128]{1,0:T(8,128)S(1)}) custom-call(s32[3]{0:T(128)S(1)} %pad_add_fusion.at, f32[256,8192]{1,0:T(8,128)} %bitcast.17, bf16[32,32,256]{2,1,0:T(8,128)(2,1)S(1)} %collective-permute-done.1.refs_1_, bf16[32,32,256]{2,1,0:T(8,128)(2,1)S(1)} %collective-permute-done.2.refs_2_, ...), custom_call_target="tpu_custom_call" | custom-call | bytes 1024 | tf_op jit(solution)/shard_map/add_own/pallas_call | solution.py:64
  27.3 8.8 %all-to-all-done.refs_2_ = bf16[32,64,256]{2,1,0:T(8,128)(2,1)S(1)} async-done(((bf16[32,64,256]{2,1,0:T(8,128)(2,1)}), bf16[32,64,256]{2,1,0:T(8,128)(2,1)S(1)}, u32[]{:S(2)}, u32[]{:S(2)}) %all-to-all-start) | async-done | bytes 1048608 | tf_op jit(solution)/shard_map/all_to_all | solution.py:482
  36.1 0.0 collective-permute-done.3.refs_1_
  36.1 2.0 %blend_rows.1 = (bf16[32,64,256]{2,1,0:T(8,128)(2,1)}, bf16[16,64,256]{2,1,0:T(8,128)(2,1)}, bf16[16,64,256]{2,1,0:T(8,128)(2,1)}, s32[8,128]{1,0:T(8,128)S(1)}) custom-call(s32[3]{0:T(128)S(1)} %pad_add_fusion.at, bf16[32,64,256]{2,1,0:T(8,128)(2,1)S(1)} %get-tuple-element.50.refs_0_, bf16[32,64,256]{2,1,0:T(8,128)(2,1)S(1)} %collective-permute-done.3.refs_1_, ...), custom_call_target="tpu_custom_call" | custom-call | bytes 1024 | tf_op jit(solution)/shard_map/blend_rows/pallas_call | solution.py:64
  38.2 0.1 collective-permute-start.4
  38.2 8.7 %all-to-all-start.1 = ((bf16[32,64,256]{2,1,0:T(8,128)(2,1)}), bf16[32,64,256]{2,1,0:T(8,128)(2,1)S(1)}, u32[]{:S(2)}, u32[]{:S(2)}) async-start(bf16[32,64,256]{2,1,0:T(8,128)(2,1)} %get-tuple-element.54.refs_2_), calls=%async_computation.1 | async-start | bytes 2097152 | tf_op jit(solution)/shard_map/all_to_all | solution.py:482
  47.0 1.5 %collective-permute-start.5 = (bf16[16,64,256]{2,1,0:T(8,128)(2,1)}, bf16[16,64,256]{2,1,0:T(8,128)(2,1)S(1)}, u32[]{:S(2)}, u32[]{:S(2)}) collective-permute-start(bf16[16,64,256]{2,1,0:T(8,128)(2,1)} %get-tuple-element.55), channel_id=1, source_target_pairs={{0,32},{32,0},{1,33},{33,1},{2,34},{34,2},{3,35},{35,3},{4,36},{36... | collective-permute-start | bytes 1572872 | tf_op jit(solution)/shard_map/ppermute | solution.py:487
  48.5 0.1 collective-permute-start.6
  48.6 1.7 %collective-permute-done.5.refs_0_ = bf16[16,64,256]{2,1,0:T(8,128)(2,1)S(1)} collective-permute-done((bf16[16,64,256]{2,1,0:T(8,128)(2,1)}, bf16[16,64,256]{2,1,0:T(8,128)(2,1)S(1)}, u32[]{:S(2)}, u32[]{:S(2)}) %collective-permute-start.5) | collective-permute-done | bytes 524320 | tf_op jit(solution)/shard_map/ppermute | solution.py:487
  50.2 0.7 collective-permute-done.6.refs_1_
  51.0 4.0 %write_rows.5 = (f32[256,8192]{1,0:T(8,128)}, s32[8,128]{1,0:T(8,128)S(1)}) custom-call(s32[3]{0:T(128)S(1)} %pad_add_fusion.at, bf16[16,64,256]{2,1,0:T(8,128)(2,1)S(1)} %collective-permute-done.5.refs_0_, bf16[16,64,256]{2,1,0:T(8,128)(2,1)S(1)} %collective-permute-done.6.refs_1_, bf16[32,64,256]{2,1,0:T(8,128)(2,1)} %get-tuple-element.54.refs_2_, ...), custom_call_target="tpu_custom_call" | custom-call | bytes 11534336 | tf_op jit(solution)/shard_map/write_rows/pallas_call | solution.py:64
  54.9 7.2 %all-to-all-done.1 = bf16[32,64,256]{2,1,0:T(8,128)(2,1)S(1)} async-done(((bf16[32,64,256]{2,1,0:T(8,128)(2,1)}), bf16[32,64,256]{2,1,0:T(8,128)(2,1)S(1)}, u32[]{:S(2)}, u32[]{:S(2)}) %all-to-all-start.1) | async-done | bytes 1048608 | tf_op jit(solution)/shard_map/all_to_all | solution.py:482
  62.1 3.4 %collective-permute-start.8 = (bf16[32,64,256]{2,1,0:T(8,128)(2,1)S(1)}, bf16[32,64,256]{2,1,0:T(8,128)(2,1)}, u32[]{:S(2)}, u32[]{:S(2)}) collective-permute-start(bf16[32,64,256]{2,1,0:T(8,128)(2,1)S(1)} %all-to-all-done.1), channel_id=1, source_target_pairs={{0,32},{32,0},{1,33},{33,1},{2,34},{34,2},{3,35},{35,3},{4,36},{36... | collective-permute-start | bytes 3145736 | tf_op jit(solution)/shard_map/ppermute | solution.py:487
  65.5 0.0 collective-permute-done.4.refs_0_
  65.5 0.0 collective-permute-start.7
  65.5 1.6 %split_planes.1 = (bf16[16,64,256]{2,1,0:T(8,128)(2,1)}, bf16[16,64,256]{2,1,0:T(8,128)(2,1)}, s32[8,128]{1,0:T(8,128)S(1)}) custom-call(s32[3]{0:T(128)S(1)} %pad_add_fusion.at, bf16[2,16,64,256]{3,2,1,0:T(8,128)(2,1)S(1)} %bitcast.12, bf16[2,16,64,256]{3,2,1,0:T(8,128)(2,1)S(1)} %bitcast.10, s32[8,128]{1,0:T(8,128)S(1)} %get-tuple-element.63.refs_2_), custom_call_target="tpu_custom_call" | custom-call | bytes 1024 | tf_op jit(solution)/shard_map/split_planes/pallas_call | solution.py:64
  67.2 0.1 collective-permute-start.9
  67.2 5.4 %all-to-all-start.2 = ((bf16[16,64,256]{2,1,0:T(8,128)(2,1)}), bf16[16,64,256]{2,1,0:T(8,128)(2,1)S(1)}, u32[]{:S(2)}, u32[]{:S(2)}) async-start(bf16[16,64,256]{2,1,0:T(8,128)(2,1)} %get-tuple-element.67), calls=%async_computation.2 | async-start | bytes 1048576 | tf_op jit(solution)/shard_map/all_to_all | solution.py:508
  72.6 0.0 collective-permute-done.8
  72.6 3.3 %place_back.1 = (bf16[16,2,256,256]{3,2,1,0:T(8,128)(2,1)}, s32[8,128]{1,0:T(8,128)S(1)}) custom-call(s32[3]{0:T(128)S(1)} %pad_add_fusion.at, bf16[2,16,64,256]{3,2,1,0:T(8,128)(2,1)S(1)} %bitcast.11, bf16[2,16,64,256]{3,2,1,0:T(8,128)(2,1)} %bitcast.7.refs_1_, s32[8,128]{1,0:T(8,128)S(1)} %get-tuple-element.64.refs_2_), custom_call_target="tpu_custom_call" | custom-call | bytes 1024 | tf_op jit(solution)/shard_map/place_back/pallas_call | solution.py:64
  75.9 0.0 collective-permute-done.7.refs_1_
  75.9 4.0 %write_rows.6 = (f32[256,8192]{1,0:T(8,128)}, s32[8,128]{1,0:T(8,128)S(1)}) custom-call(s32[3]{0:T(128)S(1)} %pad_add_fusion.at, bf16[32,64,256]{2,1,0:T(8,128)(2,1)S(1)} %collective-permute-done.4.refs_0_, bf16[32,64,256]{2,1,0:T(8,128)(2,1)} %collective-permute-done.7.refs_1_, ...), custom_call_target="tpu_custom_call", output_to_operand_aliasing={{0}: (3, {})} | custom-call | bytes 1024 | tf_op jit(solution)/shard_map/write_rows/pallas_call | solution.py:64
  79.9 0.6 collective-permute-done.9.refs_0_
  80.4 1.4 %collective-permute-start.11 = (bf16[16,64,256]{2,1,0:T(8,128)(2,1)S(1)}, bf16[16,64,256]{2,1,0:T(8,128)(2,1)S(1)}, u32[]{:S(2)}, u32[]{:S(2)}) collective-permute-start(bf16[16,64,256]{2,1,0:T(8,128)(2,1)S(1)} %collective-permute-done.9.refs_0_), channel_id=1, source_target_pairs={{0,32},{32,0},{1,33},{33,1},{2,34},{34,2},{3,35},{35,3},{4,36},{36... | collective-permute-start | bytes 1572872 | tf_op jit(solution)/shard_map/ppermute | solution.py:487
  81.8 1.4 %write_rows.7 = (bf16[16,2,256,256]{3,2,1,0:T(8,128)(2,1)}, s32[8,128]{1,0:T(8,128)S(1)}) custom-call(s32[3]{0:T(128)S(1)} %pad_add_fusion.at, bf16[16,64,256]{2,1,0:T(8,128)(2,1)S(1)} %collective-permute-done.9.refs_0_, bf16[16,2,256,256]{3,2,1,0:T(8,128)(2,1)} %get-tuple-element.71.refs_1_, ...), custom_call_target="tpu_custom_call", output_to_operand_aliasing={{0}: (2, {})} | custom-call | bytes 1024 | tf_op jit(solution)/shard_map/write_rows/pallas_call | solution.py:64
  83.2 0.0 all-to-all-done.2.refs_0_
  83.2 1.8 %collective-permute-start.10 = (bf16[16,64,256]{2,1,0:T(8,128)(2,1)S(1)}, bf16[16,64,256]{2,1,0:T(8,128)(2,1)S(1)}, u32[]{:S(2)}, u32[]{:S(2)}) collective-permute-start(bf16[16,64,256]{2,1,0:T(8,128)(2,1)S(1)} %all-to-all-done.2.refs_0_), channel_id=1, source_target_pairs={{0,32},{32,0},{1,33},{33,1},{2,34},{34,2},{3,35},{35,3},{4,36},{36... | collective-permute-start | bytes 1572872 | tf_op jit(solution)/shard_map/ppermute | solution.py:487
  85.0 0.0 collective-permute-done.11.refs_1_
  85.1 1.7 %write_rows.8 = (bf16[16,2,256,256]{3,2,1,0:T(8,128)(2,1)}, s32[8,128]{1,0:T(8,128)S(1)}) custom-call(s32[3]{0:T(128)S(1)} %pad_add_fusion.at, bf16[16,64,256]{2,1,0:T(8,128)(2,1)S(1)} %all-to-all-done.2.refs_0_, bf16[16,64,256]{2,1,0:T(8,128)(2,1)S(1)} %collective-permute-done.11.refs_1_, ...), custom_call_target="tpu_custom_call", output_to_operand_aliasing={{0}: (3, {})} | custom-call | bytes 4194304 | tf_op jit(solution)/shard_map/write_rows/pallas_call | solution.py:64
  86.7 0.0 collective-permute-done.10.refs_0_
  86.7 1.5 %write_rows.9 = (bf16[16,2,256,256]{3,2,1,0:T(8,128)(2,1)}, s32[8,128]{1,0:T(8,128)}) custom-call(s32[3]{0:T(128)S(1)} %pad_add_fusion.at, bf16[16,64,256]{2,1,0:T(8,128)(2,1)S(1)} %collective-permute-done.10.refs_0_, bf16[16,2,256,256]{3,2,1,0:T(8,128)(2,1)} %get-tuple-element.77.refs_1_, ...), custom_call_target="tpu_custom_call", output_to_operand_aliasing={{0}: (2, {})} | custom-call | bytes 1024 | tf_op jit(solution)/shard_map/write_rows/pallas_call | solution.py:64
Async XLA Ops:
  2.9 4.0 %collective-permute-start = (bf16[32,64,256]{2,1,0:T(8,128)(2,1)S(1)}, bf16[32,64,256]{2,1,0:T(8,128)(2,1)S(1)}, u32[]{:S(2)}, u32[]{:S(2)}) collective-permute-start(bf16[32,64,256]{2,1,0:T(8,128)(2,1)S(1)} %get-tuple-element.43), channel_id=1, source_target_pairs={{0,32},{32,0},{1,33},{33,1},{2,34},{34,2},{3,35},{35,3},{4,36},{36... | collective-permute-start | bytes 3145736 | tf_op jit(solution)/shard_map/ppermute | solution.py:487
  8.9 27.2 %collective-permute-start.3 = (bf16[32,64,256]{2,1,0:T(8,128)(2,1)}, bf16[32,64,256]{2,1,0:T(8,128)(2,1)S(1)}, u32[]{:S(2)}, u32[]{:S(2)}) collective-permute-start(bf16[32,64,256]{2,1,0:T(8,128)(2,1)} %get-tuple-element.51), channel_id=1, source_target_pairs={{0,64},{64,0},{1,65},{65,1},{2,66},{66,2},{3,67},{67,3},{4,68},{68... | collective-permute-start | bytes 3145736 | tf_op jit(solution)/shard_map/ppermute | solution.py:490
  10.3 25.8 %all-to-all-start = ((bf16[32,64,256]{2,1,0:T(8,128)(2,1)}), bf16[32,64,256]{2,1,0:T(8,128)(2,1)S(1)}, u32[]{:S(2)}, u32[]{:S(2)}) async-start(bf16[32,64,256]{2,1,0:T(8,128)(2,1)} %get-tuple-element.52), calls=%async_computation | async-start | bytes 2097152 | tf_op jit(solution)/shard_map/all_to_all | solution.py:482
  22.1 2.3 %collective-permute-start.1 = (bf16[32,32,256]{2,1,0:T(8,128)(2,1)S(1)}, bf16[32,32,256]{2,1,0:T(8,128)(2,1)S(1)}, u32[]{:S(2)}, u32[]{:S(2)}) collective-permute-start(bf16[32,32,256]{2,1,0:T(8,128)(2,1)S(1)} %get-tuple-element.47), channel_id=1, source_target_pairs={{0,32},{32,0},{1,33},{33,1},{2,34},{34,2},{3,35},{35,3},{4,36},{36... | collective-permute-start | bytes 1572872 | tf_op jit(solution)/shard_map/ppermute | solution.py:487
  22.8 2.3 %collective-permute-start.2 = (bf16[32,32,256]{2,1,0:T(8,128)(2,1)S(1)}, bf16[32,32,256]{2,1,0:T(8,128)(2,1)S(1)}, u32[]{:S(2)}, u32[]{:S(2)}) collective-permute-start(bf16[32,32,256]{2,1,0:T(8,128)(2,1)S(1)} %get-tuple-element.48), channel_id=1, source_target_pairs={{0,32},{32,0},{1,33},{33,1},{2,34},{34,2},{3,35},{35,3},{4,36},{36... | collective-permute-start | bytes 1572872 | tf_op jit(solution)/shard_map/ppermute | solution.py:487
  38.2 27.4 %collective-permute-start.4 = (bf16[32,64,256]{2,1,0:T(8,128)(2,1)}, bf16[32,64,256]{2,1,0:T(8,128)(2,1)S(1)}, u32[]{:S(2)}, u32[]{:S(2)}) collective-permute-start(bf16[32,64,256]{2,1,0:T(8,128)(2,1)} %get-tuple-element.54.refs_2_), channel_id=1, source_target_pairs={{0,64},{64,0},{1,65},{65,1},{2,66},{66,2},{3,67},{67,3},{4,68},{68... | collective-permute-start | bytes 3145736 | tf_op jit(solution)/shard_map/ppermute | solution.py:490
  38.2 23.9 %all-to-all-start.1 = ((bf16[32,64,256]{2,1,0:T(8,128)(2,1)}), bf16[32,64,256]{2,1,0:T(8,128)(2,1)S(1)}, u32[]{:S(2)}, u32[]{:S(2)}) async-start(bf16[32,64,256]{2,1,0:T(8,128)(2,1)} %get-tuple-element.54.refs_2_), calls=%async_computation.1 | async-start | bytes 2097152 | tf_op jit(solution)/shard_map/all_to_all | solution.py:482
  47.0 3.3 %collective-permute-start.5 = (bf16[16,64,256]{2,1,0:T(8,128)(2,1)}, bf16[16,64,256]{2,1,0:T(8,128)(2,1)S(1)}, u32[]{:S(2)}, u32[]{:S(2)}) collective-permute-start(bf16[16,64,256]{2,1,0:T(8,128)(2,1)} %get-tuple-element.55), channel_id=1, source_target_pairs={{0,32},{32,0},{1,33},{33,1},{2,34},{34,2},{3,35},{35,3},{4,36},{36... | collective-permute-start | bytes 1572872 | tf_op jit(solution)/shard_map/ppermute | solution.py:487
  48.5 2.5 %collective-permute-start.6 = (bf16[16,64,256]{2,1,0:T(8,128)(2,1)}, bf16[16,64,256]{2,1,0:T(8,128)(2,1)S(1)}, u32[]{:S(2)}, u32[]{:S(2)}) collective-permute-start(bf16[16,64,256]{2,1,0:T(8,128)(2,1)} %get-tuple-element.56), channel_id=1, source_target_pairs={{0,32},{32,0},{1,33},{33,1},{2,34},{34,2},{3,35},{35,3},{4,36},{36... | collective-permute-start | bytes 1572872 | tf_op jit(solution)/shard_map/ppermute | solution.py:487
  62.1 10.5 %collective-permute-start.8 = (bf16[32,64,256]{2,1,0:T(8,128)(2,1)S(1)}, bf16[32,64,256]{2,1,0:T(8,128)(2,1)}, u32[]{:S(2)}, u32[]{:S(2)}) collective-permute-start(bf16[32,64,256]{2,1,0:T(8,128)(2,1)S(1)} %all-to-all-done.1), channel_id=1, source_target_pairs={{0,32},{32,0},{1,33},{33,1},{2,34},{34,2},{3,35},{35,3},{4,36},{36... | collective-permute-start | bytes 3145736 | tf_op jit(solution)/shard_map/ppermute | solution.py:487
  65.5 10.3 %collective-permute-start.7 = (bf16[32,64,256]{2,1,0:T(8,128)(2,1)S(1)}, bf16[32,64,256]{2,1,0:T(8,128)(2,1)}, u32[]{:S(2)}, u32[]{:S(2)}) collective-permute-start(bf16[32,64,256]{2,1,0:T(8,128)(2,1)S(1)} %collective-permute-done.4.refs_0_), channel_id=1, source_target_pairs={{0,32},{32,0},{1,33},{33,1},{2,34},{34,2},{3,35},{35,3},{4,36},{36... | collective-permute-start | bytes 3145736 | tf_op jit(solution)/shard_map/ppermute | solution.py:487
  67.2 13.3 %collective-permute-start.9 = (bf16[16,64,256]{2,1,0:T(8,128)(2,1)}, bf16[16,64,256]{2,1,0:T(8,128)(2,1)S(1)}, u32[]{:S(2)}, u32[]{:S(2)}) collective-permute-start(bf16[16,64,256]{2,1,0:T(8,128)(2,1)} %get-tuple-element.68), channel_id=1, source_target_pairs={{0,64},{64,0},{1,65},{65,1},{2,66},{66,2},{3,67},{67,3},{4,68},{68... | collective-permute-start | bytes 1572872 | tf_op jit(solution)/shard_map/ppermute | solution.py:490
  67.2 16.0 %all-to-all-start.2 = ((bf16[16,64,256]{2,1,0:T(8,128)(2,1)}), bf16[16,64,256]{2,1,0:T(8,128)(2,1)S(1)}, u32[]{:S(2)}, u32[]{:S(2)}) async-start(bf16[16,64,256]{2,1,0:T(8,128)(2,1)} %get-tuple-element.67), calls=%async_computation.2 | async-start | bytes 1048576 | tf_op jit(solution)/shard_map/all_to_all | solution.py:508
  80.4 4.6 %collective-permute-start.11 = (bf16[16,64,256]{2,1,0:T(8,128)(2,1)S(1)}, bf16[16,64,256]{2,1,0:T(8,128)(2,1)S(1)}, u32[]{:S(2)}, u32[]{:S(2)}) collective-permute-start(bf16[16,64,256]{2,1,0:T(8,128)(2,1)S(1)} %collective-permute-done.9.refs_0_), channel_id=1, source_target_pairs={{0,32},{32,0},{1,33},{33,1},{2,34},{34,2},{3,35},{35,3},{4,36},{36... | collective-permute-start | bytes 1572872 | tf_op jit(solution)/shard_map/ppermute | solution.py:487
  83.2 3.5 %collective-permute-start.10 = (bf16[16,64,256]{2,1,0:T(8,128)(2,1)S(1)}, bf16[16,64,256]{2,1,0:T(8,128)(2,1)S(1)}, u32[]{:S(2)}, u32[]{:S(2)}) collective-permute-start(bf16[16,64,256]{2,1,0:T(8,128)(2,1)S(1)} %all-to-all-done.2.refs_0_), channel_id=1, source_target_pairs={{0,32},{32,0},{1,33},{33,1},{2,34},{34,2},{3,35},{35,3},{4,36},{36... | collective-permute-start | bytes 1572872 | tf_op jit(solution)/shard_map/ppermute | solution.py:487

commit v14 on v13

--- a/solution.py
+++ b/solution.py
@@ -88,7 +88,11 @@
 
 
 def each(count, work):
-    pl.loop(0, count)(work)
+    if count > 4:
+        pl.loop(0, count)(work)
+    else:
+        for i in range(count):
+            work(i)
 
 
 def first_row(at, core, chip, start, xl=None):

time: 88.9 us -> 88.7 us (level)
  no operation moved by 1% of the time
where the time goes in v14:
time: 88.7 us; the launch traced here: 88.1 us
  starting transfers between devices  35.9 us (40%)
  Pallas kernels  30.3 us (34%)
  waiting for transfers between devices  21 us (24%)
    pallas_call x13, Pallas kernels, run(): pl.pallas_call(ordered, out_shape=[*outs, TOKEN], grid_spec=pltpu.Prefetc...  30.3 us
    all_to_all x2, starting transfers between devices, exchange(): lax.all_to_all(tiles, AXES, split_axis=0, concat_axis=0, axis_index_group...  18.2 us
    all_to_all x2, waiting for transfers between devices, exchange(): lax.all_to_all(tiles, AXES, split_axis=0, concat_axis=0, axis_index_group...  15.8 us
    ppermute x9, starting transfers between devices, core(): return lax.ppermute(tiles, 'c', swap)  10.7 us
    all_to_all x1, starting transfers between devices, per_device(): lax.all_to_all(first, ('y', 'z'), split_axis=0, concat_axis=0, tiled=True)  5.35 us
    ppermute x9, waiting for transfers between devices, core(): return lax.ppermute(tiles, 'c', swap)  4.61 us
  transfers between devices with their start and end apart: 15, of which 7 were waited for; matrix products, arithmetic and copies ran while one was open for 0% of the time, Pallas kernels for 26%

profile of v14, /device:TPU:1, one launch (start us, length us, event | category | flops | bytes accessed | tf_op | source)
XLA Modules:
  0.0 88.1 jit_solution(9975783697129253982)
XLA Ops:
  0.6 0.1 pad_add_fusion.at
  0.7 2.2 %cast_rows.1 = (bf16[32,64,256]{2,1,0:T(8,128)(2,1)S(1)}, s32[8,128]{1,0:T(8,128)S(1)}) custom-call(s32[3]{0:T(128)S(1)} %pad_add_fusion.at, f32[256,8192]{1,0:T(8,128)} %bitcast.14), custom_call_target="tpu_custom_call" | custom-call | bytes 1024 | tf_op jit(solution)/shard_map/cast_rows/pallas_call | solution.py:64
  2.9 1.5 %collective-permute-start = (bf16[32,64,256]{2,1,0:T(8,128)(2,1)S(1)}, bf16[32,64,256]{2,1,0:T(8,128)(2,1)S(1)}, u32[]{:S(2)}, u32[]{:S(2)}) collective-permute-start(bf16[32,64,256]{2,1,0:T(8,128)(2,1)S(1)} %get-tuple-element.43), channel_id=1, source_target_pairs={{0,32},{32,0},{1,33},{33,1},{2,34},{34,2},{3,35},{35,3},{4,36},{36... | collective-permute-start | bytes 3145736 | tf_op jit(solution)/shard_map/ppermute | solution.py:491
  4.4 2.5 %pick_rows.1 = (bf16[2,16,64,256]{3,2,1,0:T(8,128)(2,1)S(1)}, f32[64,8192]{1,0:T(8,128)S(1)}, s32[8,128]{1,0:T(8,128)S(1)}) custom-call(s32[3]{0:T(128)S(1)} %pad_add_fusion.at, bf16[16,2,256,256]{3,2,1,0:T(8,128)(2,1)} %bitcast.19, f32[256,8192]{1,0:T(8,128)} %bitcast.15, s32[8,128]{1,0:T(8,128)S(1)} %get-tuple-element.41.refs_2_), custom_call_target="tpu_custom_call" | custom-call | bytes 1024 | tf_op jit(solution)/shard_map/pick_rows/pallas_call | solution.py:64
  6.9 0.0 collective-permute-done.refs_1_
  6.9 2.0 %add_theirs.1 = (bf16[32,64,256]{2,1,0:T(8,128)(2,1)}, bf16[32,64,256]{2,1,0:T(8,128)(2,1)}, s32[8,128]{1,0:T(8,128)S(1)}) custom-call(s32[3]{0:T(128)S(1)} %pad_add_fusion.at, f32[64,8192]{1,0:T(8,128)S(1)} %get-tuple-element.42.refs_0_, bf16[32,64,256]{2,1,0:T(8,128)(2,1)S(1)} %collective-permute-done.refs_1_, bf16[32,64,256]{2,1,0:T(8,128)(2,1)S(1)} %bitcast.13, ...), custom_call_target="tpu_custom_call" | custom-call | bytes 1024 | tf_op jit(solution)/shard_map/add_theirs/pallas_call | solution.py:64
  8.9 1.4 %collective-permute-start.3 = (bf16[32,64,256]{2,1,0:T(8,128)(2,1)}, bf16[32,64,256]{2,1,0:T(8,128)(2,1)S(1)}, u32[]{:S(2)}, u32[]{:S(2)}) collective-permute-start(bf16[32,64,256]{2,1,0:T(8,128)(2,1)} %get-tuple-element.51), channel_id=1, source_target_pairs={{0,64},{64,0},{1,65},{65,1},{2,66},{66,2},{3,67},{67,3},{4,68},{68... | collective-permute-start | bytes 3145736 | tf_op jit(solution)/shard_map/ppermute | solution.py:494
  10.3 9.6 %all-to-all-start = ((bf16[32,64,256]{2,1,0:T(8,128)(2,1)}), bf16[32,64,256]{2,1,0:T(8,128)(2,1)S(1)}, u32[]{:S(2)}, u32[]{:S(2)}) async-start(bf16[32,64,256]{2,1,0:T(8,128)(2,1)} %get-tuple-element.52), calls=%async_computation | async-start | bytes 2097152 | tf_op jit(solution)/shard_map/all_to_all | solution.py:486
  19.9 2.2 %cast_own.1 = (bf16[32,32,256]{2,1,0:T(8,128)(2,1)S(1)}, bf16[32,32,256]{2,1,0:T(8,128)(2,1)S(1)}, s32[8,128]{1,0:T(8,128)S(1)}) custom-call(s32[3]{0:T(128)S(1)} %pad_add_fusion.at, f32[256,8192]{1,0:T(8,128)} %bitcast.16, s32[8,128]{1,0:T(8,128)S(1)} %get-tuple-element.46.refs_1_), custom_call_target="tpu_custom_call" | custom-call | bytes 1024 | tf_op jit(solution)/shard_map/cast_own/pallas_call | solution.py:64
  22.0 0.8 collective-permute-start.1
  22.8 0.1 collective-permute-start.2
  22.9 1.4 %collective-permute-done.1.refs_1_ = bf16[32,32,256]{2,1,0:T(8,128)(2,1)S(1)} collective-permute-done((bf16[32,32,256]{2,1,0:T(8,128)(2,1)S(1)}, bf16[32,32,256]{2,1,0:T(8,128)(2,1)S(1)}, u32[]{:S(2)}, u32[]{:S(2)}) %collective-permute-start.1) | collective-permute-done | bytes 524320 | tf_op jit(solution)/shard_map/ppermute | solution.py:491
  24.4 0.7 collective-permute-done.2.refs_2_
  25.1 2.2 %add_own.1 = (bf16[32,64,256]{2,1,0:T(8,128)(2,1)S(1)}, s32[8,128]{1,0:T(8,128)S(1)}) custom-call(s32[3]{0:T(128)S(1)} %pad_add_fusion.at, f32[256,8192]{1,0:T(8,128)} %bitcast.17, bf16[32,32,256]{2,1,0:T(8,128)(2,1)S(1)} %collective-permute-done.1.refs_1_, bf16[32,32,256]{2,1,0:T(8,128)(2,1)S(1)} %collective-permute-done.2.refs_2_, ...), custom_call_target="tpu_custom_call" | custom-call | bytes 1024 | tf_op jit(solution)/shard_map/add_own/pallas_call | solution.py:64
  27.3 8.8 %all-to-all-done.refs_2_ = bf16[32,64,256]{2,1,0:T(8,128)(2,1)S(1)} async-done(((bf16[32,64,256]{2,1,0:T(8,128)(2,1)}), bf16[32,64,256]{2,1,0:T(8,128)(2,1)S(1)}, u32[]{:S(2)}, u32[]{:S(2)}) %all-to-all-start) | async-done | bytes 1048608 | tf_op jit(solution)/shard_map/all_to_all | solution.py:486
  36.1 0.0 collective-permute-done.3.refs_1_
  36.1 2.0 %blend_rows.1 = (bf16[32,64,256]{2,1,0:T(8,128)(2,1)}, bf16[16,64,256]{2,1,0:T(8,128)(2,1)}, bf16[16,64,256]{2,1,0:T(8,128)(2,1)}, s32[8,128]{1,0:T(8,128)S(1)}) custom-call(s32[3]{0:T(128)S(1)} %pad_add_fusion.at, bf16[32,64,256]{2,1,0:T(8,128)(2,1)S(1)} %get-tuple-element.50.refs_0_, bf16[32,64,256]{2,1,0:T(8,128)(2,1)S(1)} %collective-permute-done.3.refs_1_, ...), custom_call_target="tpu_custom_call" | custom-call | bytes 1024 | tf_op jit(solution)/shard_map/blend_rows/pallas_call | solution.py:64
  38.1 0.1 collective-permute-start.4
  38.2 8.6 %all-to-all-start.1 = ((bf16[32,64,256]{2,1,0:T(8,128)(2,1)}), bf16[32,64,256]{2,1,0:T(8,128)(2,1)S(1)}, u32[]{:S(2)}, u32[]{:S(2)}) async-start(bf16[32,64,256]{2,1,0:T(8,128)(2,1)} %get-tuple-element.54.refs_2_), calls=%async_computation.1 | async-start | bytes 2097152 | tf_op jit(solution)/shard_map/all_to_all | solution.py:486
  46.8 1.6 %collective-permute-start.5 = (bf16[16,64,256]{2,1,0:T(8,128)(2,1)}, bf16[16,64,256]{2,1,0:T(8,128)(2,1)S(1)}, u32[]{:S(2)}, u32[]{:S(2)}) collective-permute-start(bf16[16,64,256]{2,1,0:T(8,128)(2,1)} %get-tuple-element.55), channel_id=1, source_target_pairs={{0,32},{32,0},{1,33},{33,1},{2,34},{34,2},{3,35},{35,3},{4,36},{36... | collective-permute-start | bytes 1572872 | tf_op jit(solution)/shard_map/ppermute | solution.py:491
  48.4 0.1 collective-permute-start.6
  48.5 1.7 %collective-permute-done.5.refs_0_ = bf16[16,64,256]{2,1,0:T(8,128)(2,1)S(1)} collective-permute-done((bf16[16,64,256]{2,1,0:T(8,128)(2,1)}, bf16[16,64,256]{2,1,0:T(8,128)(2,1)S(1)}, u32[]{:S(2)}, u32[]{:S(2)}) %collective-permute-start.5) | collective-permute-done | bytes 524320 | tf_op jit(solution)/shard_map/ppermute | solution.py:491
  50.2 0.7 collective-permute-done.6.refs_1_
  50.9 4.0 %write_rows.5 = (f32[256,8192]{1,0:T(8,128)}, s32[8,128]{1,0:T(8,128)S(1)}) custom-call(s32[3]{0:T(128)S(1)} %pad_add_fusion.at, bf16[16,64,256]{2,1,0:T(8,128)(2,1)S(1)} %collective-permute-done.5.refs_0_, bf16[16,64,256]{2,1,0:T(8,128)(2,1)S(1)} %collective-permute-done.6.refs_1_, bf16[32,64,256]{2,1,0:T(8,128)(2,1)} %get-tuple-element.54.refs_2_, ...), custom_call_target="tpu_custom_call" | custom-call | bytes 11534336 | tf_op jit(solution)/shard_map/write_rows/pallas_call | solution.py:64
  54.9 7.0 %all-to-all-done.1 = bf16[32,64,256]{2,1,0:T(8,128)(2,1)S(1)} async-done(((bf16[32,64,256]{2,1,0:T(8,128)(2,1)}), bf16[32,64,256]{2,1,0:T(8,128)(2,1)S(1)}, u32[]{:S(2)}, u32[]{:S(2)}) %all-to-all-start.1) | async-done | bytes 1048608 | tf_op jit(solution)/shard_map/all_to_all | solution.py:486
  61.9 3.5 %collective-permute-start.8 = (bf16[32,64,256]{2,1,0:T(8,128)(2,1)S(1)}, bf16[32,64,256]{2,1,0:T(8,128)(2,1)}, u32[]{:S(2)}, u32[]{:S(2)}) collective-permute-start(bf16[32,64,256]{2,1,0:T(8,128)(2,1)S(1)} %all-to-all-done.1), channel_id=1, source_target_pairs={{0,32},{32,0},{1,33},{33,1},{2,34},{34,2},{3,35},{35,3},{4,36},{36... | collective-permute-start | bytes 3145736 | tf_op jit(solution)/shard_map/ppermute | solution.py:491
  65.4 0.0 collective-permute-done.4.refs_0_
  65.4 0.0 collective-permute-start.7
  65.4 1.6 %split_planes.1 = (bf16[16,64,256]{2,1,0:T(8,128)(2,1)}, bf16[16,64,256]{2,1,0:T(8,128)(2,1)}, s32[8,128]{1,0:T(8,128)S(1)}) custom-call(s32[3]{0:T(128)S(1)} %pad_add_fusion.at, bf16[2,16,64,256]{3,2,1,0:T(8,128)(2,1)S(1)} %bitcast.12, bf16[2,16,64,256]{3,2,1,0:T(8,128)(2,1)S(1)} %bitcast.10, s32[8,128]{1,0:T(8,128)S(1)} %get-tuple-element.63.refs_2_), custom_call_target="tpu_custom_call" | custom-call | bytes 1024 | tf_op jit(solution)/shard_map/split_planes/pallas_call | solution.py:64
  67.0 0.1 collective-permute-start.9
  67.1 5.4 %all-to-all-start.2 = ((bf16[16,64,256]{2,1,0:T(8,128)(2,1)}), bf16[16,64,256]{2,1,0:T(8,128)(2,1)S(1)}, u32[]{:S(2)}, u32[]{:S(2)}) async-start(bf16[16,64,256]{2,1,0:T(8,128)(2,1)} %get-tuple-element.67), calls=%async_computation.2 | async-start | bytes 1048576 | tf_op jit(solution)/shard_map/all_to_all | solution.py:512
  72.5 0.0 collective-permute-done.8
  72.5 3.2 %place_back.1 = (bf16[16,2,256,256]{3,2,1,0:T(8,128)(2,1)}, s32[8,128]{1,0:T(8,128)S(1)}) custom-call(s32[3]{0:T(128)S(1)} %pad_add_fusion.at, bf16[2,16,64,256]{3,2,1,0:T(8,128)(2,1)S(1)} %bitcast.11, bf16[2,16,64,256]{3,2,1,0:T(8,128)(2,1)} %bitcast.7.refs_1_, s32[8,128]{1,0:T(8,128)S(1)} %get-tuple-element.64.refs_2_), custom_call_target="tpu_custom_call" | custom-call | bytes 1024 | tf_op jit(solution)/shard_map/place_back/pallas_call | solution.py:64
  75.7 0.0 collective-permute-done.7.refs_1_
  75.8 4.0 %write_rows.6 = (f32[256,8192]{1,0:T(8,128)}, s32[8,128]{1,0:T(8,128)S(1)}) custom-call(s32[3]{0:T(128)S(1)} %pad_add_fusion.at, bf16[32,64,256]{2,1,0:T(8,128)(2,1)S(1)} %collective-permute-done.4.refs_0_, bf16[32,64,256]{2,1,0:T(8,128)(2,1)} %collective-permute-done.7.refs_1_, ...), custom_call_target="tpu_custom_call", output_to_operand_aliasing={{0}: (3, {})} | custom-call | bytes 1024 | tf_op jit(solution)/shard_map/write_rows/pallas_call | solution.py:64
  79.7 0.6 collective-permute-done.9.refs_0_
  80.3 1.4 %collective-permute-start.11 = (bf16[16,64,256]{2,1,0:T(8,128)(2,1)S(1)}, bf16[16,64,256]{2,1,0:T(8,128)(2,1)S(1)}, u32[]{:S(2)}, u32[]{:S(2)}) collective-permute-start(bf16[16,64,256]{2,1,0:T(8,128)(2,1)S(1)} %collective-permute-done.9.refs_0_), channel_id=1, source_target_pairs={{0,32},{32,0},{1,33},{33,1},{2,34},{34,2},{3,35},{35,3},{4,36},{36... | collective-permute-start | bytes 1572872 | tf_op jit(solution)/shard_map/ppermute | solution.py:491
  81.7 1.4 %write_rows.7 = (bf16[16,2,256,256]{3,2,1,0:T(8,128)(2,1)}, s32[8,128]{1,0:T(8,128)S(1)}) custom-call(s32[3]{0:T(128)S(1)} %pad_add_fusion.at, bf16[16,64,256]{2,1,0:T(8,128)(2,1)S(1)} %collective-permute-done.9.refs_0_, bf16[16,2,256,256]{3,2,1,0:T(8,128)(2,1)} %get-tuple-element.71.refs_1_, ...), custom_call_target="tpu_custom_call", output_to_operand_aliasing={{0}: (2, {})} | custom-call | bytes 1024 | tf_op jit(solution)/shard_map/write_rows/pallas_call | solution.py:64
  83.1 0.0 all-to-all-done.2.refs_0_
  83.1 1.8 %collective-permute-start.10 = (bf16[16,64,256]{2,1,0:T(8,128)(2,1)S(1)}, bf16[16,64,256]{2,1,0:T(8,128)(2,1)S(1)}, u32[]{:S(2)}, u32[]{:S(2)}) collective-permute-start(bf16[16,64,256]{2,1,0:T(8,128)(2,1)S(1)} %all-to-all-done.2.refs_0_), channel_id=1, source_target_pairs={{0,32},{32,0},{1,33},{33,1},{2,34},{34,2},{3,35},{35,3},{4,36},{36... | collective-permute-start | bytes 1572872 | tf_op jit(solution)/shard_map/ppermute | solution.py:491
  84.9 0.0 collective-permute-done.11.refs_1_
  84.9 1.7 %write_rows.8 = (bf16[16,2,256,256]{3,2,1,0:T(8,128)(2,1)}, s32[8,128]{1,0:T(8,128)S(1)}) custom-call(s32[3]{0:T(128)S(1)} %pad_add_fusion.at, bf16[16,64,256]{2,1,0:T(8,128)(2,1)S(1)} %all-to-all-done.2.refs_0_, bf16[16,64,256]{2,1,0:T(8,128)(2,1)S(1)} %collective-permute-done.11.refs_1_, ...), custom_call_target="tpu_custom_call", output_to_operand_aliasing={{0}: (3, {})} | custom-call | bytes 4194304 | tf_op jit(solution)/shard_map/write_rows/pallas_call | solution.py:64
  86.6 0.0 collective-permute-done.10.refs_0_
  86.6 1.4 %write_rows.9 = (bf16[16,2,256,256]{3,2,1,0:T(8,128)(2,1)}, s32[8,128]{1,0:T(8,128)}) custom-call(s32[3]{0:T(128)S(1)} %pad_add_fusion.at, bf16[16,64,256]{2,1,0:T(8,128)(2,1)S(1)} %collective-permute-done.10.refs_0_, bf16[16,2,256,256]{3,2,1,0:T(8,128)(2,1)} %get-tuple-element.77.refs_1_, ...), custom_call_target="tpu_custom_call", output_to_operand_aliasing={{0}: (2, {})} | custom-call | bytes 1024 | tf_op jit(solution)/shard_map/write_rows/pallas_call | solution.py:64
Async XLA Ops:
  2.9 4.0 %collective-permute-start = (bf16[32,64,256]{2,1,0:T(8,128)(2,1)S(1)}, bf16[32,64,256]{2,1,0:T(8,128)(2,1)S(1)}, u32[]{:S(2)}, u32[]{:S(2)}) collective-permute-start(bf16[32,64,256]{2,1,0:T(8,128)(2,1)S(1)} %get-tuple-element.43), channel_id=1, source_target_pairs={{0,32},{32,0},{1,33},{33,1},{2,34},{34,2},{3,35},{35,3},{4,36},{36... | collective-permute-start | bytes 3145736 | tf_op jit(solution)/shard_map/ppermute | solution.py:491
  8.9 27.2 %collective-permute-start.3 = (bf16[32,64,256]{2,1,0:T(8,128)(2,1)}, bf16[32,64,256]{2,1,0:T(8,128)(2,1)S(1)}, u32[]{:S(2)}, u32[]{:S(2)}) collective-permute-start(bf16[32,64,256]{2,1,0:T(8,128)(2,1)} %get-tuple-element.51), channel_id=1, source_target_pairs={{0,64},{64,0},{1,65},{65,1},{2,66},{66,2},{3,67},{67,3},{4,68},{68... | collective-permute-start | bytes 3145736 | tf_op jit(solution)/shard_map/ppermute | solution.py:494
  10.3 25.8 %all-to-all-start = ((bf16[32,64,256]{2,1,0:T(8,128)(2,1)}), bf16[32,64,256]{2,1,0:T(8,128)(2,1)S(1)}, u32[]{:S(2)}, u32[]{:S(2)}) async-start(bf16[32,64,256]{2,1,0:T(8,128)(2,1)} %get-tuple-element.52), calls=%async_computation | async-start | bytes 2097152 | tf_op jit(solution)/shard_map/all_to_all | solution.py:486
  22.0 2.3 %collective-permute-start.1 = (bf16[32,32,256]{2,1,0:T(8,128)(2,1)S(1)}, bf16[32,32,256]{2,1,0:T(8,128)(2,1)S(1)}, u32[]{:S(2)}, u32[]{:S(2)}) collective-permute-start(bf16[32,32,256]{2,1,0:T(8,128)(2,1)S(1)} %get-tuple-element.47), channel_id=1, source_target_pairs={{0,32},{32,0},{1,33},{33,1},{2,34},{34,2},{3,35},{35,3},{4,36},{36... | collective-permute-start | bytes 1572872 | tf_op jit(solution)/shard_map/ppermute | solution.py:491
  22.8 2.3 %collective-permute-start.2 = (bf16[32,32,256]{2,1,0:T(8,128)(2,1)S(1)}, bf16[32,32,256]{2,1,0:T(8,128)(2,1)S(1)}, u32[]{:S(2)}, u32[]{:S(2)}) collective-permute-start(bf16[32,32,256]{2,1,0:T(8,128)(2,1)S(1)} %get-tuple-element.48), channel_id=1, source_target_pairs={{0,32},{32,0},{1,33},{33,1},{2,34},{34,2},{3,35},{35,3},{4,36},{36... | collective-permute-start | bytes 1572872 | tf_op jit(solution)/shard_map/ppermute | solution.py:491
  38.1 27.3 %collective-permute-start.4 = (bf16[32,64,256]{2,1,0:T(8,128)(2,1)}, bf16[32,64,256]{2,1,0:T(8,128)(2,1)S(1)}, u32[]{:S(2)}, u32[]{:S(2)}) collective-permute-start(bf16[32,64,256]{2,1,0:T(8,128)(2,1)} %get-tuple-element.54.refs_2_), channel_id=1, source_target_pairs={{0,64},{64,0},{1,65},{65,1},{2,66},{66,2},{3,67},{67,3},{4,68},{68... | collective-permute-start | bytes 3145736 | tf_op jit(solution)/shard_map/ppermute | solution.py:494
  38.2 23.7 %all-to-all-start.1 = ((bf16[32,64,256]{2,1,0:T(8,128)(2,1)}), bf16[32,64,256]{2,1,0:T(8,128)(2,1)S(1)}, u32[]{:S(2)}, u32[]{:S(2)}) async-start(bf16[32,64,256]{2,1,0:T(8,128)(2,1)} %get-tuple-element.54.refs_2_), calls=%async_computation.1 | async-start | bytes 2097152 | tf_op jit(solution)/shard_map/all_to_all | solution.py:486
  46.8 3.3 %collective-permute-start.5 = (bf16[16,64,256]{2,1,0:T(8,128)(2,1)}, bf16[16,64,256]{2,1,0:T(8,128)(2,1)S(1)}, u32[]{:S(2)}, u32[]{:S(2)}) collective-permute-start(bf16[16,64,256]{2,1,0:T(8,128)(2,1)} %get-tuple-element.55), channel_id=1, source_target_pairs={{0,32},{32,0},{1,33},{33,1},{2,34},{34,2},{3,35},{35,3},{4,36},{36... | collective-permute-start | bytes 1572872 | tf_op jit(solution)/shard_map/ppermute | solution.py:491
  48.4 2.5 %collective-permute-start.6 = (bf16[16,64,256]{2,1,0:T(8,128)(2,1)}, bf16[16,64,256]{2,1,0:T(8,128)(2,1)S(1)}, u32[]{:S(2)}, u32[]{:S(2)}) collective-permute-start(bf16[16,64,256]{2,1,0:T(8,128)(2,1)} %get-tuple-element.56), channel_id=1, source_target_pairs={{0,32},{32,0},{1,33},{33,1},{2,34},{34,2},{3,35},{35,3},{4,36},{36... | collective-permute-start | bytes 1572872 | tf_op jit(solution)/shard_map/ppermute | solution.py:491
  61.9 10.6 %collective-permute-start.8 = (bf16[32,64,256]{2,1,0:T(8,128)(2,1)S(1)}, bf16[32,64,256]{2,1,0:T(8,128)(2,1)}, u32[]{:S(2)}, u32[]{:S(2)}) collective-permute-start(bf16[32,64,256]{2,1,0:T(8,128)(2,1)S(1)} %all-to-all-done.1), channel_id=1, source_target_pairs={{0,32},{32,0},{1,33},{33,1},{2,34},{34,2},{3,35},{35,3},{4,36},{36... | collective-permute-start | bytes 3145736 | tf_op jit(solution)/shard_map/ppermute | solution.py:491
  65.4 10.3 %collective-permute-start.7 = (bf16[32,64,256]{2,1,0:T(8,128)(2,1)S(1)}, bf16[32,64,256]{2,1,0:T(8,128)(2,1)}, u32[]{:S(2)}, u32[]{:S(2)}) collective-permute-start(bf16[32,64,256]{2,1,0:T(8,128)(2,1)S(1)} %collective-permute-done.4.refs_0_), channel_id=1, source_target_pairs={{0,32},{32,0},{1,33},{33,1},{2,34},{34,2},{3,35},{35,3},{4,36},{36... | collective-permute-start | bytes 3145736 | tf_op jit(solution)/shard_map/ppermute | solution.py:491
  67.0 13.3 %collective-permute-start.9 = (bf16[16,64,256]{2,1,0:T(8,128)(2,1)}, bf16[16,64,256]{2,1,0:T(8,128)(2,1)S(1)}, u32[]{:S(2)}, u32[]{:S(2)}) collective-permute-start(bf16[16,64,256]{2,1,0:T(8,128)(2,1)} %get-tuple-element.68), channel_id=1, source_target_pairs={{0,64},{64,0},{1,65},{65,1},{2,66},{66,2},{3,67},{67,3},{4,68},{68... | collective-permute-start | bytes 1572872 | tf_op jit(solution)/shard_map/ppermute | solution.py:494
  67.1 16.0 %all-to-all-start.2 = ((bf16[16,64,256]{2,1,0:T(8,128)(2,1)}), bf16[16,64,256]{2,1,0:T(8,128)(2,1)S(1)}, u32[]{:S(2)}, u32[]{:S(2)}) async-start(bf16[16,64,256]{2,1,0:T(8,128)(2,1)} %get-tuple-element.67), calls=%async_computation.2 | async-start | bytes 1048576 | tf_op jit(solution)/shard_map/all_to_all | solution.py:512
  80.3 4.6 %collective-permute-start.11 = (bf16[16,64,256]{2,1,0:T(8,128)(2,1)S(1)}, bf16[16,64,256]{2,1,0:T(8,128)(2,1)S(1)}, u32[]{:S(2)}, u32[]{:S(2)}) collective-permute-start(bf16[16,64,256]{2,1,0:T(8,128)(2,1)S(1)} %collective-permute-done.9.refs_0_), channel_id=1, source_target_pairs={{0,32},{32,0},{1,33},{33,1},{2,34},{34,2},{3,35},{35,3},{4,36},{36... | collective-permute-start | bytes 1572872 | tf_op jit(solution)/shard_map/ppermute | solution.py:491
  83.1 3.5 %collective-permute-start.10 = (bf16[16,64,256]{2,1,0:T(8,128)(2,1)S(1)}, bf16[16,64,256]{2,1,0:T(8,128)(2,1)S(1)}, u32[]{:S(2)}, u32[]{:S(2)}) collective-permute-start(bf16[16,64,256]{2,1,0:T(8,128)(2,1)S(1)} %all-to-all-done.2.refs_0_), channel_id=1, source_target_pairs={{0,32},{32,0},{1,33},{33,1},{2,34},{34,2},{3,35},{35,3},{4,36},{36... | collective-permute-start | bytes 1572872 | tf_op jit(solution)/shard_map/ppermute | solution.py:491
